TPU v7x, 32 devices: a whole 2x2x4 slice. The times are simulated.
32 devices in a mesh: dp: 2 (over x), expert: 16 (over z, y, core).
Axes of the slice: x: 2, y: 2, z: 4, core: 2. Of those that a mesh axis runs over, the one named last changes fastest.
Arguments:
- queries: bfloat16 [256, 4096], P(('dp', 'expert')), may hold values from -400 to 400
- new_kv: bfloat16 [256, 2, 1024], P(('dp', 'expert')), may hold values from -5 to 5
- cache_keys: bfloat16 [256, 32, 1024], P(('dp', 'expert')), may hold values from -6 to 6
- cache_values: bfloat16 [256, 32, 1024], P(('dp', 'expert')), may hold values from -5 to 5
- lengths: int32 [256], P(('dp', 'expert')), may hold values from 2 to 32, as said below
- residual: bfloat16 [256, 4096], P(('dp', 'expert')), may hold values from -6 to 6
- norm_gain: bfloat16 [4096], replicated, may hold values from 0.099609375 to 1.8984375
- routes: int32 [256, 8], P(('dp', 'expert')), may hold values from 0 to 15, all different within a row; in each aligned block of 8 rows (0 to 7, 8 to 15, ...) at most 8 rows name the same one
- route_weights: float32 [256, 8], P(('dp', 'expert')), may hold values from 0.05 to 1
- gate_codes: float32 [16, 1024, 2048], P('expert', None, 'dp'), may hold values from 0 to 65535, as said below
- gate_scales: bfloat16 [16, 32, 2048], P('expert', None, 'dp'), may hold values from 0.0017166138 to 0.006866455
- up_codes: float32 [16, 1024, 2048], P('expert', None, 'dp'), may hold values from 0 to 65535, as said below
- up_scales: bfloat16 [16, 32, 2048], P('expert', None, 'dp'), may hold values from 0.0017166138 to 0.006866455
- down_codes: float32 [16, 512, 4096], P('expert', None, 'dp'), may hold values from 0 to 65535, as said below
- down_scales: bfloat16 [16, 16, 4096], P('expert', None, 'dp'), may hold values from 0.0024261475 to 0.00970459
Outputs:
- layer_out: bfloat16 [256, 4096], P(('dp', 'expert'))
Inputs may be any that keep to these rules, and one draw needn't show every extreme that they name: `routes`: in the 8 rows of one device no expert is named more than 8 times; the 8 experts of a row differ. `lengths`: every device holds a row with all 32 positions valid. `gate_codes`: every entry is a whole number. `up_codes`: every entry is a whole number. `down_codes`: every entry is a whole number.
All inputs are finite; a program needn't handle non-finite values.
Results may differ from a plain program's by a relative error of at most 0.015.
Values may be sent and summed in bfloat16 or wider, within the bound.
No kernel may reach another device: no remote copies, remote signals or barrier semaphores. Data moves between devices by JAX's collectives and lax.ppermute only.
A program may use at most 128 MiB of HBM per device.

v0:
```python
import jax
import jax.numpy as jnp
from jax import lax
from jax.sharding import PartitionSpec as P

D = 4096
HEADS = 32
KV_HEADS = 8
HEAD_DIM = 128
TOP = 8
GROUP = 128
EXP_DEV = 1
CACHE = 32


def unpack(codes, scales):
    quarter = codes.shape[0]
    width = codes.shape[1]
    divisors = jnp.array([1.0, 1.0 / 16, 1.0 / 256, 1.0 / 4096], jnp.float32)[:, None, None]
    lifted = jnp.floor(codes[None, :, :] * divisors)
    levels = lifted - 16.0 * jnp.floor(lifted * (1.0 / 16)) - 8.0
    height = 4 * quarter
    grouped = levels.reshape(height // GROUP, GROUP, width) * scales.astype(jnp.float32)[:, None, :]
    return grouped.reshape(height, width).astype(jnp.bfloat16)


def attend(queries, new_kv, cache_keys, cache_values, lengths):
    row_count = queries.shape[0]
    groups = HEADS // KV_HEADS
    queried = queries.reshape(row_count, KV_HEADS, groups, HEAD_DIM)
    cached_keys = cache_keys.reshape(row_count, CACHE, KV_HEADS, HEAD_DIM)
    cached_values = cache_values.reshape(row_count, CACHE, KV_HEADS, HEAD_DIM)
    fresh_key = new_kv[:, 0].reshape(row_count, KV_HEADS, HEAD_DIM)
    fresh_value = new_kv[:, 1].reshape(row_count, KV_HEADS, HEAD_DIM)
    scaling = HEAD_DIM ** (-0.5)
    earlier = (
        jnp.einsum("bjgd,bcjd->bjgc", queried, cached_keys, preferred_element_type=jnp.float32)
        * scaling
    )
    current = (
        jnp.einsum("bjgd,bjd->bjg", queried, fresh_key, preferred_element_type=jnp.float32)
        * scaling
    )
    valid = (jnp.arange(CACHE, dtype=jnp.int32)[None, :] < lengths[:, None])[:, None, None, :]
    largest = jnp.maximum(jnp.max(jnp.where(valid, earlier, -1e30), axis=-1), current)
    earlier_w = jnp.where(valid, jnp.exp(earlier - largest[..., None]), 0.0)
    current_w = jnp.exp(current - largest)
    denominator = jnp.sum(earlier_w, axis=-1) + current_w
    earlier_p = (earlier_w / denominator[..., None]).astype(jnp.bfloat16)
    current_p = (current_w / denominator).astype(jnp.bfloat16)
    attended = jnp.einsum(
        "bjgc,bcjd->bjgd", earlier_p, cached_values, preferred_element_type=jnp.float32
    )
    attended = (
        attended
        + current_p.astype(jnp.float32)[..., None] * fresh_value.astype(jnp.float32)[:, :, None, :]
    )
    return attended.reshape(row_count, HEADS * HEAD_DIM).astype(jnp.bfloat16)


def normalize(mixed, norm_gain):
    widened = mixed.astype(jnp.float32)
    meansq = jnp.mean(widened * widened, axis=-1, keepdims=True)
    return (widened * lax.rsqrt(meansq + 1e-06) * norm_gain.astype(jnp.float32)).astype(
        jnp.bfloat16
    )


def slot_table(routes, experts, capacity):
    flattened = routes.reshape(-1)
    onehot = (flattened[:, None] == jnp.arange(experts, dtype=jnp.int32)[None, :]).astype(jnp.int32)
    ranking = jnp.sum((jnp.cumsum(onehot, axis=0) - 1) * onehot, axis=1)
    return (flattened * capacity + ranking).reshape(routes.shape)


def dispatch(block, slots, width):
    targets = jnp.arange(width, dtype=jnp.int32)
    placing = jnp.sum((slots[None, :, :] == targets[:, None, None]).astype(jnp.float32), axis=2)
    return jnp.dot(placing.astype(jnp.bfloat16), block, preferred_element_type=jnp.float32).astype(
        jnp.bfloat16
    )


def body(
    queries,
    new_kv,
    cache_keys,
    cache_values,
    lengths,
    residual,
    norm_gain,
    routes,
    route_weights,
    gate_codes,
    gate_scales,
    up_codes,
    up_scales,
    down_codes,
    down_scales,
):
    experts = lax.axis_size("expert") * EXP_DEV
    groups = lax.axis_size("dp")
    row_count = queries.shape[0]
    capacity = min(row_count, max(2, 2 * row_count * TOP // experts))
    attended = attend(queries, new_kv, cache_keys, cache_values, lengths)
    mixed = (residual.astype(jnp.float32) + attended.astype(jnp.float32)).astype(jnp.bfloat16)
    normed = normalize(mixed, norm_gain)
    own_slots = slot_table(routes, experts, capacity)
    w_gate = unpack(gate_codes[0], gate_scales[0])
    w_up = unpack(up_codes[0], up_scales[0])
    w_down = unpack(down_codes[0], down_scales[0])
    local_units = w_gate.shape[1]
    peer_rows, peer_routes = (
        lax.all_gather(normed, "dp", axis=0, tiled=True),
        lax.all_gather(routes, "dp", axis=0, tiled=True),
    )
    peer_rows = peer_rows.reshape(groups, row_count, D)
    peer_routes = peer_routes.reshape(groups, row_count, TOP)

    def build(block, table):
        return dispatch(block, slot_table(table, experts, capacity), experts * capacity)

    outgoing = jax.vmap(build)(peer_rows, peer_routes).reshape(groups, experts, capacity, D)
    items = lax.all_to_all(outgoing, "expert", split_axis=1, concat_axis=1, tiled=True)
    count = items.shape[0]
    inputs = items.reshape(-1, D)
    gate = jnp.dot(inputs, w_gate, preferred_element_type=jnp.float32)
    upward = jnp.dot(inputs, w_up, preferred_element_type=jnp.float32)
    hidden = (jax.nn.silu(gate) * upward).astype(jnp.bfloat16).reshape(count, -1, local_units)
    hidden = hidden.reshape(-1, local_units)
    produced = jnp.dot(
        lax.all_gather(hidden, "dp", axis=1, tiled=True), w_down, preferred_element_type=jnp.float32
    ).astype(jnp.bfloat16)
    produced = produced.reshape(groups, -1, produced.shape[1])
    returned = lax.all_to_all(
        lax.all_to_all(produced, "dp", split_axis=0, concat_axis=2, tiled=True),
        "expert",
        split_axis=1,
        concat_axis=0,
        tiled=True,
    )
    shares = route_weights / jnp.sum(route_weights, axis=1, keepdims=True)
    targets = jnp.arange(experts * capacity, dtype=jnp.int32)
    spreading = jnp.sum(
        jnp.where(own_slots[:, :, None] == targets[None, None, :], shares[:, :, None], 0.0), axis=1
    )
    combined = jnp.dot(
        spreading, returned.reshape(-1, D).astype(jnp.float32), precision=lax.Precision.HIGHEST
    )
    return (mixed.astype(jnp.float32) + combined).astype(jnp.bfloat16)


def solution(mesh):
    return jax.shard_map(
        body,
        mesh=mesh,
        in_specs=(
            P(("dp", "expert"), None),
            P(("dp", "expert"), None, None),
            P(("dp", "expert"), None, None),
            P(("dp", "expert"), None, None),
            P(("dp", "expert")),
            P(("dp", "expert"), None),
            P(),
            P(("dp", "expert"), None),
            P(("dp", "expert"), None),
            P("expert", None, "dp"),
            P("expert", None, "dp"),
            P("expert", None, "dp"),
            P("expert", None, "dp"),
            P("expert", None, "dp"),
            P("expert", None, "dp"),
        ),
        out_specs=P(("dp", "expert"), None),
        check_vma=False,
    )
```

profile of v0, /device:TPU:0, one launch (start us, length us, event | category | flops | bytes accessed | tf_op | source)
XLA Modules:
  0.0 193.7 jit_solution(17270972118712085169)
XLA Ops:
  6.5 5.6 %all_gather.9 = s32[16,8]{1,0:T(8,128)S(1)} all-gather(s32[8,8]{1,0:T(8,128)} %param.25), channel_id=1, replica_groups=mesh['dp'=2,'expert'=16] {'dp'}, dimensions={0}, use_global_device_ids=true | all-gather | bytes 768 | tf_op jit(solution)/shard_map/all_gather | solution.py:115
  12.1 0.1 eq.63
  12.2 0.7 iota_compare_fusion.4
  13.0 0.8 slice_convert_fusion
  13.8 1.0 fusion.28
  14.8 1.6 select_reduce_fusion
  16.4 0.3 fusion.22
  16.7 0.3 fusion.11
  17.1 1.0 fusion.18
  18.1 0.7 convert_element_type.142
  18.8 0.1 fusion.20
  18.9 4.9 %all_gather.10 = bf16[16,4096]{1,0:T(8,128)(2,1)S(1)} all-gather(bf16[8,4096]{1,0:T(8,128)(2,1)S(1)} %fusion.20), channel_id=1, replica_groups=mesh['dp'=2,'expert'=16] {'dp'}, dimensions={0}, use_global_device_ids=true | all-gather | bytes 196608 | tf_op jit(solution)/shard_map/all_gather | solution.py:114
  23.8 0.1 fusion.23
  23.9 0.1 reduce_window_sum.23
  24.0 0.2 select_reduce_fusion.1
  24.2 0.1 reduce_sum.73
  24.4 0.1 convert_reduce_fusion
  24.5 0.7 fusion.7
  25.2 1.4 copy.76
  26.7 6.4 %all-to-all-start = ((bf16[2,16,8,4096]{3,2,0,1:T(8,128)(2,1)}), bf16[2,16,8,4096]{3,2,0,1:T(8,128)(2,1)S(1)}, u32[]{:S(2)}, u32[]{:S(2)}) async-start(bf16[2,16,8,4096]{3,2,0,1:T(8,128)(2,1)} %copy.76), calls=%async_computation | async-start | bytes 4194304 | tf_op jit(solution)/shard_map/all_to_all | solution.py:124
  33.1 0.7 mul.294
  33.9 0.1 mul.295
  34.0 1.0 bitcast_convert_fusion.1
  35.0 10.6 %mul.292 = f32[4,1024,1024]{2,1,0:T(8,128)} broadcast(f32[1024,1024]{1,0:T(8,128)} %bitcast.98), dimensions={1,2} | broadcast | bytes 20971520 | tf_op jit(solution)/shard_map/mul | solution.py:20
  45.6 8.1 %mul.304 = f32[4,1024,1024]{2,1,0:T(8,128)} broadcast(f32[1024,1024]{1,0:T(8,128)S(1)} %bitcast.99), dimensions={1,2} | broadcast | bytes 20971520 | tf_op jit(solution)/shard_map/mul | solution.py:20
  53.7 19.2 %multiply_convert_fusion.1 = (bf16[32,128,1024]{2,1,0:T(8,128)(2,1)}, bf16[32,128,1024]{2,1,0:T(8,128)(2,1)}) fusion(f32[32,128,1024]{2,1,0:T(8,128)} %bitcast.90, f32[32,1024]{1,0:T(8,128)S(1)} %get-tuple-element.14, f32[32]{0:T(128)S(1)} %mul.295, f32[32,1024]{1,0:T(8,128)S(1)} %get-tuple-element.13, f32[32,128,1024]{2,1,0:T(8,128)} %bitcast.91), kind=kLoop, calls=%fused_computation.10 | loop fusion | flops 75497472 | bytes 50593920 | tf_op jit(solution)/shard_map/convert_element_type | solution.py:24
  72.9 1.3 all-to-all-done
  74.2 0.1 copy.77
  74.4 5.9 %fusion.36 = f32[256,1024]{1,0:T(8,128)S(1)} fusion(bf16[256,4096]{1,0:T(8,128)(2,1)S(1)} %bitcast.102, bf16[4096,1024]{1,0:T(8,128)(2,1)} %bitcast.95), kind=kOutput, calls=%fused_computation.75 | convolution fusion | flops 2147483648 | bytes 11534336 | tf_op jit(solution)/shard_map/dot_general | solution.py:127
  80.3 3.3 %fusion.9 = bf16[256,1024]{1,0:T(8,128)(2,1)} fusion(bf16[256,4096]{1,0:T(8,128)(2,1)S(1)} %bitcast.103, bf16[4096,1024]{1,0:T(8,128)(2,1)S(1)} %bitcast.94, f32[256,1024]{1,0:T(8,128)S(1)} %fusion.36), kind=kOutput, calls=%fused_computation.17 | convolution fusion | flops 2149056512 | bytes 12058624 | tf_op jit(solution)/shard_map/dot_general | solution.py:128
  83.7 0.1 mul.319
  83.9 9.5 %fusion = bf16[2048,2048]{1,0:T(8,128)(2,1)} fusion(f32[16,2048]{1,0:T(8,128)S(1)} %bitcast_convert_fusion, f32[2048]{0:T(1024)S(1)} %broadcast_bitcast_fusion, f32[512,2048]{1,0:T(8,128)} %bitcast.101), kind=kLoop, calls=%fused_computation.1 | loop fusion | flops 37748736 | bytes 12722176 | tf_op jit(solution)/shard_map/convert_element_type | solution.py:24
  93.4 18.3 %all-gather.2.cloned.1.call-done = bf16[256,2048]{1,0:T(8,128)(2,1)} async-done(((bf16[256,1024]{1,0:T(8,128)(2,1)}), bf16[256,2048]{1,0:T(8,128)(2,1)}) %all-gather.2.cloned.1.call-update) | async-done | bytes 1048592 | tf_op jit(solution)/shard_map/all_gather | solution.py:132
  111.6 6.0 %convolution_convert_fusion.1 = bf16[256,2048]{1,0:T(8,128)(2,1)S(1)} fusion(bf16[256,2048]{1,0:T(8,128)(2,1)} %all-gather.2.cloned.1.call-done, bf16[2048,2048]{1,0:T(8,128)(2,1)} %fusion), kind=kOutput, calls=%fused_computation.15 | convolution fusion | flops 2148007936 | bytes 10485760 | tf_op jit(solution)/shard_map/dot_general | solution.py:131
  117.7 0.7 copy.78
  118.4 17.1 %all_to_all.32 = bf16[2,128,2048]{1,2,0:T(8,128)(2,1)} all-to-all(bf16[2,128,2048]{1,2,0:T(8,128)(2,1)S(1)} %copy.78), channel_id=1, replica_groups=mesh['dp'=2,'expert'=16] {'dp'}, dimensions={0} | all-to-all | bytes 2097152 | tf_op jit(solution)/shard_map/all_to_all | solution.py:136
  135.5 4.7 %copy.79 = bf16[1,128,4096]{2,0,1:T(2,128)(2,1)S(1)} copy(bf16[1,128,4096]{1,2,0:T(8,128)(2,1)} %bitcast.100) | data formatting | bytes 2097152 | tf_op jit(solution)/shard_map/all_to_all | solution.py:136
  140.2 0.5 broadcast.223
  140.7 8.1 %reduce = bf16[128,4096]{1,0:T(8,128)(2,1)} reduce(bf16[128,1,4096]{2,1,0:T(2,128)(2,1)S(1)} %bitcast.96, bf16[]{:T(256)} %broadcast.223), dimensions={1}, to_apply=%bitcast.72.reduce_sub_computation | reduce | bytes 2097154
  148.8 2.9 %reshape.227 = bf16[16,2,16384]{2,1,0:T(2,128)(2,1)} reshape(bf16[128,4096]{1,0:T(8,128)(2,1)} %reduce) | data formatting | bytes 2097152
  151.7 5.7 %all-to-all-start.2 = ((bf16[16,2,16384]{2,1,0:T(2,128)(2,1)}), bf16[16,2,16384]{2,1,0:T(2,128)(2,1)}, u32[]{:S(2)}, u32[]{:S(2)}) async-start(bf16[16,2,16384]{2,1,0:T(2,128)(2,1)} %reshape.227), calls=%async_computation.2 | async-start | bytes 2097152 | tf_op jit(solution)/shard_map/all_to_all | solution.py:135
  157.6 0.1 reduce_window_sum.22
  157.7 0.2 select_reduce_fusion.3
  157.9 0.1 reduce_sum.70
  158.1 0.1 select_reduce_fusion.2
  158.2 22.2 %all-to-all-done.2 = bf16[16,2,16384]{2,1,0:T(2,128)(2,1)} async-done(((bf16[16,2,16384]{2,1,0:T(2,128)(2,1)}), bf16[16,2,16384]{2,1,0:T(2,128)(2,1)}, u32[]{:S(2)}, u32[]{:S(2)}) %all-to-all-start.2) | async-done | bytes 1048608 | tf_op jit(solution)/shard_map/all_to_all | solution.py:135
  180.4 4.3 %reshape.228 = bf16[128,1,4096]{2,1,0:T(2,128)(2,1)S(1)} reshape(bf16[16,2,16384]{2,1,0:T(2,128)(2,1)} %all-to-all-done.2) | data formatting | bytes 2097152
  184.7 2.2 %fusion.8 = bf16[8,4096]{1,0:T(8,128)(2,1)} fusion(f32[8,128]{1,0:T(8,128)S(1)} %select_reduce_fusion.2, bf16[1,128,4096]{2,0,1:T(2,128)(2,1)S(1)} %bitcast.97, bf16[8,4096]{1,0:T(8,128)(2,1)S(1)} %get-tuple-element.6), kind=kOutput, calls=%fused_computation.14 | convolution fusion | flops 50429952 | bytes 1183744 | tf_op jit(solution)/shard_map/dot_general | solution.py:147
  (37 shorter events, 0.8 us)
Async XLA Ops:
  6.5 10.2 %copy-start = (bf16[8,32,1024]{2,1,0:T(8,128)(2,1)S(1)}, bf16[8,32,1024]{2,1,0:T(8,128)(2,1)}, u32[]{:S(2)}) copy-start(bf16[8,32,1024]{2,1,0:T(8,128)(2,1)} %param.21) | copy-start | bytes 1572868
  26.7 47.5 %all-to-all-start = ((bf16[2,16,8,4096]{3,2,0,1:T(8,128)(2,1)}), bf16[2,16,8,4096]{3,2,0,1:T(8,128)(2,1)S(1)}, u32[]{:S(2)}, u32[]{:S(2)}) async-start(bf16[2,16,8,4096]{3,2,0,1:T(8,128)(2,1)} %copy.76), calls=%async_computation | async-start | bytes 4194304 | tf_op jit(solution)/shard_map/all_to_all | solution.py:124
  33.1 78.5 %all-gather.2.cloned.1.call-start = ((), (), s32[]{:S(2)}) async-start(), calls=%async_computation.3 | async-start | bytes 1572864 | tf_op jit(solution)/shard_map/all_gather | solution.py:132
  34.0 11.6 %copy-start.2 = (f32[1,1024,1024]{2,1,0:T(8,128)S(1)}, f32[1,1024,1024]{2,1,0:T(8,128)}, u32[]{:S(2)}) copy-start(f32[1,1024,1024]{2,1,0:T(8,128)} %param.29) | copy-start | bytes 12582916
  74.2 6.1 %slice-start = ((s8[8388608]{0:T(1024)(128)(4,1)}), s8[4194304]{0:T(1024)(128)(4,1)S(1)}, s32[]{:S(2)}) async-start(s8[8388608]{0:T(1024)(128)(4,1)} %bitcast.92), calls=%async_computation.4 | async-start | bytes 8388608
  74.3 6.0 %slice-start.1 = ((s8[8388608]{0:T(1024)(128)(4,1)}), s8[4194304]{0:T(1024)(128)(4,1)S(1)}, s32[]{:S(2)}) async-start(s8[8388608]{0:T(1024)(128)(4,1)} %bitcast.92), calls=%async_computation.5 | async-start | bytes 8388608
  80.3 3.4 %copy-start.6 = (f32[4]{0:T(128)S(1)}, f32[4]{0:T(128)}, u32[]{:S(2)}) copy-start(f32[4]{0:T(128)} %constant.49.clone) | copy-start | bytes 52
  80.3 3.6 %copy-start.3 = (bf16[1,16,2048]{2,1,0:T(8,128)(2,1)S(1)}, bf16[1,16,2048]{2,1,0:T(8,128)(2,1)}, u32[]{:S(2)}) copy-start(bf16[1,16,2048]{2,1,0:T(8,128)(2,1)} %param.32) | copy-start | bytes 196612
  83.9 103.0 %copy-start.1 = (bf16[8,32,1024]{2,1,0:T(8,128)(2,1)S(1)}, bf16[8,32,1024]{2,1,0:T(8,128)(2,1)}, u32[]{:S(2)}) copy-start(bf16[8,32,1024]{2,1,0:T(8,128)(2,1)} %param.21) | copy-start | bytes 1572868
  93.4 64.0 %copy-start.4 = (s32[8,8]{1,0:T(8,128)S(1)}, s32[8,8]{1,0:T(8,128)}, u32[]{:S(2)}) copy-start(s32[8,8]{1,0:T(8,128)} %param.25) | copy-start | bytes 772
  93.4 64.5 %copy-start.5 = (f32[8,8]{1,0:T(8,128)S(1)}, f32[8,8]{1,0:T(8,128)}, u32[]{:S(2)}) copy-start(f32[8,8]{1,0:T(8,128)} %param.26) | copy-start | bytes 772
  151.7 28.7 %all-to-all-start.2 = ((bf16[16,2,16384]{2,1,0:T(2,128)(2,1)}), bf16[16,2,16384]{2,1,0:T(2,128)(2,1)}, u32[]{:S(2)}, u32[]{:S(2)}) async-start(bf16[16,2,16384]{2,1,0:T(2,128)(2,1)} %reshape.227), calls=%async_computation.2 | async-start | bytes 2097152 | tf_op jit(solution)/shard_map/all_to_all | solution.py:135
Sparse Core Ops, SparseCore 0:
  83.8 27.8 all-gather.1
where the time goes:
time: 196 us; the launch traced here: 194 us
  other arithmetic  42.5 us (22%)
  waiting for transfers between devices  41.8 us (21%)
  local copies, waits for them, and re-layouts  35 us (18%)
  blocking collectives  27.6 us (14%)
  matrix products  21.1 us (11%)
  between operations  13.6 us (7%)
  starting transfers between devices  12.1 us (6%)
    convert_element_type x2, other arithmetic, unpack(): return grouped.reshape(height, width).astype(jnp.bfloat16)  28.6 us
    all_to_all x1, waiting for transfers between devices, body(): lax.all_to_all(lax.all_to_all(produced, 'dp', split_axis=0, concat_axis=2...  22.2 us
    mul x7, local copies, waits for them, and re-layouts, unpack(): lifted = jnp.floor(codes[None, :, :] * divisors)  19.7 us
    all_gather x1, waiting for transfers between devices, body(): lax.all_gather(hidden, 'dp', axis=1, tiled=True)  18.3 us
    all_to_all x1, blocking collectives, body(): lax.all_to_all(produced, 'dp', split_axis=0, concat_axis=2, tiled=True)  17.1 us
    unnamed x2, other arithmetic  8.06 us
    unnamed x21, local copies, waits for them, and re-layouts  7.81 us
    all_to_all x1, starting transfers between devices, body(): lax.all_to_all(outgoing, 'expert', split_axis=1, concat_axis=1, tiled=True)  6.42 us
  transfers between devices with their start and end apart: 3, of which 3 were waited for; matrix products, arithmetic and copies ran while one was open for 26% of the time, Pallas kernels for 0%

commit v1 on v0

v1 whole, which is shorter than its diff:
```python
import functools

import jax
import jax.numpy as jnp
from jax import lax
from jax.experimental import pallas as pl
from jax.experimental.pallas import tpu as pltpu
from jax.sharding import PartitionSpec as P

HEAD_DIM = 128
GROUP = 128
TOP = 8
LANES = 128
VMEM_LIMIT = 56 * 2**20
VMEM_MOST = 54 * 2**20
VMEM_SOME = 16 * 2**20
F32 = jnp.float32
BF16 = jnp.bfloat16


def front_kernel(
    lengths_ref,
    queries_ref,
    new_kv_ref,
    keys_ref,
    values_ref,
    residual_ref,
    gain_ref,
    routes_ref,
    weights_ref,
    mixed_ref,
    payload_ref,
):
    rows, cache, kv_width = keys_ref.shape
    width = queries_ref.shape[1]
    kv_heads = kv_width // HEAD_DIM
    per = width // kv_width
    scaling = HEAD_DIM ** (-0.5)
    row_id = lax.broadcasted_iota(jnp.int32, (rows, rows * cache), 0)
    lane_id = lax.broadcasted_iota(jnp.int32, (rows, rows * cache), 1)
    bound = jnp.zeros((rows, rows * cache), jnp.int32)
    for r in range(rows):
        bound = jnp.where(row_id == r, r * cache + lengths_ref[r], bound)
    valid = (lane_id >= row_id * cache) & (lane_id < bound)
    total = jnp.zeros((rows, 1), F32)
    for j in range(kv_heads):
        span = slice(j * HEAD_DIM, (j + 1) * HEAD_DIM)
        heads = [j * per + g for g in range(per)]
        queried = jnp.concatenate(
            [queries_ref[:, h * HEAD_DIM : (h + 1) * HEAD_DIM].astype(F32) for h in heads], axis=0
        )
        keys = keys_ref[:, :, span].reshape(rows * cache, HEAD_DIM)
        values = values_ref[:, :, span].reshape(rows * cache, HEAD_DIM)
        fresh_key = new_kv_ref[:, 0, span].astype(F32)
        fresh_value = new_kv_ref[:, 1, span].astype(F32)
        earlier = lax.dot_general(
            queried.astype(BF16), keys, (((1,), (1,)), ((), ())), preferred_element_type=F32
        )
        earlier = earlier.reshape(per, rows, rows * cache) * scaling
        current = (
            jnp.sum(queried.reshape(per, rows, HEAD_DIM) * fresh_key[None], axis=-1, keepdims=True)
            * scaling
        )
        earlier = jnp.where(valid[None], earlier, -1e30)
        largest = jnp.maximum(jnp.max(earlier, axis=-1, keepdims=True), current)
        earlier_w = jnp.where(valid[None], jnp.exp(earlier - largest), 0.0)
        current_w = jnp.exp(current - largest)
        denominator = jnp.sum(earlier_w, axis=-1, keepdims=True) + current_w
        earlier_p = (earlier_w / denominator).astype(BF16).reshape(per * rows, rows * cache)
        current_p = (current_w / denominator).astype(BF16).astype(F32)
        attended = jnp.dot(earlier_p, values, preferred_element_type=F32)
        attended = attended.reshape(per, rows, HEAD_DIM) + current_p * fresh_value[None]
        for g, h in enumerate(heads):
            place = slice(h * HEAD_DIM, (h + 1) * HEAD_DIM)
            mixed = (
                residual_ref[:, place].astype(F32) + attended[g].astype(BF16).astype(F32)
            ).astype(BF16)
            mixed_ref[:, place] = mixed
            widened = mixed.astype(F32)
            total = total + jnp.sum(widened * widened, axis=-1, keepdims=True)
    inverse = lax.rsqrt(total * (1.0 / width) + 1e-06)
    payload_ref[:, :width] = (
        mixed_ref[...].astype(F32) * inverse * gain_ref[...].astype(F32)
    ).astype(BF16)
    if payload_ref.shape[1] > width:
        shares = weights_ref[...] / jnp.sum(weights_ref[...], axis=1, keepdims=True)
        lane = lax.broadcasted_iota(jnp.int32, (rows, LANES), 1)
        expert = jnp.where(lane < LANES // 2, lane, lane - LANES // 2)
        table = jnp.zeros((rows, LANES), F32)
        for k in range(routes_ref.shape[1]):
            table = table + jnp.where(
                routes_ref[:, k : k + 1] == expert, shares[:, k : k + 1], 0.0
            )
        high = table.astype(BF16).astype(F32)
        payload_ref[:, width:] = jnp.where(lane < LANES // 2, high, table - high).astype(BF16)


def front(queries, new_kv, keys, values, lengths, residual, gain, routes, weights, extra):
    rows, width = queries.shape
    vmem = pl.BlockSpec(memory_space=pltpu.VMEM)
    return pl.pallas_call(
        front_kernel,
        out_shape=(
            jax.ShapeDtypeStruct((rows, width), BF16),
            jax.ShapeDtypeStruct((rows, width + extra), BF16),
        ),
        in_specs=[pl.BlockSpec(memory_space=pltpu.SMEM)] + [vmem] * 8,
        out_specs=(vmem, vmem),
        compiler_params=pltpu.CompilerParams(vmem_limit_bytes=VMEM_LIMIT),
        cost_estimate=pl.CostEstimate(
            flops=4 * 256 * 256 * 1024, bytes_accessed=2 * 2**20, transcendentals=65536
        ),
        name="front",
    )(lengths, queries, new_kv, keys, values, residual, gain.reshape(1, -1), routes, weights)


def unpack_tile(codes_ref, scales, store, digits):
    depth, width = codes_ref.shape
    step = 256 if width % 256 == 0 else LANES
    for column in range(0, width, step):
        spans = [
            jnp.broadcast_to(scales[k][:, column : column + step], (16, step)).astype(BF16)
            for k in digits
        ]

        def chunk(i, carry, column=column, spans=spans):
            start = pl.multiple_of(i * 16, 16)
            words = codes_ref[pl.ds(start, 16), column : column + step].astype(jnp.int32)
            for n, k in enumerate(digits):
                digit = words if k == 0 else lax.shift_right_logical(words, 4 * k)
                if k < 3:
                    digit = digit & 15
                level = digit.astype(F32).astype(BF16) - jnp.asarray(8, BF16)
                store(n, start, column, step, level * spans[n])
            return carry

        lax.fori_loop(0, depth // 16, chunk, 0, unroll=True)


def unpack_kernel(codes_ref, scales_ref, out_ref):
    group = pl.program_id(0)
    groups = pl.num_programs(0)
    scales = [scales_ref[pl.ds(k * groups + group, 1), :] for k in range(4)]

    def store(n, start, column, step, value):
        out_ref[n, pl.ds(start, 16), column : column + step] = value

    unpack_tile(codes_ref, scales, store, range(4))


def unpack_one(codes, scales):
    quarter, width = codes.shape
    groups = quarter // GROUP
    weight = pl.pallas_call(
        unpack_kernel,
        grid=(groups,),
        out_shape=jax.ShapeDtypeStruct((4, quarter, width), BF16),
        in_specs=[
            pl.BlockSpec((GROUP, width), lambda i: (i, 0)),
            pl.BlockSpec((4 * groups, width), lambda i: (0, 0)),
        ],
        out_specs=pl.BlockSpec((4, GROUP, width), lambda i: (0, i, 0)),
        compiler_params=pltpu.CompilerParams(vmem_limit_bytes=VMEM_LIMIT),
        cost_estimate=pl.CostEstimate(
            flops=quarter * width * 24, bytes_accessed=quarter * width * 12, transcendentals=0
        ),
        name="unpack_weights",
    )(codes, scales.astype(F32))
    return weight.reshape(4 * quarter, width)


def hidden_kernel(place_ref, *refs):
    pieces, (gate_ref, up_ref, out_ref, share_ref, rows_ref) = refs[:-5], refs[-5:]
    depth = gate_ref.shape[0]
    block = pieces[0].shape[0]

    @pl.when(pl.program_id(0) == 0)
    def _():
        for n, piece in enumerate(pieces):
            rows_ref[n * block : (n + 1) * block, :] = piece[:, :depth]
            table = piece[:, depth:].astype(F32)
            lane = lax.broadcasted_iota(jnp.int32, table.shape, 1)
            mine = place_ref[0]
            chosen = (lane == mine) | (lane == mine + LANES // 2)
            share = jnp.sum(jnp.where(chosen, table, 0.0), axis=1, keepdims=True)
            share_ref[n * block : (n + 1) * block, :] = jnp.broadcast_to(share, table.shape)

    inputs = rows_ref[...]
    gate = jnp.dot(inputs, gate_ref[...], preferred_element_type=F32)
    upward = jnp.dot(inputs, up_ref[...], preferred_element_type=F32)
    out_ref[...] = (gate / (1.0 + jnp.exp(-gate)) * upward).astype(BF16)


def hidden_units(pieces, w_gate, w_up, place):
    block, padded = pieces[0].shape
    count = block * len(pieces)
    depth, width = w_gate.shape
    step = 256
    spec = pl.BlockSpec((depth, step), lambda i: (0, i))
    piece_spec = pl.BlockSpec((block, padded), lambda i: (0, 0))
    return pl.pallas_call(
        hidden_kernel,
        grid=(width // step,),
        out_shape=(
            jax.ShapeDtypeStruct((count, width), BF16),
            jax.ShapeDtypeStruct((count, LANES), F32),
        ),
        in_specs=[pl.BlockSpec(memory_space=pltpu.SMEM)] + [piece_spec] * len(pieces) + [spec, spec],
        out_specs=(
            pl.BlockSpec((count, step), lambda i: (0, i)),
            pl.BlockSpec((count, LANES), lambda i: (0, 0)),
        ),
        scratch_shapes=[pltpu.VMEM((count, depth), BF16)],
        compiler_params=pltpu.CompilerParams(vmem_limit_bytes=VMEM_MOST),
        cost_estimate=pl.CostEstimate(
            flops=4 * count * depth * width,
            bytes_accessed=4 * depth * width + 2 * count * padded,
            transcendentals=count * width,
        ),
        name="gate_up",
    )(place, *pieces, w_gate, w_up)


def own_down_kernel(place_ref, codes_ref, scales_ref, hidden_ref, partial_ref, peer_ref, own_ref):
    quarter, width = codes_ref.shape
    groups = quarter // GROUP
    half = hidden_ref.shape[1]
    mine = place_ref[0]

    for group in range(groups):
        rows_of = codes_ref.at[group * GROUP : (group + 1) * GROUP, :]
        scales = [scales_ref[k * groups + group : k * groups + group + 1, :] for k in range(4)]

        def store_own(n, start, column, step, value, group=group):
            own_ref[pl.ds((n % 2) * quarter + group * GROUP + start, 16), column : column + step] = value

        def store_peer(n, start, column, step, value, group=group):
            peer_ref[pl.ds((n % 2) * quarter + group * GROUP + start, 16), column : column + step] = value

        @pl.when(mine == 0)
        def _():
            unpack_tile(rows_of, scales, store_own, (0, 1))
            unpack_tile(rows_of, scales, store_peer, (2, 3))

        @pl.when(mine == 1)
        def _():
            unpack_tile(rows_of, scales, store_peer, (0, 1))
            unpack_tile(rows_of, scales, store_own, (2, 3))

    partial_ref[...] = jnp.dot(hidden_ref[...], own_ref[...], preferred_element_type=F32)


def own_down(place, codes, scales, hidden):
    quarter, width = codes.shape
    count, half = hidden.shape
    step = 256
    return pl.pallas_call(
        own_down_kernel,
        grid_spec=pltpu.PrefetchScalarGridSpec(
            num_scalar_prefetch=1,
            grid=(width // step,),
            in_specs=[
                pl.BlockSpec((quarter, step), lambda i, p: (0, i)),
                pl.BlockSpec((scales.shape[0], step), lambda i, p: (0, i)),
                pl.BlockSpec((count, half), lambda i, p: (0, 0)),
            ],
            out_specs=(
                pl.BlockSpec((count, step), lambda i, p: (0, i)),
                pl.BlockSpec((half, step), lambda i, p: (0, i)),
            ),
            scratch_shapes=[pltpu.VMEM((half, step), BF16)],
        ),
        out_shape=(
            jax.ShapeDtypeStruct((count, width), F32),
            jax.ShapeDtypeStruct((half, width), BF16),
        ),
        compiler_params=pltpu.CompilerParams(vmem_limit_bytes=VMEM_MOST),
        cost_estimate=pl.CostEstimate(
            flops=2 * count * half * width + 24 * quarter * width,
            bytes_accessed=4 * quarter * width + 2 * half * width + 4 * count * width,
            transcendentals=0,
        ),
        name="down_own",
    )(place, codes, scales.astype(F32), hidden)


def peer_down_kernel(block, partial_ref, hidden_ref, weight_ref, share_ref, keep_ref, send_ref, rows_ref):
    @pl.when(pl.program_id(0) == 0)
    def _():
        for n in range(hidden_ref.shape[0] // block):
            source = (n ^ 1) * block
            rows_ref[n * block : (n + 1) * block, :] = hidden_ref[source : source + block, :]

    produced = partial_ref[...] + jnp.dot(
        rows_ref[...], weight_ref[...], preferred_element_type=F32
    )
    result = (produced.astype(BF16).astype(F32) * share_ref[:, :1]).astype(BF16)
    half = keep_ref.shape[0]
    keep_ref[...] = result[:half]
    send_ref[...] = result[half:]


def peer_down(partial, hidden, weight, share, block):
    count, width = partial.shape
    half = hidden.shape[1]
    step = 512
    shape = jax.ShapeDtypeStruct((count // 2, width), BF16)
    out_spec = pl.BlockSpec((count // 2, step), lambda i: (0, i))
    return pl.pallas_call(
        functools.partial(peer_down_kernel, block),
        grid=(width // step,),
        out_shape=(shape, shape),
        in_specs=[
            pl.BlockSpec((count, step), lambda i: (0, i)),
            pl.BlockSpec((count, half), lambda i: (0, 0)),
            pl.BlockSpec((half, step), lambda i: (0, i)),
            pl.BlockSpec((count, LANES), lambda i: (0, 0)),
        ],
        out_specs=(out_spec, out_spec),
        scratch_shapes=[pltpu.VMEM((count, half), BF16)],
        compiler_params=pltpu.CompilerParams(vmem_limit_bytes=VMEM_MOST),
        cost_estimate=pl.CostEstimate(
            flops=2 * count * half * width,
            bytes_accessed=6 * count * width + 2 * half * width,
            transcendentals=0,
        ),
        name="down_peer",
    )(partial, hidden, weight, share)


def halve_kernel(kept_ref, arrived_ref, *out_refs):
    total = kept_ref[...].astype(F32) + arrived_ref[...].astype(F32)
    size = total.shape[0] // len(out_refs)
    for n, out_ref in enumerate(out_refs):
        out_ref[...] = total[n * size : (n + 1) * size].astype(out_ref.dtype)


def add_and_cut(kept, arrived, parts):
    count, width = kept.shape
    vmem = pl.BlockSpec(memory_space=pltpu.VMEM)
    shape = jax.ShapeDtypeStruct((count // parts, width), BF16)
    return pl.pallas_call(
        halve_kernel,
        out_shape=(shape,) * parts,
        in_specs=[vmem, vmem],
        out_specs=(vmem,) * parts,
        compiler_params=pltpu.CompilerParams(vmem_limit_bytes=VMEM_SOME),
        cost_estimate=pl.CostEstimate(
            flops=count * width, bytes_accessed=6 * count * width, transcendentals=0
        ),
        name="add_and_cut",
    )(kept, arrived)


def finish_kernel(side_ref, mixed_ref, *refs):
    near, far, out_ref = refs[: len(refs) // 2], refs[len(refs) // 2 : -1], refs[-1]
    half = mixed_ref.shape[1] // 2

    def total(parts):
        result = parts[0][...].astype(F32)
        for part in parts[1:]:
            result = result + part[...].astype(F32)
        return result

    def write(first, second):
        out_ref[:, :half] = (mixed_ref[:, :half].astype(F32) + total(first)).astype(BF16)
        out_ref[:, half:] = (mixed_ref[:, half:].astype(F32) + total(second)).astype(BF16)

    @pl.when(side_ref[0] == 0)
    def _():
        write(near, far)

    @pl.when(side_ref[0] != 0)
    def _():
        write(far, near)


def finish(side, mixed, near, far):
    vmem = pl.BlockSpec(memory_space=pltpu.VMEM)
    return pl.pallas_call(
        finish_kernel,
        out_shape=jax.ShapeDtypeStruct(mixed.shape, BF16),
        in_specs=[pl.BlockSpec(memory_space=pltpu.SMEM)] + [vmem] * (1 + len(near) + len(far)),
        out_specs=vmem,
        compiler_params=pltpu.CompilerParams(vmem_limit_bytes=VMEM_SOME),
        name="finish",
    )(side, mixed, *near, *far)


def dense(payload, mixed, codes):
    gate_codes, gate_scales, up_codes, up_scales, down_codes, down_scales = codes
    groups = lax.axis_size("dp")
    experts = lax.axis_size("expert")
    devices = groups * experts
    core, line, layer, plane = 1, 2, 4, experts
    layers = experts // layer
    side = lax.axis_index("dp").reshape(1).astype(jnp.int32)
    place = lax.axis_index("expert").reshape(1).astype(jnp.int32)

    def swap(block, offset):
        return lax.ppermute(block, ("dp", "expert"), [(i, i ^ offset) for i in range(devices)])

    stack = jnp.concatenate(
        [payload] + [swap(payload, z * layer) for z in range(1, layers)], axis=0
    )
    near = [stack, swap(stack, plane), swap(stack, line), swap(stack, plane ^ line)]
    pieces = near + [swap(piece, core) for piece in near]
    w_gate = unpack_one(gate_codes, gate_scales)
    w_up = unpack_one(up_codes, up_scales)
    hidden, share = hidden_units(pieces, w_gate, w_up, place)
    peer_hidden = swap(hidden, plane)
    partial, peer_weight = own_down(side, down_codes, down_scales, hidden)
    keep, send = peer_down(partial, peer_hidden, peer_weight, share, stack.shape[0])
    keep, send = add_and_cut(keep, swap(send, core), 2)
    blocks = add_and_cut(keep, swap(send, line), 2 * layers)
    near = [blocks[0]] + [swap(blocks[z], z * layer) for z in range(1, layers)]
    far = [swap(blocks[layers + z], plane ^ (z * layer)) for z in range(layers)]
    return finish(side, mixed, near, far)


def slot_table(routes, experts, capacity):
    flattened = routes.reshape(-1)
    onehot = (flattened[:, None] == jnp.arange(experts, dtype=jnp.int32)[None, :]).astype(jnp.int32)
    ranking = jnp.sum((jnp.cumsum(onehot, axis=0) - 1) * onehot, axis=1)
    return (flattened * capacity + ranking).reshape(routes.shape)


def dispatch(block, slots, width):
    targets = jnp.arange(width, dtype=jnp.int32)
    placing = jnp.sum((slots[None, :, :] == targets[:, None, None]).astype(F32), axis=2)
    return jnp.dot(placing.astype(BF16), block, preferred_element_type=F32).astype(BF16)


def unpack(codes, scales):
    quarter, width = codes.shape
    divisors = jnp.array([1.0, 1.0 / 16, 1.0 / 256, 1.0 / 4096], F32)[:, None, None]
    lifted = jnp.floor(codes[None, :, :] * divisors)
    levels = lifted - 16.0 * jnp.floor(lifted * (1.0 / 16)) - 8.0
    height = 4 * quarter
    grouped = levels.reshape(height // GROUP, GROUP, width) * scales.astype(F32)[:, None, :]
    return grouped.reshape(height, width).astype(BF16)


def routed(normed, mixed, routes, route_weights, codes, capacity):
    gate_codes, gate_scales, up_codes, up_scales, down_codes, down_scales = codes
    experts = lax.axis_size("expert")
    groups = lax.axis_size("dp")
    row_count, width = mixed.shape
    own_slots = slot_table(routes, experts, capacity)
    w_gate = unpack(gate_codes, gate_scales)
    w_up = unpack(up_codes, up_scales)
    w_down = unpack(down_codes, down_scales)
    local_units = w_gate.shape[1]
    peer_rows = lax.all_gather(normed, "dp", axis=0, tiled=True).reshape(groups, row_count, width)
    peer_routes = lax.all_gather(routes, "dp", axis=0, tiled=True).reshape(groups, row_count, TOP)

    def build(block, table):
        return dispatch(block, slot_table(table, experts, capacity), experts * capacity)

    outgoing = jax.vmap(build)(peer_rows, peer_routes).reshape(groups, experts, capacity, width)
    items = lax.all_to_all(outgoing, "expert", split_axis=1, concat_axis=1, tiled=True)
    inputs = items.reshape(-1, width)
    gate = jnp.dot(inputs, w_gate, preferred_element_type=F32)
    upward = jnp.dot(inputs, w_up, preferred_element_type=F32)
    hidden = (jax.nn.silu(gate) * upward).astype(BF16).reshape(-1, local_units)
    produced = jnp.dot(
        lax.all_gather(hidden, "dp", axis=1, tiled=True), w_down, preferred_element_type=F32
    ).astype(BF16)
    produced = produced.reshape(groups, -1, produced.shape[1])
    returned = lax.all_to_all(
        lax.all_to_all(produced, "dp", split_axis=0, concat_axis=2, tiled=True),
        "expert",
        split_axis=1,
        concat_axis=0,
        tiled=True,
    )
    shares = route_weights / jnp.sum(route_weights, axis=1, keepdims=True)
    targets = jnp.arange(experts * capacity, dtype=jnp.int32)
    spreading = jnp.sum(
        jnp.where(own_slots[:, :, None] == targets[None, None, :], shares[:, :, None], 0.0), axis=1
    )
    combined = jnp.dot(
        spreading, returned.reshape(-1, width).astype(F32), precision=lax.Precision.HIGHEST
    )
    return (mixed.astype(F32) + combined).astype(BF16)


def body(
    queries,
    new_kv,
    cache_keys,
    cache_values,
    lengths,
    residual,
    norm_gain,
    routes,
    route_weights,
    *packed,
):
    experts = lax.axis_size("expert")
    groups = lax.axis_size("dp")
    row_count = queries.shape[0]
    capacity = min(row_count, max(2, 2 * row_count * TOP // experts))
    every = (
        capacity == row_count
        and groups == 2
        and experts <= LANES // 2
        and experts % 4 == 0
        and experts & (experts - 1) == 0
    )
    mixed, payload = front(
        queries,
        new_kv,
        cache_keys,
        cache_values,
        lengths,
        residual,
        norm_gain,
        routes,
        route_weights,
        LANES if every else 0,
    )
    codes = [array[0] for array in packed]
    if every:
        return dense(payload, mixed, codes)
    return routed(payload, mixed, routes, route_weights, codes, capacity)


def solution(mesh):
    return jax.shard_map(
        body,
        mesh=mesh,
        in_specs=(
            P(("dp", "expert"), None),
            P(("dp", "expert"), None, None),
            P(("dp", "expert"), None, None),
            P(("dp", "expert"), None, None),
            P(("dp", "expert")),
            P(("dp", "expert"), None),
            P(),
            P(("dp", "expert"), None),
            P(("dp", "expert"), None),
            P("expert", None, "dp"),
            P("expert", None, "dp"),
            P("expert", None, "dp"),
            P("expert", None, "dp"),
            P("expert", None, "dp"),
            P("expert", None, "dp"),
        ),
        out_specs=P(("dp", "expert"), None),
        check_vma=False,
    )
```

time: 196 us -> 111 us (0.57)
  Pallas kernels: 0 us -> 47 us
  other arithmetic: 42.5 us -> 2.84 us
  local copies, waits for them, and re-layouts: 35 us -> 5.09 us
  blocking collectives: 27.6 us -> 0 us
  matrix products: 21.1 us -> 0 us
  between operations: 13.6 us -> 0.12 us
  starting transfers between devices: 12.1 us -> 23.2 us
  waiting for transfers between devices: 41.8 us -> 32.2 us
    pallas_call x0 -> x9, Pallas kernels: none -> 47 us  [the longest x2 16.9 us: unpack_one(): pl.pallas_call(unpack_kernel, grid=(groups,), out_shape=jax.ShapeDtypeStr...]
    ppermute x0 -> x20, waiting for transfers between devices: none -> 32.2 us  [swap(): lax.ppermute(block, ('dp', 'expert'), [(i, i ^ offset) for i in range(dev...]
    convert_element_type x9 -> x3, other arithmetic: 31.4 us -> 2.84 us  [the longest x2 2.17 us: unpack_one(): scales.astype(F32)]
    all_to_all x2 -> x0, waiting for transfers between devices: 23.5 us -> none  [the longest x1 22.2 us: body(): lax.all_to_all(lax.all_to_all(produced, 'dp', split_axis=0, concat_axis=2...]
    ppermute x0 -> x20, starting transfers between devices: none -> 23.2 us  [swap(): lax.ppermute(block, ('dp', 'expert'), [(i, i ^ offset) for i in range(dev...]
    dot_general x8 -> x0, matrix products: 21.1 us -> none  [the longest x1 6.05 us: body(): jnp.dot(lax.all_gather(hidden, 'dp', axis=1, tiled=True), w_down, preferr...]
    mul x8 -> x0, local copies, waits for them, and re-layouts: 19.8 us -> none  [the longest x7 19.7 us: unpack(): lifted = jnp.floor(codes[None, :, :] * divisors)]
    all_gather x1 -> x0, waiting for transfers between devices: 18.3 us -> none  [body(): lax.all_gather(hidden, 'dp', axis=1, tiled=True)]
  transfers between devices with their start and end apart: 3 -> 20, of which waited for: 3 -> 9; matrix products, arithmetic and copies ran while one was open for 26% -> 3% of each run, Pallas kernels for 0% -> 23%
where the time goes in v1:
time: 111 us
  Pallas kernels  47 us (42%)
  waiting for transfers between devices  32.2 us (29%)
  starting transfers between devices  23.2 us (21%)
  local copies, waits for them, and re-layouts  5.09 us (5%)
  other arithmetic  2.84 us (3%)
    ppermute x20, waiting for transfers between devices, swap(): lax.ppermute(block, ('dp', 'expert'), [(i, i ^ offset) for i in range(dev...  32.2 us
    ppermute x20, starting transfers between devices, swap(): lax.ppermute(block, ('dp', 'expert'), [(i, i ^ offset) for i in range(dev...  23.2 us
    pallas_call x2, Pallas kernels, unpack_one(): pl.pallas_call(unpack_kernel, grid=(groups,), out_shape=jax.ShapeDtypeStr...  16.9 us
    pallas_call x1, Pallas kernels, hidden_units(): pl.pallas_call(hidden_kernel, grid=(width // step,), out_shape=(jax.Shape...  10.1 us
    pallas_call x1, Pallas kernels, own_down(): pl.pallas_call(own_down_kernel, grid_spec=pltpu.PrefetchScalarGridSpec(nu...  9 us
    pallas_call x1, Pallas kernels, peer_down(): pl.pallas_call(functools.partial(peer_down_kernel, block), grid=(width //...  5.48 us
    pallas_call x1, Pallas kernels, front(): pl.pallas_call(front_kernel, out_shape=(jax.ShapeDtypeStruct((rows, width...  4.7 us
    unnamed x29, local copies, waits for them, and re-layouts  3.78 us
  transfers between devices with their start and end apart: 20, of which 9 were waited for; matrix products, arithmetic and copies ran while one was open for 3% of the time, Pallas kernels for 23%

profile of v1, /device:TPU:0, one launch (start us, length us, event | category | flops | bytes accessed | tf_op | source)
XLA Modules:
  0.0 110.5 jit_solution(14912604991928534019)
XLA Ops:
  0.0 1.3 %reshape.22.gain_ref = bf16[1,4096]{1,0:T(2,128)(2,1)} reshape(bf16[4096]{0:T(1024)(128)(2,1)} %param.21) | data formatting | bytes 16384 | tf_op jit(solution)/shard_map/reshape | solution.py:114
  1.3 4.7 %front.1 = (bf16[8,4096]{1,0:T(8,128)(2,1)}, bf16[8,4224]{1,0:T(8,128)(2,1)}) custom-call(s32[8]{0:T(128)} %lengths_ref.1, bf16[8,4096]{1,0:T(8,128)(2,1)} %queries_ref.1, bf16[8,2,1024]{2,1,0:T(2,128)(2,1)} %new_kv_ref.1, bf16[8,32,1024]{2,1,0:T(8,128)(2,1)} %keys_ref.1, bf16[8,32,1024]{2,1,0:T(8,128)(2,1)} %values_ref.1, bf16[8,4096]{1,0:T(8,128)(2,1)} %residual_ref.1, ...), custom_call_target="tpu_custom_call" | custom-call | flops 268435456 | bytes 2097152 | tf_op jit(solution)/shard_map/front/pallas_call | solution.py:101
  6.0 3.0 %collective-permute-start = (bf16[8,4224]{1,0:T(8,128)(2,1)}, bf16[8,4224]{1,0:T(8,128)(2,1)S(1)}, u32[]{:S(2)}, u32[]{:S(2)}) collective-permute-start(bf16[8,4224]{1,0:T(8,128)(2,1)} %get-tuple-element.24), channel_id=1, source_target_pairs={{0,4},{1,5},{2,6},{3,7},{4,0},{5,1},{6,2},{7,3},{8,12},{9,13},{10,... | collective-permute-start | bytes 202760 | tf_op jit(solution)/shard_map/ppermute | solution.py:401
  9.0 2.6 %collective-permute-start.1 = (bf16[8,4224]{1,0:T(8,128)(2,1)}, bf16[8,4224]{1,0:T(8,128)(2,1)S(1)}, u32[]{:S(2)}, u32[]{:S(2)}) collective-permute-start(bf16[8,4224]{1,0:T(8,128)(2,1)} %get-tuple-element.24), channel_id=1, source_target_pairs={{0,8},{1,9},{2,10},{3,11},{4,12},{5,13},{6,14},{7,15},{8,0},{9,1},... | collective-permute-start | bytes 202760 | tf_op jit(solution)/shard_map/ppermute | solution.py:401
  11.6 0.0 collective-permute-start.2
  11.6 1.0 constant_dynamic-update-slice_fusion.3
  12.6 4.1 %collective-permute-done.1 = bf16[8,4224]{1,0:T(8,128)(2,1)S(1)} collective-permute-done((bf16[8,4224]{1,0:T(8,128)(2,1)}, bf16[8,4224]{1,0:T(8,128)(2,1)S(1)}, u32[]{:S(2)}, u32[]{:S(2)}) %collective-permute-start.1) | collective-permute-done | bytes 67616 | tf_op jit(solution)/shard_map/ppermute | solution.py:401
  16.7 1.4 %collective-permute-done.2 = bf16[8,4224]{1,0:T(8,128)(2,1)S(1)} collective-permute-done((bf16[8,4224]{1,0:T(8,128)(2,1)}, bf16[8,4224]{1,0:T(8,128)(2,1)S(1)}, u32[]{:S(2)}, u32[]{:S(2)}) %collective-permute-start.2) | collective-permute-done | bytes 67616 | tf_op jit(solution)/shard_map/ppermute | solution.py:401
  18.0 1.6 %collective-permute-start.3 = (bf16[32,4224]{1,0:T(8,128)(2,1)S(1)}, bf16[32,4224]{1,0:T(8,128)(2,1)S(1)}, u32[]{:S(2)}, u32[]{:S(2)}) collective-permute-start(bf16[32,4224]{1,0:T(8,128)(2,1)S(1)} %constant_dynamic-update-slice_fusion.refs_0_), channel_id=1, source_target_pairs={{0,16},{1,17},{2,18},{3,19},{4,20},{5,21},{6,22},{7,23},{8,24},{9,... | collective-permute-start | bytes 811016 | tf_op jit(solution)/shard_map/ppermute | solution.py:401
  19.6 1.5 %collective-permute-start.4 = (bf16[32,4224]{1,0:T(8,128)(2,1)S(1)}, bf16[32,4224]{1,0:T(8,128)(2,1)S(1)}, u32[]{:S(2)}, u32[]{:S(2)}) collective-permute-start(bf16[32,4224]{1,0:T(8,128)(2,1)S(1)} %constant_dynamic-update-slice_fusion.refs_0_), channel_id=1, source_target_pairs={{0,2},{1,3},{2,0},{3,1},{4,6},{5,7},{6,4},{7,5},{8,10},{9,11},{10,... | collective-permute-start | bytes 811016 | tf_op jit(solution)/shard_map/ppermute | solution.py:401
  21.1 0.5 collective-permute-start.5
  21.6 5.9 %collective-permute-done.3.refs_1_ = bf16[32,4224]{1,0:T(8,128)(2,1)S(1)} collective-permute-done((bf16[32,4224]{1,0:T(8,128)(2,1)S(1)}, bf16[32,4224]{1,0:T(8,128)(2,1)S(1)}, u32[]{:S(2)}, u32[]{:S(2)}) %collective-permute-start.3) | collective-permute-done | bytes 270368 | tf_op jit(solution)/shard_map/ppermute | solution.py:401
  27.5 0.0 collective-permute-start.7
  27.5 4.1 %collective-permute-done.4.refs_2_ = bf16[32,4224]{1,0:T(8,128)(2,1)S(1)} collective-permute-done((bf16[32,4224]{1,0:T(8,128)(2,1)S(1)}, bf16[32,4224]{1,0:T(8,128)(2,1)S(1)}, u32[]{:S(2)}, u32[]{:S(2)}) %collective-permute-start.4) | collective-permute-done | bytes 270368 | tf_op jit(solution)/shard_map/ppermute | solution.py:401
  31.6 0.0 collective-permute-start.8
  31.6 0.0 collective-permute-done.5.refs_3_
  31.6 0.5 collective-permute-start.9
  32.1 1.5 %bitcast_convert_fusion.1.scales_ref = f32[32,1024]{1,0:T(8,128)} fusion(bf16[1,32,1024]{2,1,0:T(8,128)(2,1)} %param.25), kind=kLoop, calls=%fused_computation.1 | loop fusion | flops 32768 | bytes 196608 | tf_op jit(solution)/shard_map/convert_element_type | solution.py:168
  33.6 8.5 %unpack_weights.2 = bf16[4,1024,1024]{2,1,0:T(8,128)(2,1)} custom-call(f32[1024,1024]{1,0:T(8,128)} %bitcast.18, f32[32,1024]{1,0:T(8,128)} %bitcast_convert_fusion.1.scales_ref), custom_call_target="tpu_custom_call" | custom-call | flops 25165824 | bytes 12582912 | tf_op jit(solution)/shard_map/unpack_weights/pallas_call | solution.py:154
  42.2 0.7 bitcast_convert_fusion.scales_ref
  42.8 8.4 %unpack_weights.3 = bf16[4,1024,1024]{2,1,0:T(8,128)(2,1)} custom-call(f32[1024,1024]{1,0:T(8,128)} %bitcast.19, f32[32,1024]{1,0:T(8,128)} %bitcast_convert_fusion.scales_ref), custom_call_target="tpu_custom_call" | custom-call | flops 25165824 | bytes 12582912 | tf_op jit(solution)/shard_map/unpack_weights/pallas_call | solution.py:154
  51.3 0.6 copy-done.7
  51.9 0.1 copy-done.8
  52.1 0.1 copy-done.9
  52.2 0.1 copy-done.10
  52.2 10.1 %gate_up.1 = (bf16[256,1024]{1,0:T(8,128)(2,1)}, f32[256,128]{1,0:T(8,128)}) custom-call(s32[1]{0:T(128)} %bitcast.3.place_ref, bf16[32,4224]{1,0:T(8,128)(2,1)} %copy-done.3, bf16[32,4224]{1,0:T(8,128)(2,1)} %copy-done.4, bf16[32,4224]{1,0:T(8,128)(2,1)} %copy-done.5, bf16[32,4224]{1,0:T(8,128)(2,1)} %copy-done.6, bf16[32,4224]{1,0:T(8,128)(2,1)} %copy-done.7, ...), custom_call_target="tpu_custom_call" | custom-call | flops 4294967296 | bytes 18939904 | tf_op jit(solution)/shard_map/gate_up/pallas_call | solution.py:201
  62.3 0.8 collective-permute-start.10
  63.1 0.7 bitcast_convert_fusion.2.scales_ref
  63.8 9.0 %down_own.1 = (f32[256,2048]{1,0:T(8,128)}, bf16[1024,2048]{1,0:T(8,128)(2,1)}) custom-call(s32[1]{0:T(128)} %bitcast.place_ref.side_ref, f32[512,2048]{1,0:T(8,128)} %bitcast.20, f32[16,2048]{1,0:T(8,128)} %bitcast_convert_fusion.2.scales_ref, bf16[256,1024]{1,0:T(8,128)(2,1)} %get-tuple-element.25.hidden_ref), custom_call_target="tpu_custom_call" | custom-call | flops 1098907648 | bytes 10485760 | tf_op jit(solution)/shard_map/down_own/pallas_call | solution.py:257
  72.8 3.7 %collective-permute-done.10.hidden_ref = bf16[256,1024]{1,0:T(8,128)(2,1)S(1)} collective-permute-done((bf16[256,1024]{1,0:T(8,128)(2,1)}, bf16[256,1024]{1,0:T(8,128)(2,1)S(1)}, u32[]{:S(2)}, u32[]{:S(2)}) %collective-permute-start.10) | collective-permute-done | bytes 524320 | tf_op jit(solution)/shard_map/ppermute | solution.py:401
  76.5 0.8 copy-done.2
  77.3 5.5 %down_peer.1 = (bf16[128,2048]{1,0:T(8,128)(2,1)}, bf16[128,2048]{1,0:T(8,128)(2,1)}) custom-call(f32[256,2048]{1,0:T(8,128)} %get-tuple-element.26.partial_ref, bf16[256,1024]{1,0:T(8,128)(2,1)} %copy-done.2, bf16[1024,2048]{1,0:T(8,128)(2,1)} %get-tuple-element.27.weight_ref, f32[256,128]{1,0:T(8,128)} %get-tuple-element.28.share_ref), custom_call_target="tpu_custom_call" | custom-call | flops 1073741824 | bytes 7340032 | tf_op jit(solution)/shard_map/down_peer/pallas_call | solution.py:309
  82.8 2.1 %collective-permute-done.11.arrived_ref = bf16[128,2048]{1,0:T(8,128)(2,1)S(1)} collective-permute-done((bf16[128,2048]{1,0:T(8,128)(2,1)}, bf16[128,2048]{1,0:T(8,128)(2,1)S(1)}, u32[]{:S(2)}, u32[]{:S(2)}) %collective-permute-start.11) | collective-permute-done | bytes 524320 | tf_op jit(solution)/shard_map/ppermute | solution.py:401
  84.9 1.0 copy-done
  85.9 0.1 add_and_cut.2
  86.1 1.6 %collective-permute-start.12 = (bf16[64,2048]{1,0:T(8,128)(2,1)S(1)}, bf16[64,2048]{1,0:T(8,128)(2,1)S(1)}, u32[]{:S(2)}, u32[]{:S(2)}) collective-permute-start(bf16[64,2048]{1,0:T(8,128)(2,1)S(1)} %get-tuple-element.32), channel_id=1, source_target_pairs={{0,2},{1,3},{2,0},{3,1},{4,6},{5,7},{6,4},{7,5},{8,10},{9,11},{10,... | collective-permute-start | bytes 786440 | tf_op jit(solution)/shard_map/ppermute | solution.py:401
  87.6 6.8 %collective-permute-done.12.arrived_ref = bf16[64,2048]{1,0:T(8,128)(2,1)S(1)} collective-permute-done((bf16[64,2048]{1,0:T(8,128)(2,1)S(1)}, bf16[64,2048]{1,0:T(8,128)(2,1)S(1)}, u32[]{:S(2)}, u32[]{:S(2)}) %collective-permute-start.12) | collective-permute-done | bytes 262176 | tf_op jit(solution)/shard_map/ppermute | solution.py:401
  94.5 0.1 add_and_cut.3
  94.5 0.9 collective-permute-start.13
  95.4 1.4 %collective-permute-start.14 = (bf16[8,2048]{1,0:T(8,128)(2,1)S(1)}, bf16[8,2048]{1,0:T(8,128)(2,1)S(1)}, u32[]{:S(2)}, u32[]{:S(2)}) collective-permute-start(bf16[8,2048]{1,0:T(8,128)(2,1)S(1)} %get-tuple-element.35), channel_id=1, source_target_pairs={{0,8},{1,9},{2,10},{3,11},{4,12},{5,13},{6,14},{7,15},{8,0},{9,1},... | collective-permute-start | bytes 98312 | tf_op jit(solution)/shard_map/ppermute | solution.py:401
  96.8 2.1 %collective-permute-start.15 = (bf16[8,2048]{1,0:T(8,128)(2,1)S(1)}, bf16[8,2048]{1,0:T(8,128)(2,1)S(1)}, u32[]{:S(2)}, u32[]{:S(2)}) collective-permute-start(bf16[8,2048]{1,0:T(8,128)(2,1)S(1)} %get-tuple-element.36), channel_id=1, source_target_pairs={{0,12},{1,13},{2,14},{3,15},{4,8},{5,9},{6,10},{7,11},{8,4},{9,5},... | collective-permute-start | bytes 98312 | tf_op jit(solution)/shard_map/ppermute | solution.py:401
  99.0 1.1 %collective-permute-start.16 = (bf16[8,2048]{1,0:T(8,128)(2,1)S(1)}, bf16[8,2048]{1,0:T(8,128)(2,1)S(1)}, u32[]{:S(2)}, u32[]{:S(2)}) collective-permute-start(bf16[8,2048]{1,0:T(8,128)(2,1)S(1)} %get-tuple-element.37), channel_id=1, source_target_pairs={{0,16},{1,17},{2,18},{3,19},{4,20},{5,21},{6,22},{7,23},{8,24},{9,... | collective-permute-start | bytes 98312 | tf_op jit(solution)/shard_map/ppermute | solution.py:401
  100.1 0.3 collective-permute-start.17
  100.4 2.9 %collective-permute-start.18 = (bf16[8,2048]{1,0:T(8,128)(2,1)S(1)}, bf16[8,2048]{1,0:T(8,128)(2,1)S(1)}, u32[]{:S(2)}, u32[]{:S(2)}) collective-permute-start(bf16[8,2048]{1,0:T(8,128)(2,1)S(1)} %get-tuple-element.39), channel_id=1, source_target_pairs={{0,24},{1,25},{2,26},{3,27},{4,28},{5,29},{6,30},{7,31},{8,16},{9,... | collective-permute-start | bytes 98312 | tf_op jit(solution)/shard_map/ppermute | solution.py:401
  103.3 2.5 %collective-permute-start.19 = (bf16[8,2048]{1,0:T(8,128)(2,1)S(1)}, bf16[8,2048]{1,0:T(8,128)(2,1)S(1)}, u32[]{:S(2)}, u32[]{:S(2)}) collective-permute-start(bf16[8,2048]{1,0:T(8,128)(2,1)S(1)} %get-tuple-element.40), channel_id=1, source_target_pairs={{0,28},{1,29},{2,30},{3,31},{4,24},{5,25},{6,26},{7,27},{8,20},{9,... | collective-permute-start | bytes 98312 | tf_op jit(solution)/shard_map/ppermute | solution.py:401
  105.8 0.3 collective-permute-done.18.refs_6_
  106.1 3.8 %collective-permute-done.19.refs_7_ = bf16[8,2048]{1,0:T(8,128)(2,1)S(1)} collective-permute-done((bf16[8,2048]{1,0:T(8,128)(2,1)S(1)}, bf16[8,2048]{1,0:T(8,128)(2,1)S(1)}, u32[]{:S(2)}, u32[]{:S(2)}) %collective-permute-start.19) | collective-permute-done | bytes 32800 | tf_op jit(solution)/shard_map/ppermute | solution.py:401
  109.9 0.7 finish.1
  (35 shorter events, 0.1 us)
Async XLA Ops:
  6.0 6.6 %collective-permute-start = (bf16[8,4224]{1,0:T(8,128)(2,1)}, bf16[8,4224]{1,0:T(8,128)(2,1)S(1)}, u32[]{:S(2)}, u32[]{:S(2)}) collective-permute-start(bf16[8,4224]{1,0:T(8,128)(2,1)} %get-tuple-element.24), channel_id=1, source_target_pairs={{0,4},{1,5},{2,6},{3,7},{4,0},{5,1},{6,2},{7,3},{8,12},{9,13},{10,... | collective-permute-start | bytes 202760 | tf_op jit(solution)/shard_map/ppermute | solution.py:401
  9.0 7.6 %collective-permute-start.1 = (bf16[8,4224]{1,0:T(8,128)(2,1)}, bf16[8,4224]{1,0:T(8,128)(2,1)S(1)}, u32[]{:S(2)}, u32[]{:S(2)}) collective-permute-start(bf16[8,4224]{1,0:T(8,128)(2,1)} %get-tuple-element.24), channel_id=1, source_target_pairs={{0,8},{1,9},{2,10},{3,11},{4,12},{5,13},{6,14},{7,15},{8,0},{9,1},... | collective-permute-start | bytes 202760 | tf_op jit(solution)/shard_map/ppermute | solution.py:401
  11.6 6.4 %collective-permute-start.2 = (bf16[8,4224]{1,0:T(8,128)(2,1)}, bf16[8,4224]{1,0:T(8,128)(2,1)S(1)}, u32[]{:S(2)}, u32[]{:S(2)}) collective-permute-start(bf16[8,4224]{1,0:T(8,128)(2,1)} %get-tuple-element.24), channel_id=1, source_target_pairs={{0,12},{1,13},{2,14},{3,15},{4,8},{5,9},{6,10},{7,11},{8,4},{9,5},... | collective-permute-start | bytes 202760 | tf_op jit(solution)/shard_map/ppermute | solution.py:401
  18.0 24.1 %copy-start.3 = (bf16[32,4224]{1,0:T(8,128)(2,1)}, bf16[32,4224]{1,0:T(8,128)(2,1)S(1)}, u32[]{:S(2)}) copy-start(bf16[32,4224]{1,0:T(8,128)(2,1)S(1)} %constant_dynamic-update-slice_fusion.refs_0_) | copy-start | bytes 811012
  18.0 9.5 %collective-permute-start.3 = (bf16[32,4224]{1,0:T(8,128)(2,1)S(1)}, bf16[32,4224]{1,0:T(8,128)(2,1)S(1)}, u32[]{:S(2)}, u32[]{:S(2)}) collective-permute-start(bf16[32,4224]{1,0:T(8,128)(2,1)S(1)} %constant_dynamic-update-slice_fusion.refs_0_), channel_id=1, source_target_pairs={{0,16},{1,17},{2,18},{3,19},{4,20},{5,21},{6,22},{7,23},{8,24},{9,... | collective-permute-start | bytes 811016 | tf_op jit(solution)/shard_map/ppermute | solution.py:401
  19.6 12.0 %collective-permute-start.4 = (bf16[32,4224]{1,0:T(8,128)(2,1)S(1)}, bf16[32,4224]{1,0:T(8,128)(2,1)S(1)}, u32[]{:S(2)}, u32[]{:S(2)}) collective-permute-start(bf16[32,4224]{1,0:T(8,128)(2,1)S(1)} %constant_dynamic-update-slice_fusion.refs_0_), channel_id=1, source_target_pairs={{0,2},{1,3},{2,0},{3,1},{4,6},{5,7},{6,4},{7,5},{8,10},{9,11},{10,... | collective-permute-start | bytes 811016 | tf_op jit(solution)/shard_map/ppermute | solution.py:401
  21.1 10.5 %collective-permute-start.5 = (bf16[32,4224]{1,0:T(8,128)(2,1)S(1)}, bf16[32,4224]{1,0:T(8,128)(2,1)S(1)}, u32[]{:S(2)}, u32[]{:S(2)}) collective-permute-start(bf16[32,4224]{1,0:T(8,128)(2,1)S(1)} %constant_dynamic-update-slice_fusion.refs_0_), channel_id=1, source_target_pairs={{0,18},{1,19},{2,16},{3,17},{4,22},{5,23},{6,20},{7,21},{8,26},{9,... | collective-permute-start | bytes 811016 | tf_op jit(solution)/shard_map/ppermute | solution.py:401
  21.6 29.7 %collective-permute-start.6 = (bf16[32,4224]{1,0:T(8,128)(2,1)S(1)}, bf16[32,4224]{1,0:T(8,128)(2,1)S(1)}, u32[]{:S(2)}, u32[]{:S(2)}) collective-permute-start(bf16[32,4224]{1,0:T(8,128)(2,1)S(1)} %constant_dynamic-update-slice_fusion.refs_0_), channel_id=1, source_target_pairs={{0,1},{1,0},{2,3},{3,2},{4,5},{5,4},{6,7},{7,6},{8,9},{9,8},{10,11... | collective-permute-start | bytes 811016 | tf_op jit(solution)/shard_map/ppermute | solution.py:401
  27.5 14.6 %copy-start.4 = (bf16[32,4224]{1,0:T(8,128)(2,1)}, bf16[32,4224]{1,0:T(8,128)(2,1)S(1)}, u32[]{:S(2)}) copy-start(bf16[32,4224]{1,0:T(8,128)(2,1)S(1)} %collective-permute-done.3.refs_1_) | copy-start | bytes 811012
  27.5 23.7 %collective-permute-start.7 = (bf16[32,4224]{1,0:T(8,128)(2,1)S(1)}, bf16[32,4224]{1,0:T(8,128)(2,1)S(1)}, u32[]{:S(2)}, u32[]{:S(2)}) collective-permute-start(bf16[32,4224]{1,0:T(8,128)(2,1)S(1)} %collective-permute-done.3.refs_1_), channel_id=1, source_target_pairs={{0,1},{1,0},{2,3},{3,2},{4,5},{5,4},{6,7},{7,6},{8,9},{9,8},{10,11... | collective-permute-start | bytes 811016 | tf_op jit(solution)/shard_map/ppermute | solution.py:401
  31.6 10.5 %copy-start.5 = (bf16[32,4224]{1,0:T(8,128)(2,1)}, bf16[32,4224]{1,0:T(8,128)(2,1)S(1)}, u32[]{:S(2)}) copy-start(bf16[32,4224]{1,0:T(8,128)(2,1)S(1)} %collective-permute-done.4.refs_2_) | copy-start | bytes 811012
  31.6 19.7 %collective-permute-start.8 = (bf16[32,4224]{1,0:T(8,128)(2,1)S(1)}, bf16[32,4224]{1,0:T(8,128)(2,1)S(1)}, u32[]{:S(2)}, u32[]{:S(2)}) collective-permute-start(bf16[32,4224]{1,0:T(8,128)(2,1)S(1)} %collective-permute-done.4.refs_2_), channel_id=1, source_target_pairs={{0,1},{1,0},{2,3},{3,2},{4,5},{5,4},{6,7},{7,6},{8,9},{9,8},{10,11... | collective-permute-start | bytes 811016 | tf_op jit(solution)/shard_map/ppermute | solution.py:401
  31.6 10.5 %copy-start.6 = (bf16[32,4224]{1,0:T(8,128)(2,1)}, bf16[32,4224]{1,0:T(8,128)(2,1)S(1)}, u32[]{:S(2)}) copy-start(bf16[32,4224]{1,0:T(8,128)(2,1)S(1)} %collective-permute-done.5.refs_3_) | copy-start | bytes 811012
  31.6 19.7 %collective-permute-start.9 = (bf16[32,4224]{1,0:T(8,128)(2,1)S(1)}, bf16[32,4224]{1,0:T(8,128)(2,1)S(1)}, u32[]{:S(2)}, u32[]{:S(2)}) collective-permute-start(bf16[32,4224]{1,0:T(8,128)(2,1)S(1)} %collective-permute-done.5.refs_3_), channel_id=1, source_target_pairs={{0,1},{1,0},{2,3},{3,2},{4,5},{5,4},{6,7},{7,6},{8,9},{9,8},{10,11... | collective-permute-start | bytes 811016 | tf_op jit(solution)/shard_map/ppermute | solution.py:401
  33.6 8.5 %copy-start.11 = (bf16[1,32,1024]{2,1,0:T(8,128)(2,1)S(1)}, bf16[1,32,1024]{2,1,0:T(8,128)(2,1)}, u32[]{:S(2)}) copy-start(bf16[1,32,1024]{2,1,0:T(8,128)(2,1)} %param.27) | copy-start | bytes 196612
  51.2 0.7 copy-start.7
  51.3 0.8 copy-start.8
  51.3 0.9 copy-start.9
  51.3 0.9 copy-start.10
  52.2 10.9 %copy-start.12 = (bf16[1,16,2048]{2,1,0:T(8,128)(2,1)S(1)}, bf16[1,16,2048]{2,1,0:T(8,128)(2,1)}, u32[]{:S(2)}) copy-start(bf16[1,16,2048]{2,1,0:T(8,128)(2,1)} %param.29) | copy-start | bytes 196612
  62.3 14.2 %collective-permute-start.10 = (bf16[256,1024]{1,0:T(8,128)(2,1)}, bf16[256,1024]{1,0:T(8,128)(2,1)S(1)}, u32[]{:S(2)}, u32[]{:S(2)}) collective-permute-start(bf16[256,1024]{1,0:T(8,128)(2,1)} %get-tuple-element.25.hidden_ref), channel_id=1, source_target_pairs={{0,16},{1,17},{2,18},{3,19},{4,20},{5,21},{6,22},{7,23},{8,24},{9,... | collective-permute-start | bytes 1572872 | tf_op jit(solution)/shard_map/ppermute | solution.py:401
  76.5 0.8 copy-start.2
  77.3 32.6 %copy-start.1 = (bf16[8,4096]{1,0:T(8,128)(2,1)S(1)}, bf16[8,4096]{1,0:T(8,128)(2,1)}, u32[]{:S(2)}) copy-start(bf16[8,4096]{1,0:T(8,128)(2,1)} %get-tuple-element.23.mixed_ref) | copy-start | bytes 196612
  82.8 2.1 %collective-permute-start.11 = (bf16[128,2048]{1,0:T(8,128)(2,1)}, bf16[128,2048]{1,0:T(8,128)(2,1)S(1)}, u32[]{:S(2)}, u32[]{:S(2)}) collective-permute-start(bf16[128,2048]{1,0:T(8,128)(2,1)} %get-tuple-element.30), channel_id=1, source_target_pairs={{0,1},{1,0},{2,3},{3,2},{4,5},{5,4},{6,7},{7,6},{8,9},{9,8},{10,11... | collective-permute-start | bytes 1572872 | tf_op jit(solution)/shard_map/ppermute | solution.py:401
  84.9 1.0 copy-start
  86.1 8.4 %collective-permute-start.12 = (bf16[64,2048]{1,0:T(8,128)(2,1)S(1)}, bf16[64,2048]{1,0:T(8,128)(2,1)S(1)}, u32[]{:S(2)}, u32[]{:S(2)}) collective-permute-start(bf16[64,2048]{1,0:T(8,128)(2,1)S(1)} %get-tuple-element.32), channel_id=1, source_target_pairs={{0,2},{1,3},{2,0},{3,1},{4,6},{5,7},{6,4},{7,5},{8,10},{9,11},{10,... | collective-permute-start | bytes 786440 | tf_op jit(solution)/shard_map/ppermute | solution.py:401
  94.5 5.8 %collective-permute-start.13 = (bf16[8,2048]{1,0:T(8,128)(2,1)S(1)}, bf16[8,2048]{1,0:T(8,128)(2,1)S(1)}, u32[]{:S(2)}, u32[]{:S(2)}) collective-permute-start(bf16[8,2048]{1,0:T(8,128)(2,1)S(1)} %get-tuple-element.34), channel_id=1, source_target_pairs={{0,4},{1,5},{2,6},{3,7},{4,0},{5,1},{6,2},{7,3},{8,12},{9,13},{10,... | collective-permute-start | bytes 98312 | tf_op jit(solution)/shard_map/ppermute | solution.py:401
  95.4 7.9 %collective-permute-start.14 = (bf16[8,2048]{1,0:T(8,128)(2,1)S(1)}, bf16[8,2048]{1,0:T(8,128)(2,1)S(1)}, u32[]{:S(2)}, u32[]{:S(2)}) collective-permute-start(bf16[8,2048]{1,0:T(8,128)(2,1)S(1)} %get-tuple-element.35), channel_id=1, source_target_pairs={{0,8},{1,9},{2,10},{3,11},{4,12},{5,13},{6,14},{7,15},{8,0},{9,1},... | collective-permute-start | bytes 98312 | tf_op jit(solution)/shard_map/ppermute | solution.py:401
  96.8 8.9 %collective-permute-start.15 = (bf16[8,2048]{1,0:T(8,128)(2,1)S(1)}, bf16[8,2048]{1,0:T(8,128)(2,1)S(1)}, u32[]{:S(2)}, u32[]{:S(2)}) collective-permute-start(bf16[8,2048]{1,0:T(8,128)(2,1)S(1)} %get-tuple-element.36), channel_id=1, source_target_pairs={{0,12},{1,13},{2,14},{3,15},{4,8},{5,9},{6,10},{7,11},{8,4},{9,5},... | collective-permute-start | bytes 98312 | tf_op jit(solution)/shard_map/ppermute | solution.py:401
  99.0 6.8 %collective-permute-start.16 = (bf16[8,2048]{1,0:T(8,128)(2,1)S(1)}, bf16[8,2048]{1,0:T(8,128)(2,1)S(1)}, u32[]{:S(2)}, u32[]{:S(2)}) collective-permute-start(bf16[8,2048]{1,0:T(8,128)(2,1)S(1)} %get-tuple-element.37), channel_id=1, source_target_pairs={{0,16},{1,17},{2,18},{3,19},{4,20},{5,21},{6,22},{7,23},{8,24},{9,... | collective-permute-start | bytes 98312 | tf_op jit(solution)/shard_map/ppermute | solution.py:401
  100.1 5.6 %collective-permute-start.17 = (bf16[8,2048]{1,0:T(8,128)(2,1)S(1)}, bf16[8,2048]{1,0:T(8,128)(2,1)S(1)}, u32[]{:S(2)}, u32[]{:S(2)}) collective-permute-start(bf16[8,2048]{1,0:T(8,128)(2,1)S(1)} %get-tuple-element.38), channel_id=1, source_target_pairs={{0,20},{1,21},{2,22},{3,23},{4,16},{5,17},{6,18},{7,19},{8,28},{9,... | collective-permute-start | bytes 98312 | tf_op jit(solution)/shard_map/ppermute | solution.py:401
  100.4 5.7 %collective-permute-start.18 = (bf16[8,2048]{1,0:T(8,128)(2,1)S(1)}, bf16[8,2048]{1,0:T(8,128)(2,1)S(1)}, u32[]{:S(2)}, u32[]{:S(2)}) collective-permute-start(bf16[8,2048]{1,0:T(8,128)(2,1)S(1)} %get-tuple-element.39), channel_id=1, source_target_pairs={{0,24},{1,25},{2,26},{3,27},{4,28},{5,29},{6,30},{7,31},{8,16},{9,... | collective-permute-start | bytes 98312 | tf_op jit(solution)/shard_map/ppermute | solution.py:401
  103.3 6.6 %collective-permute-start.19 = (bf16[8,2048]{1,0:T(8,128)(2,1)S(1)}, bf16[8,2048]{1,0:T(8,128)(2,1)S(1)}, u32[]{:S(2)}, u32[]{:S(2)}) collective-permute-start(bf16[8,2048]{1,0:T(8,128)(2,1)S(1)} %get-tuple-element.40), channel_id=1, source_target_pairs={{0,28},{1,29},{2,30},{3,31},{4,24},{5,25},{6,26},{7,27},{8,20},{9,... | collective-permute-start | bytes 98312 | tf_op jit(solution)/shard_map/ppermute | solution.py:401

commit v2 on v1

v2 whole, which is shorter than its diff:
```python
import functools

import jax
import jax.numpy as jnp
from jax import lax
from jax.experimental import pallas as pl
from jax.experimental.pallas import tpu as pltpu
from jax.sharding import PartitionSpec as P

HEAD_DIM = 128
GROUP = 128
TOP = 8
LANES = 128
VMEM_LIMIT = 56 * 2**20
VMEM_SOME = 16 * 2**20
SMALL = pl.CostEstimate(flops=1, bytes_accessed=1, transcendentals=0)
F32 = jnp.float32
BF16 = jnp.bfloat16


def front_kernel(
    lengths_ref,
    queries_ref,
    new_kv_ref,
    keys_ref,
    values_ref,
    residual_ref,
    gain_ref,
    routes_ref,
    weights_ref,
    mixed_ref,
    payload_ref,
):
    rows, cache, kv_width = keys_ref.shape
    width = queries_ref.shape[1]
    kv_heads = kv_width // HEAD_DIM
    per = width // kv_width
    scaling = HEAD_DIM ** (-0.5)
    row_id = lax.broadcasted_iota(jnp.int32, (rows, rows * cache), 0)
    lane_id = lax.broadcasted_iota(jnp.int32, (rows, rows * cache), 1)
    bound = jnp.zeros((rows, rows * cache), jnp.int32)
    for r in range(rows):
        bound = jnp.where(row_id == r, r * cache + lengths_ref[r], bound)
    valid = (lane_id >= row_id * cache) & (lane_id < bound)
    earlier, current = [], []
    for j in range(kv_heads):
        span = slice(j * HEAD_DIM, (j + 1) * HEAD_DIM)
        heads = range(j * per, (j + 1) * per)
        queried = jnp.concatenate(
            [queries_ref[:, h * HEAD_DIM : (h + 1) * HEAD_DIM].astype(F32) for h in heads], axis=0
        )
        keys = keys_ref[:, :, span].reshape(rows * cache, HEAD_DIM)
        earlier.append(
            lax.dot_general(
                queried.astype(BF16), keys, (((1,), (1,)), ((), ())), preferred_element_type=F32
            )
        )
        fresh_key = new_kv_ref[:, 0, span].astype(F32)
        current.append(queried.reshape(per, rows, HEAD_DIM) * fresh_key[None])
    earlier = jnp.concatenate(earlier, axis=0).reshape(kv_heads * per, rows, rows * cache)
    earlier = jnp.where(valid[None], earlier * scaling, -1e30)
    current = jnp.sum(jnp.concatenate(current, axis=0), axis=-1, keepdims=True) * scaling
    largest = jnp.maximum(jnp.max(earlier, axis=-1, keepdims=True), current)
    earlier_w = jnp.where(valid[None], jnp.exp(earlier - largest), 0.0)
    current_w = jnp.exp(current - largest)
    inverse = 1.0 / (jnp.sum(earlier_w, axis=-1, keepdims=True) + current_w)
    earlier_p = (earlier_w * inverse).astype(BF16).reshape(kv_heads * per * rows, rows * cache)
    current_p = (current_w * inverse).astype(BF16).astype(F32)
    total = jnp.zeros((rows, HEAD_DIM), F32)
    for j in range(kv_heads):
        span = slice(j * HEAD_DIM, (j + 1) * HEAD_DIM)
        values = values_ref[:, :, span].reshape(rows * cache, HEAD_DIM)
        fresh_value = new_kv_ref[:, 1, span].astype(F32)
        attended = jnp.dot(
            earlier_p[j * per * rows : (j + 1) * per * rows], values, preferred_element_type=F32
        )
        attended = attended.reshape(per, rows, HEAD_DIM)
        attended = attended + current_p[j * per : (j + 1) * per] * fresh_value[None]
        for g in range(per):
            h = j * per + g
            place = slice(h * HEAD_DIM, (h + 1) * HEAD_DIM)
            mixed = (
                residual_ref[:, place].astype(F32) + attended[g].astype(BF16).astype(F32)
            ).astype(BF16)
            mixed_ref[:, place] = mixed
            widened = mixed.astype(F32)
            total = total + widened * widened
    meansq = jnp.sum(total, axis=-1, keepdims=True) * (1.0 / width)
    inverse = lax.rsqrt(meansq + 1e-06)
    payload_ref[:, :width] = (
        mixed_ref[...].astype(F32) * inverse * gain_ref[...].astype(F32).reshape(1, width)
    ).astype(BF16)
    if payload_ref.shape[1] > width:
        shares = weights_ref[...] / jnp.sum(weights_ref[...], axis=1, keepdims=True)
        lane = lax.broadcasted_iota(jnp.int32, (rows, LANES), 1)
        expert = jnp.where(lane < LANES // 2, lane, lane - LANES // 2)
        table = jnp.zeros((rows, LANES), F32)
        for k in range(routes_ref.shape[1]):
            table = table + jnp.where(
                routes_ref[:, k : k + 1] == expert, shares[:, k : k + 1], 0.0
            )
        high = table.astype(BF16).astype(F32)
        payload_ref[:, width:] = jnp.where(lane < LANES // 2, high, table - high).astype(BF16)


def front(queries, new_kv, keys, values, lengths, residual, gain, routes, weights, extra):
    rows, width = queries.shape
    vmem = pl.BlockSpec(memory_space=pltpu.VMEM)
    return pl.pallas_call(
        front_kernel,
        out_shape=(
            jax.ShapeDtypeStruct((rows, width), BF16),
            jax.ShapeDtypeStruct((rows, width + extra), BF16),
        ),
        in_specs=[pl.BlockSpec(memory_space=pltpu.SMEM)] + [vmem] * 8,
        out_specs=(vmem, vmem),
        compiler_params=pltpu.CompilerParams(vmem_limit_bytes=VMEM_LIMIT),
        cost_estimate=SMALL,
        name="front",
    )(lengths, queries, new_kv, keys, values, residual, gain, routes, weights)


def in_vmem(array):
    return pltpu.with_memory_space_constraint(array, pltpu.VMEM)


def in_hbm(array):
    return pltpu.with_memory_space_constraint(array, pltpu.HBM)


def unpack_kernel(codes_ref, scales_hbm, out_ref, words_ref, scales_ref, sems, scales_sem):
    quarter, width = codes_ref.shape
    groups = quarter // GROUP
    step = 256 if width % 256 == 0 else LANES

    def fetch(group):
        rows = pl.ds(group * GROUP, GROUP)
        return pltpu.make_async_copy(codes_ref.at[rows, :], words_ref.at[rows, :], sems.at[group])

    scales_copy = pltpu.make_async_copy(scales_hbm, scales_ref, scales_sem)
    scales_copy.start()
    ahead = 3
    for group in range(min(ahead, groups)):
        fetch(group).start()
    scales_copy.wait()
    scales = scales_ref[...].astype(F32)
    for group in range(groups):
        if group + ahead < groups:
            fetch(group + ahead).start()
        fetch(group).wait()
        for column in range(0, width, step):
            spans = [
                jnp.broadcast_to(
                    scales[k * groups + group : k * groups + group + 1, column : column + step],
                    (16, step),
                ).astype(BF16)
                for k in range(4)
            ]

            def chunk(i, carry, group=group, column=column, spans=spans):
                start = pl.multiple_of(group * GROUP + i * 16, 16)
                words = words_ref[pl.ds(start, 16), column : column + step].astype(jnp.int32)
                words = (words ^ 0x8888).astype(jnp.int16)
                for k in range(4):
                    level = words if k == 3 else lax.shift_left(words, jnp.int16(12 - 4 * k))
                    level = lax.shift_right_arithmetic(level, jnp.int16(12))
                    out_ref[pl.ds(k * quarter + start, 16), column : column + step] = (
                        level.astype(BF16) * spans[k]
                    )
                return carry

            lax.fori_loop(0, GROUP // 16, chunk, 0, unroll=True)


def unpack_weights(codes, scales):
    quarter, width = codes.shape
    return pl.pallas_call(
        unpack_kernel,
        out_shape=pltpu.VMEM((4 * quarter, width), BF16),
        in_specs=[pl.BlockSpec(memory_space=pltpu.HBM)] * 2,
        out_specs=pl.BlockSpec(memory_space=pltpu.VMEM),
        scratch_shapes=[
            pltpu.VMEM((quarter, width), F32),
            pltpu.VMEM(scales.shape, BF16),
            pltpu.SemaphoreType.DMA((quarter // GROUP,)),
            pltpu.SemaphoreType.DMA,
        ],
        compiler_params=pltpu.CompilerParams(vmem_limit_bytes=VMEM_SOME),
        cost_estimate=SMALL,
        name="unpack_weights",
    )(in_hbm(codes), in_hbm(scales))


def hidden_kernel(place_ref, *refs):
    pieces, (gate_ref, up_ref, out_ref, share_ref, rows_ref) = refs[:-5], refs[-5:]
    depth, width = gate_ref.shape
    block = pieces[0].shape[0]
    for n, piece in enumerate(pieces):
        rows_ref[n * block : (n + 1) * block, :] = piece[:, :depth]
        table = piece[:, depth:].astype(F32)
        lane = lax.broadcasted_iota(jnp.int32, table.shape, 1)
        mine = place_ref[0]
        chosen = (lane == mine) | (lane == mine + LANES // 2)
        share = jnp.sum(jnp.where(chosen, table, 0.0), axis=1, keepdims=True)
        share_ref[n * block : (n + 1) * block, :] = jnp.broadcast_to(share, table.shape)
    step = 256
    for column in range(0, width, step):
        span = slice(column, column + step)
        gate = jnp.dot(rows_ref[...], gate_ref[:, span], preferred_element_type=F32)
        upward = jnp.dot(rows_ref[...], up_ref[:, span], preferred_element_type=F32)
        out_ref[:, span] = (gate / (1.0 + jnp.exp(-gate)) * upward).astype(BF16)


def hidden_units(pieces, w_gate, w_up, place):
    block, padded = pieces[0].shape
    count = block * len(pieces)
    depth, width = w_gate.shape
    vmem = pl.BlockSpec(memory_space=pltpu.VMEM)
    return pl.pallas_call(
        hidden_kernel,
        out_shape=(pltpu.VMEM((count, width), BF16), pltpu.VMEM((count, LANES), F32)),
        in_specs=[pl.BlockSpec(memory_space=pltpu.SMEM)] + [vmem] * (len(pieces) + 2),
        out_specs=(vmem, vmem),
        scratch_shapes=[pltpu.VMEM((count, depth), BF16)],
        compiler_params=pltpu.CompilerParams(vmem_limit_bytes=VMEM_SOME),
        cost_estimate=SMALL,
        name="gate_up",
    )(place, *pieces, in_vmem(w_gate), in_vmem(w_up))


def own_down_kernel(side_ref, hidden_ref, weight_ref, out_ref):
    half = hidden_ref.shape[1]
    rows = pl.ds(pl.multiple_of(side_ref[0] * half, half), half)
    step = 256
    for column in range(0, out_ref.shape[1], step):
        span = slice(column, column + step)
        out_ref[:, span] = jnp.dot(
            hidden_ref[...], weight_ref[rows, span], preferred_element_type=F32
        )


def own_down(side, hidden, weight):
    count, half = hidden.shape
    width = weight.shape[1]
    vmem = pl.BlockSpec(memory_space=pltpu.VMEM)
    return pl.pallas_call(
        own_down_kernel,
        out_shape=pltpu.VMEM((count, width), F32),
        in_specs=[pl.BlockSpec(memory_space=pltpu.SMEM), vmem, vmem],
        out_specs=vmem,
        compiler_params=pltpu.CompilerParams(vmem_limit_bytes=VMEM_SOME),
        cost_estimate=SMALL,
        name="down_own",
    )(side, in_vmem(hidden), in_vmem(weight))


def peer_down_kernel(
    side_ref, partial_ref, hidden_ref, weight_ref, share_ref, keep_ref, send_ref
):
    count, half = hidden_ref.shape
    rows = pl.ds(pl.multiple_of((1 - side_ref[0]) * half, half), half)
    step = 256
    for column in range(0, keep_ref.shape[1], step):
        span = slice(column, column + step)
        produced = partial_ref[:, span] + jnp.dot(
            hidden_ref[...], weight_ref[rows, span], preferred_element_type=F32
        )
        result = (produced.astype(BF16).astype(F32) * share_ref[:, :1]).astype(BF16)
        keep_ref[:, span] = result[: count // 2]
        send_ref[:, span] = result[count // 2 :]


def peer_down(side, partial, hidden, weight, share):
    count, width = partial.shape
    half = hidden.shape[1]
    shape = pltpu.VMEM((count // 2, width), BF16)
    vmem = pl.BlockSpec(memory_space=pltpu.VMEM)
    return pl.pallas_call(
        peer_down_kernel,
        out_shape=(shape, shape),
        in_specs=[pl.BlockSpec(memory_space=pltpu.SMEM)] + [vmem] * 4,
        out_specs=(vmem, vmem),
        compiler_params=pltpu.CompilerParams(vmem_limit_bytes=VMEM_SOME),
        cost_estimate=SMALL,
        name="down_peer",
    )(side, in_vmem(partial), hidden, in_vmem(weight), in_vmem(share))


def halve_kernel(terms, *refs):
    term_refs, out_refs = refs[:terms], refs[terms:]
    total = term_refs[0][...].astype(F32)
    for term_ref in term_refs[1:]:
        total = total + term_ref[...].astype(F32)
    size = total.shape[0] // len(out_refs)
    for n, out_ref in enumerate(out_refs):
        out_ref[...] = total[n * size : (n + 1) * size].astype(out_ref.dtype)


def add_and_cut(kept, arrived, parts):
    count, width = kept[0].shape
    vmem = pl.BlockSpec(memory_space=pltpu.VMEM)
    shape = pltpu.VMEM((count // parts, width), BF16)
    return pl.pallas_call(
        functools.partial(halve_kernel, len(kept + arrived)),
        out_shape=(shape,) * parts,
        in_specs=[vmem] * len(kept + arrived),
        out_specs=(vmem,) * parts,
        compiler_params=pltpu.CompilerParams(vmem_limit_bytes=VMEM_SOME),
        cost_estimate=SMALL,
        name="add_and_cut",
    )(*[in_vmem(part) for part in kept], *arrived)


def finish_kernel(side_ref, mixed_ref, far_ref, *refs):
    near_refs, out_ref = refs[:-1], refs[-1]
    half = far_ref.shape[1]
    near = near_refs[0][...].astype(F32)
    for near_ref in near_refs[1:]:
        near = near + near_ref[...].astype(F32)
    far = far_ref[...].astype(F32)
    first = side_ref[0] == 0
    for n, part in enumerate((jnp.where(first, near, far), jnp.where(first, far, near))):
        span = slice(n * half, (n + 1) * half)
        out_ref[:, span] = (mixed_ref[:, span].astype(F32) + part).astype(BF16)


def finish(side, mixed, far, near):
    vmem = pl.BlockSpec(memory_space=pltpu.VMEM)
    return pl.pallas_call(
        finish_kernel,
        out_shape=jax.ShapeDtypeStruct(mixed.shape, BF16),
        in_specs=[pl.BlockSpec(memory_space=pltpu.SMEM)] + [vmem] * (2 + len(near)),
        out_specs=vmem,
        compiler_params=pltpu.CompilerParams(vmem_limit_bytes=VMEM_SOME),
        name="finish",
    )(side, mixed, far, *near)


def dense(payload, mixed, codes):
    gate_codes, gate_scales, up_codes, up_scales, down_codes, down_scales = codes
    groups = lax.axis_size("dp")
    experts = lax.axis_size("expert")
    devices = groups * experts
    core, line, layer, plane = 1, 2, 4, experts
    layers = experts // layer
    side = lax.axis_index("dp").reshape(1).astype(jnp.int32)
    place = lax.axis_index("expert").reshape(1).astype(jnp.int32)

    def swap(block, offset):
        return lax.ppermute(block, ("dp", "expert"), [(i, i ^ offset) for i in range(devices)])

    side, place, gate_scales, payload = lax.optimization_barrier(
        (side, place, gate_scales, payload)
    )
    blocks = [swap(payload, z * layer) for z in range(1, layers)]
    w_gate = unpack_weights(gate_codes, gate_scales)
    blocks, w_gate = lax.optimization_barrier((blocks, w_gate))
    stack = jnp.concatenate([payload] + blocks, axis=0)
    up_scales, stack = lax.optimization_barrier((up_scales, stack))
    beside, above, stack_pair = swap(stack, plane), swap(stack, line), swap(stack, core)
    w_up = unpack_weights(up_codes, up_scales)
    above, w_up = lax.optimization_barrier((above, w_up))
    across, above_pair = swap(above, plane), swap(above, core)
    above_pair, beside = lax.optimization_barrier((above_pair, beside))
    beside_pair = swap(beside, core)
    hidden_own, share_own = hidden_units(
        [stack, above, stack_pair, above_pair], w_gate, w_up, place
    )
    other_peer = swap(hidden_own, plane)
    down_scales, hidden_own = lax.optimization_barrier((down_scales, hidden_own))
    w_down = unpack_weights(down_codes, down_scales)
    across, w_down = lax.optimization_barrier((across, w_down))
    hidden_other, share_other = hidden_units(
        [beside, across, beside_pair, swap(across, core)], w_gate, w_up, place
    )
    own_peer = swap(hidden_other, plane)

    def over_core(keep, send):
        return add_and_cut([keep], [swap(send, core)], 2)

    def over_expert(keep, send):
        parts = add_and_cut([keep], [swap(send, line)], layers)
        return [parts[0]] + [swap(parts[z], z * layer) for z in range(1, layers)]

    partial_other = own_down(side, hidden_other, w_down)
    partial_own = own_down(side, hidden_own, w_down)
    keep_other, send_other = peer_down(side, partial_other, other_peer, w_down, share_other)
    send_other, partial_own, own_peer = lax.optimization_barrier(
        (send_other, partial_own, own_peer)
    )
    keep_own, send_own = peer_down(side, partial_own, own_peer, w_down, share_own)
    parts = over_expert(*over_core(keep_other, send_other))
    near = over_expert(*over_core(keep_own, send_own))
    (far,) = add_and_cut(parts[:1], parts[1:], 1)
    return finish(side, mixed, swap(far, plane), near)


def slot_table(routes, experts, capacity):
    flattened = routes.reshape(-1)
    onehot = (flattened[:, None] == jnp.arange(experts, dtype=jnp.int32)[None, :]).astype(jnp.int32)
    ranking = jnp.sum((jnp.cumsum(onehot, axis=0) - 1) * onehot, axis=1)
    return (flattened * capacity + ranking).reshape(routes.shape)


def dispatch(block, slots, width):
    targets = jnp.arange(width, dtype=jnp.int32)
    placing = jnp.sum((slots[None, :, :] == targets[:, None, None]).astype(F32), axis=2)
    return jnp.dot(placing.astype(BF16), block, preferred_element_type=F32).astype(BF16)


def unpack(codes, scales):
    quarter, width = codes.shape
    divisors = jnp.array([1.0, 1.0 / 16, 1.0 / 256, 1.0 / 4096], F32)[:, None, None]
    lifted = jnp.floor(codes[None, :, :] * divisors)
    levels = lifted - 16.0 * jnp.floor(lifted * (1.0 / 16)) - 8.0
    height = 4 * quarter
    grouped = levels.reshape(height // GROUP, GROUP, width) * scales.astype(F32)[:, None, :]
    return grouped.reshape(height, width).astype(BF16)


def routed(normed, mixed, routes, route_weights, codes, capacity):
    gate_codes, gate_scales, up_codes, up_scales, down_codes, down_scales = codes
    experts = lax.axis_size("expert")
    groups = lax.axis_size("dp")
    row_count, width = mixed.shape
    own_slots = slot_table(routes, experts, capacity)
    w_gate = unpack(gate_codes, gate_scales)
    w_up = unpack(up_codes, up_scales)
    w_down = unpack(down_codes, down_scales)
    local_units = w_gate.shape[1]
    peer_rows = lax.all_gather(normed, "dp", axis=0, tiled=True).reshape(groups, row_count, width)
    peer_routes = lax.all_gather(routes, "dp", axis=0, tiled=True).reshape(groups, row_count, TOP)

    def build(block, table):
        return dispatch(block, slot_table(table, experts, capacity), experts * capacity)

    outgoing = jax.vmap(build)(peer_rows, peer_routes).reshape(groups, experts, capacity, width)
    items = lax.all_to_all(outgoing, "expert", split_axis=1, concat_axis=1, tiled=True)
    inputs = items.reshape(-1, width)
    gate = jnp.dot(inputs, w_gate, preferred_element_type=F32)
    upward = jnp.dot(inputs, w_up, preferred_element_type=F32)
    hidden = (jax.nn.silu(gate) * upward).astype(BF16).reshape(-1, local_units)
    produced = jnp.dot(
        lax.all_gather(hidden, "dp", axis=1, tiled=True), w_down, preferred_element_type=F32
    ).astype(BF16)
    produced = produced.reshape(groups, -1, produced.shape[1])
    returned = lax.all_to_all(
        lax.all_to_all(produced, "dp", split_axis=0, concat_axis=2, tiled=True),
        "expert",
        split_axis=1,
        concat_axis=0,
        tiled=True,
    )
    shares = route_weights / jnp.sum(route_weights, axis=1, keepdims=True)
    targets = jnp.arange(experts * capacity, dtype=jnp.int32)
    spreading = jnp.sum(
        jnp.where(own_slots[:, :, None] == targets[None, None, :], shares[:, :, None], 0.0), axis=1
    )
    combined = jnp.dot(
        spreading, returned.reshape(-1, width).astype(F32), precision=lax.Precision.HIGHEST
    )
    return (mixed.astype(F32) + combined).astype(BF16)


def body(
    queries,
    new_kv,
    cache_keys,
    cache_values,
    lengths,
    residual,
    norm_gain,
    routes,
    route_weights,
    *packed,
):
    experts = lax.axis_size("expert")
    groups = lax.axis_size("dp")
    row_count = queries.shape[0]
    capacity = min(row_count, max(2, 2 * row_count * TOP // experts))
    every = (
        capacity == row_count
        and groups == 2
        and experts <= LANES // 2
        and experts % 4 == 0
        and experts & (experts - 1) == 0
    )
    mixed, payload = front(
        queries,
        new_kv,
        cache_keys,
        cache_values,
        lengths,
        residual,
        norm_gain,
        routes,
        route_weights,
        LANES if every else 0,
    )
    codes = [array[0] for array in packed]
    if every:
        return dense(payload, mixed, codes)
    return routed(payload, mixed, routes, route_weights, codes, capacity)


def solution(mesh):
    return jax.shard_map(
        body,
        mesh=mesh,
        in_specs=(
            P(("dp", "expert"), None),
            P(("dp", "expert"), None, None),
            P(("dp", "expert"), None, None),
            P(("dp", "expert"), None, None),
            P(("dp", "expert")),
            P(("dp", "expert"), None),
            P(),
            P(("dp", "expert"), None),
            P(("dp", "expert"), None),
            P("expert", None, "dp"),
            P("expert", None, "dp"),
            P("expert", None, "dp"),
            P("expert", None, "dp"),
            P("expert", None, "dp"),
            P("expert", None, "dp"),
        ),
        out_specs=P(("dp", "expert"), None),
        check_vma=False,
    )
```

time: 111 us -> 71.1 us (0.64)
  Pallas kernels: 47 us -> 28.8 us
  waiting for transfers between devices: 32.2 us -> 18.4 us
  local copies, waits for them, and re-layouts: 5.09 us -> 0.01 us
  other arithmetic: 2.84 us -> 0.03 us
    pallas_call x7 -> x14, Pallas kernels: 41.7 us -> 25.6 us  [the longest x3 16.8 us: unpack_weights(): pl.pallas_call(unpack_kernel, out_shape=pltpu.VMEM((4 * quarter, width),...]
    ppermute x20 -> x23, waiting for transfers between devices: 32.2 us -> 18.4 us  [swap(): lax.ppermute(block, ('dp', 'expert'), [(i, i ^ offset) for i in range(dev...]
    unnamed x29 -> x4, local copies, waits for them, and re-layouts: 3.78 us -> 0.01 us
    convert_element_type x3 -> x0, other arithmetic: 2.84 us -> none  [the longest x2 2.17 us: unpack_one(): scales.astype(F32)]
    pallas_call x1, Pallas kernels: 4.7 us -> 2.6 us  [front(): pl.pallas_call(front_kernel, out_shape=(jax.ShapeDtypeStruct((rows, width...]
    reshape x1 -> x0, local copies, waits for them, and re-layouts: 1.3 us -> none  [front(): gain.reshape(1, -1)]
    ppermute x20 -> x23, starting transfers between devices: 23.2 us -> 23.6 us  [swap(): lax.ppermute(block, ('dp', 'expert'), [(i, i ^ offset) for i in range(dev...]
  transfers between devices with their start and end apart: 20 -> 23, of which waited for: 9 -> 13; matrix products, arithmetic and copies ran while one was open for 3% -> 0% of each run, Pallas kernels for 23% -> 36%
where the time goes in v2:
time: 71.1 us; the launch traced here: 71 us
  Pallas kernels  28.8 us (41%)
  starting transfers between devices  23.6 us (33%)
  waiting for transfers between devices  18.4 us (26%)
    ppermute x23, starting transfers between devices, swap(): lax.ppermute(block, ('dp', 'expert'), [(i, i ^ offset) for i in range(dev...  23.6 us
    ppermute x23, waiting for transfers between devices, swap(): lax.ppermute(block, ('dp', 'expert'), [(i, i ^ offset) for i in range(dev...  18.4 us
    pallas_call x3, Pallas kernels, unpack_weights(): pl.pallas_call(unpack_kernel, out_shape=pltpu.VMEM((4 * quarter, width),...  16.8 us
    pallas_call x2, Pallas kernels, hidden_units(): pl.pallas_call(hidden_kernel, out_shape=(pltpu.VMEM((count, width), BF16)...  5.55 us
    pallas_call x1, Pallas kernels, front(): pl.pallas_call(front_kernel, out_shape=(jax.ShapeDtypeStruct((rows, width...  2.6 us
    pallas_call x2, Pallas kernels, peer_down(): pl.pallas_call(peer_down_kernel, out_shape=(shape, shape), in_specs=[pl.B...  1.57 us
    pallas_call x2, Pallas kernels, own_down(): pl.pallas_call(own_down_kernel, out_shape=pltpu.VMEM((count, width), F32)...  1.47 us
  transfers between devices with their start and end apart: 23, of which 13 were waited for; matrix products, arithmetic and copies ran while one was open for 0% of the time, Pallas kernels for 36%

profile of v2, /device:TPU:0, one launch (start us, length us, event | category | flops | bytes accessed | tf_op | source)
XLA Modules:
  0.0 71.0 jit_solution(9734159998794103906)
XLA Ops:
  0.0 2.6 %front.1 = (bf16[8,4096]{1,0:T(8,128)(2,1)}, bf16[8,4224]{1,0:T(8,128)(2,1)}) custom-call(s32[8]{0:T(128)} %lengths_ref.1, bf16[8,4096]{1,0:T(8,128)(2,1)} %queries_ref.1, bf16[8,2,1024]{2,1,0:T(2,128)(2,1)} %new_kv_ref.1, bf16[8,32,1024]{2,1,0:T(8,128)(2,1)} %keys_ref.1, bf16[8,32,1024]{2,1,0:T(8,128)(2,1)} %values_ref.1, bf16[8,4096]{1,0:T(8,128)(2,1)} %residual_ref.1, ...), custom_call_target="tpu_custom_call" | custom-call | flops 1 | bytes 1 | tf_op jit(solution)/shard_map/front/pallas_call | solution.py:109
  2.6 3.0 %collective-permute-start = (bf16[8,4224]{1,0:T(8,128)(2,1)}, bf16[8,4224]{1,0:T(8,128)(2,1)S(1)}, u32[]{:S(2)}, u32[]{:S(2)}) collective-permute-start(bf16[8,4224]{1,0:T(8,128)(2,1)} %get-tuple-element.52), channel_id=1, source_target_pairs={{0,4},{1,5},{2,6},{3,7},{4,0},{5,1},{6,2},{7,3},{8,12},{9,13},{10,... | collective-permute-start | bytes 202760 | tf_op jit(solution)/shard_map/ppermute | solution.py:350
  5.6 2.6 %collective-permute-start.1 = (bf16[8,4224]{1,0:T(8,128)(2,1)}, bf16[8,4224]{1,0:T(8,128)(2,1)S(1)}, u32[]{:S(2)}, u32[]{:S(2)}) collective-permute-start(bf16[8,4224]{1,0:T(8,128)(2,1)} %get-tuple-element.52), channel_id=1, source_target_pairs={{0,8},{1,9},{2,10},{3,11},{4,12},{5,13},{6,14},{7,15},{8,0},{9,1},... | collective-permute-start | bytes 202760 | tf_op jit(solution)/shard_map/ppermute | solution.py:350
  8.2 0.0 collective-permute-start.2
  8.2 5.5 %unpack_weights.3.refs_4_ = bf16[4096,1024]{1,0:T(8,128)(2,1)S(1)} custom-call(f32[1024,1024]{1,0:T(8,128)} %bitcast.8, bf16[32,1024]{1,0:T(8,128)(2,1)} %bitcast.11), custom_call_target="tpu_custom_call" | custom-call | flops 1 | bytes 1 | tf_op jit(solution)/shard_map/unpack_weights/pallas_call | solution.py:177
  13.7 0.9 %collective-permute-done.2 = bf16[8,4224]{1,0:T(8,128)(2,1)S(1)} collective-permute-done((bf16[8,4224]{1,0:T(8,128)(2,1)}, bf16[8,4224]{1,0:T(8,128)(2,1)S(1)}, u32[]{:S(2)}, u32[]{:S(2)}) %collective-permute-start.2) | collective-permute-done | bytes 67616 | tf_op jit(solution)/shard_map/ppermute | solution.py:350
  14.7 1.6 %collective-permute-start.3 = (bf16[32,4224]{1,0:T(8,128)(2,1)S(1)}, bf16[32,4224]{1,0:T(8,128)(2,1)S(1)}, u32[]{:S(2)}, u32[]{:S(2)}) collective-permute-start(bf16[32,4224]{1,0:T(8,128)(2,1)S(1)} %pad_maximum_fusion.refs_0_), channel_id=1, source_target_pairs={{0,2},{1,3},{2,0},{3,1},{4,6},{5,7},{6,4},{7,5},{8,10},{9,11},{10,... | collective-permute-start | bytes 811016 | tf_op jit(solution)/shard_map/ppermute | solution.py:350
  16.2 1.5 %collective-permute-start.5 = (bf16[32,4224]{1,0:T(8,128)(2,1)S(1)}, bf16[32,4224]{1,0:T(8,128)(2,1)S(1)}, u32[]{:S(2)}, u32[]{:S(2)}) collective-permute-start(bf16[32,4224]{1,0:T(8,128)(2,1)S(1)} %pad_maximum_fusion.refs_0_), channel_id=1, source_target_pairs={{0,16},{1,17},{2,18},{3,19},{4,20},{5,21},{6,22},{7,23},{8,24},{9,... | collective-permute-start | bytes 811016 | tf_op jit(solution)/shard_map/ppermute | solution.py:350
  17.7 5.5 %unpack_weights.4.refs_5_ = bf16[4096,1024]{1,0:T(8,128)(2,1)S(1)} custom-call(f32[1024,1024]{1,0:T(8,128)} %bitcast.9, bf16[32,1024]{1,0:T(8,128)(2,1)} %bitcast.12), custom_call_target="tpu_custom_call" | custom-call | flops 1 | bytes 1 | tf_op jit(solution)/shard_map/unpack_weights/pallas_call | solution.py:177
  23.2 0.1 collective-permute-start.4
  23.3 0.5 collective-permute-start.7
  23.8 0.5 collective-permute-start.6
  24.4 0.5 collective-permute-done.4.refs_3_
  24.9 0.4 collective-permute-done.7.refs_2_
  25.2 2.9 %gate_up.2 = (bf16[128,1024]{1,0:T(8,128)(2,1)S(1)}, f32[128,128]{1,0:T(8,128)S(1)}) custom-call(s32[1]{0:T(128)} %bitcast.1.place_ref, bf16[32,4224]{1,0:T(8,128)(2,1)S(1)} %pad_maximum_fusion.refs_0_, bf16[32,4224]{1,0:T(8,128)(2,1)S(1)} %collective-permute-done.3.refs_1_, bf16[32,4224]{1,0:T(8,128)(2,1)S(1)} %collective-permute-done.7.refs_2_, ...), custom_call_target="tpu_custom_call" | custom-call | flops 1 | bytes 1 | tf_op jit(solution)/shard_map/gate_up/pallas_call | solution.py:219
  28.1 5.8 %unpack_weights.5.weight_ref = bf16[2048,2048]{1,0:T(8,128)(2,1)S(1)} custom-call(f32[512,2048]{1,0:T(8,128)} %bitcast.10, bf16[16,2048]{1,0:T(8,128)(2,1)} %bitcast.13), custom_call_target="tpu_custom_call" | custom-call | flops 1 | bytes 1 | tf_op jit(solution)/shard_map/unpack_weights/pallas_call | solution.py:177
  33.9 0.2 collective-permute-start.8
  34.1 0.4 collective-permute-start.9
  34.5 0.6 collective-permute-start.10
  35.1 0.4 collective-permute-done.8.refs_2_
  35.5 0.4 collective-permute-done.9.refs_3_
  35.9 2.7 %gate_up.3 = (bf16[128,1024]{1,0:T(8,128)(2,1)S(1)}, f32[128,128]{1,0:T(8,128)S(1)}) custom-call(s32[1]{0:T(128)} %bitcast.1.place_ref, bf16[32,4224]{1,0:T(8,128)(2,1)S(1)} %collective-permute-done.5.refs_0_, bf16[32,4224]{1,0:T(8,128)(2,1)S(1)} %collective-permute-done.6.refs_1_, bf16[32,4224]{1,0:T(8,128)(2,1)S(1)} %collective-permute-done.8.refs_2_, ...), custom_call_target="tpu_custom_call" | custom-call | flops 1 | bytes 1 | tf_op jit(solution)/shard_map/gate_up/pallas_call | solution.py:219
  38.6 0.7 collective-permute-start.11
  39.3 0.7 %down_own.3.partial_ref = f32[128,2048]{1,0:T(8,128)S(1)} custom-call(s32[1]{0:T(128)} %bitcast.side_ref, bf16[128,1024]{1,0:T(8,128)(2,1)S(1)} %get-tuple-element.72.hidden_ref, bf16[2048,2048]{1,0:T(8,128)(2,1)S(1)} %unpack_weights.5.weight_ref), custom_call_target="tpu_custom_call" | custom-call | flops 1 | bytes 1 | tf_op jit(solution)/shard_map/down_own/pallas_call | solution.py:246
  40.0 0.7 %down_own.2.partial_ref = f32[128,2048]{1,0:T(8,128)S(1)} custom-call(s32[1]{0:T(128)} %bitcast.side_ref, bf16[128,1024]{1,0:T(8,128)(2,1)S(1)} %get-tuple-element.67.hidden_ref, bf16[2048,2048]{1,0:T(8,128)(2,1)S(1)} %unpack_weights.5.weight_ref), custom_call_target="tpu_custom_call" | custom-call | flops 1 | bytes 1 | tf_op jit(solution)/shard_map/down_own/pallas_call | solution.py:246
  40.8 2.9 %collective-permute-done.10.hidden_ref = bf16[128,1024]{1,0:T(8,128)(2,1)S(1)} collective-permute-done((bf16[128,1024]{1,0:T(8,128)(2,1)S(1)}, bf16[128,1024]{1,0:T(8,128)(2,1)S(1)}, u32[]{:S(2)}, u32[]{:S(2)}) %collective-permute-start.10) | collective-permute-done | bytes 262176 | tf_op jit(solution)/shard_map/ppermute | solution.py:350
  43.6 0.8 %down_peer.2 = (bf16[64,2048]{1,0:T(8,128)(2,1)S(1)}, bf16[64,2048]{1,0:T(8,128)(2,1)S(1)}) custom-call(s32[1]{0:T(128)} %bitcast.side_ref, f32[128,2048]{1,0:T(8,128)S(1)} %down_own.2.partial_ref, bf16[128,1024]{1,0:T(8,128)(2,1)S(1)} %collective-permute-done.10.hidden_ref, bf16[2048,2048]{1,0:T(8,128)(2,1)S(1)} %unpack_weights.5.weight_ref, ...), custom_call_target="tpu_custom_call" | custom-call | flops 1 | bytes 1 | tf_op jit(solution)/shard_map/down_peer/pallas_call | solution.py:278
  44.4 4.0 %collective-permute-done.11.hidden_ref = bf16[128,1024]{1,0:T(8,128)(2,1)S(1)} collective-permute-done((bf16[128,1024]{1,0:T(8,128)(2,1)S(1)}, bf16[128,1024]{1,0:T(8,128)(2,1)S(1)}, u32[]{:S(2)}, u32[]{:S(2)}) %collective-permute-start.11) | collective-permute-done | bytes 262176 | tf_op jit(solution)/shard_map/ppermute | solution.py:350
  48.4 0.8 %down_peer.3 = (bf16[64,2048]{1,0:T(8,128)(2,1)S(1)}, bf16[64,2048]{1,0:T(8,128)(2,1)S(1)}) custom-call(s32[1]{0:T(128)} %bitcast.side_ref, f32[128,2048]{1,0:T(8,128)S(1)} %down_own.3.partial_ref, bf16[128,1024]{1,0:T(8,128)(2,1)S(1)} %collective-permute-done.11.hidden_ref, bf16[2048,2048]{1,0:T(8,128)(2,1)S(1)} %unpack_weights.5.weight_ref, ...), custom_call_target="tpu_custom_call" | custom-call | flops 1 | bytes 1 | tf_op jit(solution)/shard_map/down_peer/pallas_call | solution.py:278
  49.2 0.6 collective-permute-start.18
  49.8 0.2 collective-permute-done.12.refs_1_
  50.0 0.1 add_and_cut.5
  50.0 0.6 collective-permute-start.13
  50.6 0.4 collective-permute-done.18.refs_1_
  51.0 0.1 add_and_cut.8
  51.0 1.2 %collective-permute-start.19 = (bf16[32,2048]{1,0:T(8,128)(2,1)S(1)}, bf16[32,2048]{1,0:T(8,128)(2,1)S(1)}, u32[]{:S(2)}, u32[]{:S(2)}) collective-permute-start(bf16[32,2048]{1,0:T(8,128)(2,1)S(1)} %get-tuple-element.86), channel_id=1, source_target_pairs={{0,2},{1,3},{2,0},{3,1},{4,6},{5,7},{6,4},{7,5},{8,10},{9,11},{10,... | collective-permute-start | bytes 393224 | tf_op jit(solution)/shard_map/ppermute | solution.py:350
  52.3 4.2 %collective-permute-done.13.refs_1_ = bf16[32,2048]{1,0:T(8,128)(2,1)S(1)} collective-permute-done((bf16[32,2048]{1,0:T(8,128)(2,1)S(1)}, bf16[32,2048]{1,0:T(8,128)(2,1)S(1)}, u32[]{:S(2)}, u32[]{:S(2)}) %collective-permute-start.13) | collective-permute-done | bytes 131104 | tf_op jit(solution)/shard_map/ppermute | solution.py:350
  56.5 0.7 collective-permute-start.14
  57.2 2.9 %collective-permute-start.15 = (bf16[8,2048]{1,0:T(8,128)(2,1)S(1)}, bf16[8,2048]{1,0:T(8,128)(2,1)S(1)}, u32[]{:S(2)}, u32[]{:S(2)}) collective-permute-start(bf16[8,2048]{1,0:T(8,128)(2,1)S(1)} %get-tuple-element.78), channel_id=1, source_target_pairs={{0,8},{1,9},{2,10},{3,11},{4,12},{5,13},{6,14},{7,15},{8,0},{9,1},... | collective-permute-start | bytes 98312 | tf_op jit(solution)/shard_map/ppermute | solution.py:350
  60.1 0.8 %collective-permute-start.16 = (bf16[8,2048]{1,0:T(8,128)(2,1)S(1)}, bf16[8,2048]{1,0:T(8,128)(2,1)S(1)}, u32[]{:S(2)}, u32[]{:S(2)}) collective-permute-start(bf16[8,2048]{1,0:T(8,128)(2,1)S(1)} %get-tuple-element.79), channel_id=1, source_target_pairs={{0,12},{1,13},{2,14},{3,15},{4,8},{5,9},{6,10},{7,11},{8,4},{9,5},... | collective-permute-start | bytes 98312 | tf_op jit(solution)/shard_map/ppermute | solution.py:350
  61.0 0.1 collective-permute-start.20
  61.0 3.5 %collective-permute-start.21 = (bf16[8,2048]{1,0:T(8,128)(2,1)S(1)}, bf16[8,2048]{1,0:T(8,128)(2,1)S(1)}, u32[]{:S(2)}, u32[]{:S(2)}) collective-permute-start(bf16[8,2048]{1,0:T(8,128)(2,1)S(1)} %get-tuple-element.89), channel_id=1, source_target_pairs={{0,8},{1,9},{2,10},{3,11},{4,12},{5,13},{6,14},{7,15},{8,0},{9,1},... | collective-permute-start | bytes 98312 | tf_op jit(solution)/shard_map/ppermute | solution.py:350
  64.6 0.8 %collective-permute-start.22 = (bf16[8,2048]{1,0:T(8,128)(2,1)S(1)}, bf16[8,2048]{1,0:T(8,128)(2,1)S(1)}, u32[]{:S(2)}, u32[]{:S(2)}) collective-permute-start(bf16[8,2048]{1,0:T(8,128)(2,1)S(1)} %get-tuple-element.90), channel_id=1, source_target_pairs={{0,12},{1,13},{2,14},{3,15},{4,8},{5,9},{6,10},{7,11},{8,4},{9,5},... | collective-permute-start | bytes 98312 | tf_op jit(solution)/shard_map/ppermute | solution.py:350
  65.4 0.4 collective-permute-done.16.refs_3_
  65.8 0.6 collective-permute-start.17
  66.4 0.3 collective-permute-done.21.refs_2_
  66.8 3.5 %collective-permute-done.22.refs_3_ = bf16[8,2048]{1,0:T(8,128)(2,1)S(1)} collective-permute-done((bf16[8,2048]{1,0:T(8,128)(2,1)S(1)}, bf16[8,2048]{1,0:T(8,128)(2,1)S(1)}, u32[]{:S(2)}, u32[]{:S(2)}) %collective-permute-start.22) | collective-permute-done | bytes 32800 | tf_op jit(solution)/shard_map/ppermute | solution.py:350
  70.3 0.7 finish.1
  (19 shorter events, 0.2 us)
Async XLA Ops:
  2.6 12.0 %copy-start.1 = (bf16[8,4224]{1,0:T(8,128)(2,1)S(1)}, bf16[8,4224]{1,0:T(8,128)(2,1)}, u32[]{:S(2)}) copy-start(bf16[8,4224]{1,0:T(8,128)(2,1)} %get-tuple-element.52) | copy-start | bytes 202756
  2.6 11.1 %collective-permute-start = (bf16[8,4224]{1,0:T(8,128)(2,1)}, bf16[8,4224]{1,0:T(8,128)(2,1)S(1)}, u32[]{:S(2)}, u32[]{:S(2)}) collective-permute-start(bf16[8,4224]{1,0:T(8,128)(2,1)} %get-tuple-element.52), channel_id=1, source_target_pairs={{0,4},{1,5},{2,6},{3,7},{4,0},{5,1},{6,2},{7,3},{8,12},{9,13},{10,... | collective-permute-start | bytes 202760 | tf_op jit(solution)/shard_map/ppermute | solution.py:350
  5.6 8.1 %collective-permute-start.1 = (bf16[8,4224]{1,0:T(8,128)(2,1)}, bf16[8,4224]{1,0:T(8,128)(2,1)S(1)}, u32[]{:S(2)}, u32[]{:S(2)}) collective-permute-start(bf16[8,4224]{1,0:T(8,128)(2,1)} %get-tuple-element.52), channel_id=1, source_target_pairs={{0,8},{1,9},{2,10},{3,11},{4,12},{5,13},{6,14},{7,15},{8,0},{9,1},... | collective-permute-start | bytes 202760 | tf_op jit(solution)/shard_map/ppermute | solution.py:350
  8.2 6.4 %collective-permute-start.2 = (bf16[8,4224]{1,0:T(8,128)(2,1)}, bf16[8,4224]{1,0:T(8,128)(2,1)S(1)}, u32[]{:S(2)}, u32[]{:S(2)}) collective-permute-start(bf16[8,4224]{1,0:T(8,128)(2,1)} %get-tuple-element.52), channel_id=1, source_target_pairs={{0,12},{1,13},{2,14},{3,15},{4,8},{5,9},{6,10},{7,11},{8,4},{9,5},... | collective-permute-start | bytes 202760 | tf_op jit(solution)/shard_map/ppermute | solution.py:350
  14.7 8.6 %collective-permute-start.3 = (bf16[32,4224]{1,0:T(8,128)(2,1)S(1)}, bf16[32,4224]{1,0:T(8,128)(2,1)S(1)}, u32[]{:S(2)}, u32[]{:S(2)}) collective-permute-start(bf16[32,4224]{1,0:T(8,128)(2,1)S(1)} %pad_maximum_fusion.refs_0_), channel_id=1, source_target_pairs={{0,2},{1,3},{2,0},{3,1},{4,6},{5,7},{6,4},{7,5},{8,10},{9,11},{10,... | collective-permute-start | bytes 811016 | tf_op jit(solution)/shard_map/ppermute | solution.py:350
  16.2 8.1 %collective-permute-start.5 = (bf16[32,4224]{1,0:T(8,128)(2,1)S(1)}, bf16[32,4224]{1,0:T(8,128)(2,1)S(1)}, u32[]{:S(2)}, u32[]{:S(2)}) collective-permute-start(bf16[32,4224]{1,0:T(8,128)(2,1)S(1)} %pad_maximum_fusion.refs_0_), channel_id=1, source_target_pairs={{0,16},{1,17},{2,18},{3,19},{4,20},{5,21},{6,22},{7,23},{8,24},{9,... | collective-permute-start | bytes 811016 | tf_op jit(solution)/shard_map/ppermute | solution.py:350
  23.2 1.6 %collective-permute-start.4 = (bf16[32,4224]{1,0:T(8,128)(2,1)S(1)}, bf16[32,4224]{1,0:T(8,128)(2,1)S(1)}, u32[]{:S(2)}, u32[]{:S(2)}) collective-permute-start(bf16[32,4224]{1,0:T(8,128)(2,1)S(1)} %collective-permute-done.3.refs_1_), channel_id=1, source_target_pairs={{0,1},{1,0},{2,3},{3,2},{4,5},{5,4},{6,7},{7,6},{8,9},{9,8},{10,11... | collective-permute-start | bytes 811016 | tf_op jit(solution)/shard_map/ppermute | solution.py:350
  23.3 1.9 %collective-permute-start.7 = (bf16[32,4224]{1,0:T(8,128)(2,1)S(1)}, bf16[32,4224]{1,0:T(8,128)(2,1)S(1)}, u32[]{:S(2)}, u32[]{:S(2)}) collective-permute-start(bf16[32,4224]{1,0:T(8,128)(2,1)S(1)} %pad_maximum_fusion.refs_0_), channel_id=1, source_target_pairs={{0,1},{1,0},{2,3},{3,2},{4,5},{5,4},{6,7},{7,6},{8,9},{9,8},{10,11... | collective-permute-start | bytes 811016 | tf_op jit(solution)/shard_map/ppermute | solution.py:350
  23.8 10.1 %collective-permute-start.6 = (bf16[32,4224]{1,0:T(8,128)(2,1)S(1)}, bf16[32,4224]{1,0:T(8,128)(2,1)S(1)}, u32[]{:S(2)}, u32[]{:S(2)}) collective-permute-start(bf16[32,4224]{1,0:T(8,128)(2,1)S(1)} %collective-permute-done.3.refs_1_), channel_id=1, source_target_pairs={{0,16},{1,17},{2,18},{3,19},{4,20},{5,21},{6,22},{7,23},{8,24},{9,... | collective-permute-start | bytes 811016 | tf_op jit(solution)/shard_map/ppermute | solution.py:350
  33.9 1.6 %collective-permute-start.8 = (bf16[32,4224]{1,0:T(8,128)(2,1)S(1)}, bf16[32,4224]{1,0:T(8,128)(2,1)S(1)}, u32[]{:S(2)}, u32[]{:S(2)}) collective-permute-start(bf16[32,4224]{1,0:T(8,128)(2,1)S(1)} %collective-permute-done.5.refs_0_), channel_id=1, source_target_pairs={{0,1},{1,0},{2,3},{3,2},{4,5},{5,4},{6,7},{7,6},{8,9},{9,8},{10,11... | collective-permute-start | bytes 811016 | tf_op jit(solution)/shard_map/ppermute | solution.py:350
  34.1 1.8 %collective-permute-start.9 = (bf16[32,4224]{1,0:T(8,128)(2,1)S(1)}, bf16[32,4224]{1,0:T(8,128)(2,1)S(1)}, u32[]{:S(2)}, u32[]{:S(2)}) collective-permute-start(bf16[32,4224]{1,0:T(8,128)(2,1)S(1)} %collective-permute-done.6.refs_1_), channel_id=1, source_target_pairs={{0,1},{1,0},{2,3},{3,2},{4,5},{5,4},{6,7},{7,6},{8,9},{9,8},{10,11... | collective-permute-start | bytes 811016 | tf_op jit(solution)/shard_map/ppermute | solution.py:350
  34.5 9.1 %collective-permute-start.10 = (bf16[128,1024]{1,0:T(8,128)(2,1)S(1)}, bf16[128,1024]{1,0:T(8,128)(2,1)S(1)}, u32[]{:S(2)}, u32[]{:S(2)}) collective-permute-start(bf16[128,1024]{1,0:T(8,128)(2,1)S(1)} %get-tuple-element.72.hidden_ref), channel_id=1, source_target_pairs={{0,16},{1,17},{2,18},{3,19},{4,20},{5,21},{6,22},{7,23},{8,24},{9,... | collective-permute-start | bytes 786440 | tf_op jit(solution)/shard_map/ppermute | solution.py:350
  38.6 9.8 %collective-permute-start.11 = (bf16[128,1024]{1,0:T(8,128)(2,1)S(1)}, bf16[128,1024]{1,0:T(8,128)(2,1)S(1)}, u32[]{:S(2)}, u32[]{:S(2)}) collective-permute-start(bf16[128,1024]{1,0:T(8,128)(2,1)S(1)} %get-tuple-element.67.hidden_ref), channel_id=1, source_target_pairs={{0,16},{1,17},{2,18},{3,19},{4,20},{5,21},{6,22},{7,23},{8,24},{9,... | collective-permute-start | bytes 786440 | tf_op jit(solution)/shard_map/ppermute | solution.py:350
  43.6 26.7 %copy-start = (bf16[8,4096]{1,0:T(8,128)(2,1)S(1)}, bf16[8,4096]{1,0:T(8,128)(2,1)}, u32[]{:S(2)}) copy-start(bf16[8,4096]{1,0:T(8,128)(2,1)} %get-tuple-element.50.mixed_ref) | copy-start | bytes 196612
  48.4 1.5 %collective-permute-start.12 = (bf16[64,2048]{1,0:T(8,128)(2,1)S(1)}, bf16[64,2048]{1,0:T(8,128)(2,1)S(1)}, u32[]{:S(2)}, u32[]{:S(2)}) collective-permute-start(bf16[64,2048]{1,0:T(8,128)(2,1)S(1)} %get-tuple-element.73), channel_id=1, source_target_pairs={{0,1},{1,0},{2,3},{3,2},{4,5},{5,4},{6,7},{7,6},{8,9},{9,8},{10,11... | collective-permute-start | bytes 786440 | tf_op jit(solution)/shard_map/ppermute | solution.py:350
  49.2 1.7 %collective-permute-start.18 = (bf16[64,2048]{1,0:T(8,128)(2,1)S(1)}, bf16[64,2048]{1,0:T(8,128)(2,1)S(1)}, u32[]{:S(2)}, u32[]{:S(2)}) collective-permute-start(bf16[64,2048]{1,0:T(8,128)(2,1)S(1)} %get-tuple-element.84), channel_id=1, source_target_pairs={{0,1},{1,0},{2,3},{3,2},{4,5},{5,4},{6,7},{7,6},{8,9},{9,8},{10,11... | collective-permute-start | bytes 786440 | tf_op jit(solution)/shard_map/ppermute | solution.py:350
  50.0 6.4 %collective-permute-start.13 = (bf16[32,2048]{1,0:T(8,128)(2,1)S(1)}, bf16[32,2048]{1,0:T(8,128)(2,1)S(1)}, u32[]{:S(2)}, u32[]{:S(2)}) collective-permute-start(bf16[32,2048]{1,0:T(8,128)(2,1)S(1)} %get-tuple-element.75), channel_id=1, source_target_pairs={{0,2},{1,3},{2,0},{3,1},{4,6},{5,7},{6,4},{7,5},{8,10},{9,11},{10,... | collective-permute-start | bytes 393224 | tf_op jit(solution)/shard_map/ppermute | solution.py:350
  51.0 9.9 %collective-permute-start.19 = (bf16[32,2048]{1,0:T(8,128)(2,1)S(1)}, bf16[32,2048]{1,0:T(8,128)(2,1)S(1)}, u32[]{:S(2)}, u32[]{:S(2)}) collective-permute-start(bf16[32,2048]{1,0:T(8,128)(2,1)S(1)} %get-tuple-element.86), channel_id=1, source_target_pairs={{0,2},{1,3},{2,0},{3,1},{4,6},{5,7},{6,4},{7,5},{8,10},{9,11},{10,... | collective-permute-start | bytes 393224 | tf_op jit(solution)/shard_map/ppermute | solution.py:350
  56.5 8.1 %collective-permute-start.14 = (bf16[8,2048]{1,0:T(8,128)(2,1)S(1)}, bf16[8,2048]{1,0:T(8,128)(2,1)S(1)}, u32[]{:S(2)}, u32[]{:S(2)}) collective-permute-start(bf16[8,2048]{1,0:T(8,128)(2,1)S(1)} %get-tuple-element.77), channel_id=1, source_target_pairs={{0,4},{1,5},{2,6},{3,7},{4,0},{5,1},{6,2},{7,3},{8,12},{9,13},{10,... | collective-permute-start | bytes 98312 | tf_op jit(solution)/shard_map/ppermute | solution.py:350
  57.2 8.2 %collective-permute-start.15 = (bf16[8,2048]{1,0:T(8,128)(2,1)S(1)}, bf16[8,2048]{1,0:T(8,128)(2,1)S(1)}, u32[]{:S(2)}, u32[]{:S(2)}) collective-permute-start(bf16[8,2048]{1,0:T(8,128)(2,1)S(1)} %get-tuple-element.78), channel_id=1, source_target_pairs={{0,8},{1,9},{2,10},{3,11},{4,12},{5,13},{6,14},{7,15},{8,0},{9,1},... | collective-permute-start | bytes 98312 | tf_op jit(solution)/shard_map/ppermute | solution.py:350
  60.1 5.7 %collective-permute-start.16 = (bf16[8,2048]{1,0:T(8,128)(2,1)S(1)}, bf16[8,2048]{1,0:T(8,128)(2,1)S(1)}, u32[]{:S(2)}, u32[]{:S(2)}) collective-permute-start(bf16[8,2048]{1,0:T(8,128)(2,1)S(1)} %get-tuple-element.79), channel_id=1, source_target_pairs={{0,12},{1,13},{2,14},{3,15},{4,8},{5,9},{6,10},{7,11},{8,4},{9,5},... | collective-permute-start | bytes 98312 | tf_op jit(solution)/shard_map/ppermute | solution.py:350
  61.0 5.5 %collective-permute-start.20 = (bf16[8,2048]{1,0:T(8,128)(2,1)S(1)}, bf16[8,2048]{1,0:T(8,128)(2,1)S(1)}, u32[]{:S(2)}, u32[]{:S(2)}) collective-permute-start(bf16[8,2048]{1,0:T(8,128)(2,1)S(1)} %get-tuple-element.88), channel_id=1, source_target_pairs={{0,4},{1,5},{2,6},{3,7},{4,0},{5,1},{6,2},{7,3},{8,12},{9,13},{10,... | collective-permute-start | bytes 98312 | tf_op jit(solution)/shard_map/ppermute | solution.py:350
  61.0 5.7 %collective-permute-start.21 = (bf16[8,2048]{1,0:T(8,128)(2,1)S(1)}, bf16[8,2048]{1,0:T(8,128)(2,1)S(1)}, u32[]{:S(2)}, u32[]{:S(2)}) collective-permute-start(bf16[8,2048]{1,0:T(8,128)(2,1)S(1)} %get-tuple-element.89), channel_id=1, source_target_pairs={{0,8},{1,9},{2,10},{3,11},{4,12},{5,13},{6,14},{7,15},{8,0},{9,1},... | collective-permute-start | bytes 98312 | tf_op jit(solution)/shard_map/ppermute | solution.py:350
  64.6 5.7 %collective-permute-start.22 = (bf16[8,2048]{1,0:T(8,128)(2,1)S(1)}, bf16[8,2048]{1,0:T(8,128)(2,1)S(1)}, u32[]{:S(2)}, u32[]{:S(2)}) collective-permute-start(bf16[8,2048]{1,0:T(8,128)(2,1)S(1)} %get-tuple-element.90), channel_id=1, source_target_pairs={{0,12},{1,13},{2,14},{3,15},{4,8},{5,9},{6,10},{7,11},{8,4},{9,5},... | collective-permute-start | bytes 98312 | tf_op jit(solution)/shard_map/ppermute | solution.py:350
  65.8 4.5 %collective-permute-start.17 = (bf16[8,2048]{1,0:T(8,128)(2,1)S(1)}, bf16[8,2048]{1,0:T(8,128)(2,1)S(1)}, u32[]{:S(2)}, u32[]{:S(2)}) collective-permute-start(bf16[8,2048]{1,0:T(8,128)(2,1)S(1)} %add_and_cut.7), channel_id=1, source_target_pairs={{0,16},{1,17},{2,18},{3,19},{4,20},{5,21},{6,22},{7,23},{8,24},{9,... | collective-permute-start | bytes 98312 | tf_op jit(solution)/shard_map/ppermute | solution.py:350

commit v3 on v2

--- a/solution.py
+++ b/solution.py
@@ -13,6 +13,7 @@
 LANES = 128
 VMEM_LIMIT = 56 * 2**20
 VMEM_SOME = 16 * 2**20
+SPARE = 16
 SMALL = pl.CostEstimate(flops=1, bytes_accessed=1, transcendentals=0)
 F32 = jnp.float32
 BF16 = jnp.bfloat16
@@ -160,12 +161,13 @@
             def chunk(i, carry, group=group, column=column, spans=spans):
                 start = pl.multiple_of(group * GROUP + i * 16, 16)
                 words = words_ref[pl.ds(start, 16), column : column + step].astype(jnp.int32)
-                words = (words ^ 0x8888).astype(jnp.int16)
                 for k in range(4):
-                    level = words if k == 3 else lax.shift_left(words, jnp.int16(12 - 4 * k))
-                    level = lax.shift_right_arithmetic(level, jnp.int16(12))
+                    digit = words if k == 0 else lax.shift_right_logical(words, 4 * k)
+                    if k < 3:
+                        digit = digit & 15
+                    level = digit.astype(F32).astype(BF16) - jnp.asarray(8, BF16)
                     out_ref[pl.ds(k * quarter + start, 16), column : column + step] = (
-                        level.astype(BF16) * spans[k]
+                        level * spans[k]
                     )
                 return carry
 
@@ -195,6 +197,7 @@
     pieces, (gate_ref, up_ref, out_ref, share_ref, rows_ref) = refs[:-5], refs[-5:]
     depth, width = gate_ref.shape
     block = pieces[0].shape[0]
+    count = block * len(pieces)
     for n, piece in enumerate(pieces):
         rows_ref[n * block : (n + 1) * block, :] = piece[:, :depth]
         table = piece[:, depth:].astype(F32)
@@ -208,17 +211,19 @@
         span = slice(column, column + step)
         gate = jnp.dot(rows_ref[...], gate_ref[:, span], preferred_element_type=F32)
         upward = jnp.dot(rows_ref[...], up_ref[:, span], preferred_element_type=F32)
-        out_ref[:, span] = (gate / (1.0 + jnp.exp(-gate)) * upward).astype(BF16)
-
-
-def hidden_units(pieces, w_gate, w_up, place):
+        out_ref[:count, span] = (gate / (1.0 + jnp.exp(-gate)) * upward).astype(BF16)
+    if out_ref.shape[0] > count:
+        out_ref[count:, :] = jnp.zeros((out_ref.shape[0] - count, width), BF16)
+
+
+def hidden_units(pieces, w_gate, w_up, place, spare=0):
     block, padded = pieces[0].shape
     count = block * len(pieces)
     depth, width = w_gate.shape
     vmem = pl.BlockSpec(memory_space=pltpu.VMEM)
     return pl.pallas_call(
         hidden_kernel,
-        out_shape=(pltpu.VMEM((count, width), BF16), pltpu.VMEM((count, LANES), F32)),
+        out_shape=(pltpu.VMEM((count + spare, width), BF16), pltpu.VMEM((count, LANES), F32)),
         in_specs=[pl.BlockSpec(memory_space=pltpu.SMEM)] + [vmem] * (len(pieces) + 2),
         out_specs=(vmem, vmem),
         scratch_shapes=[pltpu.VMEM((count, depth), BF16)],
@@ -235,12 +240,12 @@
     for column in range(0, out_ref.shape[1], step):
         span = slice(column, column + step)
         out_ref[:, span] = jnp.dot(
-            hidden_ref[...], weight_ref[rows, span], preferred_element_type=F32
+            hidden_ref[: out_ref.shape[0]], weight_ref[rows, span], preferred_element_type=F32
         )
 
 
-def own_down(side, hidden, weight):
-    count, half = hidden.shape
+def own_down(side, hidden, weight, count):
+    half = hidden.shape[1]
     width = weight.shape[1]
     vmem = pl.BlockSpec(memory_space=pltpu.VMEM)
     return pl.pallas_call(
@@ -254,32 +259,29 @@
     )(side, in_vmem(hidden), in_vmem(weight))
 
 
-def peer_down_kernel(
-    side_ref, partial_ref, hidden_ref, weight_ref, share_ref, keep_ref, send_ref
-):
-    count, half = hidden_ref.shape
+def peer_down_kernel(side_ref, partial_ref, hidden_ref, weight_ref, share_ref, *out_refs):
+    count, half = partial_ref.shape[0], hidden_ref.shape[1]
     rows = pl.ds(pl.multiple_of((1 - side_ref[0]) * half, half), half)
     step = 256
-    for column in range(0, keep_ref.shape[1], step):
+    cut = count // len(out_refs)
+    for column in range(0, partial_ref.shape[1], step):
         span = slice(column, column + step)
         produced = partial_ref[:, span] + jnp.dot(
-            hidden_ref[...], weight_ref[rows, span], preferred_element_type=F32
+            hidden_ref[:count], weight_ref[rows, span], preferred_element_type=F32
         )
         result = (produced.astype(BF16).astype(F32) * share_ref[:, :1]).astype(BF16)
-        keep_ref[:, span] = result[: count // 2]
-        send_ref[:, span] = result[count // 2 :]
-
-
-def peer_down(side, partial, hidden, weight, share):
+        for n, out_ref in enumerate(out_refs):
+            out_ref[:, span] = result[n * cut : (n + 1) * cut]
+
+
+def peer_down(side, partial, hidden, weight, share, parts):
     count, width = partial.shape
-    half = hidden.shape[1]
-    shape = pltpu.VMEM((count // 2, width), BF16)
     vmem = pl.BlockSpec(memory_space=pltpu.VMEM)
     return pl.pallas_call(
         peer_down_kernel,
-        out_shape=(shape, shape),
+        out_shape=(pltpu.VMEM((count // parts, width), BF16),) * parts,
         in_specs=[pl.BlockSpec(memory_space=pltpu.SMEM)] + [vmem] * 4,
-        out_specs=(vmem, vmem),
+        out_specs=(vmem,) * parts,
         compiler_params=pltpu.CompilerParams(vmem_limit_bytes=VMEM_SOME),
         cost_estimate=SMALL,
         name="down_peer",
@@ -311,29 +313,56 @@
     )(*[in_vmem(part) for part in kept], *arrived)
 
 
-def finish_kernel(side_ref, mixed_ref, far_ref, *refs):
-    near_refs, out_ref = refs[:-1], refs[-1]
-    half = far_ref.shape[1]
+def join_kernel(parts, far_ref, *refs):
+    near_refs, out_refs = refs[:-parts], refs[-parts:]
+    size = far_ref.shape[0] // parts
     near = near_refs[0][...].astype(F32)
     for near_ref in near_refs[1:]:
         near = near + near_ref[...].astype(F32)
     far = far_ref[...].astype(F32)
+    for n, out_ref in enumerate(out_refs):
+        rows = slice(n * size, (n + 1) * size)
+        out_ref[...] = jnp.concatenate([near[rows], far[rows]], axis=0).astype(BF16)
+
+
+def join(near, far, parts):
+    count, width = far.shape
+    vmem = pl.BlockSpec(memory_space=pltpu.VMEM)
+    return pl.pallas_call(
+        functools.partial(join_kernel, parts),
+        out_shape=(pltpu.VMEM((2 * count // parts, width), BF16),) * parts,
+        in_specs=[vmem] * (1 + len(near)),
+        out_specs=(vmem,) * parts,
+        compiler_params=pltpu.CompilerParams(vmem_limit_bytes=VMEM_SOME),
+        cost_estimate=SMALL,
+        name="join",
+    )(far, *near)
+
+
+def finish_kernel(side_ref, mixed_ref, *refs):
+    block_refs, out_ref = refs[:-1], refs[-1]
+    rows, width = mixed_ref.shape
+    total = block_refs[0][...].astype(F32)
+    for block_ref in block_refs[1:]:
+        total = total + block_ref[...].astype(F32)
+    near, far = total[:rows], total[rows:]
     first = side_ref[0] == 0
+    half = width // 2
     for n, part in enumerate((jnp.where(first, near, far), jnp.where(first, far, near))):
         span = slice(n * half, (n + 1) * half)
         out_ref[:, span] = (mixed_ref[:, span].astype(F32) + part).astype(BF16)
 
 
-def finish(side, mixed, far, near):
+def finish(side, mixed, blocks):
     vmem = pl.BlockSpec(memory_space=pltpu.VMEM)
     return pl.pallas_call(
         finish_kernel,
         out_shape=jax.ShapeDtypeStruct(mixed.shape, BF16),
-        in_specs=[pl.BlockSpec(memory_space=pltpu.SMEM)] + [vmem] * (2 + len(near)),
+        in_specs=[pl.BlockSpec(memory_space=pltpu.SMEM)] + [vmem] * (1 + len(blocks)),
         out_specs=vmem,
         compiler_params=pltpu.CompilerParams(vmem_limit_bytes=VMEM_SOME),
         name="finish",
-    )(side, mixed, far, *near)
+    )(side, mixed, *blocks)
 
 
 def dense(payload, mixed, codes):
@@ -359,40 +388,37 @@
     up_scales, stack = lax.optimization_barrier((up_scales, stack))
     beside, above, stack_pair = swap(stack, plane), swap(stack, line), swap(stack, core)
     w_up = unpack_weights(up_codes, up_scales)
-    above, w_up = lax.optimization_barrier((above, w_up))
+    above, stack_pair, w_up = lax.optimization_barrier((above, stack_pair, w_up))
     across, above_pair = swap(above, plane), swap(above, core)
     above_pair, beside = lax.optimization_barrier((above_pair, beside))
     beside_pair = swap(beside, core)
     hidden_own, share_own = hidden_units(
-        [stack, above, stack_pair, above_pair], w_gate, w_up, place
+        [stack, stack_pair, above, above_pair], w_gate, w_up, place, SPARE
     )
     other_peer = swap(hidden_own, plane)
     down_scales, hidden_own = lax.optimization_barrier((down_scales, hidden_own))
     w_down = unpack_weights(down_codes, down_scales)
     across, w_down = lax.optimization_barrier((across, w_down))
     hidden_other, share_other = hidden_units(
-        [beside, across, beside_pair, swap(across, core)], w_gate, w_up, place
+        [beside, beside_pair, across, swap(across, core)], w_gate, w_up, place
     )
     own_peer = swap(hidden_other, plane)
 
-    def over_core(keep, send):
-        return add_and_cut([keep], [swap(send, core)], 2)
-
-    def over_expert(keep, send):
-        parts = add_and_cut([keep], [swap(send, line)], layers)
-        return [parts[0]] + [swap(parts[z], z * layer) for z in range(1, layers)]
-
-    partial_other = own_down(side, hidden_other, w_down)
-    partial_own = own_down(side, hidden_own, w_down)
-    keep_other, send_other = peer_down(side, partial_other, other_peer, w_down, share_other)
-    send_other, partial_own, own_peer = lax.optimization_barrier(
-        (send_other, partial_own, own_peer)
-    )
-    keep_own, send_own = peer_down(side, partial_own, own_peer, w_down, share_own)
-    parts = over_expert(*over_core(keep_other, send_other))
-    near = over_expert(*over_core(keep_own, send_own))
-    (far,) = add_and_cut(parts[:1], parts[1:], 1)
-    return finish(side, mixed, swap(far, plane), near)
+    count = share_own.shape[0]
+    partial_other = own_down(side, hidden_other, w_down, count)
+    partial_own = own_down(side, hidden_own, w_down, count)
+    keep, send = peer_down(side, partial_other, other_peer, w_down, share_other, 2)
+    keep, send = add_and_cut([keep], [swap(send, line)], 2)
+    (onward,) = add_and_cut([keep], [swap(send, core)], 1)
+    far = swap(onward, plane)
+    keep_near, send_near, keep_far, send_far = peer_down(
+        side, partial_own, own_peer, w_down, share_own, 4
+    )
+    (onward,) = add_and_cut([keep_far], [swap(send_far, core)], 1)
+    near = [in_vmem(keep_near), swap(send_near, core), swap(onward, line)]
+    blocks = join(near, far, layers)
+    blocks = [blocks[0]] + [swap(blocks[z], z * layer) for z in range(1, layers)]
+    return finish(side, mixed, blocks)
 
 
 def slot_table(routes, experts, capacity):

time: 71.1 us -> 65.6 us (0.923)
  Pallas kernels: 28.8 us -> 24.4 us
  starting transfers between devices: 23.6 us -> 20.1 us
  waiting for transfers between devices: 18.4 us -> 20.6 us
    pallas_call x3, Pallas kernels: 16.8 us -> 12.6 us  [unpack_weights(): pl.pallas_call(unpack_kernel, out_shape=pltpu.VMEM((4 * quarter, width),...]
    ppermute x23 -> x21, starting transfers between devices: 23.6 us -> 20.1 us  [swap(): lax.ppermute(block, ('dp', 'expert'), [(i, i ^ offset) for i in range(dev...]
    ppermute x23 -> x21, waiting for transfers between devices: 18.4 us -> 20.6 us  [swap(): lax.ppermute(block, ('dp', 'expert'), [(i, i ^ offset) for i in range(dev...]
    pallas_call x4 -> x5, Pallas kernels: 7.12 us -> 6.9 us  [the longest x2 5.26 us: hidden_units(): pl.pallas_call(hidden_kernel, out_shape=(pltpu.VMEM((count + spare, width...]
  transfers between devices with their start and end apart: 23 -> 21, of which waited for: 13 -> 12; matrix products, arithmetic and copies ran while one was open for 0% -> 0% of each run, Pallas kernels for 36% -> 32%
where the time goes in v3:
time: 65.6 us; the launch traced here: 65.3 us
  Pallas kernels  24.4 us (37%)
  waiting for transfers between devices  20.6 us (31%)
  starting transfers between devices  20.1 us (31%)
    ppermute x21, waiting for transfers between devices, swap(): lax.ppermute(block, ('dp', 'expert'), [(i, i ^ offset) for i in range(dev...  20.6 us
    ppermute x21, starting transfers between devices, swap(): lax.ppermute(block, ('dp', 'expert'), [(i, i ^ offset) for i in range(dev...  20.1 us
    pallas_call x3, Pallas kernels, unpack_weights(): pl.pallas_call(unpack_kernel, out_shape=pltpu.VMEM((4 * quarter, width),...  12.6 us
    pallas_call x2, Pallas kernels, hidden_units(): pl.pallas_call(hidden_kernel, out_shape=(pltpu.VMEM((count + spare, width...  5.26 us
    pallas_call x1, Pallas kernels, front(): pl.pallas_call(front_kernel, out_shape=(jax.ShapeDtypeStruct((rows, width...  2.59 us
    pallas_call x2, Pallas kernels, peer_down(): pl.pallas_call(peer_down_kernel, out_shape=(pltpu.VMEM((count // parts, w...  1.58 us
    pallas_call x2, Pallas kernels, own_down(): pl.pallas_call(own_down_kernel, out_shape=pltpu.VMEM((count, width), F32)...  1.47 us
  transfers between devices with their start and end apart: 21, of which 12 were waited for; matrix products, arithmetic and copies ran while one was open for 0% of the time, Pallas kernels for 32%

profile of v3, /device:TPU:0, one launch (start us, length us, event | category | flops | bytes accessed | tf_op | source)
XLA Modules:
  0.0 65.3 jit_solution(16080781116049558486)
XLA Ops:
  0.0 2.6 %front.1 = (bf16[8,4096]{1,0:T(8,128)(2,1)}, bf16[8,4224]{1,0:T(8,128)(2,1)}) custom-call(s32[8]{0:T(128)} %lengths_ref.1, bf16[8,4096]{1,0:T(8,128)(2,1)} %queries_ref.1, bf16[8,2,1024]{2,1,0:T(2,128)(2,1)} %new_kv_ref.1, bf16[8,32,1024]{2,1,0:T(8,128)(2,1)} %keys_ref.1, bf16[8,32,1024]{2,1,0:T(8,128)(2,1)} %values_ref.1, bf16[8,4096]{1,0:T(8,128)(2,1)} %residual_ref.1, ...), custom_call_target="tpu_custom_call" | custom-call | flops 1 | bytes 1 | tf_op jit(solution)/shard_map/front/pallas_call | solution.py:110
  2.6 3.0 %collective-permute-start = (bf16[8,4224]{1,0:T(8,128)(2,1)}, bf16[8,4224]{1,0:T(8,128)(2,1)S(1)}, u32[]{:S(2)}, u32[]{:S(2)}) collective-permute-start(bf16[8,4224]{1,0:T(8,128)(2,1)} %get-tuple-element.46), channel_id=1, source_target_pairs={{0,4},{1,5},{2,6},{3,7},{4,0},{5,1},{6,2},{7,3},{8,12},{9,13},{10,... | collective-permute-start | bytes 202760 | tf_op jit(solution)/shard_map/ppermute | solution.py:379
  5.6 2.6 %collective-permute-start.1 = (bf16[8,4224]{1,0:T(8,128)(2,1)}, bf16[8,4224]{1,0:T(8,128)(2,1)S(1)}, u32[]{:S(2)}, u32[]{:S(2)}) collective-permute-start(bf16[8,4224]{1,0:T(8,128)(2,1)} %get-tuple-element.46), channel_id=1, source_target_pairs={{0,8},{1,9},{2,10},{3,11},{4,12},{5,13},{6,14},{7,15},{8,0},{9,1},... | collective-permute-start | bytes 202760 | tf_op jit(solution)/shard_map/ppermute | solution.py:379
  8.2 0.0 collective-permute-start.2
  8.2 4.1 %unpack_weights.3.refs_4_ = bf16[4096,1024]{1,0:T(8,128)(2,1)S(1)} custom-call(f32[1024,1024]{1,0:T(8,128)} %bitcast.8, bf16[32,1024]{1,0:T(8,128)(2,1)} %bitcast.11), custom_call_target="tpu_custom_call" | custom-call | flops 1 | bytes 1 | tf_op jit(solution)/shard_map/unpack_weights/pallas_call | solution.py:179
  12.3 0.0 collective-permute-done
  12.3 0.9 %collective-permute-done.1 = bf16[8,4224]{1,0:T(8,128)(2,1)S(1)} collective-permute-done((bf16[8,4224]{1,0:T(8,128)(2,1)}, bf16[8,4224]{1,0:T(8,128)(2,1)S(1)}, u32[]{:S(2)}, u32[]{:S(2)}) %collective-permute-start.1) | collective-permute-done | bytes 67616 | tf_op jit(solution)/shard_map/ppermute | solution.py:379
  13.2 1.4 %collective-permute-done.2 = bf16[8,4224]{1,0:T(8,128)(2,1)S(1)} collective-permute-done((bf16[8,4224]{1,0:T(8,128)(2,1)}, bf16[8,4224]{1,0:T(8,128)(2,1)S(1)}, u32[]{:S(2)}, u32[]{:S(2)}) %collective-permute-start.2) | collective-permute-done | bytes 67616 | tf_op jit(solution)/shard_map/ppermute | solution.py:379
  14.6 1.6 %collective-permute-start.3 = (bf16[32,4224]{1,0:T(8,128)(2,1)S(1)}, bf16[32,4224]{1,0:T(8,128)(2,1)S(1)}, u32[]{:S(2)}, u32[]{:S(2)}) collective-permute-start(bf16[32,4224]{1,0:T(8,128)(2,1)S(1)} %pad_maximum_fusion.refs_0_), channel_id=1, source_target_pairs={{0,2},{1,3},{2,0},{3,1},{4,6},{5,7},{6,4},{7,5},{8,10},{9,11},{10,... | collective-permute-start | bytes 811016 | tf_op jit(solution)/shard_map/ppermute | solution.py:379
  16.2 0.0 collective-permute-start.4
  16.2 1.5 %collective-permute-start.6 = (bf16[32,4224]{1,0:T(8,128)(2,1)S(1)}, bf16[32,4224]{1,0:T(8,128)(2,1)S(1)}, u32[]{:S(2)}, u32[]{:S(2)}) collective-permute-start(bf16[32,4224]{1,0:T(8,128)(2,1)S(1)} %pad_maximum_fusion.refs_0_), channel_id=1, source_target_pairs={{0,16},{1,17},{2,18},{3,19},{4,20},{5,21},{6,22},{7,23},{8,24},{9,... | collective-permute-start | bytes 811016 | tf_op jit(solution)/shard_map/ppermute | solution.py:379
  17.7 4.1 %unpack_weights.4.refs_5_ = bf16[4096,1024]{1,0:T(8,128)(2,1)S(1)} custom-call(f32[1024,1024]{1,0:T(8,128)} %bitcast.9, bf16[32,1024]{1,0:T(8,128)(2,1)} %bitcast.12), custom_call_target="tpu_custom_call" | custom-call | flops 1 | bytes 1 | tf_op jit(solution)/shard_map/unpack_weights/pallas_call | solution.py:179
  21.8 0.0 collective-permute-done.3.refs_2_
  21.8 0.3 collective-permute-start.5
  22.1 0.6 collective-permute-start.8
  22.7 2.5 %collective-permute-done.6.refs_0_ = bf16[32,4224]{1,0:T(8,128)(2,1)S(1)} collective-permute-done((bf16[32,4224]{1,0:T(8,128)(2,1)S(1)}, bf16[32,4224]{1,0:T(8,128)(2,1)S(1)}, u32[]{:S(2)}, u32[]{:S(2)}) %collective-permute-start.6) | collective-permute-done | bytes 270368 | tf_op jit(solution)/shard_map/ppermute | solution.py:379
  25.2 2.6 %gate_up.2 = (bf16[144,1024]{1,0:T(8,128)(2,1)S(1)}, f32[128,128]{1,0:T(8,128)S(1)}) custom-call(s32[1]{0:T(128)} %bitcast.1.place_ref, bf16[32,4224]{1,0:T(8,128)(2,1)S(1)} %pad_maximum_fusion.refs_0_, bf16[32,4224]{1,0:T(8,128)(2,1)S(1)} %collective-permute-done.4.refs_1_, bf16[32,4224]{1,0:T(8,128)(2,1)S(1)} %collective-permute-done.3.refs_2_, ...), custom_call_target="tpu_custom_call" | custom-call | flops 1 | bytes 1 | tf_op jit(solution)/shard_map/gate_up/pallas_call | solution.py:224
  27.8 1.9 %collective-permute-start.10 = (bf16[144,1024]{1,0:T(8,128)(2,1)S(1)}, bf16[144,1024]{1,0:T(8,128)(2,1)S(1)}, u32[]{:S(2)}, u32[]{:S(2)}) collective-permute-start(bf16[144,1024]{1,0:T(8,128)(2,1)S(1)} %get-tuple-element.69.hidden_ref), channel_id=1, source_target_pairs={{0,16},{1,17},{2,18},{3,19},{4,20},{5,21},{6,22},{7,23},{8,24},{9,... | collective-permute-start | bytes 884744 | tf_op jit(solution)/shard_map/ppermute | solution.py:379
  29.7 4.5 %unpack_weights.5.weight_ref = bf16[2048,2048]{1,0:T(8,128)(2,1)S(1)} custom-call(f32[512,2048]{1,0:T(8,128)} %bitcast.10, bf16[16,2048]{1,0:T(8,128)(2,1)} %bitcast.13), custom_call_target="tpu_custom_call" | custom-call | flops 1 | bytes 1 | tf_op jit(solution)/shard_map/unpack_weights/pallas_call | solution.py:179
  34.2 0.6 collective-permute-start.9
  34.8 1.2 %collective-permute-done.9.refs_3_ = bf16[32,4224]{1,0:T(8,128)(2,1)S(1)} collective-permute-done((bf16[32,4224]{1,0:T(8,128)(2,1)S(1)}, bf16[32,4224]{1,0:T(8,128)(2,1)S(1)}, u32[]{:S(2)}, u32[]{:S(2)}) %collective-permute-start.9) | collective-permute-done | bytes 270368 | tf_op jit(solution)/shard_map/ppermute | solution.py:379
  36.0 2.6 %gate_up.3 = (bf16[128,1024]{1,0:T(8,128)(2,1)S(1)}, f32[128,128]{1,0:T(8,128)S(1)}) custom-call(s32[1]{0:T(128)} %bitcast.1.place_ref, bf16[32,4224]{1,0:T(8,128)(2,1)S(1)} %collective-permute-done.6.refs_0_, bf16[32,4224]{1,0:T(8,128)(2,1)S(1)} %collective-permute-done.7.refs_1_, bf16[32,4224]{1,0:T(8,128)(2,1)S(1)} %collective-permute-done.8.refs_2_, ...), custom_call_target="tpu_custom_call" | custom-call | flops 1 | bytes 1 | tf_op jit(solution)/shard_map/gate_up/pallas_call | solution.py:224
  38.6 0.3 collective-permute-start.14
  38.9 0.7 %down_own.2.partial_ref = f32[128,2048]{1,0:T(8,128)S(1)} custom-call(s32[1]{0:T(128)} %bitcast.side_ref, bf16[128,1024]{1,0:T(8,128)(2,1)S(1)} %get-tuple-element.62.hidden_ref, bf16[2048,2048]{1,0:T(8,128)(2,1)S(1)} %unpack_weights.5.weight_ref), custom_call_target="tpu_custom_call" | custom-call | flops 1 | bytes 1 | tf_op jit(solution)/shard_map/down_own/pallas_call | solution.py:251
  39.6 0.8 %down_peer.2 = (bf16[64,2048]{1,0:T(8,128)(2,1)S(1)}, bf16[64,2048]{1,0:T(8,128)(2,1)S(1)}) custom-call(s32[1]{0:T(128)} %bitcast.side_ref, f32[128,2048]{1,0:T(8,128)S(1)} %down_own.2.partial_ref, bf16[144,1024]{1,0:T(8,128)(2,1)S(1)} %collective-permute-done.10.hidden_ref, bf16[2048,2048]{1,0:T(8,128)(2,1)S(1)} %unpack_weights.5.weight_ref, ...), custom_call_target="tpu_custom_call" | custom-call | flops 1 | bytes 1 | tf_op jit(solution)/shard_map/down_peer/pallas_call | solution.py:280
  40.4 0.0 copy-start
  40.5 0.5 collective-permute-start.11
  41.0 0.7 %down_own.3.partial_ref = f32[128,2048]{1,0:T(8,128)S(1)} custom-call(s32[1]{0:T(128)} %bitcast.side_ref, bf16[144,1024]{1,0:T(8,128)(2,1)S(1)} %get-tuple-element.69.hidden_ref, bf16[2048,2048]{1,0:T(8,128)(2,1)S(1)} %unpack_weights.5.weight_ref), custom_call_target="tpu_custom_call" | custom-call | flops 1 | bytes 1 | tf_op jit(solution)/shard_map/down_own/pallas_call | solution.py:251
  41.7 5.5 %collective-permute-done.14.hidden_ref = bf16[128,1024]{1,0:T(8,128)(2,1)S(1)} collective-permute-done((bf16[128,1024]{1,0:T(8,128)(2,1)S(1)}, bf16[128,1024]{1,0:T(8,128)(2,1)S(1)}, u32[]{:S(2)}, u32[]{:S(2)}) %collective-permute-start.14) | collective-permute-done | bytes 262176 | tf_op jit(solution)/shard_map/ppermute | solution.py:379
  47.2 0.8 %down_peer.3 = (bf16[32,2048]{1,0:T(8,128)(2,1)S(1)}, bf16[32,2048]{1,0:T(8,128)(2,1)S(1)}, bf16[32,2048]{1,0:T(8,128)(2,1)S(1)}, bf16[32,2048]{1,0:T(8,128)(2,1)S(1)}) custom-call(s32[1]{0:T(128)} %bitcast.side_ref, f32[128,2048]{1,0:T(8,128)S(1)} %down_own.3.partial_ref, bf16[128,1024]{1,0:T(8,128)(2,1)S(1)} %collective-permute-done.14.hidden_ref, ...), custom_call_target="tpu_custom_call" | custom-call | flops 1 | bytes 1 | tf_op jit(solution)/shard_map/down_peer/pallas_call | solution.py:280
  48.0 0.1 collective-permute-start.16
  48.1 0.8 %collective-permute-done.11.refs_1_ = bf16[64,2048]{1,0:T(8,128)(2,1)S(1)} collective-permute-done((bf16[64,2048]{1,0:T(8,128)(2,1)S(1)}, bf16[64,2048]{1,0:T(8,128)(2,1)S(1)}, u32[]{:S(2)}, u32[]{:S(2)}) %collective-permute-start.11) | collective-permute-done | bytes 262176 | tf_op jit(solution)/shard_map/ppermute | solution.py:379
  48.9 0.1 add_and_cut.3
  49.0 0.1 collective-permute-start.12
  49.0 0.5 collective-permute-start.15
  49.6 0.4 collective-permute-start.17
  50.0 0.4 collective-permute-done.12.refs_1_
  50.4 1.8 %collective-permute-start.13 = (bf16[32,2048]{1,0:T(8,128)(2,1)S(1)}, bf16[32,2048]{1,0:T(8,128)(2,1)S(1)}, u32[]{:S(2)}, u32[]{:S(2)}) collective-permute-start(bf16[32,2048]{1,0:T(8,128)(2,1)S(1)} %add_and_cut.4), channel_id=1, source_target_pairs={{0,16},{1,17},{2,18},{3,19},{4,20},{5,21},{6,22},{7,23},{8,24},{9,... | collective-permute-start | bytes 393224 | tf_op jit(solution)/shard_map/ppermute | solution.py:379
  52.2 2.9 %collective-permute-done.17.refs_2_ = bf16[32,2048]{1,0:T(8,128)(2,1)S(1)} collective-permute-done((bf16[32,2048]{1,0:T(8,128)(2,1)S(1)}, bf16[32,2048]{1,0:T(8,128)(2,1)S(1)}, u32[]{:S(2)}, u32[]{:S(2)}) %collective-permute-start.17) | collective-permute-done | bytes 131104 | tf_op jit(solution)/shard_map/ppermute | solution.py:379
  55.1 0.9 %collective-permute-done.13.far_ref = bf16[32,2048]{1,0:T(8,128)(2,1)S(1)} collective-permute-done((bf16[32,2048]{1,0:T(8,128)(2,1)S(1)}, bf16[32,2048]{1,0:T(8,128)(2,1)S(1)}, u32[]{:S(2)}, u32[]{:S(2)}) %collective-permute-start.13) | collective-permute-done | bytes 131104 | tf_op jit(solution)/shard_map/ppermute | solution.py:379
  56.0 0.1 join.1
  56.1 0.7 %collective-permute-start.18 = (bf16[16,2048]{1,0:T(8,128)(2,1)S(1)}, bf16[16,2048]{1,0:T(8,128)(2,1)S(1)}, u32[]{:S(2)}, u32[]{:S(2)}) collective-permute-start(bf16[16,2048]{1,0:T(8,128)(2,1)S(1)} %get-tuple-element.76), channel_id=1, source_target_pairs={{0,4},{1,5},{2,6},{3,7},{4,0},{5,1},{6,2},{7,3},{8,12},{9,13},{10,... | collective-permute-start | bytes 196616 | tf_op jit(solution)/shard_map/ppermute | solution.py:379
  56.8 1.6 %collective-permute-start.19 = (bf16[16,2048]{1,0:T(8,128)(2,1)S(1)}, bf16[16,2048]{1,0:T(8,128)(2,1)S(1)}, u32[]{:S(2)}, u32[]{:S(2)}) collective-permute-start(bf16[16,2048]{1,0:T(8,128)(2,1)S(1)} %get-tuple-element.77), channel_id=1, source_target_pairs={{0,8},{1,9},{2,10},{3,11},{4,12},{5,13},{6,14},{7,15},{8,0},{9,1},... | collective-permute-start | bytes 196616 | tf_op jit(solution)/shard_map/ppermute | solution.py:379
  58.4 2.1 %collective-permute-start.20 = (bf16[16,2048]{1,0:T(8,128)(2,1)S(1)}, bf16[16,2048]{1,0:T(8,128)(2,1)S(1)}, u32[]{:S(2)}, u32[]{:S(2)}) collective-permute-start(bf16[16,2048]{1,0:T(8,128)(2,1)S(1)} %get-tuple-element.78), channel_id=1, source_target_pairs={{0,12},{1,13},{2,14},{3,15},{4,8},{5,9},{6,10},{7,11},{8,4},{9,5},... | collective-permute-start | bytes 196616 | tf_op jit(solution)/shard_map/ppermute | solution.py:379
  60.5 0.2 collective-permute-done.18.refs_1_
  60.7 2.9 %collective-permute-done.19.refs_2_ = bf16[16,2048]{1,0:T(8,128)(2,1)S(1)} collective-permute-done((bf16[16,2048]{1,0:T(8,128)(2,1)S(1)}, bf16[16,2048]{1,0:T(8,128)(2,1)S(1)}, u32[]{:S(2)}, u32[]{:S(2)}) %collective-permute-start.19) | collective-permute-done | bytes 65568 | tf_op jit(solution)/shard_map/ppermute | solution.py:379
  63.6 1.0 %collective-permute-done.20.refs_3_ = bf16[16,2048]{1,0:T(8,128)(2,1)S(1)} collective-permute-done((bf16[16,2048]{1,0:T(8,128)(2,1)S(1)}, bf16[16,2048]{1,0:T(8,128)(2,1)S(1)}, u32[]{:S(2)}, u32[]{:S(2)}) %collective-permute-start.20) | collective-permute-done | bytes 65568 | tf_op jit(solution)/shard_map/ppermute | solution.py:379
  64.6 0.7 %finish.1 = bf16[8,4096]{1,0:T(8,128)(2,1)} custom-call(s32[1]{0:T(128)} %bitcast.side_ref, bf16[8,4096]{1,0:T(8,128)(2,1)S(1)} %copy-done, bf16[16,2048]{1,0:T(8,128)(2,1)S(1)} %get-tuple-element.75.refs_0_, bf16[16,2048]{1,0:T(8,128)(2,1)S(1)} %collective-permute-done.18.refs_1_, bf16[16,2048]{1,0:T(8,128)(2,1)S(1)} %collective-permute-done.19.refs_2_, ...), custom_call_target="tpu_custom_call" | custom-call | tf_op jit(solution)/shard_map/finish/pallas_call | solution.py:358
  (14 shorter events, 0.1 us)
Async XLA Ops:
  2.6 12.0 %copy-start.1 = (bf16[8,4224]{1,0:T(8,128)(2,1)S(1)}, bf16[8,4224]{1,0:T(8,128)(2,1)}, u32[]{:S(2)}) copy-start(bf16[8,4224]{1,0:T(8,128)(2,1)} %get-tuple-element.46) | copy-start | bytes 202756
  2.6 9.7 %collective-permute-start = (bf16[8,4224]{1,0:T(8,128)(2,1)}, bf16[8,4224]{1,0:T(8,128)(2,1)S(1)}, u32[]{:S(2)}, u32[]{:S(2)}) collective-permute-start(bf16[8,4224]{1,0:T(8,128)(2,1)} %get-tuple-element.46), channel_id=1, source_target_pairs={{0,4},{1,5},{2,6},{3,7},{4,0},{5,1},{6,2},{7,3},{8,12},{9,13},{10,... | collective-permute-start | bytes 202760 | tf_op jit(solution)/shard_map/ppermute | solution.py:379
  5.6 7.6 %collective-permute-start.1 = (bf16[8,4224]{1,0:T(8,128)(2,1)}, bf16[8,4224]{1,0:T(8,128)(2,1)S(1)}, u32[]{:S(2)}, u32[]{:S(2)}) collective-permute-start(bf16[8,4224]{1,0:T(8,128)(2,1)} %get-tuple-element.46), channel_id=1, source_target_pairs={{0,8},{1,9},{2,10},{3,11},{4,12},{5,13},{6,14},{7,15},{8,0},{9,1},... | collective-permute-start | bytes 202760 | tf_op jit(solution)/shard_map/ppermute | solution.py:379
  8.2 6.4 %collective-permute-start.2 = (bf16[8,4224]{1,0:T(8,128)(2,1)}, bf16[8,4224]{1,0:T(8,128)(2,1)S(1)}, u32[]{:S(2)}, u32[]{:S(2)}) collective-permute-start(bf16[8,4224]{1,0:T(8,128)(2,1)} %get-tuple-element.46), channel_id=1, source_target_pairs={{0,12},{1,13},{2,14},{3,15},{4,8},{5,9},{6,10},{7,11},{8,4},{9,5},... | collective-permute-start | bytes 202760 | tf_op jit(solution)/shard_map/ppermute | solution.py:379
  14.6 7.2 %collective-permute-start.3 = (bf16[32,4224]{1,0:T(8,128)(2,1)S(1)}, bf16[32,4224]{1,0:T(8,128)(2,1)S(1)}, u32[]{:S(2)}, u32[]{:S(2)}) collective-permute-start(bf16[32,4224]{1,0:T(8,128)(2,1)S(1)} %pad_maximum_fusion.refs_0_), channel_id=1, source_target_pairs={{0,2},{1,3},{2,0},{3,1},{4,6},{5,7},{6,4},{7,5},{8,10},{9,11},{10,... | collective-permute-start | bytes 811016 | tf_op jit(solution)/shard_map/ppermute | solution.py:379
  16.2 5.6 %collective-permute-start.4 = (bf16[32,4224]{1,0:T(8,128)(2,1)S(1)}, bf16[32,4224]{1,0:T(8,128)(2,1)S(1)}, u32[]{:S(2)}, u32[]{:S(2)}) collective-permute-start(bf16[32,4224]{1,0:T(8,128)(2,1)S(1)} %pad_maximum_fusion.refs_0_), channel_id=1, source_target_pairs={{0,1},{1,0},{2,3},{3,2},{4,5},{5,4},{6,7},{7,6},{8,9},{9,8},{10,11... | collective-permute-start | bytes 811016 | tf_op jit(solution)/shard_map/ppermute | solution.py:379
  16.2 9.0 %collective-permute-start.6 = (bf16[32,4224]{1,0:T(8,128)(2,1)S(1)}, bf16[32,4224]{1,0:T(8,128)(2,1)S(1)}, u32[]{:S(2)}, u32[]{:S(2)}) collective-permute-start(bf16[32,4224]{1,0:T(8,128)(2,1)S(1)} %pad_maximum_fusion.refs_0_), channel_id=1, source_target_pairs={{0,16},{1,17},{2,18},{3,19},{4,20},{5,21},{6,22},{7,23},{8,24},{9,... | collective-permute-start | bytes 811016 | tf_op jit(solution)/shard_map/ppermute | solution.py:379
  21.8 3.4 %collective-permute-start.5 = (bf16[32,4224]{1,0:T(8,128)(2,1)S(1)}, bf16[32,4224]{1,0:T(8,128)(2,1)S(1)}, u32[]{:S(2)}, u32[]{:S(2)}) collective-permute-start(bf16[32,4224]{1,0:T(8,128)(2,1)S(1)} %collective-permute-done.3.refs_2_), channel_id=1, source_target_pairs={{0,1},{1,0},{2,3},{3,2},{4,5},{5,4},{6,7},{7,6},{8,9},{9,8},{10,11... | collective-permute-start | bytes 811016 | tf_op jit(solution)/shard_map/ppermute | solution.py:379
  22.1 12.1 %collective-permute-start.8 = (bf16[32,4224]{1,0:T(8,128)(2,1)S(1)}, bf16[32,4224]{1,0:T(8,128)(2,1)S(1)}, u32[]{:S(2)}, u32[]{:S(2)}) collective-permute-start(bf16[32,4224]{1,0:T(8,128)(2,1)S(1)} %collective-permute-done.3.refs_2_), channel_id=1, source_target_pairs={{0,16},{1,17},{2,18},{3,19},{4,20},{5,21},{6,22},{7,23},{8,24},{9,... | collective-permute-start | bytes 811016 | tf_op jit(solution)/shard_map/ppermute | solution.py:379
  27.8 11.8 %collective-permute-start.10 = (bf16[144,1024]{1,0:T(8,128)(2,1)S(1)}, bf16[144,1024]{1,0:T(8,128)(2,1)S(1)}, u32[]{:S(2)}, u32[]{:S(2)}) collective-permute-start(bf16[144,1024]{1,0:T(8,128)(2,1)S(1)} %get-tuple-element.69.hidden_ref), channel_id=1, source_target_pairs={{0,16},{1,17},{2,18},{3,19},{4,20},{5,21},{6,22},{7,23},{8,24},{9,... | collective-permute-start | bytes 884744 | tf_op jit(solution)/shard_map/ppermute | solution.py:379
  29.7 5.1 %collective-permute-start.7 = (bf16[32,4224]{1,0:T(8,128)(2,1)S(1)}, bf16[32,4224]{1,0:T(8,128)(2,1)S(1)}, u32[]{:S(2)}, u32[]{:S(2)}) collective-permute-start(bf16[32,4224]{1,0:T(8,128)(2,1)S(1)} %collective-permute-done.6.refs_0_), channel_id=1, source_target_pairs={{0,1},{1,0},{2,3},{3,2},{4,5},{5,4},{6,7},{7,6},{8,9},{9,8},{10,11... | collective-permute-start | bytes 811016 | tf_op jit(solution)/shard_map/ppermute | solution.py:379
  34.2 1.7 %collective-permute-start.9 = (bf16[32,4224]{1,0:T(8,128)(2,1)S(1)}, bf16[32,4224]{1,0:T(8,128)(2,1)S(1)}, u32[]{:S(2)}, u32[]{:S(2)}) collective-permute-start(bf16[32,4224]{1,0:T(8,128)(2,1)S(1)} %collective-permute-done.8.refs_2_), channel_id=1, source_target_pairs={{0,1},{1,0},{2,3},{3,2},{4,5},{5,4},{6,7},{7,6},{8,9},{9,8},{10,11... | collective-permute-start | bytes 811016 | tf_op jit(solution)/shard_map/ppermute | solution.py:379
  38.6 8.6 %collective-permute-start.14 = (bf16[128,1024]{1,0:T(8,128)(2,1)S(1)}, bf16[128,1024]{1,0:T(8,128)(2,1)S(1)}, u32[]{:S(2)}, u32[]{:S(2)}) collective-permute-start(bf16[128,1024]{1,0:T(8,128)(2,1)S(1)} %get-tuple-element.62.hidden_ref), channel_id=1, source_target_pairs={{0,16},{1,17},{2,18},{3,19},{4,20},{5,21},{6,22},{7,23},{8,24},{9,... | collective-permute-start | bytes 786440 | tf_op jit(solution)/shard_map/ppermute | solution.py:379
  40.4 24.2 %copy-start = (bf16[8,4096]{1,0:T(8,128)(2,1)S(1)}, bf16[8,4096]{1,0:T(8,128)(2,1)}, u32[]{:S(2)}) copy-start(bf16[8,4096]{1,0:T(8,128)(2,1)} %get-tuple-element.44.mixed_ref) | copy-start | bytes 196612
  40.5 8.4 %collective-permute-start.11 = (bf16[64,2048]{1,0:T(8,128)(2,1)S(1)}, bf16[64,2048]{1,0:T(8,128)(2,1)S(1)}, u32[]{:S(2)}, u32[]{:S(2)}) collective-permute-start(bf16[64,2048]{1,0:T(8,128)(2,1)S(1)} %get-tuple-element.66), channel_id=1, source_target_pairs={{0,2},{1,3},{2,0},{3,1},{4,6},{5,7},{6,4},{7,5},{8,10},{9,11},{10,... | collective-permute-start | bytes 786440 | tf_op jit(solution)/shard_map/ppermute | solution.py:379
  48.0 1.5 %collective-permute-start.16 = (bf16[32,2048]{1,0:T(8,128)(2,1)S(1)}, bf16[32,2048]{1,0:T(8,128)(2,1)S(1)}, u32[]{:S(2)}, u32[]{:S(2)}) collective-permute-start(bf16[32,2048]{1,0:T(8,128)(2,1)S(1)} %get-tuple-element.74), channel_id=1, source_target_pairs={{0,1},{1,0},{2,3},{3,2},{4,5},{5,4},{6,7},{7,6},{8,9},{9,8},{10,11... | collective-permute-start | bytes 393224 | tf_op jit(solution)/shard_map/ppermute | solution.py:379
  49.0 1.4 %collective-permute-start.12 = (bf16[32,2048]{1,0:T(8,128)(2,1)S(1)}, bf16[32,2048]{1,0:T(8,128)(2,1)S(1)}, u32[]{:S(2)}, u32[]{:S(2)}) collective-permute-start(bf16[32,2048]{1,0:T(8,128)(2,1)S(1)} %get-tuple-element.68), channel_id=1, source_target_pairs={{0,1},{1,0},{2,3},{3,2},{4,5},{5,4},{6,7},{7,6},{8,9},{9,8},{10,11... | collective-permute-start | bytes 393224 | tf_op jit(solution)/shard_map/ppermute | solution.py:379
  49.0 3.2 %collective-permute-start.15 = (bf16[32,2048]{1,0:T(8,128)(2,1)S(1)}, bf16[32,2048]{1,0:T(8,128)(2,1)S(1)}, u32[]{:S(2)}, u32[]{:S(2)}) collective-permute-start(bf16[32,2048]{1,0:T(8,128)(2,1)S(1)} %get-tuple-element.72), channel_id=1, source_target_pairs={{0,1},{1,0},{2,3},{3,2},{4,5},{5,4},{6,7},{7,6},{8,9},{9,8},{10,11... | collective-permute-start | bytes 393224 | tf_op jit(solution)/shard_map/ppermute | solution.py:379
  49.6 5.5 %collective-permute-start.17 = (bf16[32,2048]{1,0:T(8,128)(2,1)S(1)}, bf16[32,2048]{1,0:T(8,128)(2,1)S(1)}, u32[]{:S(2)}, u32[]{:S(2)}) collective-permute-start(bf16[32,2048]{1,0:T(8,128)(2,1)S(1)} %add_and_cut.5), channel_id=1, source_target_pairs={{0,2},{1,3},{2,0},{3,1},{4,6},{5,7},{6,4},{7,5},{8,10},{9,11},{10,... | collective-permute-start | bytes 393224 | tf_op jit(solution)/shard_map/ppermute | solution.py:379
  50.4 5.6 %collective-permute-start.13 = (bf16[32,2048]{1,0:T(8,128)(2,1)S(1)}, bf16[32,2048]{1,0:T(8,128)(2,1)S(1)}, u32[]{:S(2)}, u32[]{:S(2)}) collective-permute-start(bf16[32,2048]{1,0:T(8,128)(2,1)S(1)} %add_and_cut.4), channel_id=1, source_target_pairs={{0,16},{1,17},{2,18},{3,19},{4,20},{5,21},{6,22},{7,23},{8,24},{9,... | collective-permute-start | bytes 393224 | tf_op jit(solution)/shard_map/ppermute | solution.py:379
  56.1 4.6 %collective-permute-start.18 = (bf16[16,2048]{1,0:T(8,128)(2,1)S(1)}, bf16[16,2048]{1,0:T(8,128)(2,1)S(1)}, u32[]{:S(2)}, u32[]{:S(2)}) collective-permute-start(bf16[16,2048]{1,0:T(8,128)(2,1)S(1)} %get-tuple-element.76), channel_id=1, source_target_pairs={{0,4},{1,5},{2,6},{3,7},{4,0},{5,1},{6,2},{7,3},{8,12},{9,13},{10,... | collective-permute-start | bytes 196616 | tf_op jit(solution)/shard_map/ppermute | solution.py:379
  56.8 6.9 %collective-permute-start.19 = (bf16[16,2048]{1,0:T(8,128)(2,1)S(1)}, bf16[16,2048]{1,0:T(8,128)(2,1)S(1)}, u32[]{:S(2)}, u32[]{:S(2)}) collective-permute-start(bf16[16,2048]{1,0:T(8,128)(2,1)S(1)} %get-tuple-element.77), channel_id=1, source_target_pairs={{0,8},{1,9},{2,10},{3,11},{4,12},{5,13},{6,14},{7,15},{8,0},{9,1},... | collective-permute-start | bytes 196616 | tf_op jit(solution)/shard_map/ppermute | solution.py:379
  58.4 6.2 %collective-permute-start.20 = (bf16[16,2048]{1,0:T(8,128)(2,1)S(1)}, bf16[16,2048]{1,0:T(8,128)(2,1)S(1)}, u32[]{:S(2)}, u32[]{:S(2)}) collective-permute-start(bf16[16,2048]{1,0:T(8,128)(2,1)S(1)} %get-tuple-element.78), channel_id=1, source_target_pairs={{0,12},{1,13},{2,14},{3,15},{4,8},{5,9},{6,10},{7,11},{8,4},{9,5},... | collective-permute-start | bytes 196616 | tf_op jit(solution)/shard_map/ppermute | solution.py:379

commit v4 on v3

--- a/solution.py
+++ b/solution.py
@@ -13,6 +13,7 @@
 LANES = 128
 VMEM_LIMIT = 56 * 2**20
 VMEM_SOME = 16 * 2**20
+VMEM_MORE = 24 * 2**20
 SPARE = 16
 SMALL = pl.CostEstimate(flops=1, bytes_accessed=1, transcendentals=0)
 F32 = jnp.float32
@@ -129,26 +130,45 @@
     return pltpu.with_memory_space_constraint(array, pltpu.HBM)
 
 
-def unpack_kernel(codes_ref, scales_hbm, out_ref, words_ref, scales_ref, sems, scales_sem):
-    quarter, width = codes_ref.shape
-    groups = quarter // GROUP
-    step = 256 if width % 256 == 0 else LANES
-
-    def fetch(group):
+def unpack_kernel(firsts, codes_refs, scales_hbms, *refs):
+    out_refs, (words_refs, scales_refs, sems, scales_sem) = refs[: len(firsts)], refs[len(firsts) :]
+
+    def copy_scales(n):
+        columns = pl.ds(firsts[n], words_refs[n].shape[1])
+        return pltpu.make_async_copy(
+            scales_hbms[n].at[:, columns], scales_refs[n], scales_sem.at[n]
+        )
+
+    def fetch(turn):
+        n, group = turns[turn]
         rows = pl.ds(group * GROUP, GROUP)
-        return pltpu.make_async_copy(codes_ref.at[rows, :], words_ref.at[rows, :], sems.at[group])
-
-    scales_copy = pltpu.make_async_copy(scales_hbm, scales_ref, scales_sem)
-    scales_copy.start()
+        columns = pl.ds(firsts[n], words_refs[n].shape[1])
+        return pltpu.make_async_copy(
+            codes_refs[n].at[rows, columns], words_refs[n].at[rows, :], sems.at[turn]
+        )
+
+    turns = [
+        (n, group)
+        for n, words_ref in enumerate(words_refs)
+        for group in range(words_ref.shape[0] // GROUP)
+    ]
     ahead = 3
-    for group in range(min(ahead, groups)):
-        fetch(group).start()
-    scales_copy.wait()
-    scales = scales_ref[...].astype(F32)
-    for group in range(groups):
-        if group + ahead < groups:
-            fetch(group + ahead).start()
-        fetch(group).wait()
+    copy_scales(0).start()
+    for turn in range(min(ahead, len(turns))):
+        fetch(turn).start()
+    for n in range(1, len(firsts)):
+        copy_scales(n).start()
+    for turn, (n, group) in enumerate(turns):
+        words_ref, out_ref = words_refs[n], out_refs[n]
+        quarter, width = words_ref.shape
+        groups = quarter // GROUP
+        step = 256 if width % 256 == 0 else LANES
+        if turn + ahead < len(turns):
+            fetch(turn + ahead).start()
+        if group == 0:
+            copy_scales(n).wait()
+            scales = scales_refs[n][...].astype(F32)
+        fetch(turn).wait()
         for column in range(0, width, step):
             spans = [
                 jnp.broadcast_to(
@@ -158,7 +178,9 @@
                 for k in range(4)
             ]
 
-            def chunk(i, carry, group=group, column=column, spans=spans):
+            def chunk(
+                i, carry, group=group, column=column, spans=spans, words_ref=words_ref, out_ref=out_ref
+            ):
                 start = pl.multiple_of(group * GROUP + i * 16, 16)
                 words = words_ref[pl.ds(start, 16), column : column + step].astype(jnp.int32)
                 for k in range(4):
@@ -174,23 +196,26 @@
             lax.fori_loop(0, GROUP // 16, chunk, 0, unroll=True)
 
 
-def unpack_weights(codes, scales):
-    quarter, width = codes.shape
-    return pl.pallas_call(
-        unpack_kernel,
-        out_shape=pltpu.VMEM((4 * quarter, width), BF16),
-        in_specs=[pl.BlockSpec(memory_space=pltpu.HBM)] * 2,
-        out_specs=pl.BlockSpec(memory_space=pltpu.VMEM),
+def unpack_weights(*jobs):
+    hbm = pl.BlockSpec(memory_space=pltpu.HBM)
+    vmem = pl.BlockSpec(memory_space=pltpu.VMEM)
+    shapes = [(codes.shape[0], width) for codes, _, _, width in jobs]
+    turns = sum(quarter // GROUP for quarter, _ in shapes)
+    return pl.pallas_call(
+        functools.partial(unpack_kernel, tuple(job[2] for job in jobs)),
+        out_shape=[pltpu.VMEM((4 * quarter, width), BF16) for quarter, width in shapes],
+        in_specs=[[hbm] * len(jobs)] * 2,
+        out_specs=[vmem] * len(jobs),
         scratch_shapes=[
-            pltpu.VMEM((quarter, width), F32),
-            pltpu.VMEM(scales.shape, BF16),
-            pltpu.SemaphoreType.DMA((quarter // GROUP,)),
-            pltpu.SemaphoreType.DMA,
+            [pltpu.VMEM(shape, F32) for shape in shapes],
+            [pltpu.VMEM((4 * quarter // GROUP, width), BF16) for quarter, width in shapes],
+            pltpu.SemaphoreType.DMA((turns,)),
+            pltpu.SemaphoreType.DMA((len(jobs),)),
         ],
-        compiler_params=pltpu.CompilerParams(vmem_limit_bytes=VMEM_SOME),
+        compiler_params=pltpu.CompilerParams(vmem_limit_bytes=VMEM_MORE),
         cost_estimate=SMALL,
         name="unpack_weights",
-    )(in_hbm(codes), in_hbm(scales))
+    )([in_hbm(job[0]) for job in jobs], [in_hbm(job[1]) for job in jobs])
 
 
 def hidden_kernel(place_ref, *refs):
@@ -233,59 +258,65 @@
     )(place, *pieces, in_vmem(w_gate), in_vmem(w_up))
 
 
-def own_down_kernel(side_ref, hidden_ref, weight_ref, out_ref):
+def own_down_kernel(side_ref, hidden_ref, weight_refs, out_ref):
     half = hidden_ref.shape[1]
     rows = pl.ds(pl.multiple_of(side_ref[0] * half, half), half)
     step = 256
-    for column in range(0, out_ref.shape[1], step):
-        span = slice(column, column + step)
-        out_ref[:, span] = jnp.dot(
-            hidden_ref[: out_ref.shape[0]], weight_ref[rows, span], preferred_element_type=F32
-        )
-
-
-def own_down(side, hidden, weight, count):
-    half = hidden.shape[1]
-    width = weight.shape[1]
+    for n, weight_ref in enumerate(weight_refs):
+        width = weight_ref.shape[1]
+        for column in range(0, width, step):
+            out_ref[:, n * width + column : n * width + column + step] = jnp.dot(
+                hidden_ref[: out_ref.shape[0]],
+                weight_ref[rows, column : column + step],
+                preferred_element_type=F32,
+            )
+
+
+def own_down(side, hidden, weights, count):
+    width = sum(weight.shape[1] for weight in weights)
     vmem = pl.BlockSpec(memory_space=pltpu.VMEM)
     return pl.pallas_call(
         own_down_kernel,
         out_shape=pltpu.VMEM((count, width), F32),
-        in_specs=[pl.BlockSpec(memory_space=pltpu.SMEM), vmem, vmem],
+        in_specs=[pl.BlockSpec(memory_space=pltpu.SMEM), vmem, [vmem] * len(weights)],
         out_specs=vmem,
         compiler_params=pltpu.CompilerParams(vmem_limit_bytes=VMEM_SOME),
         cost_estimate=SMALL,
         name="down_own",
-    )(side, in_vmem(hidden), in_vmem(weight))
-
-
-def peer_down_kernel(side_ref, partial_ref, hidden_ref, weight_ref, share_ref, *out_refs):
+    )(side, in_vmem(hidden), [in_vmem(weight) for weight in weights])
+
+
+def peer_down_kernel(side_ref, partial_ref, hidden_ref, weight_refs, share_ref, *out_refs):
     count, half = partial_ref.shape[0], hidden_ref.shape[1]
     rows = pl.ds(pl.multiple_of((1 - side_ref[0]) * half, half), half)
     step = 256
     cut = count // len(out_refs)
-    for column in range(0, partial_ref.shape[1], step):
-        span = slice(column, column + step)
-        produced = partial_ref[:, span] + jnp.dot(
-            hidden_ref[:count], weight_ref[rows, span], preferred_element_type=F32
-        )
-        result = (produced.astype(BF16).astype(F32) * share_ref[:, :1]).astype(BF16)
-        for n, out_ref in enumerate(out_refs):
-            out_ref[:, span] = result[n * cut : (n + 1) * cut]
-
-
-def peer_down(side, partial, hidden, weight, share, parts):
+    for n, weight_ref in enumerate(weight_refs):
+        width = weight_ref.shape[1]
+        for column in range(0, width, step):
+            span = slice(n * width + column, n * width + column + step)
+            produced = partial_ref[:, span] + jnp.dot(
+                hidden_ref[:count],
+                weight_ref[rows, column : column + step],
+                preferred_element_type=F32,
+            )
+            result = (produced.astype(BF16).astype(F32) * share_ref[:, :1]).astype(BF16)
+            for m, out_ref in enumerate(out_refs):
+                out_ref[:, span] = result[m * cut : (m + 1) * cut]
+
+
+def peer_down(side, partial, hidden, weights, share, parts):
     count, width = partial.shape
     vmem = pl.BlockSpec(memory_space=pltpu.VMEM)
     return pl.pallas_call(
         peer_down_kernel,
         out_shape=(pltpu.VMEM((count // parts, width), BF16),) * parts,
-        in_specs=[pl.BlockSpec(memory_space=pltpu.SMEM)] + [vmem] * 4,
+        in_specs=[pl.BlockSpec(memory_space=pltpu.SMEM), vmem, vmem, [vmem] * len(weights), vmem],
         out_specs=(vmem,) * parts,
         compiler_params=pltpu.CompilerParams(vmem_limit_bytes=VMEM_SOME),
         cost_estimate=SMALL,
         name="down_peer",
-    )(side, in_vmem(partial), hidden, in_vmem(weight), in_vmem(share))
+    )(side, in_vmem(partial), hidden, [in_vmem(weight) for weight in weights], in_vmem(share))
 
 
 def halve_kernel(terms, *refs):
@@ -378,16 +409,20 @@
     def swap(block, offset):
         return lax.ppermute(block, ("dp", "expert"), [(i, i ^ offset) for i in range(devices)])
 
-    side, place, gate_scales, payload = lax.optimization_barrier(
-        (side, place, gate_scales, payload)
-    )
+    side, place, gate_scales, down_scales, payload = lax.optimization_barrier(
+        (side, place, gate_scales, down_scales, payload)
+    )
+    units = gate_codes.shape[1]
+    half = down_codes.shape[1] // 2
     blocks = [swap(payload, z * layer) for z in range(1, layers)]
-    w_gate = unpack_weights(gate_codes, gate_scales)
+    w_gate, w_down = unpack_weights(
+        (gate_codes, gate_scales, 0, units), (down_codes, down_scales, 0, half)
+    )
     blocks, w_gate = lax.optimization_barrier((blocks, w_gate))
     stack = jnp.concatenate([payload] + blocks, axis=0)
     up_scales, stack = lax.optimization_barrier((up_scales, stack))
     beside, above, stack_pair = swap(stack, plane), swap(stack, line), swap(stack, core)
-    w_up = unpack_weights(up_codes, up_scales)
+    (w_up,) = unpack_weights((up_codes, up_scales, 0, units))
     above, stack_pair, w_up = lax.optimization_barrier((above, stack_pair, w_up))
     across, above_pair = swap(above, plane), swap(above, core)
     above_pair, beside = lax.optimization_barrier((above_pair, beside))
@@ -397,8 +432,9 @@
     )
     other_peer = swap(hidden_own, plane)
     down_scales, hidden_own = lax.optimization_barrier((down_scales, hidden_own))
-    w_down = unpack_weights(down_codes, down_scales)
-    across, w_down = lax.optimization_barrier((across, w_down))
+    (w_more,) = unpack_weights((down_codes, down_scales, half, half))
+    across, w_more = lax.optimization_barrier((across, w_more))
+    w_down = [w_down, w_more]
     hidden_other, share_other = hidden_units(
         [beside, beside_pair, across, swap(across, core)], w_gate, w_up, place
     )

time: 65.6 us -> 65.1 us (level)
  waiting for transfers between devices: 20.6 us -> 19.3 us
  starting transfers between devices: 20.1 us -> 21 us
    ppermute x21, waiting for transfers between devices: 20.6 us -> 19.3 us  [swap(): lax.ppermute(block, ('dp', 'expert'), [(i, i ^ offset) for i in range(dev...]
    ppermute x21, starting transfers between devices: 20.1 us -> 21 us  [swap(): lax.ppermute(block, ('dp', 'expert'), [(i, i ^ offset) for i in range(dev...]
  transfers between devices with their start and end apart: 21 -> 21, of which waited for: 12 -> 11; matrix products, arithmetic and copies ran while one was open for 0% -> 0% of each run, Pallas kernels for 32% -> 32%
where the time goes in v4:
time: 65.1 us; the launch traced here: 64.8 us
  Pallas kernels  24.3 us (37%)
  starting transfers between devices  21 us (32%)
  waiting for transfers between devices  19.3 us (30%)
    ppermute x21, starting transfers between devices, swap(): lax.ppermute(block, ('dp', 'expert'), [(i, i ^ offset) for i in range(dev...  21 us
    ppermute x21, waiting for transfers between devices, swap(): lax.ppermute(block, ('dp', 'expert'), [(i, i ^ offset) for i in range(dev...  19.3 us
    pallas_call x3, Pallas kernels, unpack_weights(): pl.pallas_call(functools.partial(unpack_kernel, tuple((job[2] for job in...  12.6 us
    pallas_call x2, Pallas kernels, hidden_units(): pl.pallas_call(hidden_kernel, out_shape=(pltpu.VMEM((count + spare, width...  5.24 us
    pallas_call x1, Pallas kernels, front(): pl.pallas_call(front_kernel, out_shape=(jax.ShapeDtypeStruct((rows, width...  2.6 us
    pallas_call x2, Pallas kernels, peer_down(): pl.pallas_call(peer_down_kernel, out_shape=(pltpu.VMEM((count // parts, w...  1.58 us
    pallas_call x2, Pallas kernels, own_down(): pl.pallas_call(own_down_kernel, out_shape=pltpu.VMEM((count, width), F32)...  1.45 us
  transfers between devices with their start and end apart: 21, of which 11 were waited for; matrix products, arithmetic and copies ran while one was open for 0% of the time, Pallas kernels for 32%

profile of v4, /device:TPU:0, one launch (start us, length us, event | category | flops | bytes accessed | tf_op | source)
XLA Modules:
  0.0 64.8 jit_solution(17074513147123261041)
XLA Ops:
  0.0 2.6 %front.1 = (bf16[8,4096]{1,0:T(8,128)(2,1)}, bf16[8,4224]{1,0:T(8,128)(2,1)}) custom-call(s32[8]{0:T(128)} %lengths_ref.1, bf16[8,4096]{1,0:T(8,128)(2,1)} %queries_ref.1, bf16[8,2,1024]{2,1,0:T(2,128)(2,1)} %new_kv_ref.1, bf16[8,32,1024]{2,1,0:T(8,128)(2,1)} %keys_ref.1, bf16[8,32,1024]{2,1,0:T(8,128)(2,1)} %values_ref.1, bf16[8,4096]{1,0:T(8,128)(2,1)} %residual_ref.1, ...), custom_call_target="tpu_custom_call" | custom-call | flops 1 | bytes 1 | tf_op jit(solution)/shard_map/front/pallas_call | solution.py:111
  2.6 3.0 %collective-permute-start = (bf16[8,4224]{1,0:T(8,128)(2,1)}, bf16[8,4224]{1,0:T(8,128)(2,1)S(1)}, u32[]{:S(2)}, u32[]{:S(2)}) collective-permute-start(bf16[8,4224]{1,0:T(8,128)(2,1)} %get-tuple-element.49), channel_id=1, source_target_pairs={{0,4},{1,5},{2,6},{3,7},{4,0},{5,1},{6,2},{7,3},{8,12},{9,13},{10,... | collective-permute-start | bytes 202760 | tf_op jit(solution)/shard_map/ppermute | solution.py:410
  5.6 2.6 %collective-permute-start.1 = (bf16[8,4224]{1,0:T(8,128)(2,1)}, bf16[8,4224]{1,0:T(8,128)(2,1)S(1)}, u32[]{:S(2)}, u32[]{:S(2)}) collective-permute-start(bf16[8,4224]{1,0:T(8,128)(2,1)} %get-tuple-element.49), channel_id=1, source_target_pairs={{0,8},{1,9},{2,10},{3,11},{4,12},{5,13},{6,14},{7,15},{8,0},{9,1},... | collective-permute-start | bytes 202760 | tf_op jit(solution)/shard_map/ppermute | solution.py:410
  8.2 0.0 collective-permute-start.2
  8.2 5.5 %unpack_weights.3 = (bf16[4096,1024]{1,0:T(8,128)(2,1)S(1)}, bf16[2048,1024]{1,0:T(8,128)(2,1)S(1)}) custom-call(f32[1024,1024]{1,0:T(8,128)} %bitcast.11, f32[512,2048]{1,0:T(8,128)} %bitcast.8, bf16[32,1024]{1,0:T(8,128)(2,1)} %bitcast.14, bf16[16,2048]{1,0:T(8,128)(2,1)} %bitcast.12), custom_call_target="tpu_custom_call" | custom-call | flops 1 | bytes 1 | tf_op jit(solution)/shard_map/unpack_weights/pallas_call | solution.py:204
  13.8 0.8 %collective-permute-done.2 = bf16[8,4224]{1,0:T(8,128)(2,1)S(1)} collective-permute-done((bf16[8,4224]{1,0:T(8,128)(2,1)}, bf16[8,4224]{1,0:T(8,128)(2,1)S(1)}, u32[]{:S(2)}, u32[]{:S(2)}) %collective-permute-start.2) | collective-permute-done | bytes 67616 | tf_op jit(solution)/shard_map/ppermute | solution.py:410
  14.7 1.6 %collective-permute-start.3 = (bf16[32,4224]{1,0:T(8,128)(2,1)S(1)}, bf16[32,4224]{1,0:T(8,128)(2,1)S(1)}, u32[]{:S(2)}, u32[]{:S(2)}) collective-permute-start(bf16[32,4224]{1,0:T(8,128)(2,1)S(1)} %pad_maximum_fusion.refs_0_), channel_id=1, source_target_pairs={{0,2},{1,3},{2,0},{3,1},{4,6},{5,7},{6,4},{7,5},{8,10},{9,11},{10,... | collective-permute-start | bytes 811016 | tf_op jit(solution)/shard_map/ppermute | solution.py:410
  16.2 0.0 collective-permute-start.4
  16.2 1.5 %collective-permute-start.6 = (bf16[32,4224]{1,0:T(8,128)(2,1)S(1)}, bf16[32,4224]{1,0:T(8,128)(2,1)S(1)}, u32[]{:S(2)}, u32[]{:S(2)}) collective-permute-start(bf16[32,4224]{1,0:T(8,128)(2,1)S(1)} %pad_maximum_fusion.refs_0_), channel_id=1, source_target_pairs={{0,16},{1,17},{2,18},{3,19},{4,20},{5,21},{6,22},{7,23},{8,24},{9,... | collective-permute-start | bytes 811016 | tf_op jit(solution)/shard_map/ppermute | solution.py:410
  17.7 4.2 %unpack_weights.4.refs_5_ = bf16[4096,1024]{1,0:T(8,128)(2,1)S(1)} custom-call(f32[1024,1024]{1,0:T(8,128)} %bitcast.10, bf16[32,1024]{1,0:T(8,128)(2,1)} %bitcast.15), custom_call_target="tpu_custom_call" | custom-call | flops 1 | bytes 1 | tf_op jit(solution)/shard_map/unpack_weights/pallas_call | solution.py:204
  21.9 0.0 collective-permute-done.3.refs_2_
  22.0 0.0 collective-permute-done.4.refs_1_
  22.0 0.3 collective-permute-start.5
  22.3 0.8 %collective-permute-start.8 = (bf16[32,4224]{1,0:T(8,128)(2,1)S(1)}, bf16[32,4224]{1,0:T(8,128)(2,1)S(1)}, u32[]{:S(2)}, u32[]{:S(2)}) collective-permute-start(bf16[32,4224]{1,0:T(8,128)(2,1)S(1)} %collective-permute-done.3.refs_2_), channel_id=1, source_target_pairs={{0,16},{1,17},{2,18},{3,19},{4,20},{5,21},{6,22},{7,23},{8,24},{9,... | collective-permute-start | bytes 811016 | tf_op jit(solution)/shard_map/ppermute | solution.py:410
  23.1 2.1 %collective-permute-done.6.refs_0_ = bf16[32,4224]{1,0:T(8,128)(2,1)S(1)} collective-permute-done((bf16[32,4224]{1,0:T(8,128)(2,1)S(1)}, bf16[32,4224]{1,0:T(8,128)(2,1)S(1)}, u32[]{:S(2)}, u32[]{:S(2)}) %collective-permute-start.6) | collective-permute-done | bytes 270368 | tf_op jit(solution)/shard_map/ppermute | solution.py:410
  25.1 2.6 %gate_up.2 = (bf16[144,1024]{1,0:T(8,128)(2,1)S(1)}, f32[128,128]{1,0:T(8,128)S(1)}) custom-call(s32[1]{0:T(128)} %bitcast.1.place_ref, bf16[32,4224]{1,0:T(8,128)(2,1)S(1)} %pad_maximum_fusion.refs_0_, bf16[32,4224]{1,0:T(8,128)(2,1)S(1)} %collective-permute-done.4.refs_1_, bf16[32,4224]{1,0:T(8,128)(2,1)S(1)} %collective-permute-done.3.refs_2_, ...), custom_call_target="tpu_custom_call" | custom-call | flops 1 | bytes 1 | tf_op jit(solution)/shard_map/gate_up/pallas_call | solution.py:249
  27.8 1.9 %collective-permute-start.10 = (bf16[144,1024]{1,0:T(8,128)(2,1)S(1)}, bf16[144,1024]{1,0:T(8,128)(2,1)S(1)}, u32[]{:S(2)}, u32[]{:S(2)}) collective-permute-start(bf16[144,1024]{1,0:T(8,128)(2,1)S(1)} %get-tuple-element.75.hidden_ref), channel_id=1, source_target_pairs={{0,16},{1,17},{2,18},{3,19},{4,20},{5,21},{6,22},{7,23},{8,24},{9,... | collective-permute-start | bytes 884744 | tf_op jit(solution)/shard_map/ppermute | solution.py:410
  29.7 0.0 collective-permute-start.7
  29.7 2.9 %unpack_weights.5.weight_refs_1_ = bf16[2048,1024]{1,0:T(8,128)(2,1)S(1)} custom-call(f32[512,2048]{1,0:T(8,128)} %bitcast.9, bf16[16,2048]{1,0:T(8,128)(2,1)} %bitcast.13), custom_call_target="tpu_custom_call" | custom-call | flops 1 | bytes 1 | tf_op jit(solution)/shard_map/unpack_weights/pallas_call | solution.py:204
  32.6 0.0 collective-permute-done.8.refs_2_
  32.6 0.6 collective-permute-start.9
  33.2 1.2 %collective-permute-done.9.refs_3_ = bf16[32,4224]{1,0:T(8,128)(2,1)S(1)} collective-permute-done((bf16[32,4224]{1,0:T(8,128)(2,1)S(1)}, bf16[32,4224]{1,0:T(8,128)(2,1)S(1)}, u32[]{:S(2)}, u32[]{:S(2)}) %collective-permute-start.9) | collective-permute-done | bytes 270368 | tf_op jit(solution)/shard_map/ppermute | solution.py:410
  34.3 2.6 %gate_up.3 = (bf16[128,1024]{1,0:T(8,128)(2,1)S(1)}, f32[128,128]{1,0:T(8,128)S(1)}) custom-call(s32[1]{0:T(128)} %bitcast.1.place_ref, bf16[32,4224]{1,0:T(8,128)(2,1)S(1)} %collective-permute-done.6.refs_0_, bf16[32,4224]{1,0:T(8,128)(2,1)S(1)} %collective-permute-done.7.refs_1_, bf16[32,4224]{1,0:T(8,128)(2,1)S(1)} %collective-permute-done.8.refs_2_, ...), custom_call_target="tpu_custom_call" | custom-call | flops 1 | bytes 1 | tf_op jit(solution)/shard_map/gate_up/pallas_call | solution.py:249
  37.0 0.2 collective-permute-start.14
  37.2 0.7 %down_own.2.partial_ref = f32[128,2048]{1,0:T(8,128)S(1)} custom-call(s32[1]{0:T(128)} %bitcast.side_ref, bf16[128,1024]{1,0:T(8,128)(2,1)S(1)} %get-tuple-element.67.hidden_ref, bf16[2048,1024]{1,0:T(8,128)(2,1)S(1)} %get-tuple-element.68.weight_refs_0_, bf16[2048,1024]{1,0:T(8,128)(2,1)S(1)} %unpack_weights.5.weight_refs_1_), custom_call_target="tpu_custom_call" | custom-call | flops 1 | bytes 1 | tf_op jit(solution)/shard_map/down_own/pallas_call | solution.py:278
  37.9 0.8 %down_peer.2 = (bf16[64,2048]{1,0:T(8,128)(2,1)S(1)}, bf16[64,2048]{1,0:T(8,128)(2,1)S(1)}) custom-call(s32[1]{0:T(128)} %bitcast.side_ref, f32[128,2048]{1,0:T(8,128)S(1)} %down_own.2.partial_ref, bf16[144,1024]{1,0:T(8,128)(2,1)S(1)} %collective-permute-done.10.hidden_ref, bf16[2048,1024]{1,0:T(8,128)(2,1)S(1)} %get-tuple-element.68.weight_refs_0_, ...), custom_call_target="tpu_custom_call" | custom-call | flops 1 | bytes 1 | tf_op jit(solution)/shard_map/down_peer/pallas_call | solution.py:311
  38.7 1.0 %collective-permute-start.11 = (bf16[64,2048]{1,0:T(8,128)(2,1)S(1)}, bf16[64,2048]{1,0:T(8,128)(2,1)S(1)}, u32[]{:S(2)}, u32[]{:S(2)}) collective-permute-start(bf16[64,2048]{1,0:T(8,128)(2,1)S(1)} %get-tuple-element.72), channel_id=1, source_target_pairs={{0,2},{1,3},{2,0},{3,1},{4,6},{5,7},{6,4},{7,5},{8,10},{9,11},{10,... | collective-permute-start | bytes 786440 | tf_op jit(solution)/shard_map/ppermute | solution.py:410
  39.7 0.7 %down_own.3.partial_ref = f32[128,2048]{1,0:T(8,128)S(1)} custom-call(s32[1]{0:T(128)} %bitcast.side_ref, bf16[144,1024]{1,0:T(8,128)(2,1)S(1)} %get-tuple-element.75.hidden_ref, bf16[2048,1024]{1,0:T(8,128)(2,1)S(1)} %get-tuple-element.68.weight_refs_0_, bf16[2048,1024]{1,0:T(8,128)(2,1)S(1)} %unpack_weights.5.weight_refs_1_), custom_call_target="tpu_custom_call" | custom-call | flops 1 | bytes 1 | tf_op jit(solution)/shard_map/down_own/pallas_call | solution.py:278
  40.4 5.2 %collective-permute-done.14.hidden_ref = bf16[128,1024]{1,0:T(8,128)(2,1)S(1)} collective-permute-done((bf16[128,1024]{1,0:T(8,128)(2,1)S(1)}, bf16[128,1024]{1,0:T(8,128)(2,1)S(1)}, u32[]{:S(2)}, u32[]{:S(2)}) %collective-permute-start.14) | collective-permute-done | bytes 262176 | tf_op jit(solution)/shard_map/ppermute | solution.py:410
  45.6 0.8 %down_peer.3 = (bf16[32,2048]{1,0:T(8,128)(2,1)S(1)}, bf16[32,2048]{1,0:T(8,128)(2,1)S(1)}, bf16[32,2048]{1,0:T(8,128)(2,1)S(1)}, bf16[32,2048]{1,0:T(8,128)(2,1)S(1)}) custom-call(s32[1]{0:T(128)} %bitcast.side_ref, f32[128,2048]{1,0:T(8,128)S(1)} %down_own.3.partial_ref, bf16[128,1024]{1,0:T(8,128)(2,1)S(1)} %collective-permute-done.14.hidden_ref, ...), custom_call_target="tpu_custom_call" | custom-call | flops 1 | bytes 1 | tf_op jit(solution)/shard_map/down_peer/pallas_call | solution.py:311
  46.4 0.1 collective-permute-start.16
  46.5 0.8 %collective-permute-done.11.refs_1_ = bf16[64,2048]{1,0:T(8,128)(2,1)S(1)} collective-permute-done((bf16[64,2048]{1,0:T(8,128)(2,1)S(1)}, bf16[64,2048]{1,0:T(8,128)(2,1)S(1)}, u32[]{:S(2)}, u32[]{:S(2)}) %collective-permute-start.11) | collective-permute-done | bytes 262176 | tf_op jit(solution)/shard_map/ppermute | solution.py:410
  47.2 0.1 add_and_cut.3
  47.3 0.1 collective-permute-start.12
  47.4 0.5 collective-permute-start.15
  47.9 0.6 collective-permute-start.17
  48.6 0.2 collective-permute-done.12.refs_1_
  48.8 1.8 %collective-permute-start.13 = (bf16[32,2048]{1,0:T(8,128)(2,1)S(1)}, bf16[32,2048]{1,0:T(8,128)(2,1)S(1)}, u32[]{:S(2)}, u32[]{:S(2)}) collective-permute-start(bf16[32,2048]{1,0:T(8,128)(2,1)S(1)} %add_and_cut.4), channel_id=1, source_target_pairs={{0,16},{1,17},{2,18},{3,19},{4,20},{5,21},{6,22},{7,23},{8,24},{9,... | collective-permute-start | bytes 393224 | tf_op jit(solution)/shard_map/ppermute | solution.py:410
  50.6 2.9 %collective-permute-done.17.refs_2_ = bf16[32,2048]{1,0:T(8,128)(2,1)S(1)} collective-permute-done((bf16[32,2048]{1,0:T(8,128)(2,1)S(1)}, bf16[32,2048]{1,0:T(8,128)(2,1)S(1)}, u32[]{:S(2)}, u32[]{:S(2)}) %collective-permute-start.17) | collective-permute-done | bytes 131104 | tf_op jit(solution)/shard_map/ppermute | solution.py:410
  53.5 0.9 %collective-permute-done.13.far_ref = bf16[32,2048]{1,0:T(8,128)(2,1)S(1)} collective-permute-done((bf16[32,2048]{1,0:T(8,128)(2,1)S(1)}, bf16[32,2048]{1,0:T(8,128)(2,1)S(1)}, u32[]{:S(2)}, u32[]{:S(2)}) %collective-permute-start.13) | collective-permute-done | bytes 131104 | tf_op jit(solution)/shard_map/ppermute | solution.py:410
  54.4 0.1 join.1
  54.4 0.7 %collective-permute-start.18 = (bf16[16,2048]{1,0:T(8,128)(2,1)S(1)}, bf16[16,2048]{1,0:T(8,128)(2,1)S(1)}, u32[]{:S(2)}, u32[]{:S(2)}) collective-permute-start(bf16[16,2048]{1,0:T(8,128)(2,1)S(1)} %get-tuple-element.82), channel_id=1, source_target_pairs={{0,4},{1,5},{2,6},{3,7},{4,0},{5,1},{6,2},{7,3},{8,12},{9,13},{10,... | collective-permute-start | bytes 196616 | tf_op jit(solution)/shard_map/ppermute | solution.py:410
  55.1 2.9 %collective-permute-start.19 = (bf16[16,2048]{1,0:T(8,128)(2,1)S(1)}, bf16[16,2048]{1,0:T(8,128)(2,1)S(1)}, u32[]{:S(2)}, u32[]{:S(2)}) collective-permute-start(bf16[16,2048]{1,0:T(8,128)(2,1)S(1)} %get-tuple-element.83), channel_id=1, source_target_pairs={{0,8},{1,9},{2,10},{3,11},{4,12},{5,13},{6,14},{7,15},{8,0},{9,1},... | collective-permute-start | bytes 196616 | tf_op jit(solution)/shard_map/ppermute | solution.py:410
  58.1 0.8 %collective-permute-start.20 = (bf16[16,2048]{1,0:T(8,128)(2,1)S(1)}, bf16[16,2048]{1,0:T(8,128)(2,1)S(1)}, u32[]{:S(2)}, u32[]{:S(2)}) collective-permute-start(bf16[16,2048]{1,0:T(8,128)(2,1)S(1)} %get-tuple-element.84), channel_id=1, source_target_pairs={{0,12},{1,13},{2,14},{3,15},{4,8},{5,9},{6,10},{7,11},{8,4},{9,5},... | collective-permute-start | bytes 196616 | tf_op jit(solution)/shard_map/ppermute | solution.py:410
  58.9 0.2 collective-permute-done.18.refs_1_
  59.1 2.9 %collective-permute-done.19.refs_2_ = bf16[16,2048]{1,0:T(8,128)(2,1)S(1)} collective-permute-done((bf16[16,2048]{1,0:T(8,128)(2,1)S(1)}, bf16[16,2048]{1,0:T(8,128)(2,1)S(1)}, u32[]{:S(2)}, u32[]{:S(2)}) %collective-permute-start.19) | collective-permute-done | bytes 65568 | tf_op jit(solution)/shard_map/ppermute | solution.py:410
  62.0 2.1 %collective-permute-done.20.refs_3_ = bf16[16,2048]{1,0:T(8,128)(2,1)S(1)} collective-permute-done((bf16[16,2048]{1,0:T(8,128)(2,1)S(1)}, bf16[16,2048]{1,0:T(8,128)(2,1)S(1)}, u32[]{:S(2)}, u32[]{:S(2)}) %collective-permute-start.20) | collective-permute-done | bytes 65568 | tf_op jit(solution)/shard_map/ppermute | solution.py:410
  64.1 0.7 %finish.1 = bf16[8,4096]{1,0:T(8,128)(2,1)} custom-call(s32[1]{0:T(128)} %bitcast.side_ref, bf16[8,4096]{1,0:T(8,128)(2,1)S(1)} %copy-done, bf16[16,2048]{1,0:T(8,128)(2,1)S(1)} %get-tuple-element.81.refs_0_, bf16[16,2048]{1,0:T(8,128)(2,1)S(1)} %collective-permute-done.18.refs_1_, bf16[16,2048]{1,0:T(8,128)(2,1)S(1)} %collective-permute-done.19.refs_2_, ...), custom_call_target="tpu_custom_call" | custom-call | tf_op jit(solution)/shard_map/finish/pallas_call | solution.py:389
  (14 shorter events, 0.1 us)
Async XLA Ops:
  2.6 11.2 %collective-permute-start = (bf16[8,4224]{1,0:T(8,128)(2,1)}, bf16[8,4224]{1,0:T(8,128)(2,1)S(1)}, u32[]{:S(2)}, u32[]{:S(2)}) collective-permute-start(bf16[8,4224]{1,0:T(8,128)(2,1)} %get-tuple-element.49), channel_id=1, source_target_pairs={{0,4},{1,5},{2,6},{3,7},{4,0},{5,1},{6,2},{7,3},{8,12},{9,13},{10,... | collective-permute-start | bytes 202760 | tf_op jit(solution)/shard_map/ppermute | solution.py:410
  5.6 8.1 %collective-permute-start.1 = (bf16[8,4224]{1,0:T(8,128)(2,1)}, bf16[8,4224]{1,0:T(8,128)(2,1)S(1)}, u32[]{:S(2)}, u32[]{:S(2)}) collective-permute-start(bf16[8,4224]{1,0:T(8,128)(2,1)} %get-tuple-element.49), channel_id=1, source_target_pairs={{0,8},{1,9},{2,10},{3,11},{4,12},{5,13},{6,14},{7,15},{8,0},{9,1},... | collective-permute-start | bytes 202760 | tf_op jit(solution)/shard_map/ppermute | solution.py:410
  8.2 6.4 %collective-permute-start.2 = (bf16[8,4224]{1,0:T(8,128)(2,1)}, bf16[8,4224]{1,0:T(8,128)(2,1)S(1)}, u32[]{:S(2)}, u32[]{:S(2)}) collective-permute-start(bf16[8,4224]{1,0:T(8,128)(2,1)} %get-tuple-element.49), channel_id=1, source_target_pairs={{0,12},{1,13},{2,14},{3,15},{4,8},{5,9},{6,10},{7,11},{8,4},{9,5},... | collective-permute-start | bytes 202760 | tf_op jit(solution)/shard_map/ppermute | solution.py:410
  8.2 6.4 %copy-start.1 = (bf16[8,4224]{1,0:T(8,128)(2,1)S(1)}, bf16[8,4224]{1,0:T(8,128)(2,1)}, u32[]{:S(2)}) copy-start(bf16[8,4224]{1,0:T(8,128)(2,1)} %get-tuple-element.49) | copy-start | bytes 202756
  14.7 7.3 %collective-permute-start.3 = (bf16[32,4224]{1,0:T(8,128)(2,1)S(1)}, bf16[32,4224]{1,0:T(8,128)(2,1)S(1)}, u32[]{:S(2)}, u32[]{:S(2)}) collective-permute-start(bf16[32,4224]{1,0:T(8,128)(2,1)S(1)} %pad_maximum_fusion.refs_0_), channel_id=1, source_target_pairs={{0,2},{1,3},{2,0},{3,1},{4,6},{5,7},{6,4},{7,5},{8,10},{9,11},{10,... | collective-permute-start | bytes 811016 | tf_op jit(solution)/shard_map/ppermute | solution.py:410
  16.2 5.7 %collective-permute-start.4 = (bf16[32,4224]{1,0:T(8,128)(2,1)S(1)}, bf16[32,4224]{1,0:T(8,128)(2,1)S(1)}, u32[]{:S(2)}, u32[]{:S(2)}) collective-permute-start(bf16[32,4224]{1,0:T(8,128)(2,1)S(1)} %pad_maximum_fusion.refs_0_), channel_id=1, source_target_pairs={{0,1},{1,0},{2,3},{3,2},{4,5},{5,4},{6,7},{7,6},{8,9},{9,8},{10,11... | collective-permute-start | bytes 811016 | tf_op jit(solution)/shard_map/ppermute | solution.py:410
  16.2 8.9 %collective-permute-start.6 = (bf16[32,4224]{1,0:T(8,128)(2,1)S(1)}, bf16[32,4224]{1,0:T(8,128)(2,1)S(1)}, u32[]{:S(2)}, u32[]{:S(2)}) collective-permute-start(bf16[32,4224]{1,0:T(8,128)(2,1)S(1)} %pad_maximum_fusion.refs_0_), channel_id=1, source_target_pairs={{0,16},{1,17},{2,18},{3,19},{4,20},{5,21},{6,22},{7,23},{8,24},{9,... | collective-permute-start | bytes 811016 | tf_op jit(solution)/shard_map/ppermute | solution.py:410
  22.0 3.2 %collective-permute-start.5 = (bf16[32,4224]{1,0:T(8,128)(2,1)S(1)}, bf16[32,4224]{1,0:T(8,128)(2,1)S(1)}, u32[]{:S(2)}, u32[]{:S(2)}) collective-permute-start(bf16[32,4224]{1,0:T(8,128)(2,1)S(1)} %collective-permute-done.3.refs_2_), channel_id=1, source_target_pairs={{0,1},{1,0},{2,3},{3,2},{4,5},{5,4},{6,7},{7,6},{8,9},{9,8},{10,11... | collective-permute-start | bytes 811016 | tf_op jit(solution)/shard_map/ppermute | solution.py:410
  22.3 10.3 %collective-permute-start.8 = (bf16[32,4224]{1,0:T(8,128)(2,1)S(1)}, bf16[32,4224]{1,0:T(8,128)(2,1)S(1)}, u32[]{:S(2)}, u32[]{:S(2)}) collective-permute-start(bf16[32,4224]{1,0:T(8,128)(2,1)S(1)} %collective-permute-done.3.refs_2_), channel_id=1, source_target_pairs={{0,16},{1,17},{2,18},{3,19},{4,20},{5,21},{6,22},{7,23},{8,24},{9,... | collective-permute-start | bytes 811016 | tf_op jit(solution)/shard_map/ppermute | solution.py:410
  27.8 10.2 %collective-permute-start.10 = (bf16[144,1024]{1,0:T(8,128)(2,1)S(1)}, bf16[144,1024]{1,0:T(8,128)(2,1)S(1)}, u32[]{:S(2)}, u32[]{:S(2)}) collective-permute-start(bf16[144,1024]{1,0:T(8,128)(2,1)S(1)} %get-tuple-element.75.hidden_ref), channel_id=1, source_target_pairs={{0,16},{1,17},{2,18},{3,19},{4,20},{5,21},{6,22},{7,23},{8,24},{9,... | collective-permute-start | bytes 884744 | tf_op jit(solution)/shard_map/ppermute | solution.py:410
  29.7 3.5 %collective-permute-start.7 = (bf16[32,4224]{1,0:T(8,128)(2,1)S(1)}, bf16[32,4224]{1,0:T(8,128)(2,1)S(1)}, u32[]{:S(2)}, u32[]{:S(2)}) collective-permute-start(bf16[32,4224]{1,0:T(8,128)(2,1)S(1)} %collective-permute-done.6.refs_0_), channel_id=1, source_target_pairs={{0,1},{1,0},{2,3},{3,2},{4,5},{5,4},{6,7},{7,6},{8,9},{9,8},{10,11... | collective-permute-start | bytes 811016 | tf_op jit(solution)/shard_map/ppermute | solution.py:410
  32.6 1.7 %collective-permute-start.9 = (bf16[32,4224]{1,0:T(8,128)(2,1)S(1)}, bf16[32,4224]{1,0:T(8,128)(2,1)S(1)}, u32[]{:S(2)}, u32[]{:S(2)}) collective-permute-start(bf16[32,4224]{1,0:T(8,128)(2,1)S(1)} %collective-permute-done.8.refs_2_), channel_id=1, source_target_pairs={{0,1},{1,0},{2,3},{3,2},{4,5},{5,4},{6,7},{7,6},{8,9},{9,8},{10,11... | collective-permute-start | bytes 811016 | tf_op jit(solution)/shard_map/ppermute | solution.py:410
  37.0 8.7 %collective-permute-start.14 = (bf16[128,1024]{1,0:T(8,128)(2,1)S(1)}, bf16[128,1024]{1,0:T(8,128)(2,1)S(1)}, u32[]{:S(2)}, u32[]{:S(2)}) collective-permute-start(bf16[128,1024]{1,0:T(8,128)(2,1)S(1)} %get-tuple-element.67.hidden_ref), channel_id=1, source_target_pairs={{0,16},{1,17},{2,18},{3,19},{4,20},{5,21},{6,22},{7,23},{8,24},{9,... | collective-permute-start | bytes 786440 | tf_op jit(solution)/shard_map/ppermute | solution.py:410
  38.7 8.5 %collective-permute-start.11 = (bf16[64,2048]{1,0:T(8,128)(2,1)S(1)}, bf16[64,2048]{1,0:T(8,128)(2,1)S(1)}, u32[]{:S(2)}, u32[]{:S(2)}) collective-permute-start(bf16[64,2048]{1,0:T(8,128)(2,1)S(1)} %get-tuple-element.72), channel_id=1, source_target_pairs={{0,2},{1,3},{2,0},{3,1},{4,6},{5,7},{6,4},{7,5},{8,10},{9,11},{10,... | collective-permute-start | bytes 786440 | tf_op jit(solution)/shard_map/ppermute | solution.py:410
  45.6 18.5 %copy-start = (bf16[8,4096]{1,0:T(8,128)(2,1)S(1)}, bf16[8,4096]{1,0:T(8,128)(2,1)}, u32[]{:S(2)}) copy-start(bf16[8,4096]{1,0:T(8,128)(2,1)} %get-tuple-element.47.mixed_ref) | copy-start | bytes 196612
  46.4 1.5 %collective-permute-start.16 = (bf16[32,2048]{1,0:T(8,128)(2,1)S(1)}, bf16[32,2048]{1,0:T(8,128)(2,1)S(1)}, u32[]{:S(2)}, u32[]{:S(2)}) collective-permute-start(bf16[32,2048]{1,0:T(8,128)(2,1)S(1)} %get-tuple-element.80), channel_id=1, source_target_pairs={{0,1},{1,0},{2,3},{3,2},{4,5},{5,4},{6,7},{7,6},{8,9},{9,8},{10,11... | collective-permute-start | bytes 393224 | tf_op jit(solution)/shard_map/ppermute | solution.py:410
  47.3 1.4 %collective-permute-start.12 = (bf16[32,2048]{1,0:T(8,128)(2,1)S(1)}, bf16[32,2048]{1,0:T(8,128)(2,1)S(1)}, u32[]{:S(2)}, u32[]{:S(2)}) collective-permute-start(bf16[32,2048]{1,0:T(8,128)(2,1)S(1)} %get-tuple-element.74), channel_id=1, source_target_pairs={{0,1},{1,0},{2,3},{3,2},{4,5},{5,4},{6,7},{7,6},{8,9},{9,8},{10,11... | collective-permute-start | bytes 393224 | tf_op jit(solution)/shard_map/ppermute | solution.py:410
  47.4 3.2 %collective-permute-start.15 = (bf16[32,2048]{1,0:T(8,128)(2,1)S(1)}, bf16[32,2048]{1,0:T(8,128)(2,1)S(1)}, u32[]{:S(2)}, u32[]{:S(2)}) collective-permute-start(bf16[32,2048]{1,0:T(8,128)(2,1)S(1)} %get-tuple-element.78), channel_id=1, source_target_pairs={{0,1},{1,0},{2,3},{3,2},{4,5},{5,4},{6,7},{7,6},{8,9},{9,8},{10,11... | collective-permute-start | bytes 393224 | tf_op jit(solution)/shard_map/ppermute | solution.py:410
  47.9 5.5 %collective-permute-start.17 = (bf16[32,2048]{1,0:T(8,128)(2,1)S(1)}, bf16[32,2048]{1,0:T(8,128)(2,1)S(1)}, u32[]{:S(2)}, u32[]{:S(2)}) collective-permute-start(bf16[32,2048]{1,0:T(8,128)(2,1)S(1)} %add_and_cut.5), channel_id=1, source_target_pairs={{0,2},{1,3},{2,0},{3,1},{4,6},{5,7},{6,4},{7,5},{8,10},{9,11},{10,... | collective-permute-start | bytes 393224 | tf_op jit(solution)/shard_map/ppermute | solution.py:410
  48.8 5.6 %collective-permute-start.13 = (bf16[32,2048]{1,0:T(8,128)(2,1)S(1)}, bf16[32,2048]{1,0:T(8,128)(2,1)S(1)}, u32[]{:S(2)}, u32[]{:S(2)}) collective-permute-start(bf16[32,2048]{1,0:T(8,128)(2,1)S(1)} %add_and_cut.4), channel_id=1, source_target_pairs={{0,16},{1,17},{2,18},{3,19},{4,20},{5,21},{6,22},{7,23},{8,24},{9,... | collective-permute-start | bytes 393224 | tf_op jit(solution)/shard_map/ppermute | solution.py:410
  54.4 4.6 %collective-permute-start.18 = (bf16[16,2048]{1,0:T(8,128)(2,1)S(1)}, bf16[16,2048]{1,0:T(8,128)(2,1)S(1)}, u32[]{:S(2)}, u32[]{:S(2)}) collective-permute-start(bf16[16,2048]{1,0:T(8,128)(2,1)S(1)} %get-tuple-element.82), channel_id=1, source_target_pairs={{0,4},{1,5},{2,6},{3,7},{4,0},{5,1},{6,2},{7,3},{8,12},{9,13},{10,... | collective-permute-start | bytes 196616 | tf_op jit(solution)/shard_map/ppermute | solution.py:410
  55.1 6.9 %collective-permute-start.19 = (bf16[16,2048]{1,0:T(8,128)(2,1)S(1)}, bf16[16,2048]{1,0:T(8,128)(2,1)S(1)}, u32[]{:S(2)}, u32[]{:S(2)}) collective-permute-start(bf16[16,2048]{1,0:T(8,128)(2,1)S(1)} %get-tuple-element.83), channel_id=1, source_target_pairs={{0,8},{1,9},{2,10},{3,11},{4,12},{5,13},{6,14},{7,15},{8,0},{9,1},... | collective-permute-start | bytes 196616 | tf_op jit(solution)/shard_map/ppermute | solution.py:410
  58.1 6.1 %collective-permute-start.20 = (bf16[16,2048]{1,0:T(8,128)(2,1)S(1)}, bf16[16,2048]{1,0:T(8,128)(2,1)S(1)}, u32[]{:S(2)}, u32[]{:S(2)}) collective-permute-start(bf16[16,2048]{1,0:T(8,128)(2,1)S(1)} %get-tuple-element.84), channel_id=1, source_target_pairs={{0,12},{1,13},{2,14},{3,15},{4,8},{5,9},{6,10},{7,11},{8,4},{9,5},... | collective-permute-start | bytes 196616 | tf_op jit(solution)/shard_map/ppermute | solution.py:410

commit v5 on v4

--- a/solution.py
+++ b/solution.py
@@ -14,7 +14,7 @@
 VMEM_LIMIT = 56 * 2**20
 VMEM_SOME = 16 * 2**20
 VMEM_MORE = 24 * 2**20
-SPARE = 16
+SPARE = 0
 SMALL = pl.CostEstimate(flops=1, bytes_accessed=1, transcendentals=0)
 F32 = jnp.float32
 BF16 = jnp.bfloat16
@@ -286,11 +286,17 @@
     )(side, in_vmem(hidden), [in_vmem(weight) for weight in weights])
 
 
-def peer_down_kernel(side_ref, partial_ref, hidden_ref, weight_refs, share_ref, *out_refs):
+def cuts(rows, parts):
+    size = rows.shape[0] // parts
+    return [rows[n * size : (n + 1) * size] for n in range(parts)]
+
+
+def peer_down_kernel(
+    side_ref, partial_ref, hidden_ref, weight_refs, share_ref, *out_refs
+):
     count, half = partial_ref.shape[0], hidden_ref.shape[1]
     rows = pl.ds(pl.multiple_of((1 - side_ref[0]) * half, half), half)
     step = 256
-    cut = count // len(out_refs)
     for n, weight_ref in enumerate(weight_refs):
         width = weight_ref.shape[1]
         for column in range(0, width, step):
@@ -300,9 +306,9 @@
                 weight_ref[rows, column : column + step],
                 preferred_element_type=F32,
             )
-            result = (produced.astype(BF16).astype(F32) * share_ref[:, :1]).astype(BF16)
-            for m, out_ref in enumerate(out_refs):
-                out_ref[:, span] = result[m * cut : (m + 1) * cut]
+            result = produced.astype(BF16).astype(F32) * share_ref[:, :1]
+            for out_ref, cut in zip(out_refs, cuts(result, len(out_refs))):
+                out_ref[:, span] = cut.astype(BF16)
 
 
 def peer_down(side, partial, hidden, weights, share, parts):
@@ -319,22 +325,24 @@
     )(side, in_vmem(partial), hidden, [in_vmem(weight) for weight in weights], in_vmem(share))
 
 
-def halve_kernel(terms, *refs):
+def add_kernel(terms, *refs):
     term_refs, out_refs = refs[:terms], refs[terms:]
     total = term_refs[0][...].astype(F32)
     for term_ref in term_refs[1:]:
         total = total + term_ref[...].astype(F32)
-    size = total.shape[0] // len(out_refs)
-    for n, out_ref in enumerate(out_refs):
-        out_ref[...] = total[n * size : (n + 1) * size].astype(out_ref.dtype)
-
-
-def add_and_cut(kept, arrived, parts):
+    width = total.shape[1]
+    for out_ref, cut in zip(out_refs, cuts(total, len(out_refs))):
+        out_ref[:, :width] = cut.astype(out_ref.dtype)
+        if out_ref.shape[1] > width:
+            out_ref[:, width:] = jnp.zeros((cut.shape[0], out_ref.shape[1] - width), out_ref.dtype)
+
+
+def add_and_cut(kept, arrived, parts, spare=0):
     count, width = kept[0].shape
     vmem = pl.BlockSpec(memory_space=pltpu.VMEM)
-    shape = pltpu.VMEM((count // parts, width), BF16)
-    return pl.pallas_call(
-        functools.partial(halve_kernel, len(kept + arrived)),
+    shape = pltpu.VMEM((count // parts, width + spare), BF16)
+    return pl.pallas_call(
+        functools.partial(add_kernel, len(kept + arrived)),
         out_shape=(shape,) * parts,
         in_specs=[vmem] * len(kept + arrived),
         out_specs=(vmem,) * parts,
@@ -344,56 +352,30 @@
     )(*[in_vmem(part) for part in kept], *arrived)
 
 
-def join_kernel(parts, far_ref, *refs):
-    near_refs, out_refs = refs[:-parts], refs[-parts:]
-    size = far_ref.shape[0] // parts
-    near = near_refs[0][...].astype(F32)
+def finish_kernel(side_ref, mixed_ref, far_ref, *refs):
+    near_refs, out_ref = refs[:-1], refs[-1]
+    half = far_ref.shape[1]
+    near = near_refs[0][:, :half].astype(F32)
     for near_ref in near_refs[1:]:
-        near = near + near_ref[...].astype(F32)
+        near = near + near_ref[:, :half].astype(F32)
     far = far_ref[...].astype(F32)
-    for n, out_ref in enumerate(out_refs):
-        rows = slice(n * size, (n + 1) * size)
-        out_ref[...] = jnp.concatenate([near[rows], far[rows]], axis=0).astype(BF16)
-
-
-def join(near, far, parts):
-    count, width = far.shape
-    vmem = pl.BlockSpec(memory_space=pltpu.VMEM)
-    return pl.pallas_call(
-        functools.partial(join_kernel, parts),
-        out_shape=(pltpu.VMEM((2 * count // parts, width), BF16),) * parts,
-        in_specs=[vmem] * (1 + len(near)),
-        out_specs=(vmem,) * parts,
-        compiler_params=pltpu.CompilerParams(vmem_limit_bytes=VMEM_SOME),
-        cost_estimate=SMALL,
-        name="join",
-    )(far, *near)
-
-
-def finish_kernel(side_ref, mixed_ref, *refs):
-    block_refs, out_ref = refs[:-1], refs[-1]
-    rows, width = mixed_ref.shape
-    total = block_refs[0][...].astype(F32)
-    for block_ref in block_refs[1:]:
-        total = total + block_ref[...].astype(F32)
-    near, far = total[:rows], total[rows:]
     first = side_ref[0] == 0
-    half = width // 2
     for n, part in enumerate((jnp.where(first, near, far), jnp.where(first, far, near))):
         span = slice(n * half, (n + 1) * half)
         out_ref[:, span] = (mixed_ref[:, span].astype(F32) + part).astype(BF16)
 
 
-def finish(side, mixed, blocks):
+def finish(side, mixed, far, near):
     vmem = pl.BlockSpec(memory_space=pltpu.VMEM)
     return pl.pallas_call(
         finish_kernel,
         out_shape=jax.ShapeDtypeStruct(mixed.shape, BF16),
-        in_specs=[pl.BlockSpec(memory_space=pltpu.SMEM)] + [vmem] * (1 + len(blocks)),
+        in_specs=[pl.BlockSpec(memory_space=pltpu.SMEM)] + [vmem] * (2 + len(near)),
         out_specs=vmem,
         compiler_params=pltpu.CompilerParams(vmem_limit_bytes=VMEM_SOME),
+        cost_estimate=SMALL,
         name="finish",
-    )(side, mixed, *blocks)
+    )(side, mixed, far, *near)
 
 
 def dense(payload, mixed, codes):
@@ -445,16 +427,19 @@
     partial_own = own_down(side, hidden_own, w_down, count)
     keep, send = peer_down(side, partial_other, other_peer, w_down, share_other, 2)
     keep, send = add_and_cut([keep], [swap(send, line)], 2)
-    (onward,) = add_and_cut([keep], [swap(send, core)], 1)
-    far = swap(onward, plane)
+    parts = add_and_cut([keep], [swap(send, core)], layers)
+    arrived = [swap(parts[z], z * layer) for z in range(1, layers)]
     keep_near, send_near, keep_far, send_far = peer_down(
         side, partial_own, own_peer, w_down, share_own, 4
     )
     (onward,) = add_and_cut([keep_far], [swap(send_far, core)], 1)
-    near = [in_vmem(keep_near), swap(send_near, core), swap(onward, line)]
-    blocks = join(near, far, layers)
-    blocks = [blocks[0]] + [swap(blocks[z], z * layer) for z in range(1, layers)]
-    return finish(side, mixed, blocks)
+    near = add_and_cut(
+        [keep_near], [swap(send_near, core), swap(onward, line)], layers, LANES
+    )
+    arrived, _ = lax.optimization_barrier((arrived, near[0]))
+    (far,) = add_and_cut([parts[0]], arrived, 1)
+    near = [near[0]] + [swap(near[z], z * layer) for z in range(1, layers)]
+    return finish(side, mixed, swap(far, plane), near)
 
 
 def slot_table(routes, experts, capacity):

time: 65.1 us -> 65.7 us (level)
  starting transfers between devices: 21 us -> 26.5 us
  waiting for transfers between devices: 19.3 us -> 14.3 us
    ppermute x21 -> x24, starting transfers between devices: 21 us -> 26.5 us  [swap(): lax.ppermute(block, ('dp', 'expert'), [(i, i ^ offset) for i in range(dev...]
    ppermute x21 -> x24, waiting for transfers between devices: 19.3 us -> 14.3 us  [swap(): lax.ppermute(block, ('dp', 'expert'), [(i, i ^ offset) for i in range(dev...]
  transfers between devices with their start and end apart: 21 -> 24, of which waited for: 11 -> 9; matrix products, arithmetic and copies ran while one was open for 0% -> 0% of each run, Pallas kernels for 32% -> 32%
where the time goes in v5:
time: 65.7 us; the launch traced here: 65.4 us
  starting transfers between devices  26.5 us (40%)
  Pallas kernels  24.4 us (37%)
  waiting for transfers between devices  14.3 us (22%)
    ppermute x24, starting transfers between devices, swap(): lax.ppermute(block, ('dp', 'expert'), [(i, i ^ offset) for i in range(dev...  26.5 us
    ppermute x24, waiting for transfers between devices, swap(): lax.ppermute(block, ('dp', 'expert'), [(i, i ^ offset) for i in range(dev...  14.3 us
    pallas_call x3, Pallas kernels, unpack_weights(): pl.pallas_call(functools.partial(unpack_kernel, tuple((job[2] for job in...  12.6 us
    pallas_call x2, Pallas kernels, hidden_units(): pl.pallas_call(hidden_kernel, out_shape=(pltpu.VMEM((count + spare, width...  5.27 us
    pallas_call x1, Pallas kernels, front(): pl.pallas_call(front_kernel, out_shape=(jax.ShapeDtypeStruct((rows, width...  2.6 us
    pallas_call x2, Pallas kernels, peer_down(): pl.pallas_call(peer_down_kernel, out_shape=(pltpu.VMEM((count // parts, w...  1.62 us
    pallas_call x2, Pallas kernels, own_down(): pl.pallas_call(own_down_kernel, out_shape=pltpu.VMEM((count, width), F32)...  1.46 us
  transfers between devices with their start and end apart: 24, of which 9 were waited for; matrix products, arithmetic and copies ran while one was open for 0% of the time, Pallas kernels for 32%

profile of v5, /device:TPU:0, one launch (start us, length us, event | category | flops | bytes accessed | tf_op | source)
XLA Modules:
  0.0 65.4 jit_solution(5907803816380539113)
XLA Ops:
  0.0 2.6 %front.1 = (bf16[8,4096]{1,0:T(8,128)(2,1)}, bf16[8,4224]{1,0:T(8,128)(2,1)}) custom-call(s32[8]{0:T(128)} %lengths_ref.1, bf16[8,4096]{1,0:T(8,128)(2,1)} %queries_ref.1, bf16[8,2,1024]{2,1,0:T(2,128)(2,1)} %new_kv_ref.1, bf16[8,32,1024]{2,1,0:T(8,128)(2,1)} %keys_ref.1, bf16[8,32,1024]{2,1,0:T(8,128)(2,1)} %values_ref.1, bf16[8,4096]{1,0:T(8,128)(2,1)} %residual_ref.1, ...), custom_call_target="tpu_custom_call" | custom-call | flops 1 | bytes 1 | tf_op jit(solution)/shard_map/front/pallas_call | solution.py:111
  2.6 3.0 %collective-permute-start = (bf16[8,4224]{1,0:T(8,128)(2,1)}, bf16[8,4224]{1,0:T(8,128)(2,1)S(1)}, u32[]{:S(2)}, u32[]{:S(2)}) collective-permute-start(bf16[8,4224]{1,0:T(8,128)(2,1)} %get-tuple-element.56), channel_id=1, source_target_pairs={{0,4},{1,5},{2,6},{3,7},{4,0},{5,1},{6,2},{7,3},{8,12},{9,13},{10,... | collective-permute-start | bytes 202760 | tf_op jit(solution)/shard_map/ppermute | solution.py:392
  5.6 2.6 %collective-permute-start.1 = (bf16[8,4224]{1,0:T(8,128)(2,1)}, bf16[8,4224]{1,0:T(8,128)(2,1)S(1)}, u32[]{:S(2)}, u32[]{:S(2)}) collective-permute-start(bf16[8,4224]{1,0:T(8,128)(2,1)} %get-tuple-element.56), channel_id=1, source_target_pairs={{0,8},{1,9},{2,10},{3,11},{4,12},{5,13},{6,14},{7,15},{8,0},{9,1},... | collective-permute-start | bytes 202760 | tf_op jit(solution)/shard_map/ppermute | solution.py:392
  8.2 0.0 collective-permute-start.2
  8.2 5.5 %unpack_weights.3 = (bf16[4096,1024]{1,0:T(8,128)(2,1)S(1)}, bf16[2048,1024]{1,0:T(8,128)(2,1)S(1)}) custom-call(f32[1024,1024]{1,0:T(8,128)} %bitcast.11, f32[512,2048]{1,0:T(8,128)} %bitcast.8, bf16[32,1024]{1,0:T(8,128)(2,1)} %bitcast.14, bf16[16,2048]{1,0:T(8,128)(2,1)} %bitcast.12), custom_call_target="tpu_custom_call" | custom-call | flops 1 | bytes 1 | tf_op jit(solution)/shard_map/unpack_weights/pallas_call | solution.py:204
  13.8 0.0 collective-permute-done
  13.8 0.8 %collective-permute-done.2 = bf16[8,4224]{1,0:T(8,128)(2,1)S(1)} collective-permute-done((bf16[8,4224]{1,0:T(8,128)(2,1)}, bf16[8,4224]{1,0:T(8,128)(2,1)S(1)}, u32[]{:S(2)}, u32[]{:S(2)}) %collective-permute-start.2) | collective-permute-done | bytes 67616 | tf_op jit(solution)/shard_map/ppermute | solution.py:392
  14.7 1.6 %collective-permute-start.3 = (bf16[32,4224]{1,0:T(8,128)(2,1)S(1)}, bf16[32,4224]{1,0:T(8,128)(2,1)S(1)}, u32[]{:S(2)}, u32[]{:S(2)}) collective-permute-start(bf16[32,4224]{1,0:T(8,128)(2,1)S(1)} %pad_maximum_fusion.refs_0_), channel_id=1, source_target_pairs={{0,2},{1,3},{2,0},{3,1},{4,6},{5,7},{6,4},{7,5},{8,10},{9,11},{10,... | collective-permute-start | bytes 811016 | tf_op jit(solution)/shard_map/ppermute | solution.py:392
  16.2 0.0 collective-permute-start.4
  16.2 1.5 %collective-permute-start.6 = (bf16[32,4224]{1,0:T(8,128)(2,1)S(1)}, bf16[32,4224]{1,0:T(8,128)(2,1)S(1)}, u32[]{:S(2)}, u32[]{:S(2)}) collective-permute-start(bf16[32,4224]{1,0:T(8,128)(2,1)S(1)} %pad_maximum_fusion.refs_0_), channel_id=1, source_target_pairs={{0,16},{1,17},{2,18},{3,19},{4,20},{5,21},{6,22},{7,23},{8,24},{9,... | collective-permute-start | bytes 811016 | tf_op jit(solution)/shard_map/ppermute | solution.py:392
  17.7 4.2 %unpack_weights.4.refs_5_ = bf16[4096,1024]{1,0:T(8,128)(2,1)S(1)} custom-call(f32[1024,1024]{1,0:T(8,128)} %bitcast.10, bf16[32,1024]{1,0:T(8,128)(2,1)} %bitcast.15), custom_call_target="tpu_custom_call" | custom-call | flops 1 | bytes 1 | tf_op jit(solution)/shard_map/unpack_weights/pallas_call | solution.py:204
  21.9 0.0 collective-permute-done.3.refs_2_
  22.0 0.0 collective-permute-done.4.refs_1_
  22.0 0.3 collective-permute-start.5
  22.3 0.8 %collective-permute-start.8 = (bf16[32,4224]{1,0:T(8,128)(2,1)S(1)}, bf16[32,4224]{1,0:T(8,128)(2,1)S(1)}, u32[]{:S(2)}, u32[]{:S(2)}) collective-permute-start(bf16[32,4224]{1,0:T(8,128)(2,1)S(1)} %collective-permute-done.3.refs_2_), channel_id=1, source_target_pairs={{0,16},{1,17},{2,18},{3,19},{4,20},{5,21},{6,22},{7,23},{8,24},{9,... | collective-permute-start | bytes 811016 | tf_op jit(solution)/shard_map/ppermute | solution.py:392
  23.1 2.1 %collective-permute-done.6.refs_0_ = bf16[32,4224]{1,0:T(8,128)(2,1)S(1)} collective-permute-done((bf16[32,4224]{1,0:T(8,128)(2,1)S(1)}, bf16[32,4224]{1,0:T(8,128)(2,1)S(1)}, u32[]{:S(2)}, u32[]{:S(2)}) %collective-permute-start.6) | collective-permute-done | bytes 270368 | tf_op jit(solution)/shard_map/ppermute | solution.py:392
  25.1 2.6 %gate_up.2 = (bf16[128,1024]{1,0:T(8,128)(2,1)S(1)}, f32[128,128]{1,0:T(8,128)S(1)}) custom-call(s32[1]{0:T(128)} %bitcast.1.place_ref, bf16[32,4224]{1,0:T(8,128)(2,1)S(1)} %pad_maximum_fusion.refs_0_, bf16[32,4224]{1,0:T(8,128)(2,1)S(1)} %collective-permute-done.4.refs_1_, bf16[32,4224]{1,0:T(8,128)(2,1)S(1)} %collective-permute-done.3.refs_2_, ...), custom_call_target="tpu_custom_call" | custom-call | flops 1 | bytes 1 | tf_op jit(solution)/shard_map/gate_up/pallas_call | solution.py:249
  27.8 2.9 %unpack_weights.5.weight_refs_1_ = bf16[2048,1024]{1,0:T(8,128)(2,1)S(1)} custom-call(f32[512,2048]{1,0:T(8,128)} %bitcast.9, bf16[16,2048]{1,0:T(8,128)(2,1)} %bitcast.13), custom_call_target="tpu_custom_call" | custom-call | flops 1 | bytes 1 | tf_op jit(solution)/shard_map/unpack_weights/pallas_call | solution.py:204
  30.7 0.3 collective-permute-done.8.refs_2_
  30.9 0.3 collective-permute-start.9
  31.3 1.9 %collective-permute-start.10 = (bf16[128,1024]{1,0:T(8,128)(2,1)S(1)}, bf16[128,1024]{1,0:T(8,128)(2,1)S(1)}, u32[]{:S(2)}, u32[]{:S(2)}) collective-permute-start(bf16[128,1024]{1,0:T(8,128)(2,1)S(1)} %get-tuple-element.86.hidden_ref), channel_id=1, source_target_pairs={{0,16},{1,17},{2,18},{3,19},{4,20},{5,21},{6,22},{7,23},{8,24},{9,... | collective-permute-start | bytes 786440 | tf_op jit(solution)/shard_map/ppermute | solution.py:392
  33.1 2.6 %gate_up.3 = (bf16[128,1024]{1,0:T(8,128)(2,1)S(1)}, f32[128,128]{1,0:T(8,128)S(1)}) custom-call(s32[1]{0:T(128)} %bitcast.1.place_ref, bf16[32,4224]{1,0:T(8,128)(2,1)S(1)} %collective-permute-done.6.refs_0_, bf16[32,4224]{1,0:T(8,128)(2,1)S(1)} %collective-permute-done.7.refs_1_, bf16[32,4224]{1,0:T(8,128)(2,1)S(1)} %collective-permute-done.8.refs_2_, ...), custom_call_target="tpu_custom_call" | custom-call | flops 1 | bytes 1 | tf_op jit(solution)/shard_map/gate_up/pallas_call | solution.py:249
  35.8 1.3 %collective-permute-start.16 = (bf16[128,1024]{1,0:T(8,128)(2,1)S(1)}, bf16[128,1024]{1,0:T(8,128)(2,1)S(1)}, u32[]{:S(2)}, u32[]{:S(2)}) collective-permute-start(bf16[128,1024]{1,0:T(8,128)(2,1)S(1)} %get-tuple-element.74.hidden_ref), channel_id=1, source_target_pairs={{0,16},{1,17},{2,18},{3,19},{4,20},{5,21},{6,22},{7,23},{8,24},{9,... | collective-permute-start | bytes 786440 | tf_op jit(solution)/shard_map/ppermute | solution.py:392
  37.0 0.7 %down_own.2.partial_ref = f32[128,2048]{1,0:T(8,128)S(1)} custom-call(s32[1]{0:T(128)} %bitcast.side_ref, bf16[128,1024]{1,0:T(8,128)(2,1)S(1)} %get-tuple-element.74.hidden_ref, bf16[2048,1024]{1,0:T(8,128)(2,1)S(1)} %get-tuple-element.75.weight_refs_0_, bf16[2048,1024]{1,0:T(8,128)(2,1)S(1)} %unpack_weights.5.weight_refs_1_), custom_call_target="tpu_custom_call" | custom-call | flops 1 | bytes 1 | tf_op jit(solution)/shard_map/down_own/pallas_call | solution.py:278
  37.8 2.6 %collective-permute-done.10.hidden_ref = bf16[128,1024]{1,0:T(8,128)(2,1)S(1)} collective-permute-done((bf16[128,1024]{1,0:T(8,128)(2,1)S(1)}, bf16[128,1024]{1,0:T(8,128)(2,1)S(1)}, u32[]{:S(2)}, u32[]{:S(2)}) %collective-permute-start.10) | collective-permute-done | bytes 262176 | tf_op jit(solution)/shard_map/ppermute | solution.py:392
  40.4 0.8 %down_peer.2 = (bf16[64,2048]{1,0:T(8,128)(2,1)S(1)}, bf16[64,2048]{1,0:T(8,128)(2,1)S(1)}) custom-call(s32[1]{0:T(128)} %bitcast.side_ref, f32[128,2048]{1,0:T(8,128)S(1)} %down_own.2.partial_ref, bf16[128,1024]{1,0:T(8,128)(2,1)S(1)} %collective-permute-done.10.hidden_ref, bf16[2048,1024]{1,0:T(8,128)(2,1)S(1)} %get-tuple-element.75.weight_refs_0_, ...), custom_call_target="tpu_custom_call" | custom-call | flops 1 | bytes 1 | tf_op jit(solution)/shard_map/down_peer/pallas_call | solution.py:317
  41.2 0.8 %collective-permute-start.11 = (bf16[64,2048]{1,0:T(8,128)(2,1)S(1)}, bf16[64,2048]{1,0:T(8,128)(2,1)S(1)}, u32[]{:S(2)}, u32[]{:S(2)}) collective-permute-start(bf16[64,2048]{1,0:T(8,128)(2,1)S(1)} %get-tuple-element.79), channel_id=1, source_target_pairs={{0,2},{1,3},{2,0},{3,1},{4,6},{5,7},{6,4},{7,5},{8,10},{9,11},{10,... | collective-permute-start | bytes 786440 | tf_op jit(solution)/shard_map/ppermute | solution.py:392
  42.0 0.7 %down_own.3.partial_ref = f32[128,2048]{1,0:T(8,128)S(1)} custom-call(s32[1]{0:T(128)} %bitcast.side_ref, bf16[128,1024]{1,0:T(8,128)(2,1)S(1)} %get-tuple-element.86.hidden_ref, bf16[2048,1024]{1,0:T(8,128)(2,1)S(1)} %get-tuple-element.75.weight_refs_0_, bf16[2048,1024]{1,0:T(8,128)(2,1)S(1)} %unpack_weights.5.weight_refs_1_), custom_call_target="tpu_custom_call" | custom-call | flops 1 | bytes 1 | tf_op jit(solution)/shard_map/down_own/pallas_call | solution.py:278
  42.7 2.6 %collective-permute-done.16.hidden_ref = bf16[128,1024]{1,0:T(8,128)(2,1)S(1)} collective-permute-done((bf16[128,1024]{1,0:T(8,128)(2,1)S(1)}, bf16[128,1024]{1,0:T(8,128)(2,1)S(1)}, u32[]{:S(2)}, u32[]{:S(2)}) %collective-permute-start.16) | collective-permute-done | bytes 262176 | tf_op jit(solution)/shard_map/ppermute | solution.py:392
  45.3 0.8 %down_peer.3 = (bf16[32,2048]{1,0:T(8,128)(2,1)S(1)}, bf16[32,2048]{1,0:T(8,128)(2,1)S(1)}, bf16[32,2048]{1,0:T(8,128)(2,1)S(1)}, bf16[32,2048]{1,0:T(8,128)(2,1)S(1)}) custom-call(s32[1]{0:T(128)} %bitcast.side_ref, f32[128,2048]{1,0:T(8,128)S(1)} %down_own.3.partial_ref, bf16[128,1024]{1,0:T(8,128)(2,1)S(1)} %collective-permute-done.16.hidden_ref, ...), custom_call_target="tpu_custom_call" | custom-call | flops 1 | bytes 1 | tf_op jit(solution)/shard_map/down_peer/pallas_call | solution.py:317
  46.1 0.1 collective-permute-start.18
  46.2 2.0 %collective-permute-done.11.refs_1_ = bf16[64,2048]{1,0:T(8,128)(2,1)S(1)} collective-permute-done((bf16[64,2048]{1,0:T(8,128)(2,1)S(1)}, bf16[64,2048]{1,0:T(8,128)(2,1)S(1)}, u32[]{:S(2)}, u32[]{:S(2)}) %collective-permute-start.11) | collective-permute-done | bytes 262176 | tf_op jit(solution)/shard_map/ppermute | solution.py:392
  48.2 0.1 add_and_cut.5
  48.2 0.1 collective-permute-start.12
  48.3 0.5 collective-permute-start.17
  48.9 1.4 %collective-permute-start.19 = (bf16[32,2048]{1,0:T(8,128)(2,1)S(1)}, bf16[32,2048]{1,0:T(8,128)(2,1)S(1)}, u32[]{:S(2)}, u32[]{:S(2)}) collective-permute-start(bf16[32,2048]{1,0:T(8,128)(2,1)S(1)} %add_and_cut.7), channel_id=1, source_target_pairs={{0,2},{1,3},{2,0},{3,1},{4,6},{5,7},{6,4},{7,5},{8,10},{9,11},{10,... | collective-permute-start | bytes 393224 | tf_op jit(solution)/shard_map/ppermute | solution.py:392
  50.3 0.7 %collective-permute-start.13 = (bf16[8,2048]{1,0:T(8,128)(2,1)S(1)}, bf16[8,2048]{1,0:T(8,128)(2,1)S(1)}, u32[]{:S(2)}, u32[]{:S(2)}) collective-permute-start(bf16[8,2048]{1,0:T(8,128)(2,1)S(1)} %get-tuple-element.83), channel_id=1, source_target_pairs={{0,4},{1,5},{2,6},{3,7},{4,0},{5,1},{6,2},{7,3},{8,12},{9,13},{10,... | collective-permute-start | bytes 98312 | tf_op jit(solution)/shard_map/ppermute | solution.py:392
  51.0 3.5 %collective-permute-start.14 = (bf16[8,2048]{1,0:T(8,128)(2,1)S(1)}, bf16[8,2048]{1,0:T(8,128)(2,1)S(1)}, u32[]{:S(2)}, u32[]{:S(2)}) collective-permute-start(bf16[8,2048]{1,0:T(8,128)(2,1)S(1)} %get-tuple-element.84), channel_id=1, source_target_pairs={{0,8},{1,9},{2,10},{3,11},{4,12},{5,13},{6,14},{7,15},{8,0},{9,1},... | collective-permute-start | bytes 98312 | tf_op jit(solution)/shard_map/ppermute | solution.py:392
  54.5 0.3 collective-permute-start.15
  54.8 0.1 add_and_cut.8
  54.8 0.3 collective-permute-start.21
  55.2 3.8 %collective-permute-start.22 = (bf16[8,2176]{1,0:T(8,128)(2,1)S(1)}, bf16[8,2176]{1,0:T(8,128)(2,1)S(1)}, u32[]{:S(2)}, u32[]{:S(2)}) collective-permute-start(bf16[8,2176]{1,0:T(8,128)(2,1)S(1)} %get-tuple-element.97), channel_id=1, source_target_pairs={{0,8},{1,9},{2,10},{3,11},{4,12},{5,13},{6,14},{7,15},{8,0},{9,1},... | collective-permute-start | bytes 104456 | tf_op jit(solution)/shard_map/ppermute | solution.py:392
  59.0 0.3 collective-permute-start.23
  59.3 1.0 %collective-permute-done.15.refs_3_ = bf16[8,2048]{1,0:T(8,128)(2,1)S(1)} collective-permute-done((bf16[8,2048]{1,0:T(8,128)(2,1)S(1)}, bf16[8,2048]{1,0:T(8,128)(2,1)S(1)}, u32[]{:S(2)}, u32[]{:S(2)}) %collective-permute-start.15) | collective-permute-done | bytes 32800 | tf_op jit(solution)/shard_map/ppermute | solution.py:392
  60.3 1.6 %collective-permute-start.20 = (bf16[8,2048]{1,0:T(8,128)(2,1)S(1)}, bf16[8,2048]{1,0:T(8,128)(2,1)S(1)}, u32[]{:S(2)}, u32[]{:S(2)}) collective-permute-start(bf16[8,2048]{1,0:T(8,128)(2,1)S(1)} %add_and_cut.9), channel_id=1, source_target_pairs={{0,16},{1,17},{2,18},{3,19},{4,20},{5,21},{6,22},{7,23},{8,24},{9,... | collective-permute-start | bytes 98312 | tf_op jit(solution)/shard_map/ppermute | solution.py:392
  61.9 2.4 %collective-permute-done.20.far_ref = bf16[8,2048]{1,0:T(8,128)(2,1)S(1)} collective-permute-done((bf16[8,2048]{1,0:T(8,128)(2,1)S(1)}, bf16[8,2048]{1,0:T(8,128)(2,1)S(1)}, u32[]{:S(2)}, u32[]{:S(2)}) %collective-permute-start.20) | collective-permute-done | bytes 32800 | tf_op jit(solution)/shard_map/ppermute | solution.py:392
  64.3 0.4 collective-permute-done.23.refs_3_
  64.8 0.7 %finish.1 = bf16[8,4096]{1,0:T(8,128)(2,1)} custom-call(s32[1]{0:T(128)} %bitcast.side_ref, bf16[8,4096]{1,0:T(8,128)(2,1)S(1)} %copy-done, bf16[8,2048]{1,0:T(8,128)(2,1)S(1)} %collective-permute-done.20.far_ref, bf16[8,2176]{1,0:T(8,128)(2,1)S(1)} %get-tuple-element.92.refs_0_, bf16[8,2176]{1,0:T(8,128)(2,1)S(1)} %collective-permute-done.21.refs_1_, ...), custom_call_target="tpu_custom_call" | custom-call | flops 1 | bytes 1 | tf_op jit(solution)/shard_map/finish/pallas_call | solution.py:370
  (21 shorter events, 0.2 us)
Async XLA Ops:
  2.6 11.2 %collective-permute-start = (bf16[8,4224]{1,0:T(8,128)(2,1)}, bf16[8,4224]{1,0:T(8,128)(2,1)S(1)}, u32[]{:S(2)}, u32[]{:S(2)}) collective-permute-start(bf16[8,4224]{1,0:T(8,128)(2,1)} %get-tuple-element.56), channel_id=1, source_target_pairs={{0,4},{1,5},{2,6},{3,7},{4,0},{5,1},{6,2},{7,3},{8,12},{9,13},{10,... | collective-permute-start | bytes 202760 | tf_op jit(solution)/shard_map/ppermute | solution.py:392
  5.6 8.1 %collective-permute-start.1 = (bf16[8,4224]{1,0:T(8,128)(2,1)}, bf16[8,4224]{1,0:T(8,128)(2,1)S(1)}, u32[]{:S(2)}, u32[]{:S(2)}) collective-permute-start(bf16[8,4224]{1,0:T(8,128)(2,1)} %get-tuple-element.56), channel_id=1, source_target_pairs={{0,8},{1,9},{2,10},{3,11},{4,12},{5,13},{6,14},{7,15},{8,0},{9,1},... | collective-permute-start | bytes 202760 | tf_op jit(solution)/shard_map/ppermute | solution.py:392
  8.2 6.4 %collective-permute-start.2 = (bf16[8,4224]{1,0:T(8,128)(2,1)}, bf16[8,4224]{1,0:T(8,128)(2,1)S(1)}, u32[]{:S(2)}, u32[]{:S(2)}) collective-permute-start(bf16[8,4224]{1,0:T(8,128)(2,1)} %get-tuple-element.56), channel_id=1, source_target_pairs={{0,12},{1,13},{2,14},{3,15},{4,8},{5,9},{6,10},{7,11},{8,4},{9,5},... | collective-permute-start | bytes 202760 | tf_op jit(solution)/shard_map/ppermute | solution.py:392
  8.2 6.4 %copy-start.1 = (bf16[8,4224]{1,0:T(8,128)(2,1)S(1)}, bf16[8,4224]{1,0:T(8,128)(2,1)}, u32[]{:S(2)}) copy-start(bf16[8,4224]{1,0:T(8,128)(2,1)} %get-tuple-element.56) | copy-start | bytes 202756
  14.7 7.3 %collective-permute-start.3 = (bf16[32,4224]{1,0:T(8,128)(2,1)S(1)}, bf16[32,4224]{1,0:T(8,128)(2,1)S(1)}, u32[]{:S(2)}, u32[]{:S(2)}) collective-permute-start(bf16[32,4224]{1,0:T(8,128)(2,1)S(1)} %pad_maximum_fusion.refs_0_), channel_id=1, source_target_pairs={{0,2},{1,3},{2,0},{3,1},{4,6},{5,7},{6,4},{7,5},{8,10},{9,11},{10,... | collective-permute-start | bytes 811016 | tf_op jit(solution)/shard_map/ppermute | solution.py:392
  16.2 5.7 %collective-permute-start.4 = (bf16[32,4224]{1,0:T(8,128)(2,1)S(1)}, bf16[32,4224]{1,0:T(8,128)(2,1)S(1)}, u32[]{:S(2)}, u32[]{:S(2)}) collective-permute-start(bf16[32,4224]{1,0:T(8,128)(2,1)S(1)} %pad_maximum_fusion.refs_0_), channel_id=1, source_target_pairs={{0,1},{1,0},{2,3},{3,2},{4,5},{5,4},{6,7},{7,6},{8,9},{9,8},{10,11... | collective-permute-start | bytes 811016 | tf_op jit(solution)/shard_map/ppermute | solution.py:392
  16.2 8.9 %collective-permute-start.6 = (bf16[32,4224]{1,0:T(8,128)(2,1)S(1)}, bf16[32,4224]{1,0:T(8,128)(2,1)S(1)}, u32[]{:S(2)}, u32[]{:S(2)}) collective-permute-start(bf16[32,4224]{1,0:T(8,128)(2,1)S(1)} %pad_maximum_fusion.refs_0_), channel_id=1, source_target_pairs={{0,16},{1,17},{2,18},{3,19},{4,20},{5,21},{6,22},{7,23},{8,24},{9,... | collective-permute-start | bytes 811016 | tf_op jit(solution)/shard_map/ppermute | solution.py:392
  22.0 3.2 %collective-permute-start.5 = (bf16[32,4224]{1,0:T(8,128)(2,1)S(1)}, bf16[32,4224]{1,0:T(8,128)(2,1)S(1)}, u32[]{:S(2)}, u32[]{:S(2)}) collective-permute-start(bf16[32,4224]{1,0:T(8,128)(2,1)S(1)} %collective-permute-done.3.refs_2_), channel_id=1, source_target_pairs={{0,1},{1,0},{2,3},{3,2},{4,5},{5,4},{6,7},{7,6},{8,9},{9,8},{10,11... | collective-permute-start | bytes 811016 | tf_op jit(solution)/shard_map/ppermute | solution.py:392
  22.3 8.7 %collective-permute-start.8 = (bf16[32,4224]{1,0:T(8,128)(2,1)S(1)}, bf16[32,4224]{1,0:T(8,128)(2,1)S(1)}, u32[]{:S(2)}, u32[]{:S(2)}) collective-permute-start(bf16[32,4224]{1,0:T(8,128)(2,1)S(1)} %collective-permute-done.3.refs_2_), channel_id=1, source_target_pairs={{0,16},{1,17},{2,18},{3,19},{4,20},{5,21},{6,22},{7,23},{8,24},{9,... | collective-permute-start | bytes 811016 | tf_op jit(solution)/shard_map/ppermute | solution.py:392
  25.1 8.0 %collective-permute-start.7 = (bf16[32,4224]{1,0:T(8,128)(2,1)S(1)}, bf16[32,4224]{1,0:T(8,128)(2,1)S(1)}, u32[]{:S(2)}, u32[]{:S(2)}) collective-permute-start(bf16[32,4224]{1,0:T(8,128)(2,1)S(1)} %collective-permute-done.6.refs_0_), channel_id=1, source_target_pairs={{0,1},{1,0},{2,3},{3,2},{4,5},{5,4},{6,7},{7,6},{8,9},{9,8},{10,11... | collective-permute-start | bytes 811016 | tf_op jit(solution)/shard_map/ppermute | solution.py:392
  30.9 2.2 %collective-permute-start.9 = (bf16[32,4224]{1,0:T(8,128)(2,1)S(1)}, bf16[32,4224]{1,0:T(8,128)(2,1)S(1)}, u32[]{:S(2)}, u32[]{:S(2)}) collective-permute-start(bf16[32,4224]{1,0:T(8,128)(2,1)S(1)} %collective-permute-done.8.refs_2_), channel_id=1, source_target_pairs={{0,1},{1,0},{2,3},{3,2},{4,5},{5,4},{6,7},{7,6},{8,9},{9,8},{10,11... | collective-permute-start | bytes 811016 | tf_op jit(solution)/shard_map/ppermute | solution.py:392
  31.3 9.1 %collective-permute-start.10 = (bf16[128,1024]{1,0:T(8,128)(2,1)S(1)}, bf16[128,1024]{1,0:T(8,128)(2,1)S(1)}, u32[]{:S(2)}, u32[]{:S(2)}) collective-permute-start(bf16[128,1024]{1,0:T(8,128)(2,1)S(1)} %get-tuple-element.86.hidden_ref), channel_id=1, source_target_pairs={{0,16},{1,17},{2,18},{3,19},{4,20},{5,21},{6,22},{7,23},{8,24},{9,... | collective-permute-start | bytes 786440 | tf_op jit(solution)/shard_map/ppermute | solution.py:392
  35.8 9.5 %collective-permute-start.16 = (bf16[128,1024]{1,0:T(8,128)(2,1)S(1)}, bf16[128,1024]{1,0:T(8,128)(2,1)S(1)}, u32[]{:S(2)}, u32[]{:S(2)}) collective-permute-start(bf16[128,1024]{1,0:T(8,128)(2,1)S(1)} %get-tuple-element.74.hidden_ref), channel_id=1, source_target_pairs={{0,16},{1,17},{2,18},{3,19},{4,20},{5,21},{6,22},{7,23},{8,24},{9,... | collective-permute-start | bytes 786440 | tf_op jit(solution)/shard_map/ppermute | solution.py:392
  41.2 7.0 %collective-permute-start.11 = (bf16[64,2048]{1,0:T(8,128)(2,1)S(1)}, bf16[64,2048]{1,0:T(8,128)(2,1)S(1)}, u32[]{:S(2)}, u32[]{:S(2)}) collective-permute-start(bf16[64,2048]{1,0:T(8,128)(2,1)S(1)} %get-tuple-element.79), channel_id=1, source_target_pairs={{0,2},{1,3},{2,0},{3,1},{4,6},{5,7},{6,4},{7,5},{8,10},{9,11},{10,... | collective-permute-start | bytes 786440 | tf_op jit(solution)/shard_map/ppermute | solution.py:392
  45.3 19.5 %copy-start = (bf16[8,4096]{1,0:T(8,128)(2,1)S(1)}, bf16[8,4096]{1,0:T(8,128)(2,1)}, u32[]{:S(2)}) copy-start(bf16[8,4096]{1,0:T(8,128)(2,1)} %get-tuple-element.54.mixed_ref) | copy-start | bytes 196612
  46.1 2.7 %collective-permute-start.18 = (bf16[32,2048]{1,0:T(8,128)(2,1)S(1)}, bf16[32,2048]{1,0:T(8,128)(2,1)S(1)}, u32[]{:S(2)}, u32[]{:S(2)}) collective-permute-start(bf16[32,2048]{1,0:T(8,128)(2,1)S(1)} %get-tuple-element.91), channel_id=1, source_target_pairs={{0,1},{1,0},{2,3},{3,2},{4,5},{5,4},{6,7},{7,6},{8,9},{9,8},{10,11... | collective-permute-start | bytes 393224 | tf_op jit(solution)/shard_map/ppermute | solution.py:392
  48.2 2.1 %collective-permute-start.12 = (bf16[32,2048]{1,0:T(8,128)(2,1)S(1)}, bf16[32,2048]{1,0:T(8,128)(2,1)S(1)}, u32[]{:S(2)}, u32[]{:S(2)}) collective-permute-start(bf16[32,2048]{1,0:T(8,128)(2,1)S(1)} %get-tuple-element.81), channel_id=1, source_target_pairs={{0,1},{1,0},{2,3},{3,2},{4,5},{5,4},{6,7},{7,6},{8,9},{9,8},{10,11... | collective-permute-start | bytes 393224 | tf_op jit(solution)/shard_map/ppermute | solution.py:392
  48.3 6.5 %collective-permute-start.17 = (bf16[32,2048]{1,0:T(8,128)(2,1)S(1)}, bf16[32,2048]{1,0:T(8,128)(2,1)S(1)}, u32[]{:S(2)}, u32[]{:S(2)}) collective-permute-start(bf16[32,2048]{1,0:T(8,128)(2,1)S(1)} %get-tuple-element.89), channel_id=1, source_target_pairs={{0,1},{1,0},{2,3},{3,2},{4,5},{5,4},{6,7},{7,6},{8,9},{9,8},{10,11... | collective-permute-start | bytes 393224 | tf_op jit(solution)/shard_map/ppermute | solution.py:392
  48.9 5.9 %collective-permute-start.19 = (bf16[32,2048]{1,0:T(8,128)(2,1)S(1)}, bf16[32,2048]{1,0:T(8,128)(2,1)S(1)}, u32[]{:S(2)}, u32[]{:S(2)}) collective-permute-start(bf16[32,2048]{1,0:T(8,128)(2,1)S(1)} %add_and_cut.7), channel_id=1, source_target_pairs={{0,2},{1,3},{2,0},{3,1},{4,6},{5,7},{6,4},{7,5},{8,10},{9,11},{10,... | collective-permute-start | bytes 393224 | tf_op jit(solution)/shard_map/ppermute | solution.py:392
  50.3 8.7 %collective-permute-start.13 = (bf16[8,2048]{1,0:T(8,128)(2,1)S(1)}, bf16[8,2048]{1,0:T(8,128)(2,1)S(1)}, u32[]{:S(2)}, u32[]{:S(2)}) collective-permute-start(bf16[8,2048]{1,0:T(8,128)(2,1)S(1)} %get-tuple-element.83), channel_id=1, source_target_pairs={{0,4},{1,5},{2,6},{3,7},{4,0},{5,1},{6,2},{7,3},{8,12},{9,13},{10,... | collective-permute-start | bytes 98312 | tf_op jit(solution)/shard_map/ppermute | solution.py:392
  51.0 8.3 %collective-permute-start.14 = (bf16[8,2048]{1,0:T(8,128)(2,1)S(1)}, bf16[8,2048]{1,0:T(8,128)(2,1)S(1)}, u32[]{:S(2)}, u32[]{:S(2)}) collective-permute-start(bf16[8,2048]{1,0:T(8,128)(2,1)S(1)} %get-tuple-element.84), channel_id=1, source_target_pairs={{0,8},{1,9},{2,10},{3,11},{4,12},{5,13},{6,14},{7,15},{8,0},{9,1},... | collective-permute-start | bytes 98312 | tf_op jit(solution)/shard_map/ppermute | solution.py:392
  54.5 5.8 %collective-permute-start.15 = (bf16[8,2048]{1,0:T(8,128)(2,1)S(1)}, bf16[8,2048]{1,0:T(8,128)(2,1)S(1)}, u32[]{:S(2)}, u32[]{:S(2)}) collective-permute-start(bf16[8,2048]{1,0:T(8,128)(2,1)S(1)} %get-tuple-element.85), channel_id=1, source_target_pairs={{0,12},{1,13},{2,14},{3,15},{4,8},{5,9},{6,10},{7,11},{8,4},{9,5},... | collective-permute-start | bytes 98312 | tf_op jit(solution)/shard_map/ppermute | solution.py:392
  54.8 9.5 %collective-permute-start.21 = (bf16[8,2176]{1,0:T(8,128)(2,1)S(1)}, bf16[8,2176]{1,0:T(8,128)(2,1)S(1)}, u32[]{:S(2)}, u32[]{:S(2)}) collective-permute-start(bf16[8,2176]{1,0:T(8,128)(2,1)S(1)} %get-tuple-element.96), channel_id=1, source_target_pairs={{0,4},{1,5},{2,6},{3,7},{4,0},{5,1},{6,2},{7,3},{8,12},{9,13},{10,... | collective-permute-start | bytes 104456 | tf_op jit(solution)/shard_map/ppermute | solution.py:392
  55.2 9.1 %collective-permute-start.22 = (bf16[8,2176]{1,0:T(8,128)(2,1)S(1)}, bf16[8,2176]{1,0:T(8,128)(2,1)S(1)}, u32[]{:S(2)}, u32[]{:S(2)}) collective-permute-start(bf16[8,2176]{1,0:T(8,128)(2,1)S(1)} %get-tuple-element.97), channel_id=1, source_target_pairs={{0,8},{1,9},{2,10},{3,11},{4,12},{5,13},{6,14},{7,15},{8,0},{9,1},... | collective-permute-start | bytes 104456 | tf_op jit(solution)/shard_map/ppermute | solution.py:392
  59.0 5.7 %collective-permute-start.23 = (bf16[8,2176]{1,0:T(8,128)(2,1)S(1)}, bf16[8,2176]{1,0:T(8,128)(2,1)S(1)}, u32[]{:S(2)}, u32[]{:S(2)}) collective-permute-start(bf16[8,2176]{1,0:T(8,128)(2,1)S(1)} %get-tuple-element.98), channel_id=1, source_target_pairs={{0,12},{1,13},{2,14},{3,15},{4,8},{5,9},{6,10},{7,11},{8,4},{9,5},... | collective-permute-start | bytes 104456 | tf_op jit(solution)/shard_map/ppermute | solution.py:392
  60.3 4.0 %collective-permute-start.20 = (bf16[8,2048]{1,0:T(8,128)(2,1)S(1)}, bf16[8,2048]{1,0:T(8,128)(2,1)S(1)}, u32[]{:S(2)}, u32[]{:S(2)}) collective-permute-start(bf16[8,2048]{1,0:T(8,128)(2,1)S(1)} %add_and_cut.9), channel_id=1, source_target_pairs={{0,16},{1,17},{2,18},{3,19},{4,20},{5,21},{6,22},{7,23},{8,24},{9,... | collective-permute-start | bytes 98312 | tf_op jit(solution)/shard_map/ppermute | solution.py:392

commit v6 on v4

--- a/solution.py
+++ b/solution.py
@@ -14,7 +14,7 @@
 VMEM_LIMIT = 56 * 2**20
 VMEM_SOME = 16 * 2**20
 VMEM_MORE = 24 * 2**20
-SPARE = 16
+SPARE = 0
 SMALL = pl.CostEstimate(flops=1, bytes_accessed=1, transcendentals=0)
 F32 = jnp.float32
 BF16 = jnp.bfloat16
@@ -286,11 +286,17 @@
     )(side, in_vmem(hidden), [in_vmem(weight) for weight in weights])
 
 
-def peer_down_kernel(side_ref, partial_ref, hidden_ref, weight_refs, share_ref, *out_refs):
+def cuts(rows, parts):
+    size = rows.shape[0] // parts
+    return [rows[n * size : (n + 1) * size] for n in range(parts)]
+
+
+def peer_down_kernel(
+    side_ref, partial_ref, hidden_ref, weight_refs, share_ref, *out_refs
+):
     count, half = partial_ref.shape[0], hidden_ref.shape[1]
     rows = pl.ds(pl.multiple_of((1 - side_ref[0]) * half, half), half)
     step = 256
-    cut = count // len(out_refs)
     for n, weight_ref in enumerate(weight_refs):
         width = weight_ref.shape[1]
         for column in range(0, width, step):
@@ -300,9 +306,9 @@
                 weight_ref[rows, column : column + step],
                 preferred_element_type=F32,
             )
-            result = (produced.astype(BF16).astype(F32) * share_ref[:, :1]).astype(BF16)
-            for m, out_ref in enumerate(out_refs):
-                out_ref[:, span] = result[m * cut : (m + 1) * cut]
+            result = produced.astype(BF16).astype(F32) * share_ref[:, :1]
+            for out_ref, cut in zip(out_refs, cuts(result, len(out_refs))):
+                out_ref[:, span] = cut.astype(BF16)
 
 
 def peer_down(side, partial, hidden, weights, share, parts):
@@ -319,22 +325,24 @@
     )(side, in_vmem(partial), hidden, [in_vmem(weight) for weight in weights], in_vmem(share))
 
 
-def halve_kernel(terms, *refs):
+def add_kernel(terms, *refs):
     term_refs, out_refs = refs[:terms], refs[terms:]
     total = term_refs[0][...].astype(F32)
     for term_ref in term_refs[1:]:
         total = total + term_ref[...].astype(F32)
-    size = total.shape[0] // len(out_refs)
-    for n, out_ref in enumerate(out_refs):
-        out_ref[...] = total[n * size : (n + 1) * size].astype(out_ref.dtype)
-
-
-def add_and_cut(kept, arrived, parts):
+    width = total.shape[1]
+    for out_ref, cut in zip(out_refs, cuts(total, len(out_refs))):
+        out_ref[:, :width] = cut.astype(out_ref.dtype)
+        if out_ref.shape[1] > width:
+            out_ref[:, width:] = jnp.zeros((cut.shape[0], out_ref.shape[1] - width), out_ref.dtype)
+
+
+def add_and_cut(kept, arrived, parts, spare=0):
     count, width = kept[0].shape
     vmem = pl.BlockSpec(memory_space=pltpu.VMEM)
-    shape = pltpu.VMEM((count // parts, width), BF16)
-    return pl.pallas_call(
-        functools.partial(halve_kernel, len(kept + arrived)),
+    shape = pltpu.VMEM((count // parts, width + spare), BF16)
+    return pl.pallas_call(
+        functools.partial(add_kernel, len(kept + arrived)),
         out_shape=(shape,) * parts,
         in_specs=[vmem] * len(kept + arrived),
         out_specs=(vmem,) * parts,
@@ -350,14 +358,14 @@
     near = near_refs[0][...].astype(F32)
     for near_ref in near_refs[1:]:
         near = near + near_ref[...].astype(F32)
-    far = far_ref[...].astype(F32)
+    far = far_ref[:, : near.shape[1]].astype(F32)
     for n, out_ref in enumerate(out_refs):
         rows = slice(n * size, (n + 1) * size)
         out_ref[...] = jnp.concatenate([near[rows], far[rows]], axis=0).astype(BF16)
 
 
 def join(near, far, parts):
-    count, width = far.shape
+    count, width = near[0].shape
     vmem = pl.BlockSpec(memory_space=pltpu.VMEM)
     return pl.pallas_call(
         functools.partial(join_kernel, parts),
@@ -443,16 +451,17 @@
     count = share_own.shape[0]
     partial_other = own_down(side, hidden_other, w_down, count)
     partial_own = own_down(side, hidden_own, w_down, count)
-    keep, send = peer_down(side, partial_other, other_peer, w_down, share_other, 2)
-    keep, send = add_and_cut([keep], [swap(send, line)], 2)
-    (onward,) = add_and_cut([keep], [swap(send, core)], 1)
+    def over_core_and_line(keep_near, send_near, keep_far, send_far):
+        (onward,) = add_and_cut([keep_far], [swap(send_far, core)], 1)
+        return [keep_near, swap(send_near, core), swap(onward, line)]
+
+    other = over_core_and_line(
+        *peer_down(side, partial_other, other_peer, w_down, share_other, 4)
+    )
+    (onward,) = add_and_cut(other[:1], other[1:], 1, LANES)
     far = swap(onward, plane)
-    keep_near, send_near, keep_far, send_far = peer_down(
-        side, partial_own, own_peer, w_down, share_own, 4
-    )
-    (onward,) = add_and_cut([keep_far], [swap(send_far, core)], 1)
-    near = [in_vmem(keep_near), swap(send_near, core), swap(onward, line)]
-    blocks = join(near, far, layers)
+    near = over_core_and_line(*peer_down(side, partial_own, own_peer, w_down, share_own, 4))
+    blocks = join([in_vmem(near[0])] + near[1:], far, layers)
     blocks = [blocks[0]] + [swap(blocks[z], z * layer) for z in range(1, layers)]
     return finish(side, mixed, blocks)
 

time: 65.1 us -> 66.7 us (1.025)
  waiting for transfers between devices: 19.3 us -> 20.4 us
    ppermute x21 -> x22, waiting for transfers between devices: 19.3 us -> 20.4 us  [swap(): lax.ppermute(block, ('dp', 'expert'), [(i, i ^ offset) for i in range(dev...]
    ppermute x21 -> x22, starting transfers between devices: 21 us -> 21.4 us  [swap(): lax.ppermute(block, ('dp', 'expert'), [(i, i ^ offset) for i in range(dev...]
  transfers between devices with their start and end apart: 21 -> 22, of which waited for: 11 -> 13; matrix products, arithmetic and copies ran while one was open for 0% -> 0% of each run, Pallas kernels for 32% -> 32%
where the time goes in v6:
time: 66.7 us; the launch traced here: 66.5 us
  Pallas kernels  24.4 us (37%)
  starting transfers between devices  21.4 us (32%)
  waiting for transfers between devices  20.4 us (31%)
    ppermute x22, starting transfers between devices, swap(): lax.ppermute(block, ('dp', 'expert'), [(i, i ^ offset) for i in range(dev...  21.4 us
    ppermute x22, waiting for transfers between devices, swap(): lax.ppermute(block, ('dp', 'expert'), [(i, i ^ offset) for i in range(dev...  20.4 us
    pallas_call x3, Pallas kernels, unpack_weights(): pl.pallas_call(functools.partial(unpack_kernel, tuple((job[2] for job in...  12.6 us
    pallas_call x2, Pallas kernels, hidden_units(): pl.pallas_call(hidden_kernel, out_shape=(pltpu.VMEM((count + spare, width...  5.27 us
    pallas_call x1, Pallas kernels, front(): pl.pallas_call(front_kernel, out_shape=(jax.ShapeDtypeStruct((rows, width...  2.6 us
    pallas_call x2, Pallas kernels, peer_down(): pl.pallas_call(peer_down_kernel, out_shape=(pltpu.VMEM((count // parts, w...  1.62 us
    pallas_call x2, Pallas kernels, own_down(): pl.pallas_call(own_down_kernel, out_shape=pltpu.VMEM((count, width), F32)...  1.46 us
  transfers between devices with their start and end apart: 22, of which 13 were waited for; matrix products, arithmetic and copies ran while one was open for 0% of the time, Pallas kernels for 32%

profile of v6, /device:TPU:0, one launch (start us, length us, event | category | flops | bytes accessed | tf_op | source)
XLA Modules:
  0.0 66.5 jit_solution(5396194632190977467)
XLA Ops:
  0.0 2.6 %front.1 = (bf16[8,4096]{1,0:T(8,128)(2,1)}, bf16[8,4224]{1,0:T(8,128)(2,1)}) custom-call(s32[8]{0:T(128)} %lengths_ref.1, bf16[8,4096]{1,0:T(8,128)(2,1)} %queries_ref.1, bf16[8,2,1024]{2,1,0:T(2,128)(2,1)} %new_kv_ref.1, bf16[8,32,1024]{2,1,0:T(8,128)(2,1)} %keys_ref.1, bf16[8,32,1024]{2,1,0:T(8,128)(2,1)} %values_ref.1, bf16[8,4096]{1,0:T(8,128)(2,1)} %residual_ref.1, ...), custom_call_target="tpu_custom_call" | custom-call | flops 1 | bytes 1 | tf_op jit(solution)/shard_map/front/pallas_call | solution.py:111
  2.6 3.0 %collective-permute-start = (bf16[8,4224]{1,0:T(8,128)(2,1)}, bf16[8,4224]{1,0:T(8,128)(2,1)S(1)}, u32[]{:S(2)}, u32[]{:S(2)}) collective-permute-start(bf16[8,4224]{1,0:T(8,128)(2,1)} %get-tuple-element.49), channel_id=1, source_target_pairs={{0,4},{1,5},{2,6},{3,7},{4,0},{5,1},{6,2},{7,3},{8,12},{9,13},{10,... | collective-permute-start | bytes 202760 | tf_op jit(solution)/shard_map/ppermute | solution.py:418
  5.6 2.6 %collective-permute-start.1 = (bf16[8,4224]{1,0:T(8,128)(2,1)}, bf16[8,4224]{1,0:T(8,128)(2,1)S(1)}, u32[]{:S(2)}, u32[]{:S(2)}) collective-permute-start(bf16[8,4224]{1,0:T(8,128)(2,1)} %get-tuple-element.49), channel_id=1, source_target_pairs={{0,8},{1,9},{2,10},{3,11},{4,12},{5,13},{6,14},{7,15},{8,0},{9,1},... | collective-permute-start | bytes 202760 | tf_op jit(solution)/shard_map/ppermute | solution.py:418
  8.2 5.5 %unpack_weights.3 = (bf16[4096,1024]{1,0:T(8,128)(2,1)S(1)}, bf16[2048,1024]{1,0:T(8,128)(2,1)S(1)}) custom-call(f32[1024,1024]{1,0:T(8,128)} %bitcast.11, f32[512,2048]{1,0:T(8,128)} %bitcast.8, bf16[32,1024]{1,0:T(8,128)(2,1)} %bitcast.14, bf16[16,2048]{1,0:T(8,128)(2,1)} %bitcast.12), custom_call_target="tpu_custom_call" | custom-call | flops 1 | bytes 1 | tf_op jit(solution)/shard_map/unpack_weights/pallas_call | solution.py:204
  13.8 0.0 collective-permute-done.1
  13.8 0.8 %collective-permute-done.2 = bf16[8,4224]{1,0:T(8,128)(2,1)S(1)} collective-permute-done((bf16[8,4224]{1,0:T(8,128)(2,1)}, bf16[8,4224]{1,0:T(8,128)(2,1)S(1)}, u32[]{:S(2)}, u32[]{:S(2)}) %collective-permute-start.2) | collective-permute-done | bytes 67616 | tf_op jit(solution)/shard_map/ppermute | solution.py:418
  14.7 1.6 %collective-permute-start.3 = (bf16[32,4224]{1,0:T(8,128)(2,1)S(1)}, bf16[32,4224]{1,0:T(8,128)(2,1)S(1)}, u32[]{:S(2)}, u32[]{:S(2)}) collective-permute-start(bf16[32,4224]{1,0:T(8,128)(2,1)S(1)} %pad_maximum_fusion.refs_0_), channel_id=1, source_target_pairs={{0,2},{1,3},{2,0},{3,1},{4,6},{5,7},{6,4},{7,5},{8,10},{9,11},{10,... | collective-permute-start | bytes 811016 | tf_op jit(solution)/shard_map/ppermute | solution.py:418
  16.2 0.0 collective-permute-start.4
  16.2 1.5 %collective-permute-start.6 = (bf16[32,4224]{1,0:T(8,128)(2,1)S(1)}, bf16[32,4224]{1,0:T(8,128)(2,1)S(1)}, u32[]{:S(2)}, u32[]{:S(2)}) collective-permute-start(bf16[32,4224]{1,0:T(8,128)(2,1)S(1)} %pad_maximum_fusion.refs_0_), channel_id=1, source_target_pairs={{0,16},{1,17},{2,18},{3,19},{4,20},{5,21},{6,22},{7,23},{8,24},{9,... | collective-permute-start | bytes 811016 | tf_op jit(solution)/shard_map/ppermute | solution.py:418
  17.7 4.2 %unpack_weights.4.refs_5_ = bf16[4096,1024]{1,0:T(8,128)(2,1)S(1)} custom-call(f32[1024,1024]{1,0:T(8,128)} %bitcast.10, bf16[32,1024]{1,0:T(8,128)(2,1)} %bitcast.15), custom_call_target="tpu_custom_call" | custom-call | flops 1 | bytes 1 | tf_op jit(solution)/shard_map/unpack_weights/pallas_call | solution.py:204
  21.9 0.0 collective-permute-done.3.refs_2_
  22.0 0.3 collective-permute-start.5
  22.3 0.8 %collective-permute-start.8 = (bf16[32,4224]{1,0:T(8,128)(2,1)S(1)}, bf16[32,4224]{1,0:T(8,128)(2,1)S(1)}, u32[]{:S(2)}, u32[]{:S(2)}) collective-permute-start(bf16[32,4224]{1,0:T(8,128)(2,1)S(1)} %collective-permute-done.3.refs_2_), channel_id=1, source_target_pairs={{0,16},{1,17},{2,18},{3,19},{4,20},{5,21},{6,22},{7,23},{8,24},{9,... | collective-permute-start | bytes 811016 | tf_op jit(solution)/shard_map/ppermute | solution.py:418
  23.1 2.1 %collective-permute-done.6.refs_0_ = bf16[32,4224]{1,0:T(8,128)(2,1)S(1)} collective-permute-done((bf16[32,4224]{1,0:T(8,128)(2,1)S(1)}, bf16[32,4224]{1,0:T(8,128)(2,1)S(1)}, u32[]{:S(2)}, u32[]{:S(2)}) %collective-permute-start.6) | collective-permute-done | bytes 270368 | tf_op jit(solution)/shard_map/ppermute | solution.py:418
  25.1 0.0 collective-permute-done.5.refs_3_
  25.1 2.6 %gate_up.2 = (bf16[128,1024]{1,0:T(8,128)(2,1)S(1)}, f32[128,128]{1,0:T(8,128)S(1)}) custom-call(s32[1]{0:T(128)} %bitcast.1.place_ref, bf16[32,4224]{1,0:T(8,128)(2,1)S(1)} %pad_maximum_fusion.refs_0_, bf16[32,4224]{1,0:T(8,128)(2,1)S(1)} %collective-permute-done.4.refs_1_, bf16[32,4224]{1,0:T(8,128)(2,1)S(1)} %collective-permute-done.3.refs_2_, ...), custom_call_target="tpu_custom_call" | custom-call | flops 1 | bytes 1 | tf_op jit(solution)/shard_map/gate_up/pallas_call | solution.py:249
  27.8 2.9 %unpack_weights.5.weight_refs_1_ = bf16[2048,1024]{1,0:T(8,128)(2,1)S(1)} custom-call(f32[512,2048]{1,0:T(8,128)} %bitcast.9, bf16[16,2048]{1,0:T(8,128)(2,1)} %bitcast.13), custom_call_target="tpu_custom_call" | custom-call | flops 1 | bytes 1 | tf_op jit(solution)/shard_map/unpack_weights/pallas_call | solution.py:204
  30.7 0.3 collective-permute-done.8.refs_2_
  30.9 0.3 collective-permute-start.9
  31.3 1.9 %collective-permute-start.10 = (bf16[128,1024]{1,0:T(8,128)(2,1)S(1)}, bf16[128,1024]{1,0:T(8,128)(2,1)S(1)}, u32[]{:S(2)}, u32[]{:S(2)}) collective-permute-start(bf16[128,1024]{1,0:T(8,128)(2,1)S(1)} %get-tuple-element.75.hidden_ref), channel_id=1, source_target_pairs={{0,16},{1,17},{2,18},{3,19},{4,20},{5,21},{6,22},{7,23},{8,24},{9,... | collective-permute-start | bytes 786440 | tf_op jit(solution)/shard_map/ppermute | solution.py:418
  33.1 2.6 %gate_up.3 = (bf16[128,1024]{1,0:T(8,128)(2,1)S(1)}, f32[128,128]{1,0:T(8,128)S(1)}) custom-call(s32[1]{0:T(128)} %bitcast.1.place_ref, bf16[32,4224]{1,0:T(8,128)(2,1)S(1)} %collective-permute-done.6.refs_0_, bf16[32,4224]{1,0:T(8,128)(2,1)S(1)} %collective-permute-done.7.refs_1_, bf16[32,4224]{1,0:T(8,128)(2,1)S(1)} %collective-permute-done.8.refs_2_, ...), custom_call_target="tpu_custom_call" | custom-call | flops 1 | bytes 1 | tf_op jit(solution)/shard_map/gate_up/pallas_call | solution.py:249
  35.8 1.3 %collective-permute-start.15 = (bf16[128,1024]{1,0:T(8,128)(2,1)S(1)}, bf16[128,1024]{1,0:T(8,128)(2,1)S(1)}, u32[]{:S(2)}, u32[]{:S(2)}) collective-permute-start(bf16[128,1024]{1,0:T(8,128)(2,1)S(1)} %get-tuple-element.67.hidden_ref), channel_id=1, source_target_pairs={{0,16},{1,17},{2,18},{3,19},{4,20},{5,21},{6,22},{7,23},{8,24},{9,... | collective-permute-start | bytes 786440 | tf_op jit(solution)/shard_map/ppermute | solution.py:418
  37.0 0.7 %down_own.2.partial_ref = f32[128,2048]{1,0:T(8,128)S(1)} custom-call(s32[1]{0:T(128)} %bitcast.side_ref, bf16[128,1024]{1,0:T(8,128)(2,1)S(1)} %get-tuple-element.67.hidden_ref, bf16[2048,1024]{1,0:T(8,128)(2,1)S(1)} %get-tuple-element.68.weight_refs_0_, bf16[2048,1024]{1,0:T(8,128)(2,1)S(1)} %unpack_weights.5.weight_refs_1_), custom_call_target="tpu_custom_call" | custom-call | flops 1 | bytes 1 | tf_op jit(solution)/shard_map/down_own/pallas_call | solution.py:278
  37.8 2.6 %collective-permute-done.10.hidden_ref = bf16[128,1024]{1,0:T(8,128)(2,1)S(1)} collective-permute-done((bf16[128,1024]{1,0:T(8,128)(2,1)S(1)}, bf16[128,1024]{1,0:T(8,128)(2,1)S(1)}, u32[]{:S(2)}, u32[]{:S(2)}) %collective-permute-start.10) | collective-permute-done | bytes 262176 | tf_op jit(solution)/shard_map/ppermute | solution.py:418
  40.4 0.8 %down_peer.2 = (bf16[32,2048]{1,0:T(8,128)(2,1)S(1)}, bf16[32,2048]{1,0:T(8,128)(2,1)S(1)}, bf16[32,2048]{1,0:T(8,128)(2,1)S(1)}, bf16[32,2048]{1,0:T(8,128)(2,1)S(1)}) custom-call(s32[1]{0:T(128)} %bitcast.side_ref, f32[128,2048]{1,0:T(8,128)S(1)} %down_own.2.partial_ref, bf16[128,1024]{1,0:T(8,128)(2,1)S(1)} %collective-permute-done.10.hidden_ref, ...), custom_call_target="tpu_custom_call" | custom-call | flops 1 | bytes 1 | tf_op jit(solution)/shard_map/down_peer/pallas_call | solution.py:317
  41.2 0.1 collective-permute-start.12
  41.3 0.5 collective-permute-start.11
  41.8 0.8 %collective-permute-done.12.refs_1_ = bf16[32,2048]{1,0:T(8,128)(2,1)S(1)} collective-permute-done((bf16[32,2048]{1,0:T(8,128)(2,1)S(1)}, bf16[32,2048]{1,0:T(8,128)(2,1)S(1)}, u32[]{:S(2)}, u32[]{:S(2)}) %collective-permute-start.12) | collective-permute-done | bytes 131104 | tf_op jit(solution)/shard_map/ppermute | solution.py:418
  42.7 0.8 %collective-permute-start.13 = (bf16[32,2048]{1,0:T(8,128)(2,1)S(1)}, bf16[32,2048]{1,0:T(8,128)(2,1)S(1)}, u32[]{:S(2)}, u32[]{:S(2)}) collective-permute-start(bf16[32,2048]{1,0:T(8,128)(2,1)S(1)} %add_and_cut.3), channel_id=1, source_target_pairs={{0,2},{1,3},{2,0},{3,1},{4,6},{5,7},{6,4},{7,5},{8,10},{9,11},{10,... | collective-permute-start | bytes 393224 | tf_op jit(solution)/shard_map/ppermute | solution.py:418
  43.4 0.7 %down_own.3.partial_ref = f32[128,2048]{1,0:T(8,128)S(1)} custom-call(s32[1]{0:T(128)} %bitcast.side_ref, bf16[128,1024]{1,0:T(8,128)(2,1)S(1)} %get-tuple-element.75.hidden_ref, bf16[2048,1024]{1,0:T(8,128)(2,1)S(1)} %get-tuple-element.68.weight_refs_0_, bf16[2048,1024]{1,0:T(8,128)(2,1)S(1)} %unpack_weights.5.weight_refs_1_), custom_call_target="tpu_custom_call" | custom-call | flops 1 | bytes 1 | tf_op jit(solution)/shard_map/down_own/pallas_call | solution.py:278
  44.2 1.1 %collective-permute-done.15.hidden_ref = bf16[128,1024]{1,0:T(8,128)(2,1)S(1)} collective-permute-done((bf16[128,1024]{1,0:T(8,128)(2,1)S(1)}, bf16[128,1024]{1,0:T(8,128)(2,1)S(1)}, u32[]{:S(2)}, u32[]{:S(2)}) %collective-permute-start.15) | collective-permute-done | bytes 262176 | tf_op jit(solution)/shard_map/ppermute | solution.py:418
  45.3 0.8 %down_peer.3 = (bf16[32,2048]{1,0:T(8,128)(2,1)S(1)}, bf16[32,2048]{1,0:T(8,128)(2,1)S(1)}, bf16[32,2048]{1,0:T(8,128)(2,1)S(1)}, bf16[32,2048]{1,0:T(8,128)(2,1)S(1)}) custom-call(s32[1]{0:T(128)} %bitcast.side_ref, f32[128,2048]{1,0:T(8,128)S(1)} %down_own.3.partial_ref, bf16[128,1024]{1,0:T(8,128)(2,1)S(1)} %collective-permute-done.15.hidden_ref, ...), custom_call_target="tpu_custom_call" | custom-call | flops 1 | bytes 1 | tf_op jit(solution)/shard_map/down_peer/pallas_call | solution.py:317
  46.1 0.1 collective-permute-start.17
  46.2 2.1 %collective-permute-done.13.refs_2_ = bf16[32,2048]{1,0:T(8,128)(2,1)S(1)} collective-permute-done((bf16[32,2048]{1,0:T(8,128)(2,1)S(1)}, bf16[32,2048]{1,0:T(8,128)(2,1)S(1)}, u32[]{:S(2)}, u32[]{:S(2)}) %collective-permute-start.13) | collective-permute-done | bytes 131104 | tf_op jit(solution)/shard_map/ppermute | solution.py:418
  48.3 0.1 add_and_cut.4
  48.3 2.0 %collective-permute-start.14 = (bf16[32,2176]{1,0:T(8,128)(2,1)S(1)}, bf16[32,2176]{1,0:T(8,128)(2,1)S(1)}, u32[]{:S(2)}, u32[]{:S(2)}) collective-permute-start(bf16[32,2176]{1,0:T(8,128)(2,1)S(1)} %add_and_cut.4), channel_id=1, source_target_pairs={{0,16},{1,17},{2,18},{3,19},{4,20},{5,21},{6,22},{7,23},{8,24},{9,... | collective-permute-start | bytes 417800 | tf_op jit(solution)/shard_map/ppermute | solution.py:418
  50.3 0.4 collective-permute-start.18
  50.7 0.9 %collective-permute-done.16.refs_1_ = bf16[32,2048]{1,0:T(8,128)(2,1)S(1)} collective-permute-done((bf16[32,2048]{1,0:T(8,128)(2,1)S(1)}, bf16[32,2048]{1,0:T(8,128)(2,1)S(1)}, u32[]{:S(2)}, u32[]{:S(2)}) %collective-permute-start.16) | collective-permute-done | bytes 131104 | tf_op jit(solution)/shard_map/ppermute | solution.py:418
  51.6 1.8 %collective-permute-done.14.far_ref = bf16[32,2176]{1,0:T(8,128)(2,1)S(1)} collective-permute-done((bf16[32,2176]{1,0:T(8,128)(2,1)S(1)}, bf16[32,2176]{1,0:T(8,128)(2,1)S(1)}, u32[]{:S(2)}, u32[]{:S(2)}) %collective-permute-start.14) | collective-permute-done | bytes 139296 | tf_op jit(solution)/shard_map/ppermute | solution.py:418
  53.4 2.9 %collective-permute-done.18.refs_2_ = bf16[32,2048]{1,0:T(8,128)(2,1)S(1)} collective-permute-done((bf16[32,2048]{1,0:T(8,128)(2,1)S(1)}, bf16[32,2048]{1,0:T(8,128)(2,1)S(1)}, u32[]{:S(2)}, u32[]{:S(2)}) %collective-permute-start.18) | collective-permute-done | bytes 131104 | tf_op jit(solution)/shard_map/ppermute | solution.py:418
  56.3 0.1 join.1
  56.4 0.7 %collective-permute-start.19 = (bf16[16,2048]{1,0:T(8,128)(2,1)S(1)}, bf16[16,2048]{1,0:T(8,128)(2,1)S(1)}, u32[]{:S(2)}, u32[]{:S(2)}) collective-permute-start(bf16[16,2048]{1,0:T(8,128)(2,1)S(1)} %get-tuple-element.82), channel_id=1, source_target_pairs={{0,4},{1,5},{2,6},{3,7},{4,0},{5,1},{6,2},{7,3},{8,12},{9,13},{10,... | collective-permute-start | bytes 196616 | tf_op jit(solution)/shard_map/ppermute | solution.py:418
  57.1 2.5 %collective-permute-start.20 = (bf16[16,2048]{1,0:T(8,128)(2,1)S(1)}, bf16[16,2048]{1,0:T(8,128)(2,1)S(1)}, u32[]{:S(2)}, u32[]{:S(2)}) collective-permute-start(bf16[16,2048]{1,0:T(8,128)(2,1)S(1)} %get-tuple-element.83), channel_id=1, source_target_pairs={{0,8},{1,9},{2,10},{3,11},{4,12},{5,13},{6,14},{7,15},{8,0},{9,1},... | collective-permute-start | bytes 196616 | tf_op jit(solution)/shard_map/ppermute | solution.py:418
  59.6 1.2 %collective-permute-start.21 = (bf16[16,2048]{1,0:T(8,128)(2,1)S(1)}, bf16[16,2048]{1,0:T(8,128)(2,1)S(1)}, u32[]{:S(2)}, u32[]{:S(2)}) collective-permute-start(bf16[16,2048]{1,0:T(8,128)(2,1)S(1)} %get-tuple-element.84), channel_id=1, source_target_pairs={{0,12},{1,13},{2,14},{3,15},{4,8},{5,9},{6,10},{7,11},{8,4},{9,5},... | collective-permute-start | bytes 196616 | tf_op jit(solution)/shard_map/ppermute | solution.py:418
  60.8 0.6 collective-permute-done.19.refs_1_
  61.4 3.1 %collective-permute-done.20.refs_2_ = bf16[16,2048]{1,0:T(8,128)(2,1)S(1)} collective-permute-done((bf16[16,2048]{1,0:T(8,128)(2,1)S(1)}, bf16[16,2048]{1,0:T(8,128)(2,1)S(1)}, u32[]{:S(2)}, u32[]{:S(2)}) %collective-permute-start.20) | collective-permute-done | bytes 65568 | tf_op jit(solution)/shard_map/ppermute | solution.py:418
  64.5 1.3 %collective-permute-done.21.refs_3_ = bf16[16,2048]{1,0:T(8,128)(2,1)S(1)} collective-permute-done((bf16[16,2048]{1,0:T(8,128)(2,1)S(1)}, bf16[16,2048]{1,0:T(8,128)(2,1)S(1)}, u32[]{:S(2)}, u32[]{:S(2)}) %collective-permute-start.21) | collective-permute-done | bytes 65568 | tf_op jit(solution)/shard_map/ppermute | solution.py:418
  65.8 0.7 %finish.1 = bf16[8,4096]{1,0:T(8,128)(2,1)} custom-call(s32[1]{0:T(128)} %bitcast.side_ref, bf16[8,4096]{1,0:T(8,128)(2,1)S(1)} %copy-done, bf16[16,2048]{1,0:T(8,128)(2,1)S(1)} %get-tuple-element.81.refs_0_, bf16[16,2048]{1,0:T(8,128)(2,1)S(1)} %collective-permute-done.19.refs_1_, bf16[16,2048]{1,0:T(8,128)(2,1)S(1)} %collective-permute-done.20.refs_2_, ...), custom_call_target="tpu_custom_call" | custom-call | tf_op jit(solution)/shard_map/finish/pallas_call | solution.py:397
  (16 shorter events, 0.1 us)
Async XLA Ops:
  2.6 11.2 %collective-permute-start = (bf16[8,4224]{1,0:T(8,128)(2,1)}, bf16[8,4224]{1,0:T(8,128)(2,1)S(1)}, u32[]{:S(2)}, u32[]{:S(2)}) collective-permute-start(bf16[8,4224]{1,0:T(8,128)(2,1)} %get-tuple-element.49), channel_id=1, source_target_pairs={{0,4},{1,5},{2,6},{3,7},{4,0},{5,1},{6,2},{7,3},{8,12},{9,13},{10,... | collective-permute-start | bytes 202760 | tf_op jit(solution)/shard_map/ppermute | solution.py:418
  5.6 8.1 %collective-permute-start.1 = (bf16[8,4224]{1,0:T(8,128)(2,1)}, bf16[8,4224]{1,0:T(8,128)(2,1)S(1)}, u32[]{:S(2)}, u32[]{:S(2)}) collective-permute-start(bf16[8,4224]{1,0:T(8,128)(2,1)} %get-tuple-element.49), channel_id=1, source_target_pairs={{0,8},{1,9},{2,10},{3,11},{4,12},{5,13},{6,14},{7,15},{8,0},{9,1},... | collective-permute-start | bytes 202760 | tf_op jit(solution)/shard_map/ppermute | solution.py:418
  8.2 6.4 %collective-permute-start.2 = (bf16[8,4224]{1,0:T(8,128)(2,1)}, bf16[8,4224]{1,0:T(8,128)(2,1)S(1)}, u32[]{:S(2)}, u32[]{:S(2)}) collective-permute-start(bf16[8,4224]{1,0:T(8,128)(2,1)} %get-tuple-element.49), channel_id=1, source_target_pairs={{0,12},{1,13},{2,14},{3,15},{4,8},{5,9},{6,10},{7,11},{8,4},{9,5},... | collective-permute-start | bytes 202760 | tf_op jit(solution)/shard_map/ppermute | solution.py:418
  8.2 6.4 %copy-start.1 = (bf16[8,4224]{1,0:T(8,128)(2,1)S(1)}, bf16[8,4224]{1,0:T(8,128)(2,1)}, u32[]{:S(2)}) copy-start(bf16[8,4224]{1,0:T(8,128)(2,1)} %get-tuple-element.49) | copy-start | bytes 202756
  14.7 7.3 %collective-permute-start.3 = (bf16[32,4224]{1,0:T(8,128)(2,1)S(1)}, bf16[32,4224]{1,0:T(8,128)(2,1)S(1)}, u32[]{:S(2)}, u32[]{:S(2)}) collective-permute-start(bf16[32,4224]{1,0:T(8,128)(2,1)S(1)} %pad_maximum_fusion.refs_0_), channel_id=1, source_target_pairs={{0,2},{1,3},{2,0},{3,1},{4,6},{5,7},{6,4},{7,5},{8,10},{9,11},{10,... | collective-permute-start | bytes 811016 | tf_op jit(solution)/shard_map/ppermute | solution.py:418
  16.2 5.7 %collective-permute-start.4 = (bf16[32,4224]{1,0:T(8,128)(2,1)S(1)}, bf16[32,4224]{1,0:T(8,128)(2,1)S(1)}, u32[]{:S(2)}, u32[]{:S(2)}) collective-permute-start(bf16[32,4224]{1,0:T(8,128)(2,1)S(1)} %pad_maximum_fusion.refs_0_), channel_id=1, source_target_pairs={{0,1},{1,0},{2,3},{3,2},{4,5},{5,4},{6,7},{7,6},{8,9},{9,8},{10,11... | collective-permute-start | bytes 811016 | tf_op jit(solution)/shard_map/ppermute | solution.py:418
  16.2 8.9 %collective-permute-start.6 = (bf16[32,4224]{1,0:T(8,128)(2,1)S(1)}, bf16[32,4224]{1,0:T(8,128)(2,1)S(1)}, u32[]{:S(2)}, u32[]{:S(2)}) collective-permute-start(bf16[32,4224]{1,0:T(8,128)(2,1)S(1)} %pad_maximum_fusion.refs_0_), channel_id=1, source_target_pairs={{0,16},{1,17},{2,18},{3,19},{4,20},{5,21},{6,22},{7,23},{8,24},{9,... | collective-permute-start | bytes 811016 | tf_op jit(solution)/shard_map/ppermute | solution.py:418
  22.0 3.2 %collective-permute-start.5 = (bf16[32,4224]{1,0:T(8,128)(2,1)S(1)}, bf16[32,4224]{1,0:T(8,128)(2,1)S(1)}, u32[]{:S(2)}, u32[]{:S(2)}) collective-permute-start(bf16[32,4224]{1,0:T(8,128)(2,1)S(1)} %collective-permute-done.3.refs_2_), channel_id=1, source_target_pairs={{0,1},{1,0},{2,3},{3,2},{4,5},{5,4},{6,7},{7,6},{8,9},{9,8},{10,11... | collective-permute-start | bytes 811016 | tf_op jit(solution)/shard_map/ppermute | solution.py:418
  22.3 8.7 %collective-permute-start.8 = (bf16[32,4224]{1,0:T(8,128)(2,1)S(1)}, bf16[32,4224]{1,0:T(8,128)(2,1)S(1)}, u32[]{:S(2)}, u32[]{:S(2)}) collective-permute-start(bf16[32,4224]{1,0:T(8,128)(2,1)S(1)} %collective-permute-done.3.refs_2_), channel_id=1, source_target_pairs={{0,16},{1,17},{2,18},{3,19},{4,20},{5,21},{6,22},{7,23},{8,24},{9,... | collective-permute-start | bytes 811016 | tf_op jit(solution)/shard_map/ppermute | solution.py:418
  25.1 8.0 %collective-permute-start.7 = (bf16[32,4224]{1,0:T(8,128)(2,1)S(1)}, bf16[32,4224]{1,0:T(8,128)(2,1)S(1)}, u32[]{:S(2)}, u32[]{:S(2)}) collective-permute-start(bf16[32,4224]{1,0:T(8,128)(2,1)S(1)} %collective-permute-done.6.refs_0_), channel_id=1, source_target_pairs={{0,1},{1,0},{2,3},{3,2},{4,5},{5,4},{6,7},{7,6},{8,9},{9,8},{10,11... | collective-permute-start | bytes 811016 | tf_op jit(solution)/shard_map/ppermute | solution.py:418
  30.9 2.2 %collective-permute-start.9 = (bf16[32,4224]{1,0:T(8,128)(2,1)S(1)}, bf16[32,4224]{1,0:T(8,128)(2,1)S(1)}, u32[]{:S(2)}, u32[]{:S(2)}) collective-permute-start(bf16[32,4224]{1,0:T(8,128)(2,1)S(1)} %collective-permute-done.8.refs_2_), channel_id=1, source_target_pairs={{0,1},{1,0},{2,3},{3,2},{4,5},{5,4},{6,7},{7,6},{8,9},{9,8},{10,11... | collective-permute-start | bytes 811016 | tf_op jit(solution)/shard_map/ppermute | solution.py:418
  31.3 9.1 %collective-permute-start.10 = (bf16[128,1024]{1,0:T(8,128)(2,1)S(1)}, bf16[128,1024]{1,0:T(8,128)(2,1)S(1)}, u32[]{:S(2)}, u32[]{:S(2)}) collective-permute-start(bf16[128,1024]{1,0:T(8,128)(2,1)S(1)} %get-tuple-element.75.hidden_ref), channel_id=1, source_target_pairs={{0,16},{1,17},{2,18},{3,19},{4,20},{5,21},{6,22},{7,23},{8,24},{9,... | collective-permute-start | bytes 786440 | tf_op jit(solution)/shard_map/ppermute | solution.py:418
  35.8 9.5 %collective-permute-start.15 = (bf16[128,1024]{1,0:T(8,128)(2,1)S(1)}, bf16[128,1024]{1,0:T(8,128)(2,1)S(1)}, u32[]{:S(2)}, u32[]{:S(2)}) collective-permute-start(bf16[128,1024]{1,0:T(8,128)(2,1)S(1)} %get-tuple-element.67.hidden_ref), channel_id=1, source_target_pairs={{0,16},{1,17},{2,18},{3,19},{4,20},{5,21},{6,22},{7,23},{8,24},{9,... | collective-permute-start | bytes 786440 | tf_op jit(solution)/shard_map/ppermute | solution.py:418
  41.2 1.4 %collective-permute-start.12 = (bf16[32,2048]{1,0:T(8,128)(2,1)S(1)}, bf16[32,2048]{1,0:T(8,128)(2,1)S(1)}, u32[]{:S(2)}, u32[]{:S(2)}) collective-permute-start(bf16[32,2048]{1,0:T(8,128)(2,1)S(1)} %get-tuple-element.74), channel_id=1, source_target_pairs={{0,1},{1,0},{2,3},{3,2},{4,5},{5,4},{6,7},{7,6},{8,9},{9,8},{10,11... | collective-permute-start | bytes 393224 | tf_op jit(solution)/shard_map/ppermute | solution.py:418
  41.3 4.9 %collective-permute-start.11 = (bf16[32,2048]{1,0:T(8,128)(2,1)S(1)}, bf16[32,2048]{1,0:T(8,128)(2,1)S(1)}, u32[]{:S(2)}, u32[]{:S(2)}) collective-permute-start(bf16[32,2048]{1,0:T(8,128)(2,1)S(1)} %get-tuple-element.72), channel_id=1, source_target_pairs={{0,1},{1,0},{2,3},{3,2},{4,5},{5,4},{6,7},{7,6},{8,9},{9,8},{10,11... | collective-permute-start | bytes 393224 | tf_op jit(solution)/shard_map/ppermute | solution.py:418
  42.7 5.6 %collective-permute-start.13 = (bf16[32,2048]{1,0:T(8,128)(2,1)S(1)}, bf16[32,2048]{1,0:T(8,128)(2,1)S(1)}, u32[]{:S(2)}, u32[]{:S(2)}) collective-permute-start(bf16[32,2048]{1,0:T(8,128)(2,1)S(1)} %add_and_cut.3), channel_id=1, source_target_pairs={{0,2},{1,3},{2,0},{3,1},{4,6},{5,7},{6,4},{7,5},{8,10},{9,11},{10,... | collective-permute-start | bytes 393224 | tf_op jit(solution)/shard_map/ppermute | solution.py:418
  45.3 20.5 %copy-start = (bf16[8,4096]{1,0:T(8,128)(2,1)S(1)}, bf16[8,4096]{1,0:T(8,128)(2,1)}, u32[]{:S(2)}) copy-start(bf16[8,4096]{1,0:T(8,128)(2,1)} %get-tuple-element.47.mixed_ref) | copy-start | bytes 196612
  46.1 4.2 %collective-permute-start.17 = (bf16[32,2048]{1,0:T(8,128)(2,1)S(1)}, bf16[32,2048]{1,0:T(8,128)(2,1)S(1)}, u32[]{:S(2)}, u32[]{:S(2)}) collective-permute-start(bf16[32,2048]{1,0:T(8,128)(2,1)S(1)} %get-tuple-element.80), channel_id=1, source_target_pairs={{0,1},{1,0},{2,3},{3,2},{4,5},{5,4},{6,7},{7,6},{8,9},{9,8},{10,11... | collective-permute-start | bytes 393224 | tf_op jit(solution)/shard_map/ppermute | solution.py:418
  48.3 5.1 %collective-permute-start.14 = (bf16[32,2176]{1,0:T(8,128)(2,1)S(1)}, bf16[32,2176]{1,0:T(8,128)(2,1)S(1)}, u32[]{:S(2)}, u32[]{:S(2)}) collective-permute-start(bf16[32,2176]{1,0:T(8,128)(2,1)S(1)} %add_and_cut.4), channel_id=1, source_target_pairs={{0,16},{1,17},{2,18},{3,19},{4,20},{5,21},{6,22},{7,23},{8,24},{9,... | collective-permute-start | bytes 417800 | tf_op jit(solution)/shard_map/ppermute | solution.py:418
  50.3 1.3 %collective-permute-start.16 = (bf16[32,2048]{1,0:T(8,128)(2,1)S(1)}, bf16[32,2048]{1,0:T(8,128)(2,1)S(1)}, u32[]{:S(2)}, u32[]{:S(2)}) collective-permute-start(bf16[32,2048]{1,0:T(8,128)(2,1)S(1)} %get-tuple-element.78), channel_id=1, source_target_pairs={{0,1},{1,0},{2,3},{3,2},{4,5},{5,4},{6,7},{7,6},{8,9},{9,8},{10,11... | collective-permute-start | bytes 393224 | tf_op jit(solution)/shard_map/ppermute | solution.py:418
  50.3 6.0 %collective-permute-start.18 = (bf16[32,2048]{1,0:T(8,128)(2,1)S(1)}, bf16[32,2048]{1,0:T(8,128)(2,1)S(1)}, u32[]{:S(2)}, u32[]{:S(2)}) collective-permute-start(bf16[32,2048]{1,0:T(8,128)(2,1)S(1)} %add_and_cut.5), channel_id=1, source_target_pairs={{0,2},{1,3},{2,0},{3,1},{4,6},{5,7},{6,4},{7,5},{8,10},{9,11},{10,... | collective-permute-start | bytes 393224 | tf_op jit(solution)/shard_map/ppermute | solution.py:418
  56.4 5.0 %collective-permute-start.19 = (bf16[16,2048]{1,0:T(8,128)(2,1)S(1)}, bf16[16,2048]{1,0:T(8,128)(2,1)S(1)}, u32[]{:S(2)}, u32[]{:S(2)}) collective-permute-start(bf16[16,2048]{1,0:T(8,128)(2,1)S(1)} %get-tuple-element.82), channel_id=1, source_target_pairs={{0,4},{1,5},{2,6},{3,7},{4,0},{5,1},{6,2},{7,3},{8,12},{9,13},{10,... | collective-permute-start | bytes 196616 | tf_op jit(solution)/shard_map/ppermute | solution.py:418
  57.1 7.4 %collective-permute-start.20 = (bf16[16,2048]{1,0:T(8,128)(2,1)S(1)}, bf16[16,2048]{1,0:T(8,128)(2,1)S(1)}, u32[]{:S(2)}, u32[]{:S(2)}) collective-permute-start(bf16[16,2048]{1,0:T(8,128)(2,1)S(1)} %get-tuple-element.83), channel_id=1, source_target_pairs={{0,8},{1,9},{2,10},{3,11},{4,12},{5,13},{6,14},{7,15},{8,0},{9,1},... | collective-permute-start | bytes 196616 | tf_op jit(solution)/shard_map/ppermute | solution.py:418
  59.6 6.2 %collective-permute-start.21 = (bf16[16,2048]{1,0:T(8,128)(2,1)S(1)}, bf16[16,2048]{1,0:T(8,128)(2,1)S(1)}, u32[]{:S(2)}, u32[]{:S(2)}) collective-permute-start(bf16[16,2048]{1,0:T(8,128)(2,1)S(1)} %get-tuple-element.84), channel_id=1, source_target_pairs={{0,12},{1,13},{2,14},{3,15},{4,8},{5,9},{6,10},{7,11},{8,4},{9,5},... | collective-permute-start | bytes 196616 | tf_op jit(solution)/shard_map/ppermute | solution.py:418

commit v7 on v4

--- a/solution.py
+++ b/solution.py
@@ -130,9 +130,9 @@
     return pltpu.with_memory_space_constraint(array, pltpu.HBM)
 
 
-def unpack_kernel(firsts, codes_refs, scales_hbms, *refs):
-    out_refs, (words_refs, scales_refs, sems, scales_sem) = refs[: len(firsts)], refs[len(firsts) :]
-
+def unpacking(
+    firsts, codes_refs, scales_hbms, out_refs, words_refs, scales_refs, sems, scales_sem, ahead
+):
     def copy_scales(n):
         columns = pl.ds(firsts[n], words_refs[n].shape[1])
         return pltpu.make_async_copy(
@@ -152,85 +152,103 @@
         for n, words_ref in enumerate(words_refs)
         for group in range(words_ref.shape[0] // GROUP)
     ]
-    ahead = 3
-    copy_scales(0).start()
-    for turn in range(min(ahead, len(turns))):
-        fetch(turn).start()
-    for n in range(1, len(firsts)):
-        copy_scales(n).start()
-    for turn, (n, group) in enumerate(turns):
-        words_ref, out_ref = words_refs[n], out_refs[n]
-        quarter, width = words_ref.shape
-        groups = quarter // GROUP
-        step = 256 if width % 256 == 0 else LANES
-        if turn + ahead < len(turns):
-            fetch(turn + ahead).start()
-        if group == 0:
-            copy_scales(n).wait()
-            scales = scales_refs[n][...].astype(F32)
-        fetch(turn).wait()
-        for column in range(0, width, step):
-            spans = [
-                jnp.broadcast_to(
-                    scales[k * groups + group : k * groups + group + 1, column : column + step],
-                    (16, step),
-                ).astype(BF16)
-                for k in range(4)
-            ]
-
-            def chunk(
-                i, carry, group=group, column=column, spans=spans, words_ref=words_ref, out_ref=out_ref
-            ):
-                start = pl.multiple_of(group * GROUP + i * 16, 16)
-                words = words_ref[pl.ds(start, 16), column : column + step].astype(jnp.int32)
-                for k in range(4):
-                    digit = words if k == 0 else lax.shift_right_logical(words, 4 * k)
-                    if k < 3:
-                        digit = digit & 15
-                    level = digit.astype(F32).astype(BF16) - jnp.asarray(8, BF16)
-                    out_ref[pl.ds(k * quarter + start, 16), column : column + step] = (
-                        level * spans[k]
-                    )
-                return carry
-
-            lax.fori_loop(0, GROUP // 16, chunk, 0, unroll=True)
+    def start():
+        copy_scales(0).start()
+        for turn in range(min(ahead, len(turns))):
+            fetch(turn).start()
+        for n in range(1, len(firsts)):
+            copy_scales(n).start()
+
+    def run():
+        for turn, (n, group) in enumerate(turns):
+            words_ref, out_ref = words_refs[n], out_refs[n]
+            quarter, width = words_ref.shape
+            groups = quarter // GROUP
+            step = 256 if width % 256 == 0 else LANES
+            if turn + ahead < len(turns):
+                fetch(turn + ahead).start()
+            if group == 0:
+                copy_scales(n).wait()
+                scales = scales_refs[n][...].astype(F32)
+            fetch(turn).wait()
+            for column in range(0, width, step):
+                spans = [
+                    jnp.broadcast_to(
+                        scales[k * groups + group : k * groups + group + 1, column : column + step],
+                        (16, step),
+                    ).astype(BF16)
+                    for k in range(4)
+                ]
+
+                def chunk(
+                    i, carry, group=group, column=column, spans=spans, words_ref=words_ref, out_ref=out_ref
+                ):
+                    start = pl.multiple_of(group * GROUP + i * 16, 16)
+                    words = words_ref[pl.ds(start, 16), column : column + step].astype(jnp.int32)
+                    for k in range(4):
+                        digit = words if k == 0 else lax.shift_right_logical(words, 4 * k)
+                        if k < 3:
+                            digit = digit & 15
+                        level = digit.astype(F32).astype(BF16) - jnp.asarray(8, BF16)
+                        out_ref[pl.ds(k * quarter + start, 16), column : column + step] = (
+                            level * spans[k]
+                        )
+                    return carry
+
+                lax.fori_loop(0, GROUP // 16, chunk, 0, unroll=True)
+
+    return start, run
+
+
+def unpack_kernel(firsts, codes_refs, scales_hbms, *refs):
+    start, run = unpacking(
+        firsts, codes_refs, scales_hbms, refs[: len(firsts)], *refs[len(firsts) :], 3
+    )
+    start()
+    run()
+
+
+def unpack_shapes(jobs):
+    shapes = [(codes.shape[0], width) for codes, _, _, width in jobs]
+    turns = sum(quarter // GROUP for quarter, _ in shapes)
+    outs = [pltpu.VMEM((4 * quarter, width), BF16) for quarter, width in shapes]
+    scratch = [
+        [pltpu.VMEM(shape, F32) for shape in shapes],
+        [pltpu.VMEM((4 * quarter // GROUP, width), BF16) for quarter, width in shapes],
+        pltpu.SemaphoreType.DMA((turns,)),
+        pltpu.SemaphoreType.DMA((len(jobs),)),
+    ]
+    return outs, scratch
 
 
 def unpack_weights(*jobs):
     hbm = pl.BlockSpec(memory_space=pltpu.HBM)
     vmem = pl.BlockSpec(memory_space=pltpu.VMEM)
-    shapes = [(codes.shape[0], width) for codes, _, _, width in jobs]
-    turns = sum(quarter // GROUP for quarter, _ in shapes)
+    outs, scratch = unpack_shapes(jobs)
     return pl.pallas_call(
         functools.partial(unpack_kernel, tuple(job[2] for job in jobs)),
-        out_shape=[pltpu.VMEM((4 * quarter, width), BF16) for quarter, width in shapes],
+        out_shape=outs,
         in_specs=[[hbm] * len(jobs)] * 2,
         out_specs=[vmem] * len(jobs),
-        scratch_shapes=[
-            [pltpu.VMEM(shape, F32) for shape in shapes],
-            [pltpu.VMEM((4 * quarter // GROUP, width), BF16) for quarter, width in shapes],
-            pltpu.SemaphoreType.DMA((turns,)),
-            pltpu.SemaphoreType.DMA((len(jobs),)),
-        ],
+        scratch_shapes=scratch,
         compiler_params=pltpu.CompilerParams(vmem_limit_bytes=VMEM_MORE),
         cost_estimate=SMALL,
         name="unpack_weights",
     )([in_hbm(job[0]) for job in jobs], [in_hbm(job[1]) for job in jobs])
 
 
-def hidden_kernel(place_ref, *refs):
-    pieces, (gate_ref, up_ref, out_ref, share_ref, rows_ref) = refs[:-5], refs[-5:]
+def hidden_kernel(firsts, place_ref, pieces, gate_ref, up_ref, codes_refs, scales_hbms, *refs):
+    extra = len(firsts)
+    out_ref, share_ref, *refs = refs
+    more_refs, (rows_ref, *refs) = refs[:extra], refs[extra:]
+    if extra:
+        start, run = unpacking(firsts, codes_refs, scales_hbms, more_refs, *refs, 4)
+        start()
     depth, width = gate_ref.shape
     block = pieces[0].shape[0]
     count = block * len(pieces)
     for n, piece in enumerate(pieces):
         rows_ref[n * block : (n + 1) * block, :] = piece[:, :depth]
-        table = piece[:, depth:].astype(F32)
-        lane = lax.broadcasted_iota(jnp.int32, table.shape, 1)
-        mine = place_ref[0]
-        chosen = (lane == mine) | (lane == mine + LANES // 2)
-        share = jnp.sum(jnp.where(chosen, table, 0.0), axis=1, keepdims=True)
-        share_ref[n * block : (n + 1) * block, :] = jnp.broadcast_to(share, table.shape)
     step = 256
     for column in range(0, width, step):
         span = slice(column, column + step)
@@ -239,23 +257,52 @@
         out_ref[:count, span] = (gate / (1.0 + jnp.exp(-gate)) * upward).astype(BF16)
     if out_ref.shape[0] > count:
         out_ref[count:, :] = jnp.zeros((out_ref.shape[0] - count, width), BF16)
-
-
-def hidden_units(pieces, w_gate, w_up, place, spare=0):
+    for n, piece in enumerate(pieces):
+        table = piece[:, depth:].astype(F32)
+        lane = lax.broadcasted_iota(jnp.int32, table.shape, 1)
+        mine = place_ref[0]
+        chosen = (lane == mine) | (lane == mine + LANES // 2)
+        share = jnp.sum(jnp.where(chosen, table, 0.0), axis=1, keepdims=True)
+        share_ref[n * block : (n + 1) * block, :] = jnp.broadcast_to(share, table.shape)
+    if extra:
+        run()
+
+
+def hidden_units(pieces, w_gate, w_up, place, spare=0, jobs=()):
     block, padded = pieces[0].shape
     count = block * len(pieces)
     depth, width = w_gate.shape
-    vmem = pl.BlockSpec(memory_space=pltpu.VMEM)
-    return pl.pallas_call(
-        hidden_kernel,
-        out_shape=(pltpu.VMEM((count + spare, width), BF16), pltpu.VMEM((count, LANES), F32)),
-        in_specs=[pl.BlockSpec(memory_space=pltpu.SMEM)] + [vmem] * (len(pieces) + 2),
-        out_specs=(vmem, vmem),
-        scratch_shapes=[pltpu.VMEM((count, depth), BF16)],
-        compiler_params=pltpu.CompilerParams(vmem_limit_bytes=VMEM_SOME),
+    hbm = pl.BlockSpec(memory_space=pltpu.HBM)
+    vmem = pl.BlockSpec(memory_space=pltpu.VMEM)
+    outs, scratch = unpack_shapes(jobs)
+    return pl.pallas_call(
+        functools.partial(hidden_kernel, tuple(job[2] for job in jobs)),
+        out_shape=[
+            pltpu.VMEM((count + spare, width), BF16),
+            pltpu.VMEM((count, LANES), F32),
+            *outs,
+        ],
+        in_specs=[
+            pl.BlockSpec(memory_space=pltpu.SMEM),
+            [vmem] * len(pieces),
+            vmem,
+            vmem,
+            [hbm] * len(jobs),
+            [hbm] * len(jobs),
+        ],
+        out_specs=[vmem] * (2 + len(jobs)),
+        scratch_shapes=[pltpu.VMEM((count, depth), BF16), *(scratch if jobs else [])],
+        compiler_params=pltpu.CompilerParams(vmem_limit_bytes=VMEM_MORE),
         cost_estimate=SMALL,
         name="gate_up",
-    )(place, *pieces, in_vmem(w_gate), in_vmem(w_up))
+    )(
+        place,
+        list(pieces),
+        in_vmem(w_gate),
+        in_vmem(w_up),
+        [in_hbm(job[0]) for job in jobs],
+        [in_hbm(job[1]) for job in jobs],
+    )
 
 
 def own_down_kernel(side_ref, hidden_ref, weight_refs, out_ref):
@@ -427,12 +474,15 @@
     across, above_pair = swap(above, plane), swap(above, core)
     above_pair, beside = lax.optimization_barrier((above_pair, beside))
     beside_pair = swap(beside, core)
-    hidden_own, share_own = hidden_units(
-        [stack, stack_pair, above, above_pair], w_gate, w_up, place, SPARE
+    hidden_own, share_own, w_more = hidden_units(
+        [stack, stack_pair, above, above_pair],
+        w_gate,
+        w_up,
+        place,
+        SPARE,
+        [(down_codes, down_scales, half, half)],
     )
     other_peer = swap(hidden_own, plane)
-    down_scales, hidden_own = lax.optimization_barrier((down_scales, hidden_own))
-    (w_more,) = unpack_weights((down_codes, down_scales, half, half))
     across, w_more = lax.optimization_barrier((across, w_more))
     w_down = [w_down, w_more]
     hidden_other, share_other = hidden_units(

time: 65.1 us -> 66.4 us (1.020)
  starting transfers between devices: 21 us -> 23.7 us
  waiting for transfers between devices: 19.3 us -> 18.1 us
    pallas_call x3 -> x2, Pallas kernels: 12.6 us -> 9.74 us  [unpack_weights(): pl.pallas_call(functools.partial(unpack_kernel, tuple((job[2] for job in...]
    ppermute x21, starting transfers between devices: 21 us -> 23.7 us  [swap(): lax.ppermute(block, ('dp', 'expert'), [(i, i ^ offset) for i in range(dev...]
    pallas_call x2, Pallas kernels: 5.24 us -> 7.9 us  [hidden_units(): pl.pallas_call(functools.partial(hidden_kernel, tuple((job[2] for job in...]
    ppermute x21, waiting for transfers between devices: 19.3 us -> 18.1 us  [swap(): lax.ppermute(block, ('dp', 'expert'), [(i, i ^ offset) for i in range(dev...]
  transfers between devices with their start and end apart: 21 -> 21, of which waited for: 11 -> 12; matrix products, arithmetic and copies ran while one was open for 0% -> 0% of each run, Pallas kernels for 32% -> 32%
where the time goes in v7:
time: 66.4 us; the launch traced here: 66.2 us
  Pallas kernels  24.2 us (36%)
  starting transfers between devices  23.7 us (36%)
  waiting for transfers between devices  18.1 us (27%)
    ppermute x21, starting transfers between devices, swap(): lax.ppermute(block, ('dp', 'expert'), [(i, i ^ offset) for i in range(dev...  23.7 us
    ppermute x21, waiting for transfers between devices, swap(): lax.ppermute(block, ('dp', 'expert'), [(i, i ^ offset) for i in range(dev...  18.1 us
    pallas_call x2, Pallas kernels, unpack_weights(): pl.pallas_call(functools.partial(unpack_kernel, tuple((job[2] for job in...  9.74 us
    pallas_call x2, Pallas kernels, hidden_units(): pl.pallas_call(functools.partial(hidden_kernel, tuple((job[2] for job in...  7.9 us
    pallas_call x1, Pallas kernels, front(): pl.pallas_call(front_kernel, out_shape=(jax.ShapeDtypeStruct((rows, width...  2.6 us
    pallas_call x2, Pallas kernels, peer_down(): pl.pallas_call(peer_down_kernel, out_shape=(pltpu.VMEM((count // parts, w...  1.6 us
    pallas_call x2, Pallas kernels, own_down(): pl.pallas_call(own_down_kernel, out_shape=pltpu.VMEM((count, width), F32)...  1.49 us
  transfers between devices with their start and end apart: 21, of which 12 were waited for; matrix products, arithmetic and copies ran while one was open for 0% of the time, Pallas kernels for 32%

profile of v7, /device:TPU:0, one launch (start us, length us, event | category | flops | bytes accessed | tf_op | source)
XLA Modules:
  0.0 66.2 jit_solution(8904432439773840927)
XLA Ops:
  0.0 2.6 %front.1 = (bf16[8,4096]{1,0:T(8,128)(2,1)}, bf16[8,4224]{1,0:T(8,128)(2,1)}) custom-call(s32[8]{0:T(128)} %lengths_ref.1, bf16[8,4096]{1,0:T(8,128)(2,1)} %queries_ref.1, bf16[8,2,1024]{2,1,0:T(2,128)(2,1)} %new_kv_ref.1, bf16[8,32,1024]{2,1,0:T(8,128)(2,1)} %keys_ref.1, bf16[8,32,1024]{2,1,0:T(8,128)(2,1)} %values_ref.1, bf16[8,4096]{1,0:T(8,128)(2,1)} %residual_ref.1, ...), custom_call_target="tpu_custom_call" | custom-call | flops 1 | bytes 1 | tf_op jit(solution)/shard_map/front/pallas_call | solution.py:111
  2.6 5.0 %collective-permute-start.2 = (bf16[8,4224]{1,0:T(8,128)(2,1)}, bf16[8,4224]{1,0:T(8,128)(2,1)S(1)}, u32[]{:S(2)}, u32[]{:S(2)}) collective-permute-start(bf16[8,4224]{1,0:T(8,128)(2,1)} %get-tuple-element.48), channel_id=1, source_target_pairs={{0,12},{1,13},{2,14},{3,15},{4,8},{5,9},{6,10},{7,11},{8,4},{9,5},... | collective-permute-start | bytes 202760 | tf_op jit(solution)/shard_map/ppermute | solution.py:457
  7.7 0.0 collective-permute-start.1
  7.7 0.6 collective-permute-start
  8.2 5.5 %unpack_weights.2 = (bf16[4096,1024]{1,0:T(8,128)(2,1)S(1)}, bf16[2048,1024]{1,0:T(8,128)(2,1)S(1)}) custom-call(f32[1024,1024]{1,0:T(8,128)} %bitcast.11, f32[512,2048]{1,0:T(8,128)} %bitcast.8, bf16[32,1024]{1,0:T(8,128)(2,1)} %bitcast.14, bf16[16,2048]{1,0:T(8,128)(2,1)} %bitcast.12), custom_call_target="tpu_custom_call" | custom-call | flops 1 | bytes 1 | tf_op jit(solution)/shard_map/unpack_weights/pallas_call | solution.py:228
  13.8 0.0 collective-permute-done.1
  13.8 0.1 collective-permute-start.4
  13.9 1.8 %collective-permute-start.3 = (bf16[32,4224]{1,0:T(8,128)(2,1)S(1)}, bf16[32,4224]{1,0:T(8,128)(2,1)S(1)}, u32[]{:S(2)}, u32[]{:S(2)}) collective-permute-start(bf16[32,4224]{1,0:T(8,128)(2,1)S(1)} %pad_maximum_fusion.pieces_0_), channel_id=1, source_target_pairs={{0,2},{1,3},{2,0},{3,1},{4,6},{5,7},{6,4},{7,5},{8,10},{9,11},{10,... | collective-permute-start | bytes 811016 | tf_op jit(solution)/shard_map/ppermute | solution.py:457
  15.7 1.5 %collective-permute-start.6 = (bf16[32,4224]{1,0:T(8,128)(2,1)S(1)}, bf16[32,4224]{1,0:T(8,128)(2,1)S(1)}, u32[]{:S(2)}, u32[]{:S(2)}) collective-permute-start(bf16[32,4224]{1,0:T(8,128)(2,1)S(1)} %pad_maximum_fusion.pieces_0_), channel_id=1, source_target_pairs={{0,16},{1,17},{2,18},{3,19},{4,20},{5,21},{6,22},{7,23},{8,24},{9,... | collective-permute-start | bytes 811016 | tf_op jit(solution)/shard_map/ppermute | solution.py:457
  17.2 4.2 %unpack_weights.3.up_ref = bf16[4096,1024]{1,0:T(8,128)(2,1)S(1)} custom-call(f32[1024,1024]{1,0:T(8,128)} %bitcast.10, bf16[32,1024]{1,0:T(8,128)(2,1)} %bitcast.15), custom_call_target="tpu_custom_call" | custom-call | flops 1 | bytes 1 | tf_op jit(solution)/shard_map/unpack_weights/pallas_call | solution.py:228
  21.4 1.4 %collective-permute-done.3.pieces_2_ = bf16[32,4224]{1,0:T(8,128)(2,1)S(1)} collective-permute-done((bf16[32,4224]{1,0:T(8,128)(2,1)S(1)}, bf16[32,4224]{1,0:T(8,128)(2,1)S(1)}, u32[]{:S(2)}, u32[]{:S(2)}) %collective-permute-start.3) | collective-permute-done | bytes 270368 | tf_op jit(solution)/shard_map/ppermute | solution.py:457
  22.8 0.0 collective-permute-start.5
  22.8 1.7 %collective-permute-start.8 = (bf16[32,4224]{1,0:T(8,128)(2,1)S(1)}, bf16[32,4224]{1,0:T(8,128)(2,1)S(1)}, u32[]{:S(2)}, u32[]{:S(2)}) collective-permute-start(bf16[32,4224]{1,0:T(8,128)(2,1)S(1)} %collective-permute-done.3.pieces_2_), channel_id=1, source_target_pairs={{0,16},{1,17},{2,18},{3,19},{4,20},{5,21},{6,22},{7,23},{8,24},{9,... | collective-permute-start | bytes 811016 | tf_op jit(solution)/shard_map/ppermute | solution.py:457
  24.5 0.0 collective-permute-done.6.pieces_0_
  24.5 0.0 collective-permute-done.5.pieces_3_
  24.5 5.3 %gate_up.2 = (bf16[144,1024]{1,0:T(8,128)(2,1)S(1)}, f32[128,128]{1,0:T(8,128)S(1)}, bf16[2048,1024]{1,0:T(8,128)(2,1)S(1)}) custom-call(s32[1]{0:T(128)} %bitcast.1.place_ref, bf16[32,4224]{1,0:T(8,128)(2,1)S(1)} %pad_maximum_fusion.pieces_0_, bf16[32,4224]{1,0:T(8,128)(2,1)S(1)} %collective-permute-done.4.pieces_1_, ...), custom_call_target="tpu_custom_call" | custom-call | flops 1 | bytes 1 | tf_op jit(solution)/shard_map/gate_up/pallas_call | solution.py:278
  29.8 1.6 %collective-permute-start.10 = (bf16[144,1024]{1,0:T(8,128)(2,1)S(1)}, bf16[144,1024]{1,0:T(8,128)(2,1)S(1)}, u32[]{:S(2)}, u32[]{:S(2)}) collective-permute-start(bf16[144,1024]{1,0:T(8,128)(2,1)S(1)} %get-tuple-element.68.hidden_ref), channel_id=1, source_target_pairs={{0,16},{1,17},{2,18},{3,19},{4,20},{5,21},{6,22},{7,23},{8,24},{9,... | collective-permute-start | bytes 884744 | tf_op jit(solution)/shard_map/ppermute | solution.py:457
  31.4 0.0 collective-permute-start.7
  31.4 0.3 collective-permute-done.8.pieces_2_
  31.7 0.2 collective-permute-start.9
  31.9 1.0 %collective-permute-done.7.pieces_1_ = bf16[32,4224]{1,0:T(8,128)(2,1)S(1)} collective-permute-done((bf16[32,4224]{1,0:T(8,128)(2,1)S(1)}, bf16[32,4224]{1,0:T(8,128)(2,1)S(1)}, u32[]{:S(2)}, u32[]{:S(2)}) %collective-permute-start.7) | collective-permute-done | bytes 270368 | tf_op jit(solution)/shard_map/ppermute | solution.py:457
  33.0 0.4 collective-permute-done.9.pieces_3_
  33.4 2.6 %gate_up.3 = (bf16[128,1024]{1,0:T(8,128)(2,1)S(1)}, f32[128,128]{1,0:T(8,128)S(1)}) custom-call(s32[1]{0:T(128)} %bitcast.1.place_ref, bf16[32,4224]{1,0:T(8,128)(2,1)S(1)} %collective-permute-done.6.pieces_0_, bf16[32,4224]{1,0:T(8,128)(2,1)S(1)} %collective-permute-done.7.pieces_1_, bf16[32,4224]{1,0:T(8,128)(2,1)S(1)} %collective-permute-done.8.pieces_2_, ...), custom_call_target="tpu_custom_call" | custom-call | flops 1 | bytes 1 | tf_op jit(solution)/shard_map/gate_up/pallas_call | solution.py:278
  36.0 1.7 %collective-permute-start.14 = (bf16[128,1024]{1,0:T(8,128)(2,1)S(1)}, bf16[128,1024]{1,0:T(8,128)(2,1)S(1)}, u32[]{:S(2)}, u32[]{:S(2)}) collective-permute-start(bf16[128,1024]{1,0:T(8,128)(2,1)S(1)} %get-tuple-element.65.hidden_ref), channel_id=1, source_target_pairs={{0,16},{1,17},{2,18},{3,19},{4,20},{5,21},{6,22},{7,23},{8,24},{9,... | collective-permute-start | bytes 786440 | tf_op jit(solution)/shard_map/ppermute | solution.py:457
  37.7 0.7 %down_own.2.partial_ref = f32[128,2048]{1,0:T(8,128)S(1)} custom-call(s32[1]{0:T(128)} %bitcast.side_ref, bf16[128,1024]{1,0:T(8,128)(2,1)S(1)} %get-tuple-element.65.hidden_ref, bf16[2048,1024]{1,0:T(8,128)(2,1)S(1)} %get-tuple-element.66.weight_refs_0_, bf16[2048,1024]{1,0:T(8,128)(2,1)S(1)} %get-tuple-element.67.weight_refs_1_), custom_call_target="tpu_custom_call" | custom-call | flops 1 | bytes 1 | tf_op jit(solution)/shard_map/down_own/pallas_call | solution.py:325
  38.4 0.8 %collective-permute-done.10.hidden_ref = bf16[144,1024]{1,0:T(8,128)(2,1)S(1)} collective-permute-done((bf16[144,1024]{1,0:T(8,128)(2,1)S(1)}, bf16[144,1024]{1,0:T(8,128)(2,1)S(1)}, u32[]{:S(2)}, u32[]{:S(2)}) %collective-permute-start.10) | collective-permute-done | bytes 294944 | tf_op jit(solution)/shard_map/ppermute | solution.py:457
  39.3 0.8 %down_peer.2 = (bf16[64,2048]{1,0:T(8,128)(2,1)S(1)}, bf16[64,2048]{1,0:T(8,128)(2,1)S(1)}) custom-call(s32[1]{0:T(128)} %bitcast.side_ref, f32[128,2048]{1,0:T(8,128)S(1)} %down_own.2.partial_ref, bf16[144,1024]{1,0:T(8,128)(2,1)S(1)} %collective-permute-done.10.hidden_ref, bf16[2048,1024]{1,0:T(8,128)(2,1)S(1)} %get-tuple-element.66.weight_refs_0_, ...), custom_call_target="tpu_custom_call" | custom-call | flops 1 | bytes 1 | tf_op jit(solution)/shard_map/down_peer/pallas_call | solution.py:358
  40.1 1.5 %collective-permute-start.11 = (bf16[64,2048]{1,0:T(8,128)(2,1)S(1)}, bf16[64,2048]{1,0:T(8,128)(2,1)S(1)}, u32[]{:S(2)}, u32[]{:S(2)}) collective-permute-start(bf16[64,2048]{1,0:T(8,128)(2,1)S(1)} %get-tuple-element.71), channel_id=1, source_target_pairs={{0,2},{1,3},{2,0},{3,1},{4,6},{5,7},{6,4},{7,5},{8,10},{9,11},{10,... | collective-permute-start | bytes 786440 | tf_op jit(solution)/shard_map/ppermute | solution.py:457
  41.6 0.7 %down_own.3.partial_ref = f32[128,2048]{1,0:T(8,128)S(1)} custom-call(s32[1]{0:T(128)} %bitcast.side_ref, bf16[144,1024]{1,0:T(8,128)(2,1)S(1)} %get-tuple-element.68.hidden_ref, bf16[2048,1024]{1,0:T(8,128)(2,1)S(1)} %get-tuple-element.66.weight_refs_0_, bf16[2048,1024]{1,0:T(8,128)(2,1)S(1)} %get-tuple-element.67.weight_refs_1_), custom_call_target="tpu_custom_call" | custom-call | flops 1 | bytes 1 | tf_op jit(solution)/shard_map/down_own/pallas_call | solution.py:325
  42.3 2.4 %collective-permute-done.14.hidden_ref = bf16[128,1024]{1,0:T(8,128)(2,1)S(1)} collective-permute-done((bf16[128,1024]{1,0:T(8,128)(2,1)S(1)}, bf16[128,1024]{1,0:T(8,128)(2,1)S(1)}, u32[]{:S(2)}, u32[]{:S(2)}) %collective-permute-start.14) | collective-permute-done | bytes 262176 | tf_op jit(solution)/shard_map/ppermute | solution.py:457
  44.7 0.8 %down_peer.3 = (bf16[32,2048]{1,0:T(8,128)(2,1)S(1)}, bf16[32,2048]{1,0:T(8,128)(2,1)S(1)}, bf16[32,2048]{1,0:T(8,128)(2,1)S(1)}, bf16[32,2048]{1,0:T(8,128)(2,1)S(1)}) custom-call(s32[1]{0:T(128)} %bitcast.side_ref, f32[128,2048]{1,0:T(8,128)S(1)} %down_own.3.partial_ref, bf16[128,1024]{1,0:T(8,128)(2,1)S(1)} %collective-permute-done.14.hidden_ref, ...), custom_call_target="tpu_custom_call" | custom-call | flops 1 | bytes 1 | tf_op jit(solution)/shard_map/down_peer/pallas_call | solution.py:358
  45.5 0.1 collective-permute-start.16
  45.5 2.0 %collective-permute-done.11.refs_1_ = bf16[64,2048]{1,0:T(8,128)(2,1)S(1)} collective-permute-done((bf16[64,2048]{1,0:T(8,128)(2,1)S(1)}, bf16[64,2048]{1,0:T(8,128)(2,1)S(1)}, u32[]{:S(2)}, u32[]{:S(2)}) %collective-permute-start.11) | collective-permute-done | bytes 262176 | tf_op jit(solution)/shard_map/ppermute | solution.py:457
  47.6 0.1 add_and_cut.3
  47.7 0.1 collective-permute-start.12
  47.7 0.5 collective-permute-start.15
  48.3 1.5 %collective-permute-start.17 = (bf16[32,2048]{1,0:T(8,128)(2,1)S(1)}, bf16[32,2048]{1,0:T(8,128)(2,1)S(1)}, u32[]{:S(2)}, u32[]{:S(2)}) collective-permute-start(bf16[32,2048]{1,0:T(8,128)(2,1)S(1)} %add_and_cut.5), channel_id=1, source_target_pairs={{0,2},{1,3},{2,0},{3,1},{4,6},{5,7},{6,4},{7,5},{8,10},{9,11},{10,... | collective-permute-start | bytes 393224 | tf_op jit(solution)/shard_map/ppermute | solution.py:457
  49.8 1.4 %collective-permute-start.13 = (bf16[32,2048]{1,0:T(8,128)(2,1)S(1)}, bf16[32,2048]{1,0:T(8,128)(2,1)S(1)}, u32[]{:S(2)}, u32[]{:S(2)}) collective-permute-start(bf16[32,2048]{1,0:T(8,128)(2,1)S(1)} %add_and_cut.4), channel_id=1, source_target_pairs={{0,16},{1,17},{2,18},{3,19},{4,20},{5,21},{6,22},{7,23},{8,24},{9,... | collective-permute-start | bytes 393224 | tf_op jit(solution)/shard_map/ppermute | solution.py:457
  51.3 2.6 %collective-permute-done.17.refs_2_ = bf16[32,2048]{1,0:T(8,128)(2,1)S(1)} collective-permute-done((bf16[32,2048]{1,0:T(8,128)(2,1)S(1)}, bf16[32,2048]{1,0:T(8,128)(2,1)S(1)}, u32[]{:S(2)}, u32[]{:S(2)}) %collective-permute-start.17) | collective-permute-done | bytes 131104 | tf_op jit(solution)/shard_map/ppermute | solution.py:457
  53.8 1.3 %collective-permute-done.13.far_ref = bf16[32,2048]{1,0:T(8,128)(2,1)S(1)} collective-permute-done((bf16[32,2048]{1,0:T(8,128)(2,1)S(1)}, bf16[32,2048]{1,0:T(8,128)(2,1)S(1)}, u32[]{:S(2)}, u32[]{:S(2)}) %collective-permute-start.13) | collective-permute-done | bytes 131104 | tf_op jit(solution)/shard_map/ppermute | solution.py:457
  55.1 0.1 join.1
  55.1 1.3 %collective-permute-start.18 = (bf16[16,2048]{1,0:T(8,128)(2,1)S(1)}, bf16[16,2048]{1,0:T(8,128)(2,1)S(1)}, u32[]{:S(2)}, u32[]{:S(2)}) collective-permute-start(bf16[16,2048]{1,0:T(8,128)(2,1)S(1)} %get-tuple-element.80), channel_id=1, source_target_pairs={{0,4},{1,5},{2,6},{3,7},{4,0},{5,1},{6,2},{7,3},{8,12},{9,13},{10,... | collective-permute-start | bytes 196616 | tf_op jit(solution)/shard_map/ppermute | solution.py:457
  56.4 3.0 %collective-permute-start.19 = (bf16[16,2048]{1,0:T(8,128)(2,1)S(1)}, bf16[16,2048]{1,0:T(8,128)(2,1)S(1)}, u32[]{:S(2)}, u32[]{:S(2)}) collective-permute-start(bf16[16,2048]{1,0:T(8,128)(2,1)S(1)} %get-tuple-element.81), channel_id=1, source_target_pairs={{0,8},{1,9},{2,10},{3,11},{4,12},{5,13},{6,14},{7,15},{8,0},{9,1},... | collective-permute-start | bytes 196616 | tf_op jit(solution)/shard_map/ppermute | solution.py:457
  59.4 0.2 collective-permute-start.20
  59.6 0.4 collective-permute-done.18.refs_1_
  60.0 3.1 %collective-permute-done.19.refs_2_ = bf16[16,2048]{1,0:T(8,128)(2,1)S(1)} collective-permute-done((bf16[16,2048]{1,0:T(8,128)(2,1)S(1)}, bf16[16,2048]{1,0:T(8,128)(2,1)S(1)}, u32[]{:S(2)}, u32[]{:S(2)}) %collective-permute-start.19) | collective-permute-done | bytes 65568 | tf_op jit(solution)/shard_map/ppermute | solution.py:457
  63.1 2.4 %collective-permute-done.20.refs_3_ = bf16[16,2048]{1,0:T(8,128)(2,1)S(1)} collective-permute-done((bf16[16,2048]{1,0:T(8,128)(2,1)S(1)}, bf16[16,2048]{1,0:T(8,128)(2,1)S(1)}, u32[]{:S(2)}, u32[]{:S(2)}) %collective-permute-start.20) | collective-permute-done | bytes 65568 | tf_op jit(solution)/shard_map/ppermute | solution.py:457
  65.5 0.7 %finish.1 = bf16[8,4096]{1,0:T(8,128)(2,1)} custom-call(s32[1]{0:T(128)} %bitcast.side_ref, bf16[8,4096]{1,0:T(8,128)(2,1)S(1)} %copy-done, bf16[16,2048]{1,0:T(8,128)(2,1)S(1)} %get-tuple-element.79.refs_0_, bf16[16,2048]{1,0:T(8,128)(2,1)S(1)} %collective-permute-done.18.refs_1_, bf16[16,2048]{1,0:T(8,128)(2,1)S(1)} %collective-permute-done.19.refs_2_, ...), custom_call_target="tpu_custom_call" | custom-call | tf_op jit(solution)/shard_map/finish/pallas_call | solution.py:436
  (13 shorter events, 0.1 us)
Async XLA Ops:
  2.6 11.2 %collective-permute-start.2 = (bf16[8,4224]{1,0:T(8,128)(2,1)}, bf16[8,4224]{1,0:T(8,128)(2,1)S(1)}, u32[]{:S(2)}, u32[]{:S(2)}) collective-permute-start(bf16[8,4224]{1,0:T(8,128)(2,1)} %get-tuple-element.48), channel_id=1, source_target_pairs={{0,12},{1,13},{2,14},{3,15},{4,8},{5,9},{6,10},{7,11},{8,4},{9,5},... | collective-permute-start | bytes 202760 | tf_op jit(solution)/shard_map/ppermute | solution.py:457
  7.7 6.1 %collective-permute-start.1 = (bf16[8,4224]{1,0:T(8,128)(2,1)}, bf16[8,4224]{1,0:T(8,128)(2,1)S(1)}, u32[]{:S(2)}, u32[]{:S(2)}) collective-permute-start(bf16[8,4224]{1,0:T(8,128)(2,1)} %get-tuple-element.48), channel_id=1, source_target_pairs={{0,8},{1,9},{2,10},{3,11},{4,12},{5,13},{6,14},{7,15},{8,0},{9,1},... | collective-permute-start | bytes 202760 | tf_op jit(solution)/shard_map/ppermute | solution.py:457
  7.7 6.1 %collective-permute-start = (bf16[8,4224]{1,0:T(8,128)(2,1)}, bf16[8,4224]{1,0:T(8,128)(2,1)S(1)}, u32[]{:S(2)}, u32[]{:S(2)}) collective-permute-start(bf16[8,4224]{1,0:T(8,128)(2,1)} %get-tuple-element.48), channel_id=1, source_target_pairs={{0,4},{1,5},{2,6},{3,7},{4,0},{5,1},{6,2},{7,3},{8,12},{9,13},{10,... | collective-permute-start | bytes 202760 | tf_op jit(solution)/shard_map/ppermute | solution.py:457
  8.2 5.6 %copy-start.1 = (bf16[8,4224]{1,0:T(8,128)(2,1)S(1)}, bf16[8,4224]{1,0:T(8,128)(2,1)}, u32[]{:S(2)}) copy-start(bf16[8,4224]{1,0:T(8,128)(2,1)} %get-tuple-element.48) | copy-start | bytes 202756
  13.8 7.6 %collective-permute-start.4 = (bf16[32,4224]{1,0:T(8,128)(2,1)S(1)}, bf16[32,4224]{1,0:T(8,128)(2,1)S(1)}, u32[]{:S(2)}, u32[]{:S(2)}) collective-permute-start(bf16[32,4224]{1,0:T(8,128)(2,1)S(1)} %pad_maximum_fusion.pieces_0_), channel_id=1, source_target_pairs={{0,1},{1,0},{2,3},{3,2},{4,5},{5,4},{6,7},{7,6},{8,9},{9,8},{10,11... | collective-permute-start | bytes 811016 | tf_op jit(solution)/shard_map/ppermute | solution.py:457
  13.9 8.9 %collective-permute-start.3 = (bf16[32,4224]{1,0:T(8,128)(2,1)S(1)}, bf16[32,4224]{1,0:T(8,128)(2,1)S(1)}, u32[]{:S(2)}, u32[]{:S(2)}) collective-permute-start(bf16[32,4224]{1,0:T(8,128)(2,1)S(1)} %pad_maximum_fusion.pieces_0_), channel_id=1, source_target_pairs={{0,2},{1,3},{2,0},{3,1},{4,6},{5,7},{6,4},{7,5},{8,10},{9,11},{10,... | collective-permute-start | bytes 811016 | tf_op jit(solution)/shard_map/ppermute | solution.py:457
  15.7 8.8 %collective-permute-start.6 = (bf16[32,4224]{1,0:T(8,128)(2,1)S(1)}, bf16[32,4224]{1,0:T(8,128)(2,1)S(1)}, u32[]{:S(2)}, u32[]{:S(2)}) collective-permute-start(bf16[32,4224]{1,0:T(8,128)(2,1)S(1)} %pad_maximum_fusion.pieces_0_), channel_id=1, source_target_pairs={{0,16},{1,17},{2,18},{3,19},{4,20},{5,21},{6,22},{7,23},{8,24},{9,... | collective-permute-start | bytes 811016 | tf_op jit(solution)/shard_map/ppermute | solution.py:457
  22.8 1.7 %collective-permute-start.5 = (bf16[32,4224]{1,0:T(8,128)(2,1)S(1)}, bf16[32,4224]{1,0:T(8,128)(2,1)S(1)}, u32[]{:S(2)}, u32[]{:S(2)}) collective-permute-start(bf16[32,4224]{1,0:T(8,128)(2,1)S(1)} %collective-permute-done.3.pieces_2_), channel_id=1, source_target_pairs={{0,1},{1,0},{2,3},{3,2},{4,5},{5,4},{6,7},{7,6},{8,9},{9,8},{10,11... | collective-permute-start | bytes 811016 | tf_op jit(solution)/shard_map/ppermute | solution.py:457
  22.8 8.9 %collective-permute-start.8 = (bf16[32,4224]{1,0:T(8,128)(2,1)S(1)}, bf16[32,4224]{1,0:T(8,128)(2,1)S(1)}, u32[]{:S(2)}, u32[]{:S(2)}) collective-permute-start(bf16[32,4224]{1,0:T(8,128)(2,1)S(1)} %collective-permute-done.3.pieces_2_), channel_id=1, source_target_pairs={{0,16},{1,17},{2,18},{3,19},{4,20},{5,21},{6,22},{7,23},{8,24},{9,... | collective-permute-start | bytes 811016 | tf_op jit(solution)/shard_map/ppermute | solution.py:457
  29.8 9.4 %collective-permute-start.10 = (bf16[144,1024]{1,0:T(8,128)(2,1)S(1)}, bf16[144,1024]{1,0:T(8,128)(2,1)S(1)}, u32[]{:S(2)}, u32[]{:S(2)}) collective-permute-start(bf16[144,1024]{1,0:T(8,128)(2,1)S(1)} %get-tuple-element.68.hidden_ref), channel_id=1, source_target_pairs={{0,16},{1,17},{2,18},{3,19},{4,20},{5,21},{6,22},{7,23},{8,24},{9,... | collective-permute-start | bytes 884744 | tf_op jit(solution)/shard_map/ppermute | solution.py:457
  31.4 1.5 %collective-permute-start.7 = (bf16[32,4224]{1,0:T(8,128)(2,1)S(1)}, bf16[32,4224]{1,0:T(8,128)(2,1)S(1)}, u32[]{:S(2)}, u32[]{:S(2)}) collective-permute-start(bf16[32,4224]{1,0:T(8,128)(2,1)S(1)} %collective-permute-done.6.pieces_0_), channel_id=1, source_target_pairs={{0,1},{1,0},{2,3},{3,2},{4,5},{5,4},{6,7},{7,6},{8,9},{9,8},{10,11... | collective-permute-start | bytes 811016 | tf_op jit(solution)/shard_map/ppermute | solution.py:457
  31.7 1.6 %collective-permute-start.9 = (bf16[32,4224]{1,0:T(8,128)(2,1)S(1)}, bf16[32,4224]{1,0:T(8,128)(2,1)S(1)}, u32[]{:S(2)}, u32[]{:S(2)}) collective-permute-start(bf16[32,4224]{1,0:T(8,128)(2,1)S(1)} %collective-permute-done.8.pieces_2_), channel_id=1, source_target_pairs={{0,1},{1,0},{2,3},{3,2},{4,5},{5,4},{6,7},{7,6},{8,9},{9,8},{10,11... | collective-permute-start | bytes 811016 | tf_op jit(solution)/shard_map/ppermute | solution.py:457
  36.0 8.7 %collective-permute-start.14 = (bf16[128,1024]{1,0:T(8,128)(2,1)S(1)}, bf16[128,1024]{1,0:T(8,128)(2,1)S(1)}, u32[]{:S(2)}, u32[]{:S(2)}) collective-permute-start(bf16[128,1024]{1,0:T(8,128)(2,1)S(1)} %get-tuple-element.65.hidden_ref), channel_id=1, source_target_pairs={{0,16},{1,17},{2,18},{3,19},{4,20},{5,21},{6,22},{7,23},{8,24},{9,... | collective-permute-start | bytes 786440 | tf_op jit(solution)/shard_map/ppermute | solution.py:457
  40.1 7.5 %collective-permute-start.11 = (bf16[64,2048]{1,0:T(8,128)(2,1)S(1)}, bf16[64,2048]{1,0:T(8,128)(2,1)S(1)}, u32[]{:S(2)}, u32[]{:S(2)}) collective-permute-start(bf16[64,2048]{1,0:T(8,128)(2,1)S(1)} %get-tuple-element.71), channel_id=1, source_target_pairs={{0,2},{1,3},{2,0},{3,1},{4,6},{5,7},{6,4},{7,5},{8,10},{9,11},{10,... | collective-permute-start | bytes 786440 | tf_op jit(solution)/shard_map/ppermute | solution.py:457
  44.7 20.8 %copy-start = (bf16[8,4096]{1,0:T(8,128)(2,1)S(1)}, bf16[8,4096]{1,0:T(8,128)(2,1)}, u32[]{:S(2)}) copy-start(bf16[8,4096]{1,0:T(8,128)(2,1)} %get-tuple-element.46.mixed_ref) | copy-start | bytes 196612
  45.5 2.8 %collective-permute-start.16 = (bf16[32,2048]{1,0:T(8,128)(2,1)S(1)}, bf16[32,2048]{1,0:T(8,128)(2,1)S(1)}, u32[]{:S(2)}, u32[]{:S(2)}) collective-permute-start(bf16[32,2048]{1,0:T(8,128)(2,1)S(1)} %get-tuple-element.78), channel_id=1, source_target_pairs={{0,1},{1,0},{2,3},{3,2},{4,5},{5,4},{6,7},{7,6},{8,9},{9,8},{10,11... | collective-permute-start | bytes 393224 | tf_op jit(solution)/shard_map/ppermute | solution.py:457
  47.7 2.1 %collective-permute-start.12 = (bf16[32,2048]{1,0:T(8,128)(2,1)S(1)}, bf16[32,2048]{1,0:T(8,128)(2,1)S(1)}, u32[]{:S(2)}, u32[]{:S(2)}) collective-permute-start(bf16[32,2048]{1,0:T(8,128)(2,1)S(1)} %get-tuple-element.73), channel_id=1, source_target_pairs={{0,1},{1,0},{2,3},{3,2},{4,5},{5,4},{6,7},{7,6},{8,9},{9,8},{10,11... | collective-permute-start | bytes 393224 | tf_op jit(solution)/shard_map/ppermute | solution.py:457
  47.7 3.5 %collective-permute-start.15 = (bf16[32,2048]{1,0:T(8,128)(2,1)S(1)}, bf16[32,2048]{1,0:T(8,128)(2,1)S(1)}, u32[]{:S(2)}, u32[]{:S(2)}) collective-permute-start(bf16[32,2048]{1,0:T(8,128)(2,1)S(1)} %get-tuple-element.76), channel_id=1, source_target_pairs={{0,1},{1,0},{2,3},{3,2},{4,5},{5,4},{6,7},{7,6},{8,9},{9,8},{10,11... | collective-permute-start | bytes 393224 | tf_op jit(solution)/shard_map/ppermute | solution.py:457
  48.3 5.5 %collective-permute-start.17 = (bf16[32,2048]{1,0:T(8,128)(2,1)S(1)}, bf16[32,2048]{1,0:T(8,128)(2,1)S(1)}, u32[]{:S(2)}, u32[]{:S(2)}) collective-permute-start(bf16[32,2048]{1,0:T(8,128)(2,1)S(1)} %add_and_cut.5), channel_id=1, source_target_pairs={{0,2},{1,3},{2,0},{3,1},{4,6},{5,7},{6,4},{7,5},{8,10},{9,11},{10,... | collective-permute-start | bytes 393224 | tf_op jit(solution)/shard_map/ppermute | solution.py:457
  49.8 5.3 %collective-permute-start.13 = (bf16[32,2048]{1,0:T(8,128)(2,1)S(1)}, bf16[32,2048]{1,0:T(8,128)(2,1)S(1)}, u32[]{:S(2)}, u32[]{:S(2)}) collective-permute-start(bf16[32,2048]{1,0:T(8,128)(2,1)S(1)} %add_and_cut.4), channel_id=1, source_target_pairs={{0,16},{1,17},{2,18},{3,19},{4,20},{5,21},{6,22},{7,23},{8,24},{9,... | collective-permute-start | bytes 393224 | tf_op jit(solution)/shard_map/ppermute | solution.py:457
  55.1 4.9 %collective-permute-start.18 = (bf16[16,2048]{1,0:T(8,128)(2,1)S(1)}, bf16[16,2048]{1,0:T(8,128)(2,1)S(1)}, u32[]{:S(2)}, u32[]{:S(2)}) collective-permute-start(bf16[16,2048]{1,0:T(8,128)(2,1)S(1)} %get-tuple-element.80), channel_id=1, source_target_pairs={{0,4},{1,5},{2,6},{3,7},{4,0},{5,1},{6,2},{7,3},{8,12},{9,13},{10,... | collective-permute-start | bytes 196616 | tf_op jit(solution)/shard_map/ppermute | solution.py:457
  56.4 6.7 %collective-permute-start.19 = (bf16[16,2048]{1,0:T(8,128)(2,1)S(1)}, bf16[16,2048]{1,0:T(8,128)(2,1)S(1)}, u32[]{:S(2)}, u32[]{:S(2)}) collective-permute-start(bf16[16,2048]{1,0:T(8,128)(2,1)S(1)} %get-tuple-element.81), channel_id=1, source_target_pairs={{0,8},{1,9},{2,10},{3,11},{4,12},{5,13},{6,14},{7,15},{8,0},{9,1},... | collective-permute-start | bytes 196616 | tf_op jit(solution)/shard_map/ppermute | solution.py:457
  59.4 6.1 %collective-permute-start.20 = (bf16[16,2048]{1,0:T(8,128)(2,1)S(1)}, bf16[16,2048]{1,0:T(8,128)(2,1)S(1)}, u32[]{:S(2)}, u32[]{:S(2)}) collective-permute-start(bf16[16,2048]{1,0:T(8,128)(2,1)S(1)} %get-tuple-element.82), channel_id=1, source_target_pairs={{0,12},{1,13},{2,14},{3,15},{4,8},{5,9},{6,10},{7,11},{8,4},{9,5},... | collective-permute-start | bytes 196616 | tf_op jit(solution)/shard_map/ppermute | solution.py:457

commit v8 on v4

--- a/solution.py
+++ b/solution.py
@@ -108,12 +108,10 @@
 def front(queries, new_kv, keys, values, lengths, residual, gain, routes, weights, extra):
     rows, width = queries.shape
     vmem = pl.BlockSpec(memory_space=pltpu.VMEM)
+    shape = pltpu.VMEM if extra else jax.ShapeDtypeStruct
     return pl.pallas_call(
         front_kernel,
-        out_shape=(
-            jax.ShapeDtypeStruct((rows, width), BF16),
-            jax.ShapeDtypeStruct((rows, width + extra), BF16),
-        ),
+        out_shape=(shape((rows, width), BF16), shape((rows, width + extra), BF16)),
         in_specs=[pl.BlockSpec(memory_space=pltpu.SMEM)] + [vmem] * 8,
         out_specs=(vmem, vmem),
         compiler_params=pltpu.CompilerParams(vmem_limit_bytes=VMEM_LIMIT),

time: 65.1 us -> 64.5 us (level)
  transfers between devices with their start and end apart: 21 -> 21, of which waited for: 11 -> 10; matrix products, arithmetic and copies ran while one was open for 0% -> 0% of each run, Pallas kernels for 32% -> 33%
where the time goes in v8:
time: 64.5 us; the launch traced here: 64.2 us
  Pallas kernels  23.7 us (37%)
  starting transfers between devices  21.6 us (33%)
  waiting for transfers between devices  18.7 us (29%)
    ppermute x21, starting transfers between devices, swap(): lax.ppermute(block, ('dp', 'expert'), [(i, i ^ offset) for i in range(dev...  21.6 us
    ppermute x21, waiting for transfers between devices, swap(): lax.ppermute(block, ('dp', 'expert'), [(i, i ^ offset) for i in range(dev...  18.7 us
    pallas_call x3, Pallas kernels, unpack_weights(): pl.pallas_call(functools.partial(unpack_kernel, tuple((job[2] for job in...  12.6 us
    pallas_call x2, Pallas kernels, hidden_units(): pl.pallas_call(hidden_kernel, out_shape=(pltpu.VMEM((count + spare, width...  5.23 us
    pallas_call x1, Pallas kernels, front(): pl.pallas_call(front_kernel, out_shape=(shape((rows, width), BF16), shape...  1.97 us
    pallas_call x2, Pallas kernels, peer_down(): pl.pallas_call(peer_down_kernel, out_shape=(pltpu.VMEM((count // parts, w...  1.58 us
    pallas_call x2, Pallas kernels, own_down(): pl.pallas_call(own_down_kernel, out_shape=pltpu.VMEM((count, width), F32)...  1.46 us
  transfers between devices with their start and end apart: 21, of which 10 were waited for; matrix products, arithmetic and copies ran while one was open for 0% of the time, Pallas kernels for 33%

profile of v8, /device:TPU:0, one launch (start us, length us, event | category | flops | bytes accessed | tf_op | source)
XLA Modules:
  0.0 64.2 jit_solution(12645824461318569496)
XLA Ops:
  0.0 2.0 %front.1 = (bf16[8,4096]{1,0:T(8,128)(2,1)S(1)}, bf16[8,4224]{1,0:T(8,128)(2,1)S(1)}) custom-call(s32[8]{0:T(128)} %lengths_ref.1, bf16[8,4096]{1,0:T(8,128)(2,1)} %queries_ref.1, bf16[8,2,1024]{2,1,0:T(2,128)(2,1)} %new_kv_ref.1, bf16[8,32,1024]{2,1,0:T(8,128)(2,1)} %keys_ref.1, bf16[8,32,1024]{2,1,0:T(8,128)(2,1)} %values_ref.1, ...), custom_call_target="tpu_custom_call" | custom-call | flops 1 | bytes 1 | tf_op jit(solution)/shard_map/front/pallas_call | solution.py:112
  2.0 3.1 %collective-permute-start = (bf16[8,4224]{1,0:T(8,128)(2,1)S(1)}, bf16[8,4224]{1,0:T(8,128)(2,1)S(1)}, u32[]{:S(2)}, u32[]{:S(2)}) collective-permute-start(bf16[8,4224]{1,0:T(8,128)(2,1)S(1)} %get-tuple-element.49), channel_id=1, source_target_pairs={{0,4},{1,5},{2,6},{3,7},{4,0},{5,1},{6,2},{7,3},{8,12},{9,13},{10,... | collective-permute-start | bytes 202760 | tf_op jit(solution)/shard_map/ppermute | solution.py:408
  5.1 2.6 %collective-permute-start.1 = (bf16[8,4224]{1,0:T(8,128)(2,1)S(1)}, bf16[8,4224]{1,0:T(8,128)(2,1)S(1)}, u32[]{:S(2)}, u32[]{:S(2)}) collective-permute-start(bf16[8,4224]{1,0:T(8,128)(2,1)S(1)} %get-tuple-element.49), channel_id=1, source_target_pairs={{0,8},{1,9},{2,10},{3,11},{4,12},{5,13},{6,14},{7,15},{8,0},{9,1},... | collective-permute-start | bytes 202760 | tf_op jit(solution)/shard_map/ppermute | solution.py:408
  7.7 5.5 %unpack_weights.3 = (bf16[4096,1024]{1,0:T(8,128)(2,1)S(1)}, bf16[2048,1024]{1,0:T(8,128)(2,1)S(1)}) custom-call(f32[1024,1024]{1,0:T(8,128)} %bitcast.11, f32[512,2048]{1,0:T(8,128)} %bitcast.8, bf16[32,1024]{1,0:T(8,128)(2,1)} %bitcast.14, bf16[16,2048]{1,0:T(8,128)(2,1)} %bitcast.12), custom_call_target="tpu_custom_call" | custom-call | flops 1 | bytes 1 | tf_op jit(solution)/shard_map/unpack_weights/pallas_call | solution.py:202
  13.2 0.0 collective-permute-done.1
  13.2 0.7 %collective-permute-done.2 = bf16[8,4224]{1,0:T(8,128)(2,1)S(1)} collective-permute-done((bf16[8,4224]{1,0:T(8,128)(2,1)S(1)}, bf16[8,4224]{1,0:T(8,128)(2,1)S(1)}, u32[]{:S(2)}, u32[]{:S(2)}) %collective-permute-start.2) | collective-permute-done | bytes 67616 | tf_op jit(solution)/shard_map/ppermute | solution.py:408
  13.9 1.6 %collective-permute-start.3 = (bf16[32,4224]{1,0:T(8,128)(2,1)S(1)}, bf16[32,4224]{1,0:T(8,128)(2,1)S(1)}, u32[]{:S(2)}, u32[]{:S(2)}) collective-permute-start(bf16[32,4224]{1,0:T(8,128)(2,1)S(1)} %pad_maximum_fusion.refs_0_), channel_id=1, source_target_pairs={{0,2},{1,3},{2,0},{3,1},{4,6},{5,7},{6,4},{7,5},{8,10},{9,11},{10,... | collective-permute-start | bytes 811016 | tf_op jit(solution)/shard_map/ppermute | solution.py:408
  15.5 0.0 collective-permute-start.4
  15.5 1.5 %collective-permute-start.6 = (bf16[32,4224]{1,0:T(8,128)(2,1)S(1)}, bf16[32,4224]{1,0:T(8,128)(2,1)S(1)}, u32[]{:S(2)}, u32[]{:S(2)}) collective-permute-start(bf16[32,4224]{1,0:T(8,128)(2,1)S(1)} %pad_maximum_fusion.refs_0_), channel_id=1, source_target_pairs={{0,16},{1,17},{2,18},{3,19},{4,20},{5,21},{6,22},{7,23},{8,24},{9,... | collective-permute-start | bytes 811016 | tf_op jit(solution)/shard_map/ppermute | solution.py:408
  17.0 4.2 %unpack_weights.4.refs_5_ = bf16[4096,1024]{1,0:T(8,128)(2,1)S(1)} custom-call(f32[1024,1024]{1,0:T(8,128)} %bitcast.10, bf16[32,1024]{1,0:T(8,128)(2,1)} %bitcast.15), custom_call_target="tpu_custom_call" | custom-call | flops 1 | bytes 1 | tf_op jit(solution)/shard_map/unpack_weights/pallas_call | solution.py:202
  21.2 0.0 collective-permute-done.3.refs_2_
  21.2 0.3 collective-permute-start.5
  21.5 1.0 %collective-permute-start.8 = (bf16[32,4224]{1,0:T(8,128)(2,1)S(1)}, bf16[32,4224]{1,0:T(8,128)(2,1)S(1)}, u32[]{:S(2)}, u32[]{:S(2)}) collective-permute-start(bf16[32,4224]{1,0:T(8,128)(2,1)S(1)} %collective-permute-done.3.refs_2_), channel_id=1, source_target_pairs={{0,16},{1,17},{2,18},{3,19},{4,20},{5,21},{6,22},{7,23},{8,24},{9,... | collective-permute-start | bytes 811016 | tf_op jit(solution)/shard_map/ppermute | solution.py:408
  22.5 1.9 %collective-permute-done.6.refs_0_ = bf16[32,4224]{1,0:T(8,128)(2,1)S(1)} collective-permute-done((bf16[32,4224]{1,0:T(8,128)(2,1)S(1)}, bf16[32,4224]{1,0:T(8,128)(2,1)S(1)}, u32[]{:S(2)}, u32[]{:S(2)}) %collective-permute-start.6) | collective-permute-done | bytes 270368 | tf_op jit(solution)/shard_map/ppermute | solution.py:408
  24.4 0.0 collective-permute-done.5.refs_3_
  24.4 2.6 %gate_up.2 = (bf16[144,1024]{1,0:T(8,128)(2,1)S(1)}, f32[128,128]{1,0:T(8,128)S(1)}) custom-call(s32[1]{0:T(128)} %bitcast.1.place_ref, bf16[32,4224]{1,0:T(8,128)(2,1)S(1)} %pad_maximum_fusion.refs_0_, bf16[32,4224]{1,0:T(8,128)(2,1)S(1)} %collective-permute-done.4.refs_1_, bf16[32,4224]{1,0:T(8,128)(2,1)S(1)} %collective-permute-done.3.refs_2_, ...), custom_call_target="tpu_custom_call" | custom-call | flops 1 | bytes 1 | tf_op jit(solution)/shard_map/gate_up/pallas_call | solution.py:247
  27.0 1.8 %collective-permute-start.10 = (bf16[144,1024]{1,0:T(8,128)(2,1)S(1)}, bf16[144,1024]{1,0:T(8,128)(2,1)S(1)}, u32[]{:S(2)}, u32[]{:S(2)}) collective-permute-start(bf16[144,1024]{1,0:T(8,128)(2,1)S(1)} %get-tuple-element.75.hidden_ref), channel_id=1, source_target_pairs={{0,16},{1,17},{2,18},{3,19},{4,20},{5,21},{6,22},{7,23},{8,24},{9,... | collective-permute-start | bytes 884744 | tf_op jit(solution)/shard_map/ppermute | solution.py:408
  28.8 0.0 collective-permute-start.7
  28.8 2.9 %unpack_weights.5.weight_refs_1_ = bf16[2048,1024]{1,0:T(8,128)(2,1)S(1)} custom-call(f32[512,2048]{1,0:T(8,128)} %bitcast.9, bf16[16,2048]{1,0:T(8,128)(2,1)} %bitcast.13), custom_call_target="tpu_custom_call" | custom-call | flops 1 | bytes 1 | tf_op jit(solution)/shard_map/unpack_weights/pallas_call | solution.py:202
  31.6 0.0 collective-permute-done.8.refs_2_
  31.6 0.6 collective-permute-start.9
  32.2 0.0 collective-permute-done.7.refs_1_
  32.2 1.2 %collective-permute-done.9.refs_3_ = bf16[32,4224]{1,0:T(8,128)(2,1)S(1)} collective-permute-done((bf16[32,4224]{1,0:T(8,128)(2,1)S(1)}, bf16[32,4224]{1,0:T(8,128)(2,1)S(1)}, u32[]{:S(2)}, u32[]{:S(2)}) %collective-permute-start.9) | collective-permute-done | bytes 270368 | tf_op jit(solution)/shard_map/ppermute | solution.py:408
  33.4 2.6 %gate_up.3 = (bf16[128,1024]{1,0:T(8,128)(2,1)S(1)}, f32[128,128]{1,0:T(8,128)S(1)}) custom-call(s32[1]{0:T(128)} %bitcast.1.place_ref, bf16[32,4224]{1,0:T(8,128)(2,1)S(1)} %collective-permute-done.6.refs_0_, bf16[32,4224]{1,0:T(8,128)(2,1)S(1)} %collective-permute-done.7.refs_1_, bf16[32,4224]{1,0:T(8,128)(2,1)S(1)} %collective-permute-done.8.refs_2_, ...), custom_call_target="tpu_custom_call" | custom-call | flops 1 | bytes 1 | tf_op jit(solution)/shard_map/gate_up/pallas_call | solution.py:247
  36.0 0.4 collective-permute-start.14
  36.4 0.7 %down_own.2.partial_ref = f32[128,2048]{1,0:T(8,128)S(1)} custom-call(s32[1]{0:T(128)} %bitcast.side_ref, bf16[128,1024]{1,0:T(8,128)(2,1)S(1)} %get-tuple-element.67.hidden_ref, bf16[2048,1024]{1,0:T(8,128)(2,1)S(1)} %get-tuple-element.68.weight_refs_0_, bf16[2048,1024]{1,0:T(8,128)(2,1)S(1)} %unpack_weights.5.weight_refs_1_), custom_call_target="tpu_custom_call" | custom-call | flops 1 | bytes 1 | tf_op jit(solution)/shard_map/down_own/pallas_call | solution.py:276
  37.2 0.8 %down_peer.2 = (bf16[64,2048]{1,0:T(8,128)(2,1)S(1)}, bf16[64,2048]{1,0:T(8,128)(2,1)S(1)}) custom-call(s32[1]{0:T(128)} %bitcast.side_ref, f32[128,2048]{1,0:T(8,128)S(1)} %down_own.2.partial_ref, bf16[144,1024]{1,0:T(8,128)(2,1)S(1)} %collective-permute-done.10.hidden_ref, bf16[2048,1024]{1,0:T(8,128)(2,1)S(1)} %get-tuple-element.68.weight_refs_0_, ...), custom_call_target="tpu_custom_call" | custom-call | flops 1 | bytes 1 | tf_op jit(solution)/shard_map/down_peer/pallas_call | solution.py:309
  38.0 1.2 %collective-permute-start.11 = (bf16[64,2048]{1,0:T(8,128)(2,1)S(1)}, bf16[64,2048]{1,0:T(8,128)(2,1)S(1)}, u32[]{:S(2)}, u32[]{:S(2)}) collective-permute-start(bf16[64,2048]{1,0:T(8,128)(2,1)S(1)} %get-tuple-element.72), channel_id=1, source_target_pairs={{0,2},{1,3},{2,0},{3,1},{4,6},{5,7},{6,4},{7,5},{8,10},{9,11},{10,... | collective-permute-start | bytes 786440 | tf_op jit(solution)/shard_map/ppermute | solution.py:408
  39.1 0.7 %down_own.3.partial_ref = f32[128,2048]{1,0:T(8,128)S(1)} custom-call(s32[1]{0:T(128)} %bitcast.side_ref, bf16[144,1024]{1,0:T(8,128)(2,1)S(1)} %get-tuple-element.75.hidden_ref, bf16[2048,1024]{1,0:T(8,128)(2,1)S(1)} %get-tuple-element.68.weight_refs_0_, bf16[2048,1024]{1,0:T(8,128)(2,1)S(1)} %unpack_weights.5.weight_refs_1_), custom_call_target="tpu_custom_call" | custom-call | flops 1 | bytes 1 | tf_op jit(solution)/shard_map/down_own/pallas_call | solution.py:276
  39.8 4.8 %collective-permute-done.14.hidden_ref = bf16[128,1024]{1,0:T(8,128)(2,1)S(1)} collective-permute-done((bf16[128,1024]{1,0:T(8,128)(2,1)S(1)}, bf16[128,1024]{1,0:T(8,128)(2,1)S(1)}, u32[]{:S(2)}, u32[]{:S(2)}) %collective-permute-start.14) | collective-permute-done | bytes 262176 | tf_op jit(solution)/shard_map/ppermute | solution.py:408
  44.7 0.8 %down_peer.3 = (bf16[32,2048]{1,0:T(8,128)(2,1)S(1)}, bf16[32,2048]{1,0:T(8,128)(2,1)S(1)}, bf16[32,2048]{1,0:T(8,128)(2,1)S(1)}, bf16[32,2048]{1,0:T(8,128)(2,1)S(1)}) custom-call(s32[1]{0:T(128)} %bitcast.side_ref, f32[128,2048]{1,0:T(8,128)S(1)} %down_own.3.partial_ref, bf16[128,1024]{1,0:T(8,128)(2,1)S(1)} %collective-permute-done.14.hidden_ref, ...), custom_call_target="tpu_custom_call" | custom-call | flops 1 | bytes 1 | tf_op jit(solution)/shard_map/down_peer/pallas_call | solution.py:309
  45.5 0.1 collective-permute-start.16
  45.5 0.8 %collective-permute-done.11.refs_1_ = bf16[64,2048]{1,0:T(8,128)(2,1)S(1)} collective-permute-done((bf16[64,2048]{1,0:T(8,128)(2,1)S(1)}, bf16[64,2048]{1,0:T(8,128)(2,1)S(1)}, u32[]{:S(2)}, u32[]{:S(2)}) %collective-permute-start.11) | collective-permute-done | bytes 262176 | tf_op jit(solution)/shard_map/ppermute | solution.py:408
  46.3 0.1 add_and_cut.3
  46.4 0.1 collective-permute-start.12
  46.5 0.5 collective-permute-start.15
  47.0 0.9 %collective-permute-start.17 = (bf16[32,2048]{1,0:T(8,128)(2,1)S(1)}, bf16[32,2048]{1,0:T(8,128)(2,1)S(1)}, u32[]{:S(2)}, u32[]{:S(2)}) collective-permute-start(bf16[32,2048]{1,0:T(8,128)(2,1)S(1)} %add_and_cut.5), channel_id=1, source_target_pairs={{0,2},{1,3},{2,0},{3,1},{4,6},{5,7},{6,4},{7,5},{8,10},{9,11},{10,... | collective-permute-start | bytes 393224 | tf_op jit(solution)/shard_map/ppermute | solution.py:408
  48.0 1.6 %collective-permute-start.13 = (bf16[32,2048]{1,0:T(8,128)(2,1)S(1)}, bf16[32,2048]{1,0:T(8,128)(2,1)S(1)}, u32[]{:S(2)}, u32[]{:S(2)}) collective-permute-start(bf16[32,2048]{1,0:T(8,128)(2,1)S(1)} %add_and_cut.4), channel_id=1, source_target_pairs={{0,16},{1,17},{2,18},{3,19},{4,20},{5,21},{6,22},{7,23},{8,24},{9,... | collective-permute-start | bytes 393224 | tf_op jit(solution)/shard_map/ppermute | solution.py:408
  49.6 2.9 %collective-permute-done.17.refs_2_ = bf16[32,2048]{1,0:T(8,128)(2,1)S(1)} collective-permute-done((bf16[32,2048]{1,0:T(8,128)(2,1)S(1)}, bf16[32,2048]{1,0:T(8,128)(2,1)S(1)}, u32[]{:S(2)}, u32[]{:S(2)}) %collective-permute-start.17) | collective-permute-done | bytes 131104 | tf_op jit(solution)/shard_map/ppermute | solution.py:408
  52.5 0.9 %collective-permute-done.13.far_ref = bf16[32,2048]{1,0:T(8,128)(2,1)S(1)} collective-permute-done((bf16[32,2048]{1,0:T(8,128)(2,1)S(1)}, bf16[32,2048]{1,0:T(8,128)(2,1)S(1)}, u32[]{:S(2)}, u32[]{:S(2)}) %collective-permute-start.13) | collective-permute-done | bytes 131104 | tf_op jit(solution)/shard_map/ppermute | solution.py:408
  53.5 0.1 join.1
  53.5 0.7 %collective-permute-start.18 = (bf16[16,2048]{1,0:T(8,128)(2,1)S(1)}, bf16[16,2048]{1,0:T(8,128)(2,1)S(1)}, u32[]{:S(2)}, u32[]{:S(2)}) collective-permute-start(bf16[16,2048]{1,0:T(8,128)(2,1)S(1)} %get-tuple-element.82), channel_id=1, source_target_pairs={{0,4},{1,5},{2,6},{3,7},{4,0},{5,1},{6,2},{7,3},{8,12},{9,13},{10,... | collective-permute-start | bytes 196616 | tf_op jit(solution)/shard_map/ppermute | solution.py:408
  54.2 3.2 %collective-permute-start.19 = (bf16[16,2048]{1,0:T(8,128)(2,1)S(1)}, bf16[16,2048]{1,0:T(8,128)(2,1)S(1)}, u32[]{:S(2)}, u32[]{:S(2)}) collective-permute-start(bf16[16,2048]{1,0:T(8,128)(2,1)S(1)} %get-tuple-element.83), channel_id=1, source_target_pairs={{0,8},{1,9},{2,10},{3,11},{4,12},{5,13},{6,14},{7,15},{8,0},{9,1},... | collective-permute-start | bytes 196616 | tf_op jit(solution)/shard_map/ppermute | solution.py:408
  57.5 0.5 collective-permute-start.20
  58.0 0.2 collective-permute-done.18.refs_1_
  58.2 3.0 %collective-permute-done.19.refs_2_ = bf16[16,2048]{1,0:T(8,128)(2,1)S(1)} collective-permute-done((bf16[16,2048]{1,0:T(8,128)(2,1)S(1)}, bf16[16,2048]{1,0:T(8,128)(2,1)S(1)}, u32[]{:S(2)}, u32[]{:S(2)}) %collective-permute-start.19) | collective-permute-done | bytes 65568 | tf_op jit(solution)/shard_map/ppermute | solution.py:408
  61.2 2.4 %collective-permute-done.20.refs_3_ = bf16[16,2048]{1,0:T(8,128)(2,1)S(1)} collective-permute-done((bf16[16,2048]{1,0:T(8,128)(2,1)S(1)}, bf16[16,2048]{1,0:T(8,128)(2,1)S(1)}, u32[]{:S(2)}, u32[]{:S(2)}) %collective-permute-start.20) | collective-permute-done | bytes 65568 | tf_op jit(solution)/shard_map/ppermute | solution.py:408
  63.5 0.7 %finish.1 = bf16[8,4096]{1,0:T(8,128)(2,1)} custom-call(s32[1]{0:T(128)} %bitcast.side_ref, bf16[8,4096]{1,0:T(8,128)(2,1)S(1)} %get-tuple-element.47.mixed_ref, bf16[16,2048]{1,0:T(8,128)(2,1)S(1)} %get-tuple-element.81.refs_0_, bf16[16,2048]{1,0:T(8,128)(2,1)S(1)} %collective-permute-done.18.refs_1_, bf16[16,2048]{1,0:T(8,128)(2,1)S(1)} %collective-permute-done.19.refs_2_, ...), custom_call_target="tpu_custom_call" | custom-call | tf_op jit(solution)/shard_map/finish/pallas_call | solution.py:387
  (10 shorter events, 0.1 us)
Async XLA Ops:
  2.0 11.2 %collective-permute-start = (bf16[8,4224]{1,0:T(8,128)(2,1)S(1)}, bf16[8,4224]{1,0:T(8,128)(2,1)S(1)}, u32[]{:S(2)}, u32[]{:S(2)}) collective-permute-start(bf16[8,4224]{1,0:T(8,128)(2,1)S(1)} %get-tuple-element.49), channel_id=1, source_target_pairs={{0,4},{1,5},{2,6},{3,7},{4,0},{5,1},{6,2},{7,3},{8,12},{9,13},{10,... | collective-permute-start | bytes 202760 | tf_op jit(solution)/shard_map/ppermute | solution.py:408
  5.1 8.1 %collective-permute-start.1 = (bf16[8,4224]{1,0:T(8,128)(2,1)S(1)}, bf16[8,4224]{1,0:T(8,128)(2,1)S(1)}, u32[]{:S(2)}, u32[]{:S(2)}) collective-permute-start(bf16[8,4224]{1,0:T(8,128)(2,1)S(1)} %get-tuple-element.49), channel_id=1, source_target_pairs={{0,8},{1,9},{2,10},{3,11},{4,12},{5,13},{6,14},{7,15},{8,0},{9,1},... | collective-permute-start | bytes 202760 | tf_op jit(solution)/shard_map/ppermute | solution.py:408
  7.7 6.2 %collective-permute-start.2 = (bf16[8,4224]{1,0:T(8,128)(2,1)S(1)}, bf16[8,4224]{1,0:T(8,128)(2,1)S(1)}, u32[]{:S(2)}, u32[]{:S(2)}) collective-permute-start(bf16[8,4224]{1,0:T(8,128)(2,1)S(1)} %get-tuple-element.49), channel_id=1, source_target_pairs={{0,12},{1,13},{2,14},{3,15},{4,8},{5,9},{6,10},{7,11},{8,4},{9,5},... | collective-permute-start | bytes 202760 | tf_op jit(solution)/shard_map/ppermute | solution.py:408
  13.9 7.3 %collective-permute-start.3 = (bf16[32,4224]{1,0:T(8,128)(2,1)S(1)}, bf16[32,4224]{1,0:T(8,128)(2,1)S(1)}, u32[]{:S(2)}, u32[]{:S(2)}) collective-permute-start(bf16[32,4224]{1,0:T(8,128)(2,1)S(1)} %pad_maximum_fusion.refs_0_), channel_id=1, source_target_pairs={{0,2},{1,3},{2,0},{3,1},{4,6},{5,7},{6,4},{7,5},{8,10},{9,11},{10,... | collective-permute-start | bytes 811016 | tf_op jit(solution)/shard_map/ppermute | solution.py:408
  15.5 5.7 %collective-permute-start.4 = (bf16[32,4224]{1,0:T(8,128)(2,1)S(1)}, bf16[32,4224]{1,0:T(8,128)(2,1)S(1)}, u32[]{:S(2)}, u32[]{:S(2)}) collective-permute-start(bf16[32,4224]{1,0:T(8,128)(2,1)S(1)} %pad_maximum_fusion.refs_0_), channel_id=1, source_target_pairs={{0,1},{1,0},{2,3},{3,2},{4,5},{5,4},{6,7},{7,6},{8,9},{9,8},{10,11... | collective-permute-start | bytes 811016 | tf_op jit(solution)/shard_map/ppermute | solution.py:408
  15.5 8.9 %collective-permute-start.6 = (bf16[32,4224]{1,0:T(8,128)(2,1)S(1)}, bf16[32,4224]{1,0:T(8,128)(2,1)S(1)}, u32[]{:S(2)}, u32[]{:S(2)}) collective-permute-start(bf16[32,4224]{1,0:T(8,128)(2,1)S(1)} %pad_maximum_fusion.refs_0_), channel_id=1, source_target_pairs={{0,16},{1,17},{2,18},{3,19},{4,20},{5,21},{6,22},{7,23},{8,24},{9,... | collective-permute-start | bytes 811016 | tf_op jit(solution)/shard_map/ppermute | solution.py:408
  21.2 3.2 %collective-permute-start.5 = (bf16[32,4224]{1,0:T(8,128)(2,1)S(1)}, bf16[32,4224]{1,0:T(8,128)(2,1)S(1)}, u32[]{:S(2)}, u32[]{:S(2)}) collective-permute-start(bf16[32,4224]{1,0:T(8,128)(2,1)S(1)} %collective-permute-done.3.refs_2_), channel_id=1, source_target_pairs={{0,1},{1,0},{2,3},{3,2},{4,5},{5,4},{6,7},{7,6},{8,9},{9,8},{10,11... | collective-permute-start | bytes 811016 | tf_op jit(solution)/shard_map/ppermute | solution.py:408
  21.5 10.2 %collective-permute-start.8 = (bf16[32,4224]{1,0:T(8,128)(2,1)S(1)}, bf16[32,4224]{1,0:T(8,128)(2,1)S(1)}, u32[]{:S(2)}, u32[]{:S(2)}) collective-permute-start(bf16[32,4224]{1,0:T(8,128)(2,1)S(1)} %collective-permute-done.3.refs_2_), channel_id=1, source_target_pairs={{0,16},{1,17},{2,18},{3,19},{4,20},{5,21},{6,22},{7,23},{8,24},{9,... | collective-permute-start | bytes 811016 | tf_op jit(solution)/shard_map/ppermute | solution.py:408
  27.0 10.2 %collective-permute-start.10 = (bf16[144,1024]{1,0:T(8,128)(2,1)S(1)}, bf16[144,1024]{1,0:T(8,128)(2,1)S(1)}, u32[]{:S(2)}, u32[]{:S(2)}) collective-permute-start(bf16[144,1024]{1,0:T(8,128)(2,1)S(1)} %get-tuple-element.75.hidden_ref), channel_id=1, source_target_pairs={{0,16},{1,17},{2,18},{3,19},{4,20},{5,21},{6,22},{7,23},{8,24},{9,... | collective-permute-start | bytes 884744 | tf_op jit(solution)/shard_map/ppermute | solution.py:408
  28.8 3.5 %collective-permute-start.7 = (bf16[32,4224]{1,0:T(8,128)(2,1)S(1)}, bf16[32,4224]{1,0:T(8,128)(2,1)S(1)}, u32[]{:S(2)}, u32[]{:S(2)}) collective-permute-start(bf16[32,4224]{1,0:T(8,128)(2,1)S(1)} %collective-permute-done.6.refs_0_), channel_id=1, source_target_pairs={{0,1},{1,0},{2,3},{3,2},{4,5},{5,4},{6,7},{7,6},{8,9},{9,8},{10,11... | collective-permute-start | bytes 811016 | tf_op jit(solution)/shard_map/ppermute | solution.py:408
  31.6 1.7 %collective-permute-start.9 = (bf16[32,4224]{1,0:T(8,128)(2,1)S(1)}, bf16[32,4224]{1,0:T(8,128)(2,1)S(1)}, u32[]{:S(2)}, u32[]{:S(2)}) collective-permute-start(bf16[32,4224]{1,0:T(8,128)(2,1)S(1)} %collective-permute-done.8.refs_2_), channel_id=1, source_target_pairs={{0,1},{1,0},{2,3},{3,2},{4,5},{5,4},{6,7},{7,6},{8,9},{9,8},{10,11... | collective-permute-start | bytes 811016 | tf_op jit(solution)/shard_map/ppermute | solution.py:408
  36.0 8.6 %collective-permute-start.14 = (bf16[128,1024]{1,0:T(8,128)(2,1)S(1)}, bf16[128,1024]{1,0:T(8,128)(2,1)S(1)}, u32[]{:S(2)}, u32[]{:S(2)}) collective-permute-start(bf16[128,1024]{1,0:T(8,128)(2,1)S(1)} %get-tuple-element.67.hidden_ref), channel_id=1, source_target_pairs={{0,16},{1,17},{2,18},{3,19},{4,20},{5,21},{6,22},{7,23},{8,24},{9,... | collective-permute-start | bytes 786440 | tf_op jit(solution)/shard_map/ppermute | solution.py:408
  38.0 8.4 %collective-permute-start.11 = (bf16[64,2048]{1,0:T(8,128)(2,1)S(1)}, bf16[64,2048]{1,0:T(8,128)(2,1)S(1)}, u32[]{:S(2)}, u32[]{:S(2)}) collective-permute-start(bf16[64,2048]{1,0:T(8,128)(2,1)S(1)} %get-tuple-element.72), channel_id=1, source_target_pairs={{0,2},{1,3},{2,0},{3,1},{4,6},{5,7},{6,4},{7,5},{8,10},{9,11},{10,... | collective-permute-start | bytes 786440 | tf_op jit(solution)/shard_map/ppermute | solution.py:408
  45.5 1.5 %collective-permute-start.16 = (bf16[32,2048]{1,0:T(8,128)(2,1)S(1)}, bf16[32,2048]{1,0:T(8,128)(2,1)S(1)}, u32[]{:S(2)}, u32[]{:S(2)}) collective-permute-start(bf16[32,2048]{1,0:T(8,128)(2,1)S(1)} %get-tuple-element.80), channel_id=1, source_target_pairs={{0,1},{1,0},{2,3},{3,2},{4,5},{5,4},{6,7},{7,6},{8,9},{9,8},{10,11... | collective-permute-start | bytes 393224 | tf_op jit(solution)/shard_map/ppermute | solution.py:408
  46.4 1.6 %collective-permute-start.12 = (bf16[32,2048]{1,0:T(8,128)(2,1)S(1)}, bf16[32,2048]{1,0:T(8,128)(2,1)S(1)}, u32[]{:S(2)}, u32[]{:S(2)}) collective-permute-start(bf16[32,2048]{1,0:T(8,128)(2,1)S(1)} %get-tuple-element.74), channel_id=1, source_target_pairs={{0,1},{1,0},{2,3},{3,2},{4,5},{5,4},{6,7},{7,6},{8,9},{9,8},{10,11... | collective-permute-start | bytes 393224 | tf_op jit(solution)/shard_map/ppermute | solution.py:408
  46.5 3.2 %collective-permute-start.15 = (bf16[32,2048]{1,0:T(8,128)(2,1)S(1)}, bf16[32,2048]{1,0:T(8,128)(2,1)S(1)}, u32[]{:S(2)}, u32[]{:S(2)}) collective-permute-start(bf16[32,2048]{1,0:T(8,128)(2,1)S(1)} %get-tuple-element.78), channel_id=1, source_target_pairs={{0,1},{1,0},{2,3},{3,2},{4,5},{5,4},{6,7},{7,6},{8,9},{9,8},{10,11... | collective-permute-start | bytes 393224 | tf_op jit(solution)/shard_map/ppermute | solution.py:408
  47.0 5.5 %collective-permute-start.17 = (bf16[32,2048]{1,0:T(8,128)(2,1)S(1)}, bf16[32,2048]{1,0:T(8,128)(2,1)S(1)}, u32[]{:S(2)}, u32[]{:S(2)}) collective-permute-start(bf16[32,2048]{1,0:T(8,128)(2,1)S(1)} %add_and_cut.5), channel_id=1, source_target_pairs={{0,2},{1,3},{2,0},{3,1},{4,6},{5,7},{6,4},{7,5},{8,10},{9,11},{10,... | collective-permute-start | bytes 393224 | tf_op jit(solution)/shard_map/ppermute | solution.py:408
  48.0 5.5 %collective-permute-start.13 = (bf16[32,2048]{1,0:T(8,128)(2,1)S(1)}, bf16[32,2048]{1,0:T(8,128)(2,1)S(1)}, u32[]{:S(2)}, u32[]{:S(2)}) collective-permute-start(bf16[32,2048]{1,0:T(8,128)(2,1)S(1)} %add_and_cut.4), channel_id=1, source_target_pairs={{0,16},{1,17},{2,18},{3,19},{4,20},{5,21},{6,22},{7,23},{8,24},{9,... | collective-permute-start | bytes 393224 | tf_op jit(solution)/shard_map/ppermute | solution.py:408
  53.5 4.7 %collective-permute-start.18 = (bf16[16,2048]{1,0:T(8,128)(2,1)S(1)}, bf16[16,2048]{1,0:T(8,128)(2,1)S(1)}, u32[]{:S(2)}, u32[]{:S(2)}) collective-permute-start(bf16[16,2048]{1,0:T(8,128)(2,1)S(1)} %get-tuple-element.82), channel_id=1, source_target_pairs={{0,4},{1,5},{2,6},{3,7},{4,0},{5,1},{6,2},{7,3},{8,12},{9,13},{10,... | collective-permute-start | bytes 196616 | tf_op jit(solution)/shard_map/ppermute | solution.py:408
  54.2 7.0 %collective-permute-start.19 = (bf16[16,2048]{1,0:T(8,128)(2,1)S(1)}, bf16[16,2048]{1,0:T(8,128)(2,1)S(1)}, u32[]{:S(2)}, u32[]{:S(2)}) collective-permute-start(bf16[16,2048]{1,0:T(8,128)(2,1)S(1)} %get-tuple-element.83), channel_id=1, source_target_pairs={{0,8},{1,9},{2,10},{3,11},{4,12},{5,13},{6,14},{7,15},{8,0},{9,1},... | collective-permute-start | bytes 196616 | tf_op jit(solution)/shard_map/ppermute | solution.py:408
  57.5 6.1 %collective-permute-start.20 = (bf16[16,2048]{1,0:T(8,128)(2,1)S(1)}, bf16[16,2048]{1,0:T(8,128)(2,1)S(1)}, u32[]{:S(2)}, u32[]{:S(2)}) collective-permute-start(bf16[16,2048]{1,0:T(8,128)(2,1)S(1)} %get-tuple-element.84), channel_id=1, source_target_pairs={{0,12},{1,13},{2,14},{3,15},{4,8},{5,9},{6,10},{7,11},{8,4},{9,5},... | collective-permute-start | bytes 196616 | tf_op jit(solution)/shard_map/ppermute | solution.py:408

commit v9 on v8

--- a/solution.py
+++ b/solution.py
@@ -412,7 +412,9 @@
     )
     units = gate_codes.shape[1]
     half = down_codes.shape[1] // 2
-    blocks = [swap(payload, z * layer) for z in range(1, layers)]
+    order = sorted(range(1, layers), key=lambda z: -z.bit_length())
+    moved = {z: swap(payload, z * layer) for z in order}
+    blocks = [moved[z] for z in range(1, layers)]
     w_gate, w_down = unpack_weights(
         (gate_codes, gate_scales, 0, units), (down_codes, down_scales, 0, half)
     )
@@ -451,7 +453,7 @@
     (onward,) = add_and_cut([keep_far], [swap(send_far, core)], 1)
     near = [in_vmem(keep_near), swap(send_near, core), swap(onward, line)]
     blocks = join(near, far, layers)
-    blocks = [blocks[0]] + [swap(blocks[z], z * layer) for z in range(1, layers)]
+    blocks = [blocks[0]] + [swap(blocks[z], z * layer) for z in order]
     return finish(side, mixed, blocks)
 
 

time: 64.5 us -> 63 us (0.977)
  waiting for transfers between devices: 18.7 us -> 17.8 us
    ppermute x21, waiting for transfers between devices: 18.7 us -> 17.8 us  [swap(): lax.ppermute(block, ('dp', 'expert'), [(i, i ^ offset) for i in range(dev...]
  transfers between devices with their start and end apart: 21 -> 21, of which waited for: 10 -> 9; matrix products, arithmetic and copies ran while one was open for 0% -> 0% of each run, Pallas kernels for 33% -> 33%
where the time goes in v9:
time: 63 us; the launch traced here: 62.7 us
  Pallas kernels  23.7 us (38%)
  starting transfers between devices  21.1 us (33%)
  waiting for transfers between devices  17.8 us (28%)
    ppermute x21, starting transfers between devices, swap(): lax.ppermute(block, ('dp', 'expert'), [(i, i ^ offset) for i in range(dev...  21.1 us
    ppermute x21, waiting for transfers between devices, swap(): lax.ppermute(block, ('dp', 'expert'), [(i, i ^ offset) for i in range(dev...  17.8 us
    pallas_call x3, Pallas kernels, unpack_weights(): pl.pallas_call(functools.partial(unpack_kernel, tuple((job[2] for job in...  12.6 us
    pallas_call x2, Pallas kernels, hidden_units(): pl.pallas_call(hidden_kernel, out_shape=(pltpu.VMEM((count + spare, width...  5.23 us
    pallas_call x1, Pallas kernels, front(): pl.pallas_call(front_kernel, out_shape=(shape((rows, width), BF16), shape...  1.97 us
    pallas_call x2, Pallas kernels, peer_down(): pl.pallas_call(peer_down_kernel, out_shape=(pltpu.VMEM((count // parts, w...  1.58 us
    pallas_call x2, Pallas kernels, own_down(): pl.pallas_call(own_down_kernel, out_shape=pltpu.VMEM((count, width), F32)...  1.46 us
  transfers between devices with their start and end apart: 21, of which 9 were waited for; matrix products, arithmetic and copies ran while one was open for 0% of the time, Pallas kernels for 33%

profile of v9, /device:TPU:0, one launch (start us, length us, event | category | flops | bytes accessed | tf_op | source)
XLA Modules:
  0.0 62.7 jit_solution(6930654253327411487)
XLA Ops:
  0.0 2.0 %front.1 = (bf16[8,4096]{1,0:T(8,128)(2,1)S(1)}, bf16[8,4224]{1,0:T(8,128)(2,1)S(1)}) custom-call(s32[8]{0:T(128)} %lengths_ref.1, bf16[8,4096]{1,0:T(8,128)(2,1)} %queries_ref.1, bf16[8,2,1024]{2,1,0:T(2,128)(2,1)} %new_kv_ref.1, bf16[8,32,1024]{2,1,0:T(8,128)(2,1)} %keys_ref.1, bf16[8,32,1024]{2,1,0:T(8,128)(2,1)} %values_ref.1, ...), custom_call_target="tpu_custom_call" | custom-call | flops 1 | bytes 1 | tf_op jit(solution)/shard_map/front/pallas_call | solution.py:112
  2.0 3.1 %collective-permute-start = (bf16[8,4224]{1,0:T(8,128)(2,1)S(1)}, bf16[8,4224]{1,0:T(8,128)(2,1)S(1)}, u32[]{:S(2)}, u32[]{:S(2)}) collective-permute-start(bf16[8,4224]{1,0:T(8,128)(2,1)S(1)} %get-tuple-element.49), channel_id=1, source_target_pairs={{0,4},{1,5},{2,6},{3,7},{4,0},{5,1},{6,2},{7,3},{8,12},{9,13},{10,... | collective-permute-start | bytes 202760 | tf_op jit(solution)/shard_map/ppermute | solution.py:408
  5.1 2.6 %collective-permute-start.1 = (bf16[8,4224]{1,0:T(8,128)(2,1)S(1)}, bf16[8,4224]{1,0:T(8,128)(2,1)S(1)}, u32[]{:S(2)}, u32[]{:S(2)}) collective-permute-start(bf16[8,4224]{1,0:T(8,128)(2,1)S(1)} %get-tuple-element.49), channel_id=1, source_target_pairs={{0,8},{1,9},{2,10},{3,11},{4,12},{5,13},{6,14},{7,15},{8,0},{9,1},... | collective-permute-start | bytes 202760 | tf_op jit(solution)/shard_map/ppermute | solution.py:408
  7.7 5.5 %unpack_weights.3 = (bf16[4096,1024]{1,0:T(8,128)(2,1)S(1)}, bf16[2048,1024]{1,0:T(8,128)(2,1)S(1)}) custom-call(f32[1024,1024]{1,0:T(8,128)} %bitcast.11, f32[512,2048]{1,0:T(8,128)} %bitcast.8, bf16[32,1024]{1,0:T(8,128)(2,1)} %bitcast.14, bf16[16,2048]{1,0:T(8,128)(2,1)} %bitcast.12), custom_call_target="tpu_custom_call" | custom-call | flops 1 | bytes 1 | tf_op jit(solution)/shard_map/unpack_weights/pallas_call | solution.py:202
  13.2 0.0 collective-permute-done
  13.2 0.0 collective-permute-done.1
  13.2 0.7 %collective-permute-done.2 = bf16[8,4224]{1,0:T(8,128)(2,1)S(1)} collective-permute-done((bf16[8,4224]{1,0:T(8,128)(2,1)S(1)}, bf16[8,4224]{1,0:T(8,128)(2,1)S(1)}, u32[]{:S(2)}, u32[]{:S(2)}) %collective-permute-start.2) | collective-permute-done | bytes 67616 | tf_op jit(solution)/shard_map/ppermute | solution.py:408
  13.9 1.6 %collective-permute-start.3 = (bf16[32,4224]{1,0:T(8,128)(2,1)S(1)}, bf16[32,4224]{1,0:T(8,128)(2,1)S(1)}, u32[]{:S(2)}, u32[]{:S(2)}) collective-permute-start(bf16[32,4224]{1,0:T(8,128)(2,1)S(1)} %pad_maximum_fusion.refs_0_), channel_id=1, source_target_pairs={{0,2},{1,3},{2,0},{3,1},{4,6},{5,7},{6,4},{7,5},{8,10},{9,11},{10,... | collective-permute-start | bytes 811016 | tf_op jit(solution)/shard_map/ppermute | solution.py:408
  15.5 0.0 collective-permute-start.4
  15.5 1.5 %collective-permute-start.6 = (bf16[32,4224]{1,0:T(8,128)(2,1)S(1)}, bf16[32,4224]{1,0:T(8,128)(2,1)S(1)}, u32[]{:S(2)}, u32[]{:S(2)}) collective-permute-start(bf16[32,4224]{1,0:T(8,128)(2,1)S(1)} %pad_maximum_fusion.refs_0_), channel_id=1, source_target_pairs={{0,16},{1,17},{2,18},{3,19},{4,20},{5,21},{6,22},{7,23},{8,24},{9,... | collective-permute-start | bytes 811016 | tf_op jit(solution)/shard_map/ppermute | solution.py:408
  17.0 4.2 %unpack_weights.4.refs_5_ = bf16[4096,1024]{1,0:T(8,128)(2,1)S(1)} custom-call(f32[1024,1024]{1,0:T(8,128)} %bitcast.10, bf16[32,1024]{1,0:T(8,128)(2,1)} %bitcast.15), custom_call_target="tpu_custom_call" | custom-call | flops 1 | bytes 1 | tf_op jit(solution)/shard_map/unpack_weights/pallas_call | solution.py:202
  21.2 0.0 collective-permute-done.3.refs_2_
  21.2 0.3 collective-permute-start.5
  21.5 1.0 %collective-permute-start.8 = (bf16[32,4224]{1,0:T(8,128)(2,1)S(1)}, bf16[32,4224]{1,0:T(8,128)(2,1)S(1)}, u32[]{:S(2)}, u32[]{:S(2)}) collective-permute-start(bf16[32,4224]{1,0:T(8,128)(2,1)S(1)} %collective-permute-done.3.refs_2_), channel_id=1, source_target_pairs={{0,16},{1,17},{2,18},{3,19},{4,20},{5,21},{6,22},{7,23},{8,24},{9,... | collective-permute-start | bytes 811016 | tf_op jit(solution)/shard_map/ppermute | solution.py:408
  22.5 1.9 %collective-permute-done.6.refs_0_ = bf16[32,4224]{1,0:T(8,128)(2,1)S(1)} collective-permute-done((bf16[32,4224]{1,0:T(8,128)(2,1)S(1)}, bf16[32,4224]{1,0:T(8,128)(2,1)S(1)}, u32[]{:S(2)}, u32[]{:S(2)}) %collective-permute-start.6) | collective-permute-done | bytes 270368 | tf_op jit(solution)/shard_map/ppermute | solution.py:408
  24.4 0.0 collective-permute-done.5.refs_3_
  24.4 2.6 %gate_up.2 = (bf16[144,1024]{1,0:T(8,128)(2,1)S(1)}, f32[128,128]{1,0:T(8,128)S(1)}) custom-call(s32[1]{0:T(128)} %bitcast.1.place_ref, bf16[32,4224]{1,0:T(8,128)(2,1)S(1)} %pad_maximum_fusion.refs_0_, bf16[32,4224]{1,0:T(8,128)(2,1)S(1)} %collective-permute-done.4.refs_1_, bf16[32,4224]{1,0:T(8,128)(2,1)S(1)} %collective-permute-done.3.refs_2_, ...), custom_call_target="tpu_custom_call" | custom-call | flops 1 | bytes 1 | tf_op jit(solution)/shard_map/gate_up/pallas_call | solution.py:247
  27.0 1.8 %collective-permute-start.10 = (bf16[144,1024]{1,0:T(8,128)(2,1)S(1)}, bf16[144,1024]{1,0:T(8,128)(2,1)S(1)}, u32[]{:S(2)}, u32[]{:S(2)}) collective-permute-start(bf16[144,1024]{1,0:T(8,128)(2,1)S(1)} %get-tuple-element.75.hidden_ref), channel_id=1, source_target_pairs={{0,16},{1,17},{2,18},{3,19},{4,20},{5,21},{6,22},{7,23},{8,24},{9,... | collective-permute-start | bytes 884744 | tf_op jit(solution)/shard_map/ppermute | solution.py:408
  28.8 0.0 collective-permute-start.7
  28.8 2.9 %unpack_weights.5.weight_refs_1_ = bf16[2048,1024]{1,0:T(8,128)(2,1)S(1)} custom-call(f32[512,2048]{1,0:T(8,128)} %bitcast.9, bf16[16,2048]{1,0:T(8,128)(2,1)} %bitcast.13), custom_call_target="tpu_custom_call" | custom-call | flops 1 | bytes 1 | tf_op jit(solution)/shard_map/unpack_weights/pallas_call | solution.py:202
  31.6 0.6 collective-permute-start.9
  32.2 1.2 %collective-permute-done.9.refs_3_ = bf16[32,4224]{1,0:T(8,128)(2,1)S(1)} collective-permute-done((bf16[32,4224]{1,0:T(8,128)(2,1)S(1)}, bf16[32,4224]{1,0:T(8,128)(2,1)S(1)}, u32[]{:S(2)}, u32[]{:S(2)}) %collective-permute-start.9) | collective-permute-done | bytes 270368 | tf_op jit(solution)/shard_map/ppermute | solution.py:408
  33.4 2.6 %gate_up.3 = (bf16[128,1024]{1,0:T(8,128)(2,1)S(1)}, f32[128,128]{1,0:T(8,128)S(1)}) custom-call(s32[1]{0:T(128)} %bitcast.1.place_ref, bf16[32,4224]{1,0:T(8,128)(2,1)S(1)} %collective-permute-done.6.refs_0_, bf16[32,4224]{1,0:T(8,128)(2,1)S(1)} %collective-permute-done.7.refs_1_, bf16[32,4224]{1,0:T(8,128)(2,1)S(1)} %collective-permute-done.8.refs_2_, ...), custom_call_target="tpu_custom_call" | custom-call | flops 1 | bytes 1 | tf_op jit(solution)/shard_map/gate_up/pallas_call | solution.py:247
  36.0 0.4 collective-permute-start.14
  36.4 0.7 %down_own.2.partial_ref = f32[128,2048]{1,0:T(8,128)S(1)} custom-call(s32[1]{0:T(128)} %bitcast.side_ref, bf16[128,1024]{1,0:T(8,128)(2,1)S(1)} %get-tuple-element.67.hidden_ref, bf16[2048,1024]{1,0:T(8,128)(2,1)S(1)} %get-tuple-element.68.weight_refs_0_, bf16[2048,1024]{1,0:T(8,128)(2,1)S(1)} %unpack_weights.5.weight_refs_1_), custom_call_target="tpu_custom_call" | custom-call | flops 1 | bytes 1 | tf_op jit(solution)/shard_map/down_own/pallas_call | solution.py:276
  37.2 0.8 %down_peer.2 = (bf16[64,2048]{1,0:T(8,128)(2,1)S(1)}, bf16[64,2048]{1,0:T(8,128)(2,1)S(1)}) custom-call(s32[1]{0:T(128)} %bitcast.side_ref, f32[128,2048]{1,0:T(8,128)S(1)} %down_own.2.partial_ref, bf16[144,1024]{1,0:T(8,128)(2,1)S(1)} %collective-permute-done.10.hidden_ref, bf16[2048,1024]{1,0:T(8,128)(2,1)S(1)} %get-tuple-element.68.weight_refs_0_, ...), custom_call_target="tpu_custom_call" | custom-call | flops 1 | bytes 1 | tf_op jit(solution)/shard_map/down_peer/pallas_call | solution.py:309
  38.0 1.2 %collective-permute-start.11 = (bf16[64,2048]{1,0:T(8,128)(2,1)S(1)}, bf16[64,2048]{1,0:T(8,128)(2,1)S(1)}, u32[]{:S(2)}, u32[]{:S(2)}) collective-permute-start(bf16[64,2048]{1,0:T(8,128)(2,1)S(1)} %get-tuple-element.72), channel_id=1, source_target_pairs={{0,2},{1,3},{2,0},{3,1},{4,6},{5,7},{6,4},{7,5},{8,10},{9,11},{10,... | collective-permute-start | bytes 786440 | tf_op jit(solution)/shard_map/ppermute | solution.py:408
  39.1 0.7 %down_own.3.partial_ref = f32[128,2048]{1,0:T(8,128)S(1)} custom-call(s32[1]{0:T(128)} %bitcast.side_ref, bf16[144,1024]{1,0:T(8,128)(2,1)S(1)} %get-tuple-element.75.hidden_ref, bf16[2048,1024]{1,0:T(8,128)(2,1)S(1)} %get-tuple-element.68.weight_refs_0_, bf16[2048,1024]{1,0:T(8,128)(2,1)S(1)} %unpack_weights.5.weight_refs_1_), custom_call_target="tpu_custom_call" | custom-call | flops 1 | bytes 1 | tf_op jit(solution)/shard_map/down_own/pallas_call | solution.py:276
  39.8 4.8 %collective-permute-done.14.hidden_ref = bf16[128,1024]{1,0:T(8,128)(2,1)S(1)} collective-permute-done((bf16[128,1024]{1,0:T(8,128)(2,1)S(1)}, bf16[128,1024]{1,0:T(8,128)(2,1)S(1)}, u32[]{:S(2)}, u32[]{:S(2)}) %collective-permute-start.14) | collective-permute-done | bytes 262176 | tf_op jit(solution)/shard_map/ppermute | solution.py:408
  44.7 0.8 %down_peer.3 = (bf16[32,2048]{1,0:T(8,128)(2,1)S(1)}, bf16[32,2048]{1,0:T(8,128)(2,1)S(1)}, bf16[32,2048]{1,0:T(8,128)(2,1)S(1)}, bf16[32,2048]{1,0:T(8,128)(2,1)S(1)}) custom-call(s32[1]{0:T(128)} %bitcast.side_ref, f32[128,2048]{1,0:T(8,128)S(1)} %down_own.3.partial_ref, bf16[128,1024]{1,0:T(8,128)(2,1)S(1)} %collective-permute-done.14.hidden_ref, ...), custom_call_target="tpu_custom_call" | custom-call | flops 1 | bytes 1 | tf_op jit(solution)/shard_map/down_peer/pallas_call | solution.py:309
  45.5 0.1 collective-permute-start.16
  45.5 0.8 %collective-permute-done.11.refs_1_ = bf16[64,2048]{1,0:T(8,128)(2,1)S(1)} collective-permute-done((bf16[64,2048]{1,0:T(8,128)(2,1)S(1)}, bf16[64,2048]{1,0:T(8,128)(2,1)S(1)}, u32[]{:S(2)}, u32[]{:S(2)}) %collective-permute-start.11) | collective-permute-done | bytes 262176 | tf_op jit(solution)/shard_map/ppermute | solution.py:408
  46.3 0.1 add_and_cut.3
  46.4 0.1 collective-permute-start.12
  46.5 0.5 collective-permute-start.15
  47.0 0.0 collective-permute-done.16.refs_1_
  47.0 0.9 %collective-permute-start.17 = (bf16[32,2048]{1,0:T(8,128)(2,1)S(1)}, bf16[32,2048]{1,0:T(8,128)(2,1)S(1)}, u32[]{:S(2)}, u32[]{:S(2)}) collective-permute-start(bf16[32,2048]{1,0:T(8,128)(2,1)S(1)} %add_and_cut.5), channel_id=1, source_target_pairs={{0,2},{1,3},{2,0},{3,1},{4,6},{5,7},{6,4},{7,5},{8,10},{9,11},{10,... | collective-permute-start | bytes 393224 | tf_op jit(solution)/shard_map/ppermute | solution.py:408
  47.9 0.0 collective-permute-done.12.refs_1_
  48.0 1.6 %collective-permute-start.13 = (bf16[32,2048]{1,0:T(8,128)(2,1)S(1)}, bf16[32,2048]{1,0:T(8,128)(2,1)S(1)}, u32[]{:S(2)}, u32[]{:S(2)}) collective-permute-start(bf16[32,2048]{1,0:T(8,128)(2,1)S(1)} %add_and_cut.4), channel_id=1, source_target_pairs={{0,16},{1,17},{2,18},{3,19},{4,20},{5,21},{6,22},{7,23},{8,24},{9,... | collective-permute-start | bytes 393224 | tf_op jit(solution)/shard_map/ppermute | solution.py:408
  49.6 2.9 %collective-permute-done.17.refs_2_ = bf16[32,2048]{1,0:T(8,128)(2,1)S(1)} collective-permute-done((bf16[32,2048]{1,0:T(8,128)(2,1)S(1)}, bf16[32,2048]{1,0:T(8,128)(2,1)S(1)}, u32[]{:S(2)}, u32[]{:S(2)}) %collective-permute-start.17) | collective-permute-done | bytes 131104 | tf_op jit(solution)/shard_map/ppermute | solution.py:408
  52.5 0.9 %collective-permute-done.13.far_ref = bf16[32,2048]{1,0:T(8,128)(2,1)S(1)} collective-permute-done((bf16[32,2048]{1,0:T(8,128)(2,1)S(1)}, bf16[32,2048]{1,0:T(8,128)(2,1)S(1)}, u32[]{:S(2)}, u32[]{:S(2)}) %collective-permute-start.13) | collective-permute-done | bytes 131104 | tf_op jit(solution)/shard_map/ppermute | solution.py:408
  53.5 0.1 join.1
  53.5 1.7 %collective-permute-start.18 = (bf16[16,2048]{1,0:T(8,128)(2,1)S(1)}, bf16[16,2048]{1,0:T(8,128)(2,1)S(1)}, u32[]{:S(2)}, u32[]{:S(2)}) collective-permute-start(bf16[16,2048]{1,0:T(8,128)(2,1)S(1)} %get-tuple-element.82), channel_id=1, source_target_pairs={{0,8},{1,9},{2,10},{3,11},{4,12},{5,13},{6,14},{7,15},{8,0},{9,1},... | collective-permute-start | bytes 196616 | tf_op jit(solution)/shard_map/ppermute | solution.py:408
  55.2 1.8 %collective-permute-start.19 = (bf16[16,2048]{1,0:T(8,128)(2,1)S(1)}, bf16[16,2048]{1,0:T(8,128)(2,1)S(1)}, u32[]{:S(2)}, u32[]{:S(2)}) collective-permute-start(bf16[16,2048]{1,0:T(8,128)(2,1)S(1)} %get-tuple-element.83), channel_id=1, source_target_pairs={{0,12},{1,13},{2,14},{3,15},{4,8},{5,9},{6,10},{7,11},{8,4},{9,5},... | collective-permute-start | bytes 196616 | tf_op jit(solution)/shard_map/ppermute | solution.py:408
  57.0 0.5 collective-permute-start.20
  57.5 4.0 %collective-permute-done.18.refs_1_ = bf16[16,2048]{1,0:T(8,128)(2,1)S(1)} collective-permute-done((bf16[16,2048]{1,0:T(8,128)(2,1)S(1)}, bf16[16,2048]{1,0:T(8,128)(2,1)S(1)}, u32[]{:S(2)}, u32[]{:S(2)}) %collective-permute-start.18) | collective-permute-done | bytes 65568 | tf_op jit(solution)/shard_map/ppermute | solution.py:408
  61.5 0.6 collective-permute-done.20.refs_3_
  62.1 0.7 %finish.1 = bf16[8,4096]{1,0:T(8,128)(2,1)} custom-call(s32[1]{0:T(128)} %bitcast.side_ref, bf16[8,4096]{1,0:T(8,128)(2,1)S(1)} %get-tuple-element.47.mixed_ref, bf16[16,2048]{1,0:T(8,128)(2,1)S(1)} %get-tuple-element.81.refs_0_, bf16[16,2048]{1,0:T(8,128)(2,1)S(1)} %collective-permute-done.18.refs_1_, bf16[16,2048]{1,0:T(8,128)(2,1)S(1)} %collective-permute-done.19.refs_2_, ...), custom_call_target="tpu_custom_call" | custom-call | tf_op jit(solution)/shard_map/finish/pallas_call | solution.py:387
  (10 shorter events, 0.1 us)
Async XLA Ops:
  2.0 11.2 %collective-permute-start = (bf16[8,4224]{1,0:T(8,128)(2,1)S(1)}, bf16[8,4224]{1,0:T(8,128)(2,1)S(1)}, u32[]{:S(2)}, u32[]{:S(2)}) collective-permute-start(bf16[8,4224]{1,0:T(8,128)(2,1)S(1)} %get-tuple-element.49), channel_id=1, source_target_pairs={{0,4},{1,5},{2,6},{3,7},{4,0},{5,1},{6,2},{7,3},{8,12},{9,13},{10,... | collective-permute-start | bytes 202760 | tf_op jit(solution)/shard_map/ppermute | solution.py:408
  5.1 8.1 %collective-permute-start.1 = (bf16[8,4224]{1,0:T(8,128)(2,1)S(1)}, bf16[8,4224]{1,0:T(8,128)(2,1)S(1)}, u32[]{:S(2)}, u32[]{:S(2)}) collective-permute-start(bf16[8,4224]{1,0:T(8,128)(2,1)S(1)} %get-tuple-element.49), channel_id=1, source_target_pairs={{0,8},{1,9},{2,10},{3,11},{4,12},{5,13},{6,14},{7,15},{8,0},{9,1},... | collective-permute-start | bytes 202760 | tf_op jit(solution)/shard_map/ppermute | solution.py:408
  7.7 6.2 %collective-permute-start.2 = (bf16[8,4224]{1,0:T(8,128)(2,1)S(1)}, bf16[8,4224]{1,0:T(8,128)(2,1)S(1)}, u32[]{:S(2)}, u32[]{:S(2)}) collective-permute-start(bf16[8,4224]{1,0:T(8,128)(2,1)S(1)} %get-tuple-element.49), channel_id=1, source_target_pairs={{0,12},{1,13},{2,14},{3,15},{4,8},{5,9},{6,10},{7,11},{8,4},{9,5},... | collective-permute-start | bytes 202760 | tf_op jit(solution)/shard_map/ppermute | solution.py:408
  13.9 7.3 %collective-permute-start.3 = (bf16[32,4224]{1,0:T(8,128)(2,1)S(1)}, bf16[32,4224]{1,0:T(8,128)(2,1)S(1)}, u32[]{:S(2)}, u32[]{:S(2)}) collective-permute-start(bf16[32,4224]{1,0:T(8,128)(2,1)S(1)} %pad_maximum_fusion.refs_0_), channel_id=1, source_target_pairs={{0,2},{1,3},{2,0},{3,1},{4,6},{5,7},{6,4},{7,5},{8,10},{9,11},{10,... | collective-permute-start | bytes 811016 | tf_op jit(solution)/shard_map/ppermute | solution.py:408
  15.5 5.7 %collective-permute-start.4 = (bf16[32,4224]{1,0:T(8,128)(2,1)S(1)}, bf16[32,4224]{1,0:T(8,128)(2,1)S(1)}, u32[]{:S(2)}, u32[]{:S(2)}) collective-permute-start(bf16[32,4224]{1,0:T(8,128)(2,1)S(1)} %pad_maximum_fusion.refs_0_), channel_id=1, source_target_pairs={{0,1},{1,0},{2,3},{3,2},{4,5},{5,4},{6,7},{7,6},{8,9},{9,8},{10,11... | collective-permute-start | bytes 811016 | tf_op jit(solution)/shard_map/ppermute | solution.py:408
  15.5 8.9 %collective-permute-start.6 = (bf16[32,4224]{1,0:T(8,128)(2,1)S(1)}, bf16[32,4224]{1,0:T(8,128)(2,1)S(1)}, u32[]{:S(2)}, u32[]{:S(2)}) collective-permute-start(bf16[32,4224]{1,0:T(8,128)(2,1)S(1)} %pad_maximum_fusion.refs_0_), channel_id=1, source_target_pairs={{0,16},{1,17},{2,18},{3,19},{4,20},{5,21},{6,22},{7,23},{8,24},{9,... | collective-permute-start | bytes 811016 | tf_op jit(solution)/shard_map/ppermute | solution.py:408
  21.2 3.2 %collective-permute-start.5 = (bf16[32,4224]{1,0:T(8,128)(2,1)S(1)}, bf16[32,4224]{1,0:T(8,128)(2,1)S(1)}, u32[]{:S(2)}, u32[]{:S(2)}) collective-permute-start(bf16[32,4224]{1,0:T(8,128)(2,1)S(1)} %collective-permute-done.3.refs_2_), channel_id=1, source_target_pairs={{0,1},{1,0},{2,3},{3,2},{4,5},{5,4},{6,7},{7,6},{8,9},{9,8},{10,11... | collective-permute-start | bytes 811016 | tf_op jit(solution)/shard_map/ppermute | solution.py:408
  21.5 10.2 %collective-permute-start.8 = (bf16[32,4224]{1,0:T(8,128)(2,1)S(1)}, bf16[32,4224]{1,0:T(8,128)(2,1)S(1)}, u32[]{:S(2)}, u32[]{:S(2)}) collective-permute-start(bf16[32,4224]{1,0:T(8,128)(2,1)S(1)} %collective-permute-done.3.refs_2_), channel_id=1, source_target_pairs={{0,16},{1,17},{2,18},{3,19},{4,20},{5,21},{6,22},{7,23},{8,24},{9,... | collective-permute-start | bytes 811016 | tf_op jit(solution)/shard_map/ppermute | solution.py:408
  27.0 10.2 %collective-permute-start.10 = (bf16[144,1024]{1,0:T(8,128)(2,1)S(1)}, bf16[144,1024]{1,0:T(8,128)(2,1)S(1)}, u32[]{:S(2)}, u32[]{:S(2)}) collective-permute-start(bf16[144,1024]{1,0:T(8,128)(2,1)S(1)} %get-tuple-element.75.hidden_ref), channel_id=1, source_target_pairs={{0,16},{1,17},{2,18},{3,19},{4,20},{5,21},{6,22},{7,23},{8,24},{9,... | collective-permute-start | bytes 884744 | tf_op jit(solution)/shard_map/ppermute | solution.py:408
  28.8 3.5 %collective-permute-start.7 = (bf16[32,4224]{1,0:T(8,128)(2,1)S(1)}, bf16[32,4224]{1,0:T(8,128)(2,1)S(1)}, u32[]{:S(2)}, u32[]{:S(2)}) collective-permute-start(bf16[32,4224]{1,0:T(8,128)(2,1)S(1)} %collective-permute-done.6.refs_0_), channel_id=1, source_target_pairs={{0,1},{1,0},{2,3},{3,2},{4,5},{5,4},{6,7},{7,6},{8,9},{9,8},{10,11... | collective-permute-start | bytes 811016 | tf_op jit(solution)/shard_map/ppermute | solution.py:408
  31.6 1.7 %collective-permute-start.9 = (bf16[32,4224]{1,0:T(8,128)(2,1)S(1)}, bf16[32,4224]{1,0:T(8,128)(2,1)S(1)}, u32[]{:S(2)}, u32[]{:S(2)}) collective-permute-start(bf16[32,4224]{1,0:T(8,128)(2,1)S(1)} %collective-permute-done.8.refs_2_), channel_id=1, source_target_pairs={{0,1},{1,0},{2,3},{3,2},{4,5},{5,4},{6,7},{7,6},{8,9},{9,8},{10,11... | collective-permute-start | bytes 811016 | tf_op jit(solution)/shard_map/ppermute | solution.py:408
  36.0 8.6 %collective-permute-start.14 = (bf16[128,1024]{1,0:T(8,128)(2,1)S(1)}, bf16[128,1024]{1,0:T(8,128)(2,1)S(1)}, u32[]{:S(2)}, u32[]{:S(2)}) collective-permute-start(bf16[128,1024]{1,0:T(8,128)(2,1)S(1)} %get-tuple-element.67.hidden_ref), channel_id=1, source_target_pairs={{0,16},{1,17},{2,18},{3,19},{4,20},{5,21},{6,22},{7,23},{8,24},{9,... | collective-permute-start | bytes 786440 | tf_op jit(solution)/shard_map/ppermute | solution.py:408
  38.0 8.4 %collective-permute-start.11 = (bf16[64,2048]{1,0:T(8,128)(2,1)S(1)}, bf16[64,2048]{1,0:T(8,128)(2,1)S(1)}, u32[]{:S(2)}, u32[]{:S(2)}) collective-permute-start(bf16[64,2048]{1,0:T(8,128)(2,1)S(1)} %get-tuple-element.72), channel_id=1, source_target_pairs={{0,2},{1,3},{2,0},{3,1},{4,6},{5,7},{6,4},{7,5},{8,10},{9,11},{10,... | collective-permute-start | bytes 786440 | tf_op jit(solution)/shard_map/ppermute | solution.py:408
  45.5 1.5 %collective-permute-start.16 = (bf16[32,2048]{1,0:T(8,128)(2,1)S(1)}, bf16[32,2048]{1,0:T(8,128)(2,1)S(1)}, u32[]{:S(2)}, u32[]{:S(2)}) collective-permute-start(bf16[32,2048]{1,0:T(8,128)(2,1)S(1)} %get-tuple-element.80), channel_id=1, source_target_pairs={{0,1},{1,0},{2,3},{3,2},{4,5},{5,4},{6,7},{7,6},{8,9},{9,8},{10,11... | collective-permute-start | bytes 393224 | tf_op jit(solution)/shard_map/ppermute | solution.py:408
  46.4 1.6 %collective-permute-start.12 = (bf16[32,2048]{1,0:T(8,128)(2,1)S(1)}, bf16[32,2048]{1,0:T(8,128)(2,1)S(1)}, u32[]{:S(2)}, u32[]{:S(2)}) collective-permute-start(bf16[32,2048]{1,0:T(8,128)(2,1)S(1)} %get-tuple-element.74), channel_id=1, source_target_pairs={{0,1},{1,0},{2,3},{3,2},{4,5},{5,4},{6,7},{7,6},{8,9},{9,8},{10,11... | collective-permute-start | bytes 393224 | tf_op jit(solution)/shard_map/ppermute | solution.py:408
  46.5 3.2 %collective-permute-start.15 = (bf16[32,2048]{1,0:T(8,128)(2,1)S(1)}, bf16[32,2048]{1,0:T(8,128)(2,1)S(1)}, u32[]{:S(2)}, u32[]{:S(2)}) collective-permute-start(bf16[32,2048]{1,0:T(8,128)(2,1)S(1)} %get-tuple-element.78), channel_id=1, source_target_pairs={{0,1},{1,0},{2,3},{3,2},{4,5},{5,4},{6,7},{7,6},{8,9},{9,8},{10,11... | collective-permute-start | bytes 393224 | tf_op jit(solution)/shard_map/ppermute | solution.py:408
  47.0 5.5 %collective-permute-start.17 = (bf16[32,2048]{1,0:T(8,128)(2,1)S(1)}, bf16[32,2048]{1,0:T(8,128)(2,1)S(1)}, u32[]{:S(2)}, u32[]{:S(2)}) collective-permute-start(bf16[32,2048]{1,0:T(8,128)(2,1)S(1)} %add_and_cut.5), channel_id=1, source_target_pairs={{0,2},{1,3},{2,0},{3,1},{4,6},{5,7},{6,4},{7,5},{8,10},{9,11},{10,... | collective-permute-start | bytes 393224 | tf_op jit(solution)/shard_map/ppermute | solution.py:408
  48.0 5.5 %collective-permute-start.13 = (bf16[32,2048]{1,0:T(8,128)(2,1)S(1)}, bf16[32,2048]{1,0:T(8,128)(2,1)S(1)}, u32[]{:S(2)}, u32[]{:S(2)}) collective-permute-start(bf16[32,2048]{1,0:T(8,128)(2,1)S(1)} %add_and_cut.4), channel_id=1, source_target_pairs={{0,16},{1,17},{2,18},{3,19},{4,20},{5,21},{6,22},{7,23},{8,24},{9,... | collective-permute-start | bytes 393224 | tf_op jit(solution)/shard_map/ppermute | solution.py:408
  53.5 8.0 %collective-permute-start.18 = (bf16[16,2048]{1,0:T(8,128)(2,1)S(1)}, bf16[16,2048]{1,0:T(8,128)(2,1)S(1)}, u32[]{:S(2)}, u32[]{:S(2)}) collective-permute-start(bf16[16,2048]{1,0:T(8,128)(2,1)S(1)} %get-tuple-element.82), channel_id=1, source_target_pairs={{0,8},{1,9},{2,10},{3,11},{4,12},{5,13},{6,14},{7,15},{8,0},{9,1},... | collective-permute-start | bytes 196616 | tf_op jit(solution)/shard_map/ppermute | solution.py:408
  55.2 6.3 %collective-permute-start.19 = (bf16[16,2048]{1,0:T(8,128)(2,1)S(1)}, bf16[16,2048]{1,0:T(8,128)(2,1)S(1)}, u32[]{:S(2)}, u32[]{:S(2)}) collective-permute-start(bf16[16,2048]{1,0:T(8,128)(2,1)S(1)} %get-tuple-element.83), channel_id=1, source_target_pairs={{0,12},{1,13},{2,14},{3,15},{4,8},{5,9},{6,10},{7,11},{8,4},{9,5},... | collective-permute-start | bytes 196616 | tf_op jit(solution)/shard_map/ppermute | solution.py:408
  57.0 5.1 %collective-permute-start.20 = (bf16[16,2048]{1,0:T(8,128)(2,1)S(1)}, bf16[16,2048]{1,0:T(8,128)(2,1)S(1)}, u32[]{:S(2)}, u32[]{:S(2)}) collective-permute-start(bf16[16,2048]{1,0:T(8,128)(2,1)S(1)} %get-tuple-element.84), channel_id=1, source_target_pairs={{0,4},{1,5},{2,6},{3,7},{4,0},{5,1},{6,2},{7,3},{8,12},{9,13},{10,... | collective-permute-start | bytes 196616 | tf_op jit(solution)/shard_map/ppermute | solution.py:408

commit v10 on v9

--- a/solution.py
+++ b/solution.py
@@ -413,8 +413,7 @@
     units = gate_codes.shape[1]
     half = down_codes.shape[1] // 2
     order = sorted(range(1, layers), key=lambda z: -z.bit_length())
-    moved = {z: swap(payload, z * layer) for z in order}
-    blocks = [moved[z] for z in range(1, layers)]
+    blocks = [swap(payload, z * layer) for z in order]
     w_gate, w_down = unpack_weights(
         (gate_codes, gate_scales, 0, units), (down_codes, down_scales, 0, half)
     )
@@ -453,7 +452,7 @@
     (onward,) = add_and_cut([keep_far], [swap(send_far, core)], 1)
     near = [in_vmem(keep_near), swap(send_near, core), swap(onward, line)]
     blocks = join(near, far, layers)
-    blocks = [blocks[0]] + [swap(blocks[z], z * layer) for z in order]
+    blocks = [blocks[0]] + [swap(block, z * layer) for block, z in zip(blocks[1:], order)]
     return finish(side, mixed, blocks)
 
 

time: 63 us -> 63.2 us (level)
  starting transfers between devices: 21.1 us -> 21.9 us
    ppermute x21, starting transfers between devices: 21.1 us -> 21.9 us  [swap(): lax.ppermute(block, ('dp', 'expert'), [(i, i ^ offset) for i in range(dev...]
  transfers between devices with their start and end apart: 21 -> 21, of which waited for: 9 -> 10; matrix products, arithmetic and copies ran while one was open for 0% -> 0% of each run, Pallas kernels for 33% -> 33%
where the time goes in v10:
time: 63.2 us; the launch traced here: 62.9 us
  Pallas kernels  23.7 us (38%)
  starting transfers between devices  21.9 us (35%)
  waiting for transfers between devices  17.2 us (27%)
    ppermute x21, starting transfers between devices, swap(): lax.ppermute(block, ('dp', 'expert'), [(i, i ^ offset) for i in range(dev...  21.9 us
    ppermute x21, waiting for transfers between devices, swap(): lax.ppermute(block, ('dp', 'expert'), [(i, i ^ offset) for i in range(dev...  17.2 us
    pallas_call x3, Pallas kernels, unpack_weights(): pl.pallas_call(functools.partial(unpack_kernel, tuple((job[2] for job in...  12.6 us
    pallas_call x2, Pallas kernels, hidden_units(): pl.pallas_call(hidden_kernel, out_shape=(pltpu.VMEM((count + spare, width...  5.25 us
    pallas_call x1, Pallas kernels, front(): pl.pallas_call(front_kernel, out_shape=(shape((rows, width), BF16), shape...  1.97 us
    pallas_call x2, Pallas kernels, peer_down(): pl.pallas_call(peer_down_kernel, out_shape=(pltpu.VMEM((count // parts, w...  1.58 us
    pallas_call x2, Pallas kernels, own_down(): pl.pallas_call(own_down_kernel, out_shape=pltpu.VMEM((count, width), F32)...  1.45 us
  transfers between devices with their start and end apart: 21, of which 10 were waited for; matrix products, arithmetic and copies ran while one was open for 0% of the time, Pallas kernels for 33%

profile of v10, /device:TPU:0, one launch (start us, length us, event | category | flops | bytes accessed | tf_op | source)
XLA Modules:
  0.0 62.9 jit_solution(5574933291101521554)
XLA Ops:
  0.0 2.0 %front.1 = (bf16[8,4096]{1,0:T(8,128)(2,1)S(1)}, bf16[8,4224]{1,0:T(8,128)(2,1)S(1)}) custom-call(s32[8]{0:T(128)} %lengths_ref.1, bf16[8,4096]{1,0:T(8,128)(2,1)} %queries_ref.1, bf16[8,2,1024]{2,1,0:T(2,128)(2,1)} %new_kv_ref.1, bf16[8,32,1024]{2,1,0:T(8,128)(2,1)} %keys_ref.1, bf16[8,32,1024]{2,1,0:T(8,128)(2,1)} %values_ref.1, ...), custom_call_target="tpu_custom_call" | custom-call | flops 1 | bytes 1 | tf_op jit(solution)/shard_map/front/pallas_call | solution.py:112
  2.0 4.1 %collective-permute-start = (bf16[8,4224]{1,0:T(8,128)(2,1)S(1)}, bf16[8,4224]{1,0:T(8,128)(2,1)S(1)}, u32[]{:S(2)}, u32[]{:S(2)}) collective-permute-start(bf16[8,4224]{1,0:T(8,128)(2,1)S(1)} %get-tuple-element.49), channel_id=1, source_target_pairs={{0,8},{1,9},{2,10},{3,11},{4,12},{5,13},{6,14},{7,15},{8,0},{9,1},... | collective-permute-start | bytes 202760 | tf_op jit(solution)/shard_map/ppermute | solution.py:408
  6.1 1.3 %collective-permute-start.1 = (bf16[8,4224]{1,0:T(8,128)(2,1)S(1)}, bf16[8,4224]{1,0:T(8,128)(2,1)S(1)}, u32[]{:S(2)}, u32[]{:S(2)}) collective-permute-start(bf16[8,4224]{1,0:T(8,128)(2,1)S(1)} %get-tuple-element.49), channel_id=1, source_target_pairs={{0,12},{1,13},{2,14},{3,15},{4,8},{5,9},{6,10},{7,11},{8,4},{9,5},... | collective-permute-start | bytes 202760 | tf_op jit(solution)/shard_map/ppermute | solution.py:408
  7.4 0.2 collective-permute-start.2
  7.7 5.5 %unpack_weights.3 = (bf16[4096,1024]{1,0:T(8,128)(2,1)S(1)}, bf16[2048,1024]{1,0:T(8,128)(2,1)S(1)}) custom-call(f32[1024,1024]{1,0:T(8,128)} %bitcast.11, f32[512,2048]{1,0:T(8,128)} %bitcast.8, bf16[32,1024]{1,0:T(8,128)(2,1)} %bitcast.14, bf16[16,2048]{1,0:T(8,128)(2,1)} %bitcast.12), custom_call_target="tpu_custom_call" | custom-call | flops 1 | bytes 1 | tf_op jit(solution)/shard_map/unpack_weights/pallas_call | solution.py:202
  13.2 0.0 collective-permute-done
  13.2 0.0 collective-permute-done.1
  13.2 1.6 %collective-permute-start.3 = (bf16[32,4224]{1,0:T(8,128)(2,1)S(1)}, bf16[32,4224]{1,0:T(8,128)(2,1)S(1)}, u32[]{:S(2)}, u32[]{:S(2)}) collective-permute-start(bf16[32,4224]{1,0:T(8,128)(2,1)S(1)} %pad_maximum_fusion.refs_0_), channel_id=1, source_target_pairs={{0,2},{1,3},{2,0},{3,1},{4,6},{5,7},{6,4},{7,5},{8,10},{9,11},{10,... | collective-permute-start | bytes 811016 | tf_op jit(solution)/shard_map/ppermute | solution.py:408
  14.8 1.5 %collective-permute-start.6 = (bf16[32,4224]{1,0:T(8,128)(2,1)S(1)}, bf16[32,4224]{1,0:T(8,128)(2,1)S(1)}, u32[]{:S(2)}, u32[]{:S(2)}) collective-permute-start(bf16[32,4224]{1,0:T(8,128)(2,1)S(1)} %pad_maximum_fusion.refs_0_), channel_id=1, source_target_pairs={{0,16},{1,17},{2,18},{3,19},{4,20},{5,21},{6,22},{7,23},{8,24},{9,... | collective-permute-start | bytes 811016 | tf_op jit(solution)/shard_map/ppermute | solution.py:408
  16.3 4.2 %unpack_weights.4.refs_5_ = bf16[4096,1024]{1,0:T(8,128)(2,1)S(1)} custom-call(f32[1024,1024]{1,0:T(8,128)} %bitcast.10, bf16[32,1024]{1,0:T(8,128)(2,1)} %bitcast.15), custom_call_target="tpu_custom_call" | custom-call | flops 1 | bytes 1 | tf_op jit(solution)/shard_map/unpack_weights/pallas_call | solution.py:202
  20.5 0.4 collective-permute-done.3.refs_2_
  21.0 0.0 collective-permute-done.4.refs_1_
  21.0 0.0 collective-permute-start.5
  21.0 1.5 %collective-permute-start.8 = (bf16[32,4224]{1,0:T(8,128)(2,1)S(1)}, bf16[32,4224]{1,0:T(8,128)(2,1)S(1)}, u32[]{:S(2)}, u32[]{:S(2)}) collective-permute-start(bf16[32,4224]{1,0:T(8,128)(2,1)S(1)} %collective-permute-done.3.refs_2_), channel_id=1, source_target_pairs={{0,16},{1,17},{2,18},{3,19},{4,20},{5,21},{6,22},{7,23},{8,24},{9,... | collective-permute-start | bytes 811016 | tf_op jit(solution)/shard_map/ppermute | solution.py:408
  22.5 1.3 %collective-permute-done.6.refs_0_ = bf16[32,4224]{1,0:T(8,128)(2,1)S(1)} collective-permute-done((bf16[32,4224]{1,0:T(8,128)(2,1)S(1)}, bf16[32,4224]{1,0:T(8,128)(2,1)S(1)}, u32[]{:S(2)}, u32[]{:S(2)}) %collective-permute-start.6) | collective-permute-done | bytes 270368 | tf_op jit(solution)/shard_map/ppermute | solution.py:408
  23.7 2.6 %gate_up.2 = (bf16[144,1024]{1,0:T(8,128)(2,1)S(1)}, f32[128,128]{1,0:T(8,128)S(1)}) custom-call(s32[1]{0:T(128)} %bitcast.1.place_ref, bf16[32,4224]{1,0:T(8,128)(2,1)S(1)} %pad_maximum_fusion.refs_0_, bf16[32,4224]{1,0:T(8,128)(2,1)S(1)} %collective-permute-done.4.refs_1_, bf16[32,4224]{1,0:T(8,128)(2,1)S(1)} %collective-permute-done.3.refs_2_, ...), custom_call_target="tpu_custom_call" | custom-call | flops 1 | bytes 1 | tf_op jit(solution)/shard_map/gate_up/pallas_call | solution.py:247
  26.4 1.5 %collective-permute-start.10 = (bf16[144,1024]{1,0:T(8,128)(2,1)S(1)}, bf16[144,1024]{1,0:T(8,128)(2,1)S(1)}, u32[]{:S(2)}, u32[]{:S(2)}) collective-permute-start(bf16[144,1024]{1,0:T(8,128)(2,1)S(1)} %get-tuple-element.75.hidden_ref), channel_id=1, source_target_pairs={{0,16},{1,17},{2,18},{3,19},{4,20},{5,21},{6,22},{7,23},{8,24},{9,... | collective-permute-start | bytes 884744 | tf_op jit(solution)/shard_map/ppermute | solution.py:408
  27.9 0.0 collective-permute-start.7
  27.9 2.9 %unpack_weights.5.weight_refs_1_ = bf16[2048,1024]{1,0:T(8,128)(2,1)S(1)} custom-call(f32[512,2048]{1,0:T(8,128)} %bitcast.9, bf16[16,2048]{1,0:T(8,128)(2,1)} %bitcast.13), custom_call_target="tpu_custom_call" | custom-call | flops 1 | bytes 1 | tf_op jit(solution)/shard_map/unpack_weights/pallas_call | solution.py:202
  30.8 0.0 collective-permute-done.8.refs_2_
  30.8 0.6 collective-permute-start.9
  31.3 0.0 collective-permute-done.7.refs_1_
  31.4 1.2 %collective-permute-done.9.refs_3_ = bf16[32,4224]{1,0:T(8,128)(2,1)S(1)} collective-permute-done((bf16[32,4224]{1,0:T(8,128)(2,1)S(1)}, bf16[32,4224]{1,0:T(8,128)(2,1)S(1)}, u32[]{:S(2)}, u32[]{:S(2)}) %collective-permute-start.9) | collective-permute-done | bytes 270368 | tf_op jit(solution)/shard_map/ppermute | solution.py:408
  32.5 2.6 %gate_up.3 = (bf16[128,1024]{1,0:T(8,128)(2,1)S(1)}, f32[128,128]{1,0:T(8,128)S(1)}) custom-call(s32[1]{0:T(128)} %bitcast.1.place_ref, bf16[32,4224]{1,0:T(8,128)(2,1)S(1)} %collective-permute-done.6.refs_0_, bf16[32,4224]{1,0:T(8,128)(2,1)S(1)} %collective-permute-done.7.refs_1_, bf16[32,4224]{1,0:T(8,128)(2,1)S(1)} %collective-permute-done.8.refs_2_, ...), custom_call_target="tpu_custom_call" | custom-call | flops 1 | bytes 1 | tf_op jit(solution)/shard_map/gate_up/pallas_call | solution.py:247
  35.1 0.8 %collective-permute-start.14 = (bf16[128,1024]{1,0:T(8,128)(2,1)S(1)}, bf16[128,1024]{1,0:T(8,128)(2,1)S(1)}, u32[]{:S(2)}, u32[]{:S(2)}) collective-permute-start(bf16[128,1024]{1,0:T(8,128)(2,1)S(1)} %get-tuple-element.67.hidden_ref), channel_id=1, source_target_pairs={{0,16},{1,17},{2,18},{3,19},{4,20},{5,21},{6,22},{7,23},{8,24},{9,... | collective-permute-start | bytes 786440 | tf_op jit(solution)/shard_map/ppermute | solution.py:408
  36.0 0.7 %down_own.2.partial_ref = f32[128,2048]{1,0:T(8,128)S(1)} custom-call(s32[1]{0:T(128)} %bitcast.side_ref, bf16[128,1024]{1,0:T(8,128)(2,1)S(1)} %get-tuple-element.67.hidden_ref, bf16[2048,1024]{1,0:T(8,128)(2,1)S(1)} %get-tuple-element.68.weight_refs_0_, bf16[2048,1024]{1,0:T(8,128)(2,1)S(1)} %unpack_weights.5.weight_refs_1_), custom_call_target="tpu_custom_call" | custom-call | flops 1 | bytes 1 | tf_op jit(solution)/shard_map/down_own/pallas_call | solution.py:276
  36.7 0.0 collective-permute-done.10.hidden_ref
  36.7 0.8 %down_peer.2 = (bf16[64,2048]{1,0:T(8,128)(2,1)S(1)}, bf16[64,2048]{1,0:T(8,128)(2,1)S(1)}) custom-call(s32[1]{0:T(128)} %bitcast.side_ref, f32[128,2048]{1,0:T(8,128)S(1)} %down_own.2.partial_ref, bf16[144,1024]{1,0:T(8,128)(2,1)S(1)} %collective-permute-done.10.hidden_ref, bf16[2048,1024]{1,0:T(8,128)(2,1)S(1)} %get-tuple-element.68.weight_refs_0_, ...), custom_call_target="tpu_custom_call" | custom-call | flops 1 | bytes 1 | tf_op jit(solution)/shard_map/down_peer/pallas_call | solution.py:309
  37.5 1.6 %collective-permute-start.11 = (bf16[64,2048]{1,0:T(8,128)(2,1)S(1)}, bf16[64,2048]{1,0:T(8,128)(2,1)S(1)}, u32[]{:S(2)}, u32[]{:S(2)}) collective-permute-start(bf16[64,2048]{1,0:T(8,128)(2,1)S(1)} %get-tuple-element.72), channel_id=1, source_target_pairs={{0,2},{1,3},{2,0},{3,1},{4,6},{5,7},{6,4},{7,5},{8,10},{9,11},{10,... | collective-permute-start | bytes 786440 | tf_op jit(solution)/shard_map/ppermute | solution.py:408
  39.1 0.7 %down_own.3.partial_ref = f32[128,2048]{1,0:T(8,128)S(1)} custom-call(s32[1]{0:T(128)} %bitcast.side_ref, bf16[144,1024]{1,0:T(8,128)(2,1)S(1)} %get-tuple-element.75.hidden_ref, bf16[2048,1024]{1,0:T(8,128)(2,1)S(1)} %get-tuple-element.68.weight_refs_0_, bf16[2048,1024]{1,0:T(8,128)(2,1)S(1)} %unpack_weights.5.weight_refs_1_), custom_call_target="tpu_custom_call" | custom-call | flops 1 | bytes 1 | tf_op jit(solution)/shard_map/down_own/pallas_call | solution.py:276
  39.8 4.0 %collective-permute-done.14.hidden_ref = bf16[128,1024]{1,0:T(8,128)(2,1)S(1)} collective-permute-done((bf16[128,1024]{1,0:T(8,128)(2,1)S(1)}, bf16[128,1024]{1,0:T(8,128)(2,1)S(1)}, u32[]{:S(2)}, u32[]{:S(2)}) %collective-permute-start.14) | collective-permute-done | bytes 262176 | tf_op jit(solution)/shard_map/ppermute | solution.py:408
  43.8 0.8 %down_peer.3 = (bf16[32,2048]{1,0:T(8,128)(2,1)S(1)}, bf16[32,2048]{1,0:T(8,128)(2,1)S(1)}, bf16[32,2048]{1,0:T(8,128)(2,1)S(1)}, bf16[32,2048]{1,0:T(8,128)(2,1)S(1)}) custom-call(s32[1]{0:T(128)} %bitcast.side_ref, f32[128,2048]{1,0:T(8,128)S(1)} %down_own.3.partial_ref, bf16[128,1024]{1,0:T(8,128)(2,1)S(1)} %collective-permute-done.14.hidden_ref, ...), custom_call_target="tpu_custom_call" | custom-call | flops 1 | bytes 1 | tf_op jit(solution)/shard_map/down_peer/pallas_call | solution.py:309
  44.6 0.1 collective-permute-start.16
  44.7 1.0 %collective-permute-done.11.refs_1_ = bf16[64,2048]{1,0:T(8,128)(2,1)S(1)} collective-permute-done((bf16[64,2048]{1,0:T(8,128)(2,1)S(1)}, bf16[64,2048]{1,0:T(8,128)(2,1)S(1)}, u32[]{:S(2)}, u32[]{:S(2)}) %collective-permute-start.11) | collective-permute-done | bytes 262176 | tf_op jit(solution)/shard_map/ppermute | solution.py:408
  45.7 0.1 add_and_cut.3
  45.7 0.1 collective-permute-start.12
  45.8 0.5 collective-permute-start.15
  46.4 1.6 %collective-permute-start.17 = (bf16[32,2048]{1,0:T(8,128)(2,1)S(1)}, bf16[32,2048]{1,0:T(8,128)(2,1)S(1)}, u32[]{:S(2)}, u32[]{:S(2)}) collective-permute-start(bf16[32,2048]{1,0:T(8,128)(2,1)S(1)} %add_and_cut.5), channel_id=1, source_target_pairs={{0,2},{1,3},{2,0},{3,1},{4,6},{5,7},{6,4},{7,5},{8,10},{9,11},{10,... | collective-permute-start | bytes 393224 | tf_op jit(solution)/shard_map/ppermute | solution.py:408
  48.0 0.9 %collective-permute-start.13 = (bf16[32,2048]{1,0:T(8,128)(2,1)S(1)}, bf16[32,2048]{1,0:T(8,128)(2,1)S(1)}, u32[]{:S(2)}, u32[]{:S(2)}) collective-permute-start(bf16[32,2048]{1,0:T(8,128)(2,1)S(1)} %add_and_cut.4), channel_id=1, source_target_pairs={{0,16},{1,17},{2,18},{3,19},{4,20},{5,21},{6,22},{7,23},{8,24},{9,... | collective-permute-start | bytes 393224 | tf_op jit(solution)/shard_map/ppermute | solution.py:408
  48.9 3.1 %collective-permute-done.17.refs_2_ = bf16[32,2048]{1,0:T(8,128)(2,1)S(1)} collective-permute-done((bf16[32,2048]{1,0:T(8,128)(2,1)S(1)}, bf16[32,2048]{1,0:T(8,128)(2,1)S(1)}, u32[]{:S(2)}, u32[]{:S(2)}) %collective-permute-start.17) | collective-permute-done | bytes 131104 | tf_op jit(solution)/shard_map/ppermute | solution.py:408
  51.9 1.3 %collective-permute-done.13.far_ref = bf16[32,2048]{1,0:T(8,128)(2,1)S(1)} collective-permute-done((bf16[32,2048]{1,0:T(8,128)(2,1)S(1)}, bf16[32,2048]{1,0:T(8,128)(2,1)S(1)}, u32[]{:S(2)}, u32[]{:S(2)}) %collective-permute-start.13) | collective-permute-done | bytes 131104 | tf_op jit(solution)/shard_map/ppermute | solution.py:408
  53.2 0.1 join.1
  53.3 2.6 %collective-permute-start.18 = (bf16[16,2048]{1,0:T(8,128)(2,1)S(1)}, bf16[16,2048]{1,0:T(8,128)(2,1)S(1)}, u32[]{:S(2)}, u32[]{:S(2)}) collective-permute-start(bf16[16,2048]{1,0:T(8,128)(2,1)S(1)} %get-tuple-element.82), channel_id=1, source_target_pairs={{0,8},{1,9},{2,10},{3,11},{4,12},{5,13},{6,14},{7,15},{8,0},{9,1},... | collective-permute-start | bytes 196616 | tf_op jit(solution)/shard_map/ppermute | solution.py:408
  55.9 1.4 %collective-permute-start.19 = (bf16[16,2048]{1,0:T(8,128)(2,1)S(1)}, bf16[16,2048]{1,0:T(8,128)(2,1)S(1)}, u32[]{:S(2)}, u32[]{:S(2)}) collective-permute-start(bf16[16,2048]{1,0:T(8,128)(2,1)S(1)} %get-tuple-element.83), channel_id=1, source_target_pairs={{0,12},{1,13},{2,14},{3,15},{4,8},{5,9},{6,10},{7,11},{8,4},{9,5},... | collective-permute-start | bytes 196616 | tf_op jit(solution)/shard_map/ppermute | solution.py:408
  57.3 1.7 %collective-permute-done.18.refs_1_ = bf16[16,2048]{1,0:T(8,128)(2,1)S(1)} collective-permute-done((bf16[16,2048]{1,0:T(8,128)(2,1)S(1)}, bf16[16,2048]{1,0:T(8,128)(2,1)S(1)}, u32[]{:S(2)}, u32[]{:S(2)}) %collective-permute-start.18) | collective-permute-done | bytes 65568 | tf_op jit(solution)/shard_map/ppermute | solution.py:408
  59.0 3.1 %collective-permute-done.19.refs_2_ = bf16[16,2048]{1,0:T(8,128)(2,1)S(1)} collective-permute-done((bf16[16,2048]{1,0:T(8,128)(2,1)S(1)}, bf16[16,2048]{1,0:T(8,128)(2,1)S(1)}, u32[]{:S(2)}, u32[]{:S(2)}) %collective-permute-start.19) | collective-permute-done | bytes 65568 | tf_op jit(solution)/shard_map/ppermute | solution.py:408
  62.1 0.2 collective-permute-done.20.refs_3_
  62.2 0.7 %finish.1 = bf16[8,4096]{1,0:T(8,128)(2,1)} custom-call(s32[1]{0:T(128)} %bitcast.side_ref, bf16[8,4096]{1,0:T(8,128)(2,1)S(1)} %get-tuple-element.47.mixed_ref, bf16[16,2048]{1,0:T(8,128)(2,1)S(1)} %get-tuple-element.81.refs_0_, bf16[16,2048]{1,0:T(8,128)(2,1)S(1)} %collective-permute-done.18.refs_1_, bf16[16,2048]{1,0:T(8,128)(2,1)S(1)} %collective-permute-done.19.refs_2_, ...), custom_call_target="tpu_custom_call" | custom-call | tf_op jit(solution)/shard_map/finish/pallas_call | solution.py:387
  (10 shorter events, 0.1 us)
Async XLA Ops:
  2.0 11.2 %collective-permute-start = (bf16[8,4224]{1,0:T(8,128)(2,1)S(1)}, bf16[8,4224]{1,0:T(8,128)(2,1)S(1)}, u32[]{:S(2)}, u32[]{:S(2)}) collective-permute-start(bf16[8,4224]{1,0:T(8,128)(2,1)S(1)} %get-tuple-element.49), channel_id=1, source_target_pairs={{0,8},{1,9},{2,10},{3,11},{4,12},{5,13},{6,14},{7,15},{8,0},{9,1},... | collective-permute-start | bytes 202760 | tf_op jit(solution)/shard_map/ppermute | solution.py:408
  6.1 7.1 %collective-permute-start.1 = (bf16[8,4224]{1,0:T(8,128)(2,1)S(1)}, bf16[8,4224]{1,0:T(8,128)(2,1)S(1)}, u32[]{:S(2)}, u32[]{:S(2)}) collective-permute-start(bf16[8,4224]{1,0:T(8,128)(2,1)S(1)} %get-tuple-element.49), channel_id=1, source_target_pairs={{0,12},{1,13},{2,14},{3,15},{4,8},{5,9},{6,10},{7,11},{8,4},{9,5},... | collective-permute-start | bytes 202760 | tf_op jit(solution)/shard_map/ppermute | solution.py:408
  7.4 5.8 %collective-permute-start.2 = (bf16[8,4224]{1,0:T(8,128)(2,1)S(1)}, bf16[8,4224]{1,0:T(8,128)(2,1)S(1)}, u32[]{:S(2)}, u32[]{:S(2)}) collective-permute-start(bf16[8,4224]{1,0:T(8,128)(2,1)S(1)} %get-tuple-element.49), channel_id=1, source_target_pairs={{0,4},{1,5},{2,6},{3,7},{4,0},{5,1},{6,2},{7,3},{8,12},{9,13},{10,... | collective-permute-start | bytes 202760 | tf_op jit(solution)/shard_map/ppermute | solution.py:408
  13.2 7.7 %collective-permute-start.3 = (bf16[32,4224]{1,0:T(8,128)(2,1)S(1)}, bf16[32,4224]{1,0:T(8,128)(2,1)S(1)}, u32[]{:S(2)}, u32[]{:S(2)}) collective-permute-start(bf16[32,4224]{1,0:T(8,128)(2,1)S(1)} %pad_maximum_fusion.refs_0_), channel_id=1, source_target_pairs={{0,2},{1,3},{2,0},{3,1},{4,6},{5,7},{6,4},{7,5},{8,10},{9,11},{10,... | collective-permute-start | bytes 811016 | tf_op jit(solution)/shard_map/ppermute | solution.py:408
  14.8 6.1 %collective-permute-start.4 = (bf16[32,4224]{1,0:T(8,128)(2,1)S(1)}, bf16[32,4224]{1,0:T(8,128)(2,1)S(1)}, u32[]{:S(2)}, u32[]{:S(2)}) collective-permute-start(bf16[32,4224]{1,0:T(8,128)(2,1)S(1)} %pad_maximum_fusion.refs_0_), channel_id=1, source_target_pairs={{0,1},{1,0},{2,3},{3,2},{4,5},{5,4},{6,7},{7,6},{8,9},{9,8},{10,11... | collective-permute-start | bytes 811016 | tf_op jit(solution)/shard_map/ppermute | solution.py:408
  14.8 8.9 %collective-permute-start.6 = (bf16[32,4224]{1,0:T(8,128)(2,1)S(1)}, bf16[32,4224]{1,0:T(8,128)(2,1)S(1)}, u32[]{:S(2)}, u32[]{:S(2)}) collective-permute-start(bf16[32,4224]{1,0:T(8,128)(2,1)S(1)} %pad_maximum_fusion.refs_0_), channel_id=1, source_target_pairs={{0,16},{1,17},{2,18},{3,19},{4,20},{5,21},{6,22},{7,23},{8,24},{9,... | collective-permute-start | bytes 811016 | tf_op jit(solution)/shard_map/ppermute | solution.py:408
  21.0 2.8 %collective-permute-start.5 = (bf16[32,4224]{1,0:T(8,128)(2,1)S(1)}, bf16[32,4224]{1,0:T(8,128)(2,1)S(1)}, u32[]{:S(2)}, u32[]{:S(2)}) collective-permute-start(bf16[32,4224]{1,0:T(8,128)(2,1)S(1)} %collective-permute-done.3.refs_2_), channel_id=1, source_target_pairs={{0,1},{1,0},{2,3},{3,2},{4,5},{5,4},{6,7},{7,6},{8,9},{9,8},{10,11... | collective-permute-start | bytes 811016 | tf_op jit(solution)/shard_map/ppermute | solution.py:408
  21.0 9.8 %collective-permute-start.8 = (bf16[32,4224]{1,0:T(8,128)(2,1)S(1)}, bf16[32,4224]{1,0:T(8,128)(2,1)S(1)}, u32[]{:S(2)}, u32[]{:S(2)}) collective-permute-start(bf16[32,4224]{1,0:T(8,128)(2,1)S(1)} %collective-permute-done.3.refs_2_), channel_id=1, source_target_pairs={{0,16},{1,17},{2,18},{3,19},{4,20},{5,21},{6,22},{7,23},{8,24},{9,... | collective-permute-start | bytes 811016 | tf_op jit(solution)/shard_map/ppermute | solution.py:408
  26.4 10.4 %collective-permute-start.10 = (bf16[144,1024]{1,0:T(8,128)(2,1)S(1)}, bf16[144,1024]{1,0:T(8,128)(2,1)S(1)}, u32[]{:S(2)}, u32[]{:S(2)}) collective-permute-start(bf16[144,1024]{1,0:T(8,128)(2,1)S(1)} %get-tuple-element.75.hidden_ref), channel_id=1, source_target_pairs={{0,16},{1,17},{2,18},{3,19},{4,20},{5,21},{6,22},{7,23},{8,24},{9,... | collective-permute-start | bytes 884744 | tf_op jit(solution)/shard_map/ppermute | solution.py:408
  27.9 3.5 %collective-permute-start.7 = (bf16[32,4224]{1,0:T(8,128)(2,1)S(1)}, bf16[32,4224]{1,0:T(8,128)(2,1)S(1)}, u32[]{:S(2)}, u32[]{:S(2)}) collective-permute-start(bf16[32,4224]{1,0:T(8,128)(2,1)S(1)} %collective-permute-done.6.refs_0_), channel_id=1, source_target_pairs={{0,1},{1,0},{2,3},{3,2},{4,5},{5,4},{6,7},{7,6},{8,9},{9,8},{10,11... | collective-permute-start | bytes 811016 | tf_op jit(solution)/shard_map/ppermute | solution.py:408
  30.8 1.7 %collective-permute-start.9 = (bf16[32,4224]{1,0:T(8,128)(2,1)S(1)}, bf16[32,4224]{1,0:T(8,128)(2,1)S(1)}, u32[]{:S(2)}, u32[]{:S(2)}) collective-permute-start(bf16[32,4224]{1,0:T(8,128)(2,1)S(1)} %collective-permute-done.8.refs_2_), channel_id=1, source_target_pairs={{0,1},{1,0},{2,3},{3,2},{4,5},{5,4},{6,7},{7,6},{8,9},{9,8},{10,11... | collective-permute-start | bytes 811016 | tf_op jit(solution)/shard_map/ppermute | solution.py:408
  35.1 8.6 %collective-permute-start.14 = (bf16[128,1024]{1,0:T(8,128)(2,1)S(1)}, bf16[128,1024]{1,0:T(8,128)(2,1)S(1)}, u32[]{:S(2)}, u32[]{:S(2)}) collective-permute-start(bf16[128,1024]{1,0:T(8,128)(2,1)S(1)} %get-tuple-element.67.hidden_ref), channel_id=1, source_target_pairs={{0,16},{1,17},{2,18},{3,19},{4,20},{5,21},{6,22},{7,23},{8,24},{9,... | collective-permute-start | bytes 786440 | tf_op jit(solution)/shard_map/ppermute | solution.py:408
  37.5 8.1 %collective-permute-start.11 = (bf16[64,2048]{1,0:T(8,128)(2,1)S(1)}, bf16[64,2048]{1,0:T(8,128)(2,1)S(1)}, u32[]{:S(2)}, u32[]{:S(2)}) collective-permute-start(bf16[64,2048]{1,0:T(8,128)(2,1)S(1)} %get-tuple-element.72), channel_id=1, source_target_pairs={{0,2},{1,3},{2,0},{3,1},{4,6},{5,7},{6,4},{7,5},{8,10},{9,11},{10,... | collective-permute-start | bytes 786440 | tf_op jit(solution)/shard_map/ppermute | solution.py:408
  44.6 1.7 %collective-permute-start.16 = (bf16[32,2048]{1,0:T(8,128)(2,1)S(1)}, bf16[32,2048]{1,0:T(8,128)(2,1)S(1)}, u32[]{:S(2)}, u32[]{:S(2)}) collective-permute-start(bf16[32,2048]{1,0:T(8,128)(2,1)S(1)} %get-tuple-element.80), channel_id=1, source_target_pairs={{0,1},{1,0},{2,3},{3,2},{4,5},{5,4},{6,7},{7,6},{8,9},{9,8},{10,11... | collective-permute-start | bytes 393224 | tf_op jit(solution)/shard_map/ppermute | solution.py:408
  45.7 2.2 %collective-permute-start.12 = (bf16[32,2048]{1,0:T(8,128)(2,1)S(1)}, bf16[32,2048]{1,0:T(8,128)(2,1)S(1)}, u32[]{:S(2)}, u32[]{:S(2)}) collective-permute-start(bf16[32,2048]{1,0:T(8,128)(2,1)S(1)} %get-tuple-element.74), channel_id=1, source_target_pairs={{0,1},{1,0},{2,3},{3,2},{4,5},{5,4},{6,7},{7,6},{8,9},{9,8},{10,11... | collective-permute-start | bytes 393224 | tf_op jit(solution)/shard_map/ppermute | solution.py:408
  45.8 3.0 %collective-permute-start.15 = (bf16[32,2048]{1,0:T(8,128)(2,1)S(1)}, bf16[32,2048]{1,0:T(8,128)(2,1)S(1)}, u32[]{:S(2)}, u32[]{:S(2)}) collective-permute-start(bf16[32,2048]{1,0:T(8,128)(2,1)S(1)} %get-tuple-element.78), channel_id=1, source_target_pairs={{0,1},{1,0},{2,3},{3,2},{4,5},{5,4},{6,7},{7,6},{8,9},{9,8},{10,11... | collective-permute-start | bytes 393224 | tf_op jit(solution)/shard_map/ppermute | solution.py:408
  46.4 5.5 %collective-permute-start.17 = (bf16[32,2048]{1,0:T(8,128)(2,1)S(1)}, bf16[32,2048]{1,0:T(8,128)(2,1)S(1)}, u32[]{:S(2)}, u32[]{:S(2)}) collective-permute-start(bf16[32,2048]{1,0:T(8,128)(2,1)S(1)} %add_and_cut.5), channel_id=1, source_target_pairs={{0,2},{1,3},{2,0},{3,1},{4,6},{5,7},{6,4},{7,5},{8,10},{9,11},{10,... | collective-permute-start | bytes 393224 | tf_op jit(solution)/shard_map/ppermute | solution.py:408
  48.0 5.3 %collective-permute-start.13 = (bf16[32,2048]{1,0:T(8,128)(2,1)S(1)}, bf16[32,2048]{1,0:T(8,128)(2,1)S(1)}, u32[]{:S(2)}, u32[]{:S(2)}) collective-permute-start(bf16[32,2048]{1,0:T(8,128)(2,1)S(1)} %add_and_cut.4), channel_id=1, source_target_pairs={{0,16},{1,17},{2,18},{3,19},{4,20},{5,21},{6,22},{7,23},{8,24},{9,... | collective-permute-start | bytes 393224 | tf_op jit(solution)/shard_map/ppermute | solution.py:408
  53.3 5.7 %collective-permute-start.18 = (bf16[16,2048]{1,0:T(8,128)(2,1)S(1)}, bf16[16,2048]{1,0:T(8,128)(2,1)S(1)}, u32[]{:S(2)}, u32[]{:S(2)}) collective-permute-start(bf16[16,2048]{1,0:T(8,128)(2,1)S(1)} %get-tuple-element.82), channel_id=1, source_target_pairs={{0,8},{1,9},{2,10},{3,11},{4,12},{5,13},{6,14},{7,15},{8,0},{9,1},... | collective-permute-start | bytes 196616 | tf_op jit(solution)/shard_map/ppermute | solution.py:408
  55.9 6.2 %collective-permute-start.19 = (bf16[16,2048]{1,0:T(8,128)(2,1)S(1)}, bf16[16,2048]{1,0:T(8,128)(2,1)S(1)}, u32[]{:S(2)}, u32[]{:S(2)}) collective-permute-start(bf16[16,2048]{1,0:T(8,128)(2,1)S(1)} %get-tuple-element.83), channel_id=1, source_target_pairs={{0,12},{1,13},{2,14},{3,15},{4,8},{5,9},{6,10},{7,11},{8,4},{9,5},... | collective-permute-start | bytes 196616 | tf_op jit(solution)/shard_map/ppermute | solution.py:408
  57.3 5.0 %collective-permute-start.20 = (bf16[16,2048]{1,0:T(8,128)(2,1)S(1)}, bf16[16,2048]{1,0:T(8,128)(2,1)S(1)}, u32[]{:S(2)}, u32[]{:S(2)}) collective-permute-start(bf16[16,2048]{1,0:T(8,128)(2,1)S(1)} %get-tuple-element.84), channel_id=1, source_target_pairs={{0,4},{1,5},{2,6},{3,7},{4,0},{5,1},{6,2},{7,3},{8,12},{9,13},{10,... | collective-permute-start | bytes 196616 | tf_op jit(solution)/shard_map/ppermute | solution.py:408
